TPU v7x, 32 devices: a whole 2x2x4 slice. The times are simulated.
32 devices in a mesh: seq: 8 (over y, x, core), wshard: 4 (over z).
Axes of the slice: x: 2, y: 2, z: 4, core: 2. Of those that a mesh axis runs over, the one named last changes fastest.
Arguments:
- hidden: bfloat16 [2, 4, 2048, 1536], P(None, 'wshard', 'seq'), may hold values from -6 to 6
- lengths: int32 [2, 4], P(None, 'wshard'), may hold values from 512 to 2048, as said below
- out_grad: bfloat16 [2, 4, 2048, 1536], P(None, 'wshard', 'seq'), may hold values from -6 to 6
- norm_gain: bfloat16 [1536], P('wshard'), may hold values from 0.099609375 to 1.8984375
- in_weight: bfloat16 [1536, 6448], P('wshard'), may hold values from -0.15625 to 0.15625
- conv_weight: bfloat16 [3328, 4], P('wshard'), may hold values from -0.5 to 0.5
- conv_bias: bfloat16 [3328], P('wshard'), may hold values from -0.5 to 0.5
- dt_bias: bfloat16 [48], P('wshard'), may hold values from -8 to -3
- a_log: bfloat16 [48], P('wshard'), may hold values from -1 to 1
- skip_gain: bfloat16 [48], P('wshard'), may hold values from 0.5 to 1.5
- gated_gain: bfloat16 [3072], P('wshard'), may hold values from 0.099609375 to 1.8984375
- out_weight: bfloat16 [3072, 1536], P('wshard'), may hold values from -0.109375 to 0.109375
Outputs:
- output: bfloat16 [2, 4, 2048, 1536], P(None, 'wshard', 'seq')
- input_grad: bfloat16 [2, 4, 2048, 1536], P(None, 'wshard', 'seq')
- norm_gain_grad: float32 [1536], P('wshard')
- in_weight_grad: float32 [1536, 6448], P('wshard')
- conv_weight_grad: float32 [3328, 4], P('wshard')
- conv_bias_grad: float32 [3328], P('wshard')
- dt_bias_grad: float32 [48], P('wshard')
- a_log_grad: float32 [48], P('wshard')
- skip_gain_grad: float32 [48], P('wshard')
- gated_gain_grad: float32 [3072], P('wshard')
- out_weight_grad: float32 [3072, 1536], P('wshard')
Inputs may be any that keep to these rules, and one draw needn't show every extreme that they name: `lengths`: for every sequence index, one micro-batch drawn from the seed has length 2048.
All inputs are finite; a program needn't handle non-finite values.
Results may differ from a plain program's by a relative error of at most 0.011.
Values may be sent and summed in bfloat16 or wider, within the bound.
A program may use at most 256 MiB of HBM per device.

v0:
```python
from functools import partial

import jax
import jax.numpy as jnp
from jax import lax
from jax.sharding import PartitionSpec as P

STRETCH = 256


epsilon = 1e-05
highest = lax.Precision.HIGHEST


def from_behind(x, axis, by):
    count = lax.axis_size(axis)
    pairs = [(i, i + by) for i in range(count) if 0 <= i + by < count]
    return lax.ppermute(x, axis, pairs)


def rms_front(hidden_rows, gain):
    power = jnp.mean(hidden_rows * hidden_rows, axis=-1, keepdims=True)
    return hidden_rows * lax.rsqrt(power + epsilon) * gain


def conv_act(padded, conv_w, conv_b):
    taps = conv_w.shape[1]
    rows_out = padded.shape[0] - taps + 1
    total = conv_b[None, :] + padded[0:rows_out] * conv_w[:, 0]
    for offset in range(1, taps):
        total = total + padded[offset : offset + rows_out] * conv_w[:, offset]
    return jax.nn.silu(total)


def gate_norm(values, gate_in, gain):
    gated = values * jax.nn.silu(gate_in)
    power = jnp.mean(gated * gated, axis=-1, keepdims=True)
    return gated * lax.rsqrt(power + epsilon) * gain


def ssd_scan(x_heads, dt_raw, b_rows, c_rows, dt_shift, a_logs, skip, block_len):
    seq_length, head_count, head_size = x_heads.shape
    blocks = seq_length // block_len
    state_dim = b_rows.shape[1]
    steps_dt = jax.nn.softplus(dt_raw + dt_shift[None, :])
    log_decay = steps_dt * (-jnp.exp(a_logs))[None, :]
    causal = jnp.arange(block_len)[:, None] >= jnp.arange(block_len)[None, :]

    def advance(carry_state, pieces):
        x_blk, dt_blk, decay_blk, b_blk, c_blk = pieces
        cumulative = jnp.cumsum(decay_blk, axis=0)
        across = cumulative.T
        spans = across[:, :, None] - across[:, None, :]
        within = jnp.where(causal[None], jnp.exp(jnp.where(causal[None], spans, 0.0)), 0.0)
        scores = jnp.dot(c_blk, b_blk.T, precision=highest)
        weighted = x_blk * dt_blk[:, :, None]
        local_part = jnp.einsum("hij,jhp->ihp", within * scores[None], weighted, precision=highest)
        carried = jnp.exp(cumulative)[:, :, None] * jnp.einsum(
            "in,hpn->ihp", c_blk, carry_state, precision=highest
        )
        to_end = jnp.exp(cumulative[-1][None, :] - cumulative)
        new_state = jnp.exp(cumulative[-1])[:, None, None] * carry_state + jnp.einsum(
            "jhp,jn->hpn", weighted * to_end[:, :, None], b_blk, precision=highest
        )
        return (new_state, local_part + carried)

    pieces = (
        x_heads.reshape(blocks, block_len, head_count, head_size),
        steps_dt.reshape(blocks, block_len, head_count),
        log_decay.reshape(blocks, block_len, head_count),
        b_rows.reshape(blocks, block_len, state_dim),
        c_rows.reshape(blocks, block_len, state_dim),
    )
    initial = jnp.zeros((head_count, head_size, state_dim), jnp.float32)
    last_state, results = lax.scan(jax.checkpoint(advance), initial, pieces)
    return results.reshape(seq_length, head_count, head_size) + skip[None, :, None] * x_heads


def local(
    hidden,
    lengths,
    out_grad,
    norm_gain,
    in_weight,
    conv_weight,
    conv_bias,
    dt_bias,
    a_log,
    skip_gain,
    gated_gain,
    out_weight,
):
    gathered = (
        lax.all_gather(norm_gain, "wshard", axis=0, tiled=True),
        lax.all_gather(in_weight, "wshard", axis=0, tiled=True),
        lax.all_gather(conv_weight, "wshard", axis=0, tiled=True),
        lax.all_gather(conv_bias, "wshard", axis=0, tiled=True),
        lax.all_gather(dt_bias, "wshard", axis=0, tiled=True),
        lax.all_gather(a_log, "wshard", axis=0, tiled=True),
        lax.all_gather(skip_gain, "wshard", axis=0, tiled=True),
        lax.all_gather(gated_gain, "wshard", axis=0, tiled=True),
        lax.all_gather(out_weight, "wshard", axis=0, tiled=True),
    )
    norm_g = gathered[0].astype(jnp.float32)
    in_w = gathered[1]
    conv_w = gathered[2].astype(jnp.float32)
    conv_b = gathered[3].astype(jnp.float32)
    dt_shift = gathered[4].astype(jnp.float32)
    a_logs = gathered[5].astype(jnp.float32)
    skip_all = gathered[6].astype(jnp.float32)
    gated_g = gathered[7].astype(jnp.float32)
    out_w = gathered[8]
    groups = lax.axis_size("seq")
    rank = lax.axis_index("seq")
    tokens = hidden.shape[2]
    seq_length = tokens * groups
    inner_dim = out_w.shape[0]
    channels = conv_w.shape[0]
    taps = conv_w.shape[1]
    head_count = dt_shift.shape[0]
    head_block = head_count // groups
    head_size = inner_dim // head_count
    state_dim = (channels - inner_dim) // 2
    first_head = rank * head_block
    dt_mine = lax.dynamic_slice_in_dim(dt_shift, first_head, head_block)
    alog_mine = lax.dynamic_slice_in_dim(a_logs, first_head, head_block)
    skip_mine = lax.dynamic_slice_in_dim(skip_all, first_head, head_block)
    positions = rank * tokens + jnp.arange(tokens, dtype=jnp.int32)
    head_zeros = jnp.zeros((head_count,), jnp.float32)
    acc_norm = jnp.zeros_like(norm_g)
    acc_in = jnp.zeros(in_w.shape, jnp.float32)
    acc_conv_w = jnp.zeros_like(conv_w)
    acc_conv_b = jnp.zeros_like(conv_b)
    acc_dt = head_zeros
    acc_alog = head_zeros
    acc_skip = head_zeros
    acc_gated = jnp.zeros_like(gated_g)
    acc_out = jnp.zeros(out_w.shape, jnp.float32)
    out_list = []
    grad_list = []
    for micro in range(hidden.shape[0]):
        rows_in = hidden[micro, 0].astype(jnp.float32)
        cotangent = out_grad[micro, 0].astype(jnp.float32)
        valid = (positions < lengths[micro, 0]).astype(jnp.float32)
        normed, front_back = jax.vjp(rms_front, rows_in, norm_g)
        normed_low = normed.astype(jnp.bfloat16)
        projected = jnp.dot(normed_low, in_w, preferred_element_type=jnp.float32)
        gate_in = projected[:, :inner_dim]
        conv_low = projected[:, inner_dim : inner_dim + channels].astype(jnp.bfloat16)
        dt_low = projected[:, inner_dim + channels :].astype(jnp.bfloat16)
        prior_rows = from_behind(conv_low[tokens - (taps - 1) :], "seq", 1)
        padded = jnp.concatenate([prior_rows, conv_low], axis=0).astype(jnp.float32)
        mixed, conv_back = jax.vjp(conv_act, padded, conv_w, conv_b)
        x_low = mixed[:, :inner_dim].astype(jnp.bfloat16)
        bc_low = mixed[:, inner_dim:].astype(jnp.bfloat16)
        x_send = x_low.reshape(tokens, groups, head_block * head_size)
        dt_send = dt_low.reshape(tokens, groups, head_block)
        bc_send = jnp.broadcast_to(bc_low[:, None, :], (tokens, groups, 2 * state_dim))
        x_recv, dt_recv, bc_recv = (
            lax.all_to_all(x_send, "seq", split_axis=1, concat_axis=0, tiled=True),
            lax.all_to_all(dt_send, "seq", split_axis=1, concat_axis=0, tiled=True),
            lax.all_to_all(bc_send, "seq", split_axis=1, concat_axis=0, tiled=True),
        )
        bc_whole = bc_recv.reshape(seq_length, 2 * state_dim)
        x_heads = x_recv.reshape(seq_length, head_block, head_size).astype(jnp.float32)
        dt_heads = dt_recv.reshape(seq_length, head_block).astype(jnp.float32)
        b_whole = bc_whole[:, :state_dim].astype(jnp.float32)
        c_whole = bc_whole[:, state_dim:].astype(jnp.float32)
        scanned, scan_back = jax.vjp(
            partial(ssd_scan, block_len=STRETCH),
            x_heads,
            dt_heads,
            b_whole,
            c_whole,
            dt_mine,
            alog_mine,
            skip_mine,
        )
        scan_send = scanned.astype(jnp.bfloat16).reshape(seq_length, 1, head_block * head_size)
        scan_tok = lax.all_to_all(
            scan_send, "seq", split_axis=0, concat_axis=1, tiled=True
        ).reshape(tokens, inner_dim)
        normed_out, gate_back = jax.vjp(gate_norm, scan_tok.astype(jnp.float32), gate_in, gated_g)
        normed_out_low = normed_out.astype(jnp.bfloat16)
        branch = jnp.dot(normed_out_low, out_w, preferred_element_type=jnp.float32)
        out_list.append((rows_in + valid[:, None] * branch).astype(jnp.bfloat16))
        branch_grad = (cotangent * valid[:, None]).astype(jnp.bfloat16)
        acc_out = acc_out + jnp.dot(
            normed_out_low.T, branch_grad, preferred_element_type=jnp.float32
        )
        d_normed_out = jnp.dot(branch_grad, out_w.T, preferred_element_type=jnp.float32)
        d_scanned, d_gate_in, d_gated = gate_back(d_normed_out)
        acc_gated = acc_gated + d_gated
        grad_send = d_scanned.astype(jnp.bfloat16).reshape(tokens, groups, head_block * head_size)
        grad_heads = lax.all_to_all(grad_send, "seq", split_axis=1, concat_axis=0, tiled=True)
        grad_heads = grad_heads.reshape(seq_length, head_block, head_size).astype(jnp.float32)
        d_x_heads, d_dt_heads, d_b_whole, d_c_whole, d_dt_mine, d_alog_mine, d_skip_mine = (
            scan_back(grad_heads)
        )
        acc_dt = acc_dt + lax.dynamic_update_slice_in_dim(head_zeros, d_dt_mine, first_head, 0)
        acc_alog = acc_alog + lax.dynamic_update_slice_in_dim(
            head_zeros, d_alog_mine, first_head, 0
        )
        acc_skip = acc_skip + lax.dynamic_update_slice_in_dim(
            head_zeros, d_skip_mine, first_head, 0
        )
        dx_send = d_x_heads.astype(jnp.bfloat16).reshape(seq_length, 1, head_block * head_size)
        ddt_send = d_dt_heads.astype(jnp.bfloat16).reshape(seq_length, 1, head_block)
        dx_tok, ddt_tok = (
            lax.all_to_all(dx_send, "seq", split_axis=0, concat_axis=1, tiled=True),
            lax.all_to_all(ddt_send, "seq", split_axis=0, concat_axis=1, tiled=True),
        )
        bc_terms = jnp.concatenate([d_b_whole, d_c_whole], axis=1)
        bc_parts = lax.all_to_all(
            bc_terms.reshape(seq_length, 1, 2 * state_dim).astype(jnp.bfloat16),
            "seq",
            split_axis=0,
            concat_axis=1,
            tiled=True,
        ).astype(jnp.float32)
        bc_grad = jnp.sum(bc_parts, axis=1)
        mixed_grad = jnp.concatenate(
            [dx_tok.reshape(tokens, inner_dim).astype(jnp.float32), bc_grad], axis=1
        )
        d_padded, d_conv_w, d_conv_b = conv_back(mixed_grad)
        acc_conv_w = acc_conv_w + d_conv_w
        acc_conv_b = acc_conv_b + d_conv_b
        from_next = from_behind(d_padded[: taps - 1].astype(jnp.bfloat16), "seq", -1).astype(
            jnp.float32
        )
        d_conv_in = d_padded[taps - 1 :].at[tokens - (taps - 1) :].add(from_next)
        d_projected = jnp.concatenate(
            [d_gate_in, d_conv_in, ddt_tok.reshape(tokens, head_count).astype(jnp.float32)], axis=1
        ).astype(jnp.bfloat16)
        acc_in = acc_in + jnp.dot(normed_low.T, d_projected, preferred_element_type=jnp.float32)
        d_normed = jnp.dot(d_projected, in_w.T, preferred_element_type=jnp.float32)
        d_hidden, d_norm_g = front_back(d_normed)
        acc_norm = acc_norm + d_norm_g
        grad_list.append((d_hidden + cotangent).astype(jnp.bfloat16))
    shards = (
        lax.psum_scatter(acc_norm, "wshard", scatter_dimension=0, tiled=True),
        lax.psum_scatter(acc_in, "wshard", scatter_dimension=0, tiled=True),
        lax.psum_scatter(acc_conv_w, "wshard", scatter_dimension=0, tiled=True),
        lax.psum_scatter(acc_conv_b, "wshard", scatter_dimension=0, tiled=True),
        lax.psum_scatter(acc_dt, "wshard", scatter_dimension=0, tiled=True),
        lax.psum_scatter(acc_alog, "wshard", scatter_dimension=0, tiled=True),
        lax.psum_scatter(acc_skip, "wshard", scatter_dimension=0, tiled=True),
        lax.psum_scatter(acc_gated, "wshard", scatter_dimension=0, tiled=True),
        lax.psum_scatter(acc_out, "wshard", scatter_dimension=0, tiled=True),
    )
    totals = lax.psum(
        (
            shards[0],
            shards[1],
            shards[2],
            shards[3],
            shards[4],
            shards[5],
            shards[6],
            shards[7],
            shards[8],
        ),
        "seq",
    )
    output = jnp.stack(out_list)[:, None]
    input_grad = jnp.stack(grad_list)[:, None]
    return (
        output,
        input_grad,
        totals[0],
        totals[1],
        totals[2],
        totals[3],
        totals[4],
        totals[5],
        totals[6],
        totals[7],
        totals[8],
    )


def solution(mesh):
    return jax.shard_map(
        local,
        mesh=mesh,
        in_specs=(
            P(None, "wshard", "seq", None),
            P(None, "wshard"),
            P(None, "wshard", "seq", None),
            P("wshard"),
            P("wshard", None),
            P("wshard", None),
            P("wshard"),
            P("wshard"),
            P("wshard"),
            P("wshard"),
            P("wshard"),
            P("wshard", None),
        ),
        out_specs=(
            P(None, "wshard", "seq", None),
            P(None, "wshard", "seq", None),
            P("wshard"),
            P("wshard", None),
            P("wshard", None),
            P("wshard"),
            P("wshard"),
            P("wshard"),
            P("wshard"),
            P("wshard"),
            P("wshard", None),
        ),
        check_vma=False,
    )
```

profile of v0, /device:TPU:0, one launch (start us, length us, event | category | flops | bytes accessed | tf_op | source)
XLA Modules:
  0.0 2774.9 jit_solution(9382950742292388579)
XLA Ops:
  8.0 13.5 all-gather
  23.6 13.2 all-gather.1
  37.9 33.1 %all-reduce.33 = (bf16[48]{0:T(256)(128)(2,1)S(1)}, bf16[48]{0:T(256)(128)(2,1)S(1)}, bf16[3328]{0:T(1024)(128)(2,1)S(1)}, bf16[48]{0:T(256)(128)(2,1)}) all-reduce(bf16[48]{0:T(256)(128)(2,1)S(1)} %dynamic-update-slice.9, bf16[48]{0:T(256)(128)(2,1)S(1)} %dynamic-update-slice.12, ...), channel_id=1, replica_groups=mesh['seq'=8,'wshard'=4] {'wshard'}, use_global_device_ids=true, to_apply=%add.20 | all-reduce | flops 3472 | bytes 13888
  71.7 279.5 %all-gather.6.cloned.1.call-done = bf16[1536,6448]{0,1:T(8,128)(2,1)} async-done(((bf16[384,6448]{0,1:T(8,128)(2,1)}), bf16[1536,6448]{0,1:T(8,128)(2,1)}) %all-gather.6.cloned.1.call-update) | async-done | bytes 19808272 | tf_op jit(solution)/shard_map/all_gather | solution.py:95
  351.3 12.8 fusion.267
  369.7 12.9 fusion.268
  409.1 21.6 multiply_convert_fusion.1
  437.4 15.3 all-to-all-done.2
  463.8 9.6 all-to-all-done.6
  483.4 14.5 all-to-all-done.1
  508.1 171.7 %while.90 = (s32[]{:T(128)}, f32[6,64,128]{2,1,0:T(8,128)S(1)}, f32[8,256,6,64]{1,0,3,2:T(8,128)}, f32[8,6,64,128]{3,2,1,0:T(8,128)}, f32[8,256,6]{1,2,0:T(8,128...) while((s32[]{:T(128)}, f32[6,64,128]{2,1,0:T(8,128)S(1)}, ...), condition=%wide.region_4.6_spmd.clone.clone, body=%wide.region_1.5_spmd.clone.clone.sunk | while | flops 707151360 | bytes 5774692 | solution.py:75
  519.7 9.9 dynamic_update_slice.211
  541.2 9.9 dynamic_update_slice.211
  562.7 9.9 dynamic_update_slice.211
  584.2 9.9 dynamic_update_slice.211
  605.6 9.9 dynamic_update_slice.211
  627.1 9.9 dynamic_update_slice.211
  648.5 9.9 dynamic_update_slice.211
  670.0 9.9 dynamic_update_slice.211
  698.1 171.3 %while.91 = (s32[]{:T(128)}, f32[6,64,128]{2,1,0:T(8,128)S(1)}, f32[8,256,6,64]{1,0,3,2:T(8,128)}, f32[8,6,64,128]{3,2,1,0:T(8,128)}, f32[8,256,6]{1,2,0:T(8,128...) while((s32[]{:T(128)}, f32[6,64,128]{2,1,0:T(8,128)S(1)}, ...), condition=%wide.region_10.12_spmd.clone.clone, body=%wide.region_7.11_spmd.clone.clone.sunk | while | flops 707151360 | bytes 5774692 | solution.py:75
  709.7 9.8 dynamic_update_slice.213
  731.1 9.8 dynamic_update_slice.213
  752.5 9.8 dynamic_update_slice.213
  773.9 9.8 dynamic_update_slice.213
  795.3 9.8 dynamic_update_slice.213
  816.8 9.8 dynamic_update_slice.213
  838.2 9.8 dynamic_update_slice.213
  859.6 9.8 dynamic_update_slice.213
  876.3 12.8 copy.536
  906.8 13.0 all-gather.2
  972.2 8.9 multiply_reduce_fusion.19
  994.0 11.4 fusion.232
  1005.4 11.9 convolution_add_fusion.9
  1030.5 278.3 %while.89 = (s32[]{:T(128)}, f32[6,64,128]{2,1,0:T(8,128)S(1)}, f32[8,256,6,64]{1,0,3,2:T(8,128)}, f32[8,256,6]{1,2,0:T(8,128)S(1)}, f32[8,256,6]{1,2,0:T(8,128)...) while((s32[]{:T(128)}, f32[6,64,128]{2,1,0:T(8,128)S(1)}, ...), condition=%wide.region_43.45_spmd.clone, body=%wide.region_30.44_spmd.clone.sunk | while | flops 1669035520 | bytes 14124695 | solution.py:75
  1043.7 9.8 dynamic_update_slice.209
  1078.4 9.8 dynamic_update_slice.209
  1113.2 9.8 dynamic_update_slice.209
  1148.0 9.8 dynamic_update_slice.209
  1182.8 9.8 dynamic_update_slice.209
  1217.5 9.8 dynamic_update_slice.209
  1252.3 9.9 dynamic_update_slice.209
  1287.0 9.8 dynamic_update_slice.209
  1317.2 278.0 %while.88 = (s32[]{:T(128)}, f32[6,64,128]{2,1,0:T(8,128)S(1)}, f32[8,256,6,64]{1,0,3,2:T(8,128)}, f32[8,256,6]{1,2,0:T(8,128)S(1)}, f32[8,256,6]{1,2,0:T(8,128)...) while((s32[]{:T(128)}, f32[6,64,128]{2,1,0:T(8,128)S(1)}, ...), condition=%wide.region_26.28_spmd.clone, body=%wide.region_13.27_spmd.clone.sunk | while | flops 1669035520 | bytes 14124695 | solution.py:75
  1330.4 9.8 dynamic_update_slice.204
  1365.1 9.8 dynamic_update_slice.204
  1399.8 9.8 dynamic_update_slice.204
  1434.5 9.8 dynamic_update_slice.204
  1469.2 9.8 dynamic_update_slice.204
  1504.0 9.8 dynamic_update_slice.204
  1538.7 9.8 dynamic_update_slice.204
  1573.4 9.8 dynamic_update_slice.204
  1626.7 8.6 all-to-all-done.14
  1679.2 14.8 all-to-all-done.13
  1737.7 12.3 multiply_reduce_fusion.13
  1793.8 10.2 scatter-add.9
  1809.0 10.1 scatter-add.6
  1819.1 17.6 fusion.225
  1836.7 29.3 %convolution_add_fusion.8 = f32[1536,6448]{0,1:T(8,128)} fusion(f32[1536,6448]{0,1:T(8,128)} %fusion.225, bf16[256,48]{0,1:T(8,128)(2,1)S(1)} %convert_element_type.518, bf16[256,3328]{0,1:T(8,128)(2,1)S(1)} %copy-done.23, bf16[256,3072]{0,1:T(8,128)(2,1)} %get-tuple-element.1847, f32[256]{0:T(256)S(1)} %copy-done.79, f32[1536]{0:T(1024)S(1)} %copy-done.56, ...), kind=kOutput, calls=%fused_computation.250 | convolution fusion | flops 5092294656 | bytes 83330048 | tf_op jit(solution)/shard_map/dot_general | solution.py:235
  1871.6 643.9 %reduce-scatter.6.cloned.1.call-done = f32[384,6448]{0,1:T(8,128)} async-done(((f32[1536,6448]{0,1:T(8,128)}), f32[384,6448]{0,1:T(8,128)}) %reduce-scatter.6.cloned.1.call-update) | async-done | bytes 9904144 | tf_op jit(solution)/shard_map/reduce_scatter | solution.py:242
  2538.7 10.2 fusion.224
  2549.0 14.4 fusion.215
  2563.5 20.2 all-reduce.32
  2589.6 24.5 all-reduce.30
  2614.0 142.9 %all-reduce.36.cloned.1.call-done = (f32[384,6448]{0,1:T(8,128)}, f32[768,1536]{1,0:T(8,128)}) async-done(((f32[384,6448]{0,1:T(8,128)}, f32[768,1536]{1,0:T(8,128)}), (f32[384,6448]{0,1:T(8,128)}, f32[768,1536]{1,0:T(8,128)})) %all-reduce.36.cloned.1.call-update) | async-done | bytes 14622736 | tf_op jit(solution)/shard_map/psum | solution.py:251
  (1478 shorter events, 993.3 us)
Async XLA Ops:
  7.2 16.4 copy-start.85
  7.2 29.7 %copy-start.101 = (bf16[12]{0:T(256)(128)(2,1)S(1)}, bf16[12]{0:T(256)(128)(2,1)}, u32[]{:S(2)}) copy-start(bf16[12]{0:T(256)(128)(2,1)} %param.32) | copy-start | bytes 76
  7.2 30.0 %copy-start.102 = (bf16[12]{0:T(256)(128)(2,1)S(1)}, bf16[12]{0:T(256)(128)(2,1)}, u32[]{:S(2)}) copy-start(bf16[12]{0:T(256)(128)(2,1)} %param.34) | copy-start | bytes 76
  7.2 30.2 %copy-start.103 = (bf16[12]{0:T(256)(128)(2,1)S(1)}, bf16[12]{0:T(256)(128)(2,1)}, u32[]{:S(2)}) copy-start(bf16[12]{0:T(256)(128)(2,1)} %param.33) | copy-start | bytes 76
  7.2 30.4 %copy-start.94 = (bf16[832]{0:T(1024)(128)(2,1)S(1)}, bf16[832]{0:T(1024)(128)(2,1)}, u32[]{:S(2)}) copy-start(bf16[832]{0:T(1024)(128)(2,1)} %param.31) | copy-start | bytes 4996
  7.3 64.0 %copy-start.6 = (bf16[2,1,256,1536]{3,2,1,0:T(8,128)(2,1)S(1)}, bf16[2,1,256,1536]{3,2,1,0:T(8,128)(2,1)}, u32[]{:S(2)}) copy-start(bf16[2,1,256,1536]{3,2,1,0:T(8,128)(2,1)} %param.25) | copy-start | bytes 4718596
  7.3 344.0 %all-gather.6.cloned.1.call-start = ((), (), s32[]{:S(2)}) async-start(), calls=%async_computation.19 | async-start | bytes 24760320 | tf_op jit(solution)/shard_map/all_gather | solution.py:95
  21.6 348.1 %copy-start.55 = (f32[1536]{0:T(1024)}, f32[1536]{0:T(1024)S(1)}, u32[]{:S(2)}) copy-start(f32[1536]{0:T(1024)S(1)} %reshape.1239) | copy-start | bytes 18436
  71.2 337.9 %copy-start.47 = (f32[3328]{0:T(1024)}, f32[3328]{0:T(1024)S(1)}, u32[]{:S(2)}) copy-start(f32[3328]{0:T(1024)S(1)} %get-tuple-element.1633) | copy-start | bytes 39940
  71.2 337.9 %copy-start.49 = (f32[3328]{0:T(1024)}, f32[3328]{0:T(1024)S(1)}, u32[]{:S(2)}) copy-start(f32[3328]{0:T(1024)S(1)} %get-tuple-element.1634) | copy-start | bytes 39940
  71.2 337.9 %copy-start.51 = (f32[3328]{0:T(1024)}, f32[3328]{0:T(1024)S(1)}, u32[]{:S(2)}) copy-start(f32[3328]{0:T(1024)S(1)} %get-tuple-element.1635) | copy-start | bytes 39940
  71.3 337.9 %copy-start.53 = (f32[3328]{0:T(1024)}, f32[3328]{0:T(1024)S(1)}, u32[]{:S(2)}) copy-start(f32[3328]{0:T(1024)S(1)} %get-tuple-element.1636) | copy-start | bytes 39940
  71.6 292.4 %copy-start.74 = (f32[256]{0:T(256)}, f32[256]{0:T(256)S(1)}, u32[]{:S(2)}) copy-start(f32[256]{0:T(256)S(1)} %get-tuple-element.1631) | copy-start | bytes 3076
  71.7 292.4 %copy-start.76 = (f32[256]{0:T(256)}, f32[256]{0:T(256)S(1)}, u32[]{:S(2)}) copy-start(f32[256]{0:T(256)S(1)} %get-tuple-element.1632) | copy-start | bytes 3076
  71.7 298.0 %copy-start.78 = (f32[256]{0:T(256)}, f32[256]{0:T(256)S(1)}, u32[]{:S(2)}) copy-start(f32[256]{0:T(256)S(1)} %fusion.250) | copy-start | bytes 3076
  71.7 292.4 %copy-start.80 = (f32[256]{0:T(256)}, f32[256]{0:T(256)S(1)}, u32[]{:S(2)}) copy-start(f32[256]{0:T(256)S(1)} %fusion.248) | copy-start | bytes 3076
  367.1 15.5 copy-start.38
  367.1 27.2 collective-permute-start
  384.6 20.9 all-to-all-start.4
  390.9 10.0 collective-permute-start.1
  405.5 26.6 all-to-all-start
  433.1 19.6 all-to-all-start.2
  437.3 21.5 copy-start.104
  453.7 19.7 all-to-all-start.6
  458.0 475.0 %all-gather.8.cloned.1.call-start = ((), (), s32[]{:S(2)}) async-start(), calls=%async_computation.20 | async-start | bytes 11796480 | tf_op jit(solution)/shard_map/all_gather | solution.py:102
  458.9 18.1 copy-start.86
  459.1 430.1 %copy-start.66 = (f32[384]{0:T(512)}, f32[384]{0:T(512)S(1)}, u32[]{:S(2)}) copy-start(f32[384]{0:T(512)S(1)} %mul.1231) | copy-start | bytes 4612
  459.2 17.8 copy-start.88
  463.7 15.2 copy-start.43
  463.8 15.2 copy-start.45
  473.4 24.5 all-to-all-start.1
  497.9 193.6 %all-to-all-start.5 = ((bf16[256,8,384]{0,2,1:T(8,128)(2,1)}), bf16[256,8,384]{0,2,1:T(8,128)(2,1)S(1)}, u32[]{:S(2)}, u32[]{:S(2)}) async-start(bf16[256,8,384]{0,2,1:T(8,128)(2,1)} %bitcast.819), calls=%async_computation.5 | async-start | bytes 3145728 | tf_op jit(solution)/shard_map/all_to_all | solution.py:160
  900.5 19.3 copy-start.96
  902.4 26.3 all-to-all-start.7
  919.9 85.5 %copy-start.39 = (f32[4,1,768]{2,1,0:T(1,128)}, f32[4,1,768]{2,1,0:T(1,128)S(1)}, u32[]{:S(2)}) copy-start(f32[4,1,768]{2,1,0:T(1,128)S(1)} %convert_element_type.574) | copy-start | bytes 36868
  928.7 25.3 all-to-all-start.3
  952.6 52.8 %copy-start = (f32[256,3072]{0,1:T(8,128)}, f32[256,3072]{0,1:T(8,128)S(1)}, u32[]{:S(2)}) copy-start(f32[256,3072]{0,1:T(8,128)S(1)} %get-tuple-element.1765) | copy-start | bytes 9437188
  953.2 52.2 %copy-start.62 = (f32[256]{0:T(256)}, f32[256]{0:T(256)S(1)}, u32[]{:S(2)}) copy-start(f32[256]{0:T(256)S(1)} %fusion.251) | copy-start | bytes 3076
  989.2 28.1 %all-to-all-start.12 = ((bf16[256,8,384]{0,2,1:T(8,128)(2,1)}), bf16[256,8,384]{0,2,1:T(8,128)(2,1)}, u32[]{:S(2)}, u32[]{:S(2)}) async-start(bf16[256,8,384]{0,2,1:T(8,128)(2,1)} %bitcast.818), calls=%async_computation.12 | async-start | bytes 3145728 | tf_op jit(solution)/shard_map/all_to_all | solution.py:195
  993.5 878.1 %reduce-scatter.8.cloned.1.call-start = ((), (), s32[]{:S(2)}) async-start(), calls=%async_computation.22 | async-start | bytes 23592960 | tf_op jit(solution)/shard_map/reduce_scatter | solution.py:249
  1017.3 291.5 %all-to-all-start.8 = ((bf16[256,8,384]{0,2,1:T(8,128)(2,1)}), bf16[256,8,384]{0,2,1:T(8,128)(2,1)}, u32[]{:S(2)}, u32[]{:S(2)}) async-start(bf16[256,8,384]{0,2,1:T(8,128)(2,1)} %bitcast.57), calls=%async_computation.8 | async-start | bytes 3145728 | tf_op jit(solution)/shard_map/all_to_all | solution.py:195
  1317.2 278.0 %copy-start.44 = (f32[256,8,1,6]{0,3,1,2:T(8,128)S(1)}, f32[256,8,1,6]{0,3,1,2:T(8,128)}, u32[]{:S(2)}) copy-start(f32[256,8,1,6]{0,3,1,2:T(8,128)} %copy-done.43) | copy-start | bytes 147460
  1317.2 278.0 %copy-start.46 = (f32[256,8,1,6]{0,3,1,2:T(8,128)S(1)}, f32[256,8,1,6]{0,3,1,2:T(8,128)}, u32[]{:S(2)}) copy-start(f32[256,8,1,6]{0,3,1,2:T(8,128)} %copy-done.45) | copy-start | bytes 147460
  1317.2 278.0 %copy-start.87 = (f32[6]{0:T(128)S(1)}, f32[6]{0:T(128)}, u32[]{:S(2)}) copy-start(f32[6]{0:T(128)} %copy-done.86) | copy-start | bytes 76
  1317.2 278.0 %copy-start.89 = (f32[6]{0:T(128)S(1)}, f32[6]{0:T(128)}, u32[]{:S(2)}) copy-start(f32[6]{0:T(128)} %copy-done.88) | copy-start | bytes 76
  1595.2 15.7 copy-start.33
  1595.2 15.7 copy-start.34
  1598.6 9.0 all-to-all-start.15
  1607.6 8.1 all-to-all-start.11
  1615.6 19.7 all-to-all-start.14
  1621.0 18.6 copy-start.19
  1635.3 33.5 %all-to-all-start.10 = ((bf16[8,2,32768]{2,1,0:T(2,128)(2,1)}), bf16[8,2,32768]{2,1,0:T(2,128)(2,1)}, u32[]{:S(2)}, u32[]{:S(2)}) async-start(bf16[8,2,32768]{2,1,0:T(2,128)(2,1)} %reshape.1295), calls=%async_computation.10 | async-start | bytes 2097152 | tf_op jit(solution)/shard_map/all_to_all | solution.py:214
  1668.9 25.1 all-to-all-start.13
  1694.0 33.0 %all-to-all-start.9 = ((bf16[8,2,49152]{2,1,0:T(2,128)(2,1)}), bf16[8,2,49152]{2,1,0:T(2,128)(2,1)}, u32[]{:S(2)}, u32[]{:S(2)}) async-start(bf16[8,2,49152]{2,1,0:T(2,128)(2,1)} %reshape.1297), calls=%async_computation.9 | async-start | bytes 3145728 | tf_op jit(solution)/shard_map/all_to_all | solution.py:210
  1698.3 817.3 %reduce-scatter.6.cloned.1.call-start = ((), (), s32[]{:S(2)}) async-start(), calls=%async_computation.21 | async-start | bytes 49520640 | tf_op jit(solution)/shard_map/reduce_scatter | solution.py:242
  1772.9 17.2 collective-permute-start.3
  1788.8 16.4 collective-permute-start.2
  1819.1 17.6 copy-start.23
  1819.1 17.6 copy-start.79
  1866.1 722.3 %reduce-scatter.10.cloned.1.call-start = ((), (), s32[]{:S(2)}) async-start(), calls=%async_computation.23 | async-start | bytes 2129920
  1868.7 888.2 %all-reduce.36.cloned.1.call-start = ((), (), s32[]{:S(2)}) async-start(), calls=%async_computation.24 | async-start | bytes 29245440 | tf_op jit(solution)/shard_map/psum | solution.py:251
  2549.0 35.2 %copy-start.75 = (f32[256]{0:T(256)S(1)}, f32[256]{0:T(256)}, u32[]{:S(2)}) copy-start(f32[256]{0:T(256)} %copy-done.74) | copy-start | bytes 3076
  2549.0 35.2 %copy-start.77 = (f32[256]{0:T(256)S(1)}, f32[256]{0:T(256)}, u32[]{:S(2)}) copy-start(f32[256]{0:T(256)} %copy-done.76) | copy-start | bytes 3076
  2549.0 35.2 %copy-start.28 = (bf16[2,1,256,1536]{3,2,1,0:T(8,128)(2,1)S(1)}, bf16[2,1,256,1536]{3,2,1,0:T(8,128)(2,1)}, u32[]{:S(2)}) copy-start(bf16[2,1,256,1536]{3,2,1,0:T(8,128)(2,1)} %param.27) | copy-start | bytes 4718596
  (69 other events, 446.9 us)
Sparse Core Ops, SparseCore 0:
  9.7 341.4 all-gather.5
  460.4 165.8 all-gather.7
  1017.4 312.7 reduce-scatter.7
  1866.2 649.3 reduce-scatter.5
  2518.4 39.4 reduce-scatter.9
  2562.0 194.9 all-reduce.35
where the time goes:
time: 2800 us; the launch traced here: 2770 us
  waiting for transfers between devices  1140 us (41%)
  local copies, waits for them, and re-layouts  638 us (23%)
  matrix products  419 us (15%)
  other arithmetic  367 us (13%)
  blocking collectives  118 us (4%)
  starting transfers between devices  73.8 us (3%)
    reduce_scatter x1, waiting for transfers between devices, local(): lax.psum_scatter(acc_in, 'wshard', scatter_dimension=0, tiled=True)  644 us
    dynamic_update_slice x96, local copies, waits for them, and re-layouts, ssd_scan(): last_state, results = lax.scan(jax.checkpoint(advance), initial, pieces)  328 us
    all_gather x1, waiting for transfers between devices, local(): lax.all_gather(in_weight, 'wshard', axis=0, tiled=True)  280 us
    another operation x114, other arithmetic  212 us
    psum x1, waiting for transfers between devices, local(): lax.psum((shards[0], shards[1], shards[2], shards[3], shards[4], shards[5...  143 us
    dot_general x48, matrix products, advance(): jnp.einsum('hij,jhp->ihp', within * scores[None], weighted, precision=hig...  107 us
    unnamed x261, local copies, waits for them, and re-layouts  86 us
    dot_general x64, matrix products, advance(): scores = jnp.dot(c_blk, b_blk.T, precision=highest)  63.4 us
  transfers between devices with their start and end apart: 26, of which 11 were waited for; matrix products, arithmetic and copies ran while one was open for 49% of the time, Pallas kernels for 0%

commit v1 on v0

v1 whole, which is shorter than its diff:
```python
from functools import partial

import jax
import jax.numpy as jnp
from jax import lax
from jax.experimental import pallas as pl
from jax.experimental.pallas import tpu as pltpu
from jax.sharding import PartitionSpec as P

epsilon = 1e-05
highest = lax.Precision.HIGHEST
f32 = jnp.float32
bf16 = jnp.bfloat16
GROUP = 8
VMEM = 48 * 1024 * 1024

NN = (((1,), (0,)), ((), ()))
NT = (((1,), (1,)), ((), ()))
TN = (((0,), (0,)), ((), ()))


def mm(a, b, dims=NN):
    return lax.dot_general(a, b, dims, preferred_element_type=f32)


def params():
    return pltpu.CompilerParams(
        dimension_semantics=("arbitrary", "arbitrary"), vmem_limit_bytes=VMEM
    )


def widen(cols, head_size):
    t, heads = cols.shape
    lane = lax.broadcasted_iota(jnp.int32, (t, 2 * head_size), 1)
    parts = []
    for k in range(0, heads, 2):
        parts.append(jnp.where(lane < head_size, cols[:, k : k + 1], cols[:, k + 1 : k + 2]))
    return jnp.concatenate(parts, axis=1)


def state_kernel(hs, x_ref, w_ref, bt_ref, o_ref):
    weighted = (x_ref[0].astype(f32) * widen(w_ref[0, 0], hs)).astype(bf16)
    o_ref[0] = mm(bt_ref[0], weighted)


def block_states(x, weights, bt, hs):
    micro, t, cols = x.shape
    n = bt.shape[1]
    gc = GROUP * hs
    return pl.pallas_call(
        partial(state_kernel, hs),
        grid=(micro, cols // gc),
        in_specs=[
            pl.BlockSpec((1, t, gc), lambda m, g: (m, 0, g)),
            pl.BlockSpec((1, 1, t, GROUP), lambda m, g: (m, g, 0, 0)),
            pl.BlockSpec((1, n, t), lambda m, g: (m, 0, 0)),
        ],
        out_specs=pl.BlockSpec((1, n, gc), lambda m, g: (m, 0, g)),
        out_shape=jax.ShapeDtypeStruct((micro, n, cols), f32),
        compiler_params=params(),
        name="block_states",
    )(x, weights, bt)


def local_kernel(hs, x_ref, dt_ref, cum_ref, row_ref, b_ref, c_ref, o_ref, scores):
    t = x_ref.shape[1]
    half = t // 2

    @pl.when(pl.program_id(1) == 0)
    def _():
        s = mm(c_ref[0], b_ref[0], NT)
        i = lax.broadcasted_iota(jnp.int32, (t, t), 0)
        j = lax.broadcasted_iota(jnp.int32, (t, t), 1)
        scores[...] = jnp.where(i >= j, s, 0.0)

    cum, dt, rows = cum_ref[0, 0], dt_ref[0, 0], row_ref[0, 0]
    lane = lax.broadcasted_iota(jnp.int32, (half, 2 * hs), 1)
    weighted = (x_ref[0].astype(f32) * widen(dt, hs)).astype(bf16)
    for k in range(0, GROUP, 2):
        at = slice(k * hs, (k + 2) * hs)
        pair = weighted[:, at]
        top, low = [], []
        for h in (k, k + 1):
            col, row = cum[:, h : h + 1], rows[h : h + 1, :]
            m1 = jnp.exp(jnp.minimum(col[:half] - row[:, :half], 0.0)) * scores[:half, :half]
            m2 = jnp.exp(jnp.minimum(col[half:] - row, 0.0)) * scores[half:, :]
            top.append(mm(m1.astype(bf16), pair[:half]))
            low.append(mm(m2.astype(bf16), pair))
        o_ref[0, :half, at] = jnp.where(lane < hs, top[0], top[1])
        o_ref[0, half:, at] = jnp.where(lane < hs, low[0], low[1])


def local_scan(x, dt, cum, rows, b, c, hs):
    micro, t, cols = x.shape
    n = b.shape[2]
    gc = GROUP * hs
    return pl.pallas_call(
        partial(local_kernel, hs),
        grid=(micro, cols // gc),
        in_specs=[
            pl.BlockSpec((1, t, gc), lambda m, g: (m, 0, g)),
            pl.BlockSpec((1, 1, t, GROUP), lambda m, g: (m, g, 0, 0)),
            pl.BlockSpec((1, 1, t, GROUP), lambda m, g: (m, g, 0, 0)),
            pl.BlockSpec((1, 1, GROUP, t), lambda m, g: (m, g, 0, 0)),
            pl.BlockSpec((1, t, n), lambda m, g: (m, 0, 0)),
            pl.BlockSpec((1, t, n), lambda m, g: (m, 0, 0)),
        ],
        out_specs=pl.BlockSpec((1, t, gc), lambda m, g: (m, 0, g)),
        out_shape=jax.ShapeDtypeStruct((micro, t, cols), f32),
        scratch_shapes=[pltpu.VMEM((t, t), f32)],
        compiler_params=params(),
        name="local_scan",
    )(x, dt, cum, rows, b, c)


def carry_kernel(hs, x_ref, y_ref, cum_ref, c_ref, s_ref, skip_ref, scan_ref, low_ref):
    carried = mm(c_ref[0], s_ref[0].astype(bf16)) * widen(jnp.exp(cum_ref[0, 0]), hs)
    scan = y_ref[0] + carried
    scan_ref[0] = scan
    low_ref[0] = (scan + skip_ref[...] * x_ref[0].astype(f32)).astype(bf16)


def add_carry(x, y, cum, c, s_in, skip_wide, hs):
    micro, t, cols = x.shape
    n = c.shape[2]
    gc = GROUP * hs
    wide = pl.BlockSpec((1, t, gc), lambda m, g: (m, 0, g))
    return pl.pallas_call(
        partial(carry_kernel, hs),
        grid=(micro, cols // gc),
        in_specs=[
            wide,
            wide,
            pl.BlockSpec((1, 1, t, GROUP), lambda m, g: (m, g, 0, 0)),
            pl.BlockSpec((1, t, n), lambda m, g: (m, 0, 0)),
            pl.BlockSpec((1, n, gc), lambda m, g: (m, 0, g)),
            pl.BlockSpec((1, gc), lambda m, g: (0, g)),
        ],
        out_specs=[wide, wide],
        out_shape=[
            jax.ShapeDtypeStruct((micro, t, cols), f32),
            jax.ShapeDtypeStruct((micro, t, cols), bf16),
        ],
        compiler_params=params(),
        name="add_carry",
    )(x, y, cum, c, s_in, skip_wide)


def local_back_kernel(
    hs, x_ref, dy_ref, dt_ref, cum_ref, row_ref, b_ref, c_ref, dx_ref, db_ref, dc_ref, scores, total
):
    t = x_ref.shape[1]
    half = t // 2

    @pl.when(pl.program_id(1) == 0)
    def _():
        s = mm(b_ref[0], c_ref[0], NT)
        j = lax.broadcasted_iota(jnp.int32, (t, t), 0)
        i = lax.broadcasted_iota(jnp.int32, (t, t), 1)
        scores[...] = jnp.where(i >= j, s, 0.0)
        total[...] = jnp.zeros_like(total)

    cum, dt, rows = cum_ref[0, 0], dt_ref[0, 0], row_ref[0, 0]
    lane = lax.broadcasted_iota(jnp.int32, (t, 2 * hs), 1)
    lane_half = lax.broadcasted_iota(jnp.int32, (half, 2 * hs), 1)
    weighted = (x_ref[0].astype(f32) * widen(dt, hs)).astype(bf16)
    for k in range(0, GROUP, 2):
        at = slice(k * hs, (k + 2) * hs)
        pair = weighted[:, at]
        dy = dy_ref[0, :, at]
        top, low = [], []
        for h in (k, k + 1):
            col, row = cum[:, h : h + 1], rows[h : h + 1, :]
            mine = jnp.where(lane < hs, pair, 0) if h == k else jnp.where(lane < hs, 0, pair)
            l1 = jnp.exp(jnp.minimum(row - col[:half], 0.0))
            l2 = jnp.exp(jnp.minimum(row[:, half:] - col[half:], 0.0))
            total[:half, :] += l1 * mm(mine[:half], dy, NT)
            total[half:, half:] += l2 * mm(mine[half:], dy[half:], NT)
            top.append(mm((l1 * scores[:half, :]).astype(bf16), dy))
            low.append(mm((l2 * scores[half:, half:]).astype(bf16), dy[half:]))
        dx_ref[0, :half, at] = jnp.where(lane_half < hs, top[0], top[1])
        dx_ref[0, half:, at] = jnp.where(lane_half < hs, low[0], low[1])

    @pl.when(pl.program_id(1) == pl.num_programs(1) - 1)
    def _():
        j = lax.broadcasted_iota(jnp.int32, (t, t), 0)
        i = lax.broadcasted_iota(jnp.int32, (t, t), 1)
        d = jnp.where(i >= j, total[...], 0.0)
        db_ref[0] = mm(d.astype(bf16), c_ref[0])
        dc_ref[0] = mm(d.T.astype(bf16), b_ref[0])


def local_back(x, dy, dt, cum, rows, b, c, hs):
    micro, t, cols = x.shape
    n = b.shape[2]
    gc = GROUP * hs
    wide = pl.BlockSpec((1, t, gc), lambda m, g: (m, 0, g))
    small = pl.BlockSpec((1, 1, t, GROUP), lambda m, g: (m, g, 0, 0))
    state = pl.BlockSpec((1, t, n), lambda m, g: (m, 0, 0))
    return pl.pallas_call(
        partial(local_back_kernel, hs),
        grid=(micro, cols // gc),
        in_specs=[
            wide,
            wide,
            small,
            small,
            pl.BlockSpec((1, 1, GROUP, t), lambda m, g: (m, g, 0, 0)),
            state,
            state,
        ],
        out_specs=[wide, state, state],
        out_shape=[
            jax.ShapeDtypeStruct((micro, t, cols), f32),
            jax.ShapeDtypeStruct((micro, t, n), f32),
            jax.ShapeDtypeStruct((micro, t, n), f32),
        ],
        scratch_shapes=[pltpu.VMEM((t, t), f32), pltpu.VMEM((t, t), f32)],
        compiler_params=params(),
        name="local_back",
    )(x, dy, dt, cum, rows, b, c)


def head_sums(values, ones):
    high = values.astype(bf16)
    rest = (values - high.astype(f32)).astype(bf16)
    return mm(high, ones) + mm(rest, ones)


def carry_back_kernel(
    hs,
    x_ref,
    dy_ref,
    dxl_ref,
    y_ref,
    dt_ref,
    cum_ref,
    b_ref,
    si_ref,
    ds_ref,
    dbl_ref,
    dcl_ref,
    skip_ref,
    dx_ref,
    ddt_ref,
    dcum_ref,
    db_ref,
    dc_ref,
    last_ref,
    dskip_ref,
):
    t = x_ref.shape[1]
    gc = x_ref.shape[2]

    @pl.when(pl.program_id(1) == 0)
    def _():
        db_ref[0] = dbl_ref[0]
        dc_ref[0] = dcl_ref[0]

    cum, dt = cum_ref[0, 0], dt_ref[0, 0]
    x, dy = x_ref[0].astype(f32), dy_ref[0].astype(f32)
    dt_wide = widen(dt, hs)
    weighted = (x * dt_wide).astype(bf16).astype(f32)
    decay = widen(jnp.exp(cum), hs)
    to_end = widen(jnp.exp(cum[t - 1 :, :] - cum), hs)
    s_in, ds = si_ref[0], ds_ref[0]
    s_low, ds_low = s_in.astype(bf16), ds.astype(bf16)
    through = to_end * mm(b_ref[0], ds_low)
    d_weighted = dxl_ref[0] + through
    dx_ref[0] = (dt_wide * d_weighted + skip_ref[...] * dy).astype(bf16)
    db_ref[0] += mm((weighted * to_end).astype(bf16), ds_low, NT)
    dc_ref[0] += mm((dy * decay).astype(bf16), s_low, NT)
    r = lax.broadcasted_iota(jnp.int32, (gc, 128), 0)
    c = lax.broadcasted_iota(jnp.int32, (gc, 128), 1)
    ones = jnp.where(r // hs == c, 1.0, 0.0).astype(bf16)
    ddt_ref[0, 0] = head_sums(x * d_weighted, ones)[:, :GROUP]
    dcum_ref[0, 0] = head_sums(dy * y_ref[0] - weighted * d_weighted, ones)[:, :GROUP]
    last_decay = decay[t - 1 :, :]
    last_ref[0] = jnp.sum(weighted * through, axis=0, keepdims=True) + last_decay * jnp.sum(
        s_low.astype(f32) * ds, axis=0, keepdims=True
    )
    dskip_ref[0] = jnp.sum(x * dy, axis=0, keepdims=True)


def carry_back(x, dy, dxl, y, dt, cum, b, s_in, ds, dbl, dcl, skip_wide, hs):
    micro, t, cols = x.shape
    n = b.shape[2]
    gc = GROUP * hs
    groups = cols // gc
    wide = pl.BlockSpec((1, t, gc), lambda m, g: (m, 0, g))
    small = pl.BlockSpec((1, 1, t, GROUP), lambda m, g: (m, g, 0, 0))
    state = pl.BlockSpec((1, t, n), lambda m, g: (m, 0, 0))
    st = pl.BlockSpec((1, n, gc), lambda m, g: (m, 0, g))
    line = pl.BlockSpec((1, 1, gc), lambda m, g: (m, 0, g))
    return pl.pallas_call(
        partial(carry_back_kernel, hs),
        grid=(micro, groups),
        in_specs=[
            wide,
            wide,
            wide,
            wide,
            small,
            small,
            state,
            st,
            st,
            state,
            state,
            pl.BlockSpec((1, gc), lambda m, g: (0, g)),
        ],
        out_specs=[wide, small, small, state, state, line, line],
        out_shape=[
            jax.ShapeDtypeStruct((micro, t, cols), bf16),
            jax.ShapeDtypeStruct((micro, groups, t, GROUP), f32),
            jax.ShapeDtypeStruct((micro, groups, t, GROUP), f32),
            jax.ShapeDtypeStruct((micro, t, n), f32),
            jax.ShapeDtypeStruct((micro, t, n), f32),
            jax.ShapeDtypeStruct((micro, 1, cols), f32),
            jax.ShapeDtypeStruct((micro, 1, cols), f32),
        ],
        compiler_params=params(),
        name="carry_back",
    )(x, dy, dxl, y, dt, cum, b, s_in, ds, dbl, dcl, skip_wide)


def from_behind(x, axis, by):
    count = lax.axis_size(axis)
    pairs = [(i, i + by) for i in range(count) if 0 <= i + by < count]
    return lax.ppermute(x, axis, pairs)


def swap(x, by):
    count = lax.axis_size("seq")
    return lax.ppermute(x, "seq", [(i, i ^ by) for i in range(count)])


def running_states(terms, decays, hs, forward):
    count = lax.axis_size("seq")
    rank = lax.axis_index("seq")
    index = jnp.arange(count)

    def product(mask):
        d = jnp.prod(jnp.where(mask[:, None, None], decays, 1.0), axis=0)
        return jnp.repeat(d, hs, axis=1)[:, None, :]

    total, before = terms, jnp.zeros_like(terms)
    size = 1
    while size < count:
        other = swap(total.astype(bf16), size).astype(f32)
        mine = index // size == rank // size
        theirs = index // size == (rank // size) ^ 1
        later = (rank // size) % 2 == (1 if forward else 0)
        passed = mine & ((index < rank) if forward else (index > rank))
        before = before + jnp.where(later, product(passed), 0.0) * other
        if 2 * size < count:
            total = total * jnp.where(later, 1.0, product(theirs)) + other * jnp.where(
                later, product(mine), 1.0
            )
        size *= 2
    return before


def rms_front(hidden_rows, gain):
    power = jnp.mean(hidden_rows * hidden_rows, axis=-1, keepdims=True)
    return hidden_rows * lax.rsqrt(power + epsilon) * gain


def conv_act(padded, conv_w, conv_b):
    taps = conv_w.shape[0]
    rows_out = padded.shape[1] - taps + 1
    total = conv_b + padded[:, 0:rows_out] * conv_w[0]
    for offset in range(1, taps):
        total = total + padded[:, offset : offset + rows_out] * conv_w[offset]
    return jax.nn.silu(total)


def gate_norm(values, gate_in, gain):
    gated = values * jax.nn.silu(gate_in)
    power = jnp.mean(gated * gated, axis=-1, keepdims=True)
    return gated * lax.rsqrt(power + epsilon) * gain


def local(
    hidden,
    lengths,
    out_grad,
    norm_gain,
    in_weight,
    conv_weight,
    conv_bias,
    dt_bias,
    a_log,
    skip_gain,
    gated_gain,
    out_weight,
):
    count = lax.axis_size("seq")
    shards = lax.axis_size("wshard")
    rank = lax.axis_index("seq")
    shard = lax.axis_index("wshard")
    micro, _, tokens, width = hidden.shape
    taps = conv_weight.shape[1]
    small = [norm_gain, conv_weight.T.reshape(-1), conv_bias, dt_bias, a_log, skip_gain, gated_gain]
    sizes = [v.shape[0] for v in small]
    packed = lax.all_gather(jnp.concatenate(small), "wshard", axis=0).astype(f32)
    parts, at = [], 0
    for size in sizes:
        parts.append(packed[:, at : at + size])
        at += size
    norm_g = parts[0].reshape(-1)
    conv_w = parts[1].reshape(shards, taps, -1).transpose(1, 0, 2).reshape(taps, -1)
    conv_b = parts[2].reshape(-1)
    dt_shift = parts[3].reshape(-1)
    rate = -jnp.exp(parts[4].reshape(-1))
    skip = parts[5].reshape(-1)
    gated_g = parts[6].reshape(-1)

    in_t = lax.all_gather(in_weight.T, "wshard", axis=0)
    out_w = lax.all_gather(out_weight, "wshard", axis=0, tiled=True)
    in_t = in_t.transpose(1, 0, 2).reshape(in_t.shape[1], -1)

    inner = out_w.shape[0]
    channels = conv_b.shape[0]
    heads = dt_shift.shape[0]
    hs = inner // heads
    n = (channels - inner) // 2
    groups = heads // GROUP
    rows = micro * tokens

    def grouped(v):
        return v.reshape(micro, tokens, groups, GROUP).transpose(0, 2, 1, 3)

    rows_in = hidden.reshape(rows, width).astype(f32)
    cot = out_grad.reshape(rows, width).astype(f32)
    positions = rank * tokens + jnp.arange(tokens, dtype=jnp.int32)
    valid = (positions[None, :] < lengths[:, 0][:, None]).astype(f32).reshape(rows, 1)
    normed, front_back = jax.vjp(rms_front, rows_in, norm_g)
    normed_low = normed.astype(bf16)
    gate_in = mm(normed_low, in_t[:inner], NT)
    conv_low = mm(normed_low, in_t[inner : inner + channels], NT).astype(bf16)
    dt_low = mm(normed_low, in_t[inner + channels :], NT).astype(bf16)
    conv_low = conv_low.reshape(micro, tokens, channels)
    prior = from_behind(conv_low[:, tokens - (taps - 1) :], "seq", 1)
    padded = jnp.concatenate([prior, conv_low], axis=1).astype(f32)
    mixed, conv_back = jax.vjp(conv_act, padded, conv_w, conv_b)
    x_low = mixed[..., :inner].astype(bf16)
    b_low = mixed[..., inner : inner + n].astype(bf16)
    c_low = mixed[..., inner + n :].astype(bf16)

    dt_raw = dt_low.astype(f32).reshape(micro, tokens, heads) + dt_shift
    dt = jax.nn.softplus(dt_raw)
    tri = (jnp.arange(tokens)[:, None] >= jnp.arange(tokens)[None, :]).astype(f32)
    cum = jnp.einsum("ij,mjh->mih", tri, dt * rate, precision=highest)
    dt_g, cum_g = grouped(dt), grouped(cum)
    row_g = cum_g.transpose(0, 1, 3, 2)
    last = cum[:, tokens - 1, :]
    decays = lax.all_gather(jnp.exp(last), "seq", axis=0)
    end_w = grouped(dt * jnp.exp(last[:, None, :] - cum))
    decay_w = grouped(jnp.exp(cum))
    skip_wide = jnp.repeat(skip, hs)[None, :]

    own_state = block_states(x_low, end_w, b_low.transpose(0, 2, 1), hs)
    y_local = local_scan(x_low, dt_g, cum_g, row_g, b_low, c_low, hs)
    s_in = running_states(own_state, decays, hs, True)
    y_scan, scanned_low = add_carry(x_low, y_local, cum_g, c_low, s_in, skip_wide, hs)

    scanned = scanned_low.reshape(rows, inner).astype(f32)
    normed_out, gate_back = jax.vjp(gate_norm, scanned, gate_in, gated_g)
    normed_out_low = normed_out.astype(bf16)
    branch = mm(normed_out_low, out_w)
    output = (rows_in + valid * branch).astype(bf16).reshape(hidden.shape)

    g = (cot * valid).astype(bf16)
    out_terms = mm(normed_out_low, g, TN)
    d_scanned, d_gate_in, d_gated = gate_back(mm(g, out_w, NT))
    dy = d_scanned.astype(bf16).reshape(micro, tokens, inner)
    own_grad = block_states(dy, decay_w, c_low.transpose(0, 2, 1), hs)
    dx_local, db_local, dc_local = local_back(x_low, dy, dt_g, cum_g, row_g, b_low, c_low, hs)
    ds = running_states(own_grad, decays, hs, False)
    dx_low, ddt_g, dcum_g, db, dc, last_term, dskip = carry_back(
        x_low, dy, dx_local, y_scan, dt_g, cum_g, b_low, s_in, ds, db_local, dc_local, skip_wide, hs
    )

    def ungrouped(v):
        return v.transpose(0, 2, 1, 3).reshape(micro, tokens, heads)

    at_end = jnp.sum(last_term.reshape(micro, heads, hs), axis=-1)[:, None, :]
    d_log = jnp.einsum("ij,mih->mjh", tri, ungrouped(dcum_g), precision=highest) + at_end
    d_dt = (ungrouped(ddt_g) + d_log * rate) * jax.nn.sigmoid(dt_raw)
    d_dt_bias = jnp.sum(d_dt, axis=(0, 1))
    d_a_log = jnp.sum(d_log * dt, axis=(0, 1)) * rate
    d_skip = jnp.sum(dskip.reshape(-1, heads, hs), axis=(0, 2))
    mixed_grad = jnp.concatenate([dx_low.astype(f32), db, dc], axis=2)
    d_padded, d_conv_w, d_conv_b = conv_back(mixed_grad)
    from_next = from_behind(d_padded[:, : taps - 1].astype(bf16), "seq", -1).astype(f32)
    d_conv = d_padded[:, taps - 1 :].at[:, tokens - (taps - 1) :].add(from_next)
    d_proj = jnp.concatenate(
        [
            d_gate_in.astype(bf16),
            d_conv.astype(bf16).reshape(rows, channels),
            d_dt.astype(bf16).reshape(rows, heads),
        ],
        axis=1,
    )
    in_terms = mm(d_proj, normed_low, TN)
    d_normed = mm(d_proj, in_t)
    d_hidden, d_norm_g = front_back(d_normed)
    input_grad = (d_hidden + cot).astype(bf16).reshape(hidden.shape)

    def summed(terms, axis):
        t = lax.psum_scatter(terms.astype(bf16), "seq", scatter_dimension=0, tiled=True)
        t = lax.psum_scatter(t, "wshard", scatter_dimension=axis, tiled=True)
        return lax.all_gather(t, "seq", axis=0, tiled=True).astype(f32)

    in_grad = summed(in_terms, 1).T
    blocks = out_terms.reshape(shards, count, -1, width).transpose(1, 0, 2, 3)
    blocks = blocks.reshape(inner, width)
    out_w_grad = summed_rows(blocks, shards, count)
    smalls = [
        d_norm_g.reshape(shards, -1),
        d_conv_w.reshape(taps, shards, -1).transpose(1, 0, 2).reshape(shards, -1),
        d_conv_b.reshape(shards, -1),
        d_dt_bias.reshape(shards, -1),
        d_a_log.reshape(shards, -1),
        d_skip.reshape(shards, -1),
        d_gated.reshape(shards, -1),
    ]
    sums = lax.psum(jnp.concatenate(smalls, axis=1), ("seq", "wshard"))
    sums = lax.dynamic_index_in_dim(sums, shard, 0, keepdims=False)
    found, at = [], 0
    for size in sizes:
        found.append(sums[at : at + size])
        at += size
    return (
        output,
        input_grad,
        found[0],
        in_grad,
        found[1].reshape(taps, -1).T,
        found[2],
        found[3],
        found[4],
        found[5],
        found[6],
        out_w_grad,
    )


def summed_rows(blocks, shards, count):
    t = lax.psum_scatter(blocks.astype(bf16), "seq", scatter_dimension=0, tiled=True)
    t = lax.psum_scatter(t, "wshard", scatter_dimension=0, tiled=True)
    return lax.all_gather(t, "seq", axis=0, tiled=True).astype(f32)


def solution(mesh):
    return jax.shard_map(
        local,
        mesh=mesh,
        in_specs=(
            P(None, "wshard", "seq", None),
            P(None, "wshard"),
            P(None, "wshard", "seq", None),
            P("wshard"),
            P("wshard", None),
            P("wshard", None),
            P("wshard"),
            P("wshard"),
            P("wshard"),
            P("wshard"),
            P("wshard"),
            P("wshard", None),
        ),
        out_specs=(
            P(None, "wshard", "seq", None),
            P(None, "wshard", "seq", None),
            P("wshard"),
            P("wshard", None),
            P("wshard", None),
            P("wshard"),
            P("wshard"),
            P("wshard"),
            P("wshard"),
            P("wshard"),
            P("wshard", None),
        ),
        check_vma=False,
    )
```

time: 2800 us -> 1340 us (0.48)
  waiting for transfers between devices: 1140 us -> 603 us
  local copies, waits for them, and re-layouts: 638 us -> 188 us
  matrix products: 419 us -> 89.1 us
  other arithmetic: 367 us -> 104 us
  blocking collectives: 118 us -> 229 us
  Pallas kernels: 0 us -> 85.7 us
  starting transfers between devices: 73.8 us -> 11.3 us
    reduce_scatter x2, waiting for transfers between devices: 644 us -> 28.9 us  [the longest x1 28.9 us: summed_rows(): t = lax.psum_scatter(t, 'wshard', scatter_dimension=0, tiled=True)]
    dot_general x236 -> x10, matrix products: 419 us -> 89.1 us  [the longest x8 87.9 us: mm(): return lax.dot_general(a, b, dims, preferred_element_type=f32)]
    dynamic_update_slice x98 -> x0, local copies, waits for them, and re-layouts: 328 us -> none  [the longest x96 328 us: ssd_scan(): last_state, results = lax.scan(jax.checkpoint(advance), initial, pieces)]
    another operation x131 -> x1, other arithmetic: 215 us -> 6.16 us
    unnamed x2, blocking collectives: 53.4 us -> 220 us
    all_gather x2 -> x4, waiting for transfers between devices: 280 us -> 372 us  [the longest x1 313 us: local(): in_t = lax.all_gather(in_weight.T, 'wshard', axis=0)]
    pallas_call x0 -> x6, Pallas kernels: none -> 85.7 us  [the longest x1 23.1 us: carry_back(): pl.pallas_call(partial(carry_back_kernel, hs), grid=(micro, groups), in_s...]
    all_to_all x16 -> x0, waiting for transfers between devices: 68 us -> none  [the longest x2 24.9 us: local(): lax.all_to_all(bc_send, 'seq', split_axis=1, concat_axis=0, tiled=True)]
  transfers between devices with their start and end apart: 26 -> 17, of which waited for: 11 -> 8; matrix products, arithmetic and copies ran while one was open for 49% -> 40% of each run, Pallas kernels for 0% -> 6%
where the time goes in v1:
time: 1340 us; the launch traced here: 1330 us
  waiting for transfers between devices  603 us (45%)
  blocking collectives  229 us (17%)
  local copies, waits for them, and re-layouts  188 us (14%)
  other arithmetic  104 us (8%)
  matrix products  89.1 us (7%)
  Pallas kernels  85.7 us (6%)
  between operations  16.9 us (1%)
    all_gather x1, waiting for transfers between devices, local(): in_t = lax.all_gather(in_weight.T, 'wshard', axis=0)  313 us
    unnamed x2, blocking collectives  220 us
    psum x1, waiting for transfers between devices, local(): sums = lax.psum(jnp.concatenate(smalls, axis=1), ('seq', 'wshard'))  111 us
    dot_general x8, matrix products, mm(): return lax.dot_general(a, b, dims, preferred_element_type=f32)  87.9 us
    unnamed x10, waiting for transfers between devices  56.2 us
    unnamed x208, local copies, waits for them, and re-layouts  39.1 us
    all_gather x1, waiting for transfers between devices, summed(): return lax.all_gather(t, 'seq', axis=0, tiled=True).astype(f32)  37.3 us
    ppermute x6, waiting for transfers between devices, swap(): return lax.ppermute(x, 'seq', [(i, i ^ by) for i in range(count)])  34.1 us
  transfers between devices with their start and end apart: 17, of which 8 were waited for; matrix products, arithmetic and copies ran while one was open for 40% of the time, Pallas kernels for 6%

profile of v1, /device:TPU:0, one launch (start us, length us, event | category | flops | bytes accessed | tf_op | source)
XLA Modules:
  0.0 1326.1 jit_solution(13173706474475288069)
XLA Ops:
  10.6 21.2 %all-reduce.8 = bf16[21392]{0:T(1024)(128)(2,1)S(1)} all-reduce(bf16[21392]{0:T(1024)(128)(2,1)S(1)} %dynamic-update-slice.3), channel_id=2, replica_groups=mesh['seq'=8,'wshard'=4] {'wshard'}, use_global_device_ids=true, to_apply=%add.8 | all-reduce | flops 21392 | bytes 85568
  37.2 313.1 %all-gather.13.cloned.1.call-done = bf16[25792,384]{1,0:T(8,128)(2,1)} async-done(((bf16[6448,384]{1,0:T(8,128)(2,1)}), bf16[25792,384]{1,0:T(8,128)(2,1)}) %all-gather.13.cloned.1.call-update) | async-done | bytes 19808272 | tf_op jit(solution)/shard_map/all_gather | solution.py:419
  350.3 9.6 slice.201
  359.9 13.4 %copy.140 = bf16[3328,4,384]{0,2,1:T(8,128)(2,1)} copy(bf16[3328,4,384]{2,0,1:T(8,128)(2,1)} %slice.201) | data formatting | bytes 20447232 | tf_op jit(solution)/shard_map/slice | solution.py:441
  373.3 9.5 convolution_convert_fusion.1
  382.8 1.7 copy-done.31
  385.2 2.5 collective-permute-start
  390.0 2.1 copy.147
  392.1 2.3 broadcast_multiply_fusion.4
  395.4 1.7 copy.149
  398.3 2.1 bitcast_exponential_fusion
  400.4 1.7 copy.153
  402.1 2.5 copy.154
  406.2 6.2 multiply_convert_fusion
  412.4 2.1 slice.212.x_ref
  416.8 9.8 block_states.2
  429.3 8.8 all-gather.2
  440.4 3.1 fusion.33
  449.2 31.2 %collective-permute-done.2 = bf16[2,128,3072]{2,1,0:T(8,128)(2,1)} collective-permute-done((bf16[2,128,3072]{2,1,0:T(8,128)(2,1)}, bf16[2,128,3072]{2,1,0:T(8,128)(2,1)}, u32[]{:S(2)}, u32[]{:S(2)}) %collective-permute-start.2) | collective-permute-done | bytes 1572896 | tf_op jit(solution)/shard_map/ppermute | solution.py:335
  480.4 3.9 fusion.12
  486.6 8.4 slice.220
  500.3 13.1 copy.156
  515.3 2.4 select_bitcast_fusion.dt_ref
  517.7 1.8 copy.159.bt_ref
  519.5 14.0 %local_scan.1.y_ref = f32[2,256,3072]{2,1,0:T(8,128)} custom-call(bf16[2,256,3072]{2,1,0:T(8,128)(2,1)} %slice.212.x_ref, f32[2,6,256,8]{3,2,1,0:T(8,128)S(1)} %select_bitcast_fusion.dt_ref, f32[2,6,256,8]{3,2,1,0:T(8,128)S(1)} %bitcast.153, f32[2,6,8,256]{3,2,1,0:T(8,128)S(1)} %bitcast.160, bf16[2,256,128]{2,1,0:T(8,128)(2,1)S(1)} %get-tuple-element.166.b_ref, ...), custom_call_target="tpu_custom_call" | custom-call | tf_op jit(solution)/shard_map/local_scan/pallas_call | solution.py:97
  533.5 5.1 fusion.9.s_ref.si_ref
  538.6 12.6 add_carry.1
  551.3 8.1 multiply_reduce_fusion.6
  559.5 13.7 %multiply_reduce_fusion.4 = (f32[3072]{0:T(1024)}, f32[512]{0:T(512)S(1)}, f32[512,3072]{1,0:T(8,128)}) fusion(f32[512]{0:T(512)S(1)} %fusion.45, bf16[2,256,3072]{2,1,0:T(8,128)(2,1)} %copy-done.7, f32[512,3072]{1,0:T(8,128)} %get-tuple-element.192, f32[3072]{0:T(1024)S(1)} %copy-done.58, bf16[512,1536]{1,0:T(8,128)(2,1)S(1)} %copy-done.37, ...), kind=kOutput, calls=%fused_computation.22 | convolution fusion | flops 4850708992 | bytes 26767360 | tf_op jit(solution)/shard_map/dot_general | solution.py:23
  573.3 10.3 fusion.5
  583.6 9.8 block_states.3
  598.6 3.1 fusion.32
  603.8 2.9 fusion.20
  606.7 24.9 %copy.166 = bf16[6448,4,384]{0,2,1:T(8,128)(2,1)} copy(bf16[6448,4,384]{2,0,1:T(8,128)(2,1)} %bitcast.167) | data formatting | bytes 39616512 | tf_op jit(solution)/shard_map/transpose | solution.py:421
  636.0 2.9 collective-permute-done.5
  638.8 3.9 fusion.17
  649.4 16.3 %local_back.1 = (f32[2,256,3072]{2,1,0:T(8,128)}, f32[2,256,128]{2,1,0:T(8,128)S(1)}, f32[2,256,128]{2,1,0:T(8,128)S(1)}) custom-call(bf16[2,256,3072]{2,1,0:T(8,128)(2,1)} %slice.212.x_ref, bf16[2,256,3072]{2,1,0:T(8,128)(2,1)} %bitcast.169, f32[2,6,256,8]{3,2,1,0:T(8,128)S(1)} %copy-done.3, f32[2,6,256,8]{3,2,1,0:T(8,128)S(1)} %bitcast.156, ...), custom_call_target="tpu_custom_call" | custom-call | tf_op jit(solution)/shard_map/local_back/pallas_call | solution.py:200
  667.1 2.8 copy.168
  669.9 9.3 convert_bitcast_fusion
  679.2 8.3 copy.169
  688.3 5.0 fusion.14.ds_ref
  693.3 23.1 %carry_back.1 = (bf16[2,256,3072]{2,1,0:T(8,128)(2,1)}, f32[2,6,256,8]{3,2,1,0:T(8,128)S(1)}, f32[2,6,256,8]{3,2,1,0:T(8,128)S(1)}, f32[2,256,128]{2,1,0:T(8,128...) custom-call(bf16[2,256,3072]{2,1,0:T(8,128)(2,1)} %slice.212.x_ref, ...), custom_call_target="tpu_custom_call" | custom-call | tf_op jit(solution)/shard_map/carry_back/pallas_call | solution.py:295
  720.2 2.0 copy.160
  723.4 3.0 convert_element_type.190
  726.5 14.7 %multiply_reduce_fusion.3 = (f32[3328]{0:T(1024)S(1)}, f32[3328]{0:T(1024)S(1)}, f32[3328]{0:T(1024)S(1)}, f32[3328]{0:T(1024)S(1)}, f32[3328]{0:T(1024)S(1)}, /*index=5*/f32[2,256,3328]{2,1,0:T(8,128)S(1)}) fusion(f32[2,259,3328]{2,1,0:T(8,128)} %copy-done.23, f32[2,256,3328]{2,1,0:T(8,128)} %get-tuple-element.155, f32[2,256,128]{2,1,0:T(8,128)S(1)} %copy-done.18, ...), kind=kLoop, calls=%fused_computation.14 | loop fusion | flops 34062080 | bytes 47776768 | tf_op jit(solution)/shard_map/transpose(jvp())/reduce_sum | solution.py:374
  741.2 6.1 broadcast_multiply_fusion
  747.3 8.0 pad_add_fusion
  758.7 5.4 slice.222
  766.8 18.4 %fusion.24 = (f32[1536]{0:T(1024)S(1)}, f32[512]{0:T(512)S(1)}, bf16[512,1536]{1,0:T(8,128)(2,1)}, f32[512,1536]{1,0:T(8,128)}) fusion(bf16[2,1,256,1536]{3,2,1,0:T(8,128)(2,1)S(1)} %copy-done.25, f32[512]{0:T(512)S(1)} %copy-done.69, f32[1536]{0:T(1024)S(1)} %copy-done.56, bf16[6448,1536]{0,1:T(8,128)(2,1)} %bitcast.172, ...), kind=kOutput, calls=%fused_computation.69 | convolution fusion | flops 10168711168 | bytes 32718848 | tf_op jit(solution)/shard_map/dot_general | solution.py:23
  785.2 17.8 %convolution_convert_fusion = bf16[6448,1536]{1,0:T(8,128)(2,1)} fusion(bf16[512,1536]{1,0:T(8,128)(2,1)} %get-tuple-element.167, bf16[512,48]{1,0:T(8,128)(2,1)S(1)} %bitcast.205, bf16[512,3328]{1,0:T(8,128)(2,1)} %bitcast.190, bf16[512,3072]{1,0:T(8,128)(2,1)} %get-tuple-element.156), kind=kOutput, calls=%fused_computation | convolution fusion | flops 10171539456 | bytes 27983872 | tf_op jit(solution)/shard_map/dot_general | solution.py:23
  803.0 198.8 %fusion = bf16[816,1536]{1,0:T(8,128)(2,1)} fusion(bf16[6448,1536]{1,0:T(8,128)(2,1)} %convolution_convert_fusion), kind=kCustom, calls=%all-reduce-scatter | all-reduce-scatter fusion | flops 10027009 | bytes 22315520
  1005.3 13.3 %concatenate.22 = bf16[886,1536]{1,0:T(8,128)(2,1)} concatenate(bf16[70,1536]{1,0:T(8,128)(2,1)S(1)} %collective-permute-done.8, bf16[816,1536]{1,0:T(8,128)(2,1)} %fusion), dimensions={0} | concatenate | bytes 5443584
  1018.7 3.7 constant_dynamic-slice_fusion
  1022.4 4.4 copy.174
  1030.1 54.4 %reduce-scatter.12.cloned.1.call-done = bf16[384,806]{1,0:T(8,128)(2,1)} async-done(((bf16[1536,806]{1,0:T(8,128)(2,1)}), bf16[384,806]{1,0:T(8,128)(2,1)}) %reduce-scatter.12.cloned.1.call-update) | async-done | bytes 619024
  1084.4 2.2 copy.175
  1086.7 28.9 %reduce-scatter.10.cloned.1.call-done = bf16[96,1536]{1,0:T(8,128)(2,1)} async-done(((bf16[384,1536]{1,0:T(8,128)(2,1)}), bf16[96,1536]{1,0:T(8,128)(2,1)}) %reduce-scatter.10.cloned.1.call-update) | async-done | bytes 294928 | tf_op jit(solution)/shard_map/reduce_scatter | solution.py:552
  1115.6 10.4 fusion.30
  1126.1 2.1 fusion.19
  1128.2 111.0 %all-reduce.13.cloned.1.call-done = f32[4,5348]{1,0:T(4,128)} async-done(((f32[4,5348]{1,0:T(4,128)}), f32[4,5348]{1,0:T(4,128)}) %all-reduce.13.cloned.1.call-update) | async-done | bytes 85584 | tf_op jit(solution)/shard_map/psum | solution.py:529
  1246.3 37.3 %all-gather.15.cloned.1.call-done = bf16[8,806,384]{2,1,0:T(8,128)(2,1)} async-done(((bf16[1,806,384]{2,1,0:T(8,128)(2,1)}), bf16[8,806,384]{2,1,0:T(8,128)(2,1)}) %all-gather.15.cloned.1.call-update) | async-done | bytes 4952080 | tf_op jit(solution)/shard_map/all_gather | solution.py:514
  1283.6 9.0 reshape.586
  1292.6 21.9 %all-gather.11.cloned.1.call-done = bf16[768,1536]{1,0:T(8,128)(2,1)} async-done(((bf16[96,1536]{1,0:T(8,128)(2,1)}), bf16[768,1536]{1,0:T(8,128)(2,1)}) %all-gather.11.cloned.1.call-update) | async-done | bytes 2359312 | tf_op jit(solution)/shard_map/all_gather | solution.py:553
  1314.5 4.5 convert_element_type.204
  (371 shorter events, 81.1 us)
Async XLA Ops:
  7.2 343.1 %all-gather.13.cloned.1.call-start = ((), (), s32[]{:S(2)}) async-start(), calls=%async_computation.8 | async-start | bytes 24760320 | tf_op jit(solution)/shard_map/all_gather | solution.py:419
  7.3 25.7 %copy-start.24 = (bf16[2,1,256,1536]{3,2,1,0:T(8,128)(2,1)S(1)}, bf16[2,1,256,1536]{3,2,1,0:T(8,128)(2,1)}, u32[]{:S(2)}) copy-start(bf16[2,1,256,1536]{3,2,1,0:T(8,128)(2,1)} %param.14) | copy-start | bytes 4718596
  7.9 551.5 %all-gather.9.cloned.1.call-start = ((), (), s32[]{:S(2)}) async-start(), calls=%async_computation.3 | async-start | bytes 11796480 | tf_op jit(solution)/shard_map/all_gather | solution.py:420
  8.7 1018.3 %reduce-scatter.8.cloned.1.call-start = ((), (), s32[]{:S(2)}) async-start(), calls=%async_computation.5 | async-start | bytes 10616832 | tf_op jit(solution)/shard_map/reduce_scatter | solution.py:551
  32.7 327.2 %copy-start.61 = (f32[4,12]{1,0:T(4,128)}, f32[4,12]{1,0:T(4,128)S(1)}, u32[]{:S(2)}) copy-start(f32[4,12]{1,0:T(4,128)S(1)} %get-tuple-element.178) | copy-start | bytes 580
  33.0 373.1 %copy-start.42 = (f32[3328]{0:T(1024)}, f32[3328]{0:T(1024)S(1)}, u32[]{:S(2)}) copy-start(f32[3328]{0:T(1024)S(1)} %mul.428) | copy-start | bytes 39940
  33.0 326.9 %copy-start.55 = (f32[1536]{0:T(1024)}, f32[1536]{0:T(1024)S(1)}, u32[]{:S(2)}) copy-start(f32[1536]{0:T(1024)S(1)} %mul.416) | copy-start | bytes 18436
  34.1 372.1 %copy-start.44 = (f32[3328]{0:T(1024)}, f32[3328]{0:T(1024)S(1)}, u32[]{:S(2)}) copy-start(f32[3328]{0:T(1024)S(1)} %mul.425) | copy-start | bytes 39940
  34.2 372.0 %copy-start.46 = (f32[3328]{0:T(1024)}, f32[3328]{0:T(1024)S(1)}, u32[]{:S(2)}) copy-start(f32[3328]{0:T(1024)S(1)} %mul.422) | copy-start | bytes 39940
  37.2 351.5 %copy-start.29 = (bf16[2,1,256,1536]{3,2,1,0:T(8,128)(2,1)}, bf16[2,1,256,1536]{3,2,1,0:T(8,128)(2,1)S(1)}, u32[]{:S(2)}) copy-start(bf16[2,1,256,1536]{3,2,1,0:T(8,128)(2,1)S(1)} %fusion.28) | copy-start | bytes 4718596
  385.2 19.4 %collective-permute-start = (bf16[2,3,3328]{2,1,0:T(4,128)(2,1)}, bf16[2,3,3328]{2,1,0:T(4,128)(2,1)}, u32[]{:S(2)}, u32[]{:S(2)}) collective-permute-start(bf16[2,3,3328]{2,1,0:T(4,128)(2,1)} %slice.202), channel_id=1, source_target_pairs={{0,4},{4,8},{8,12},{12,16},{16,20},{20,24},{24,28},{1,5},{5,9},{9,... | collective-permute-start | bytes 119816 | tf_op jit(solution)/shard_map/ppermute | solution.py:330
  389.2 17.0 %copy-start.39 = (f32[512,48]{0,1:T(8,128)}, f32[512,48]{0,1:T(8,128)S(1)}, u32[]{:S(2)}) copy-start(f32[512,48]{0,1:T(8,128)S(1)} %fusion.34) | copy-start | bytes 294916
  389.3 15.4 %copy-start.32 = (bf16[512,3328]{1,0:T(8,128)(2,1)S(1)}, bf16[512,3328]{1,0:T(8,128)(2,1)}, u32[]{:S(2)}) copy-start(bf16[512,3328]{1,0:T(8,128)(2,1)} %copy-done.31) | copy-start | bytes 10223620
  428.0 12.4 collective-permute-start.1
  443.5 36.9 %collective-permute-start.2 = (bf16[2,128,3072]{2,1,0:T(8,128)(2,1)}, bf16[2,128,3072]{2,1,0:T(8,128)(2,1)}, u32[]{:S(2)}, u32[]{:S(2)}) collective-permute-start(bf16[2,128,3072]{2,1,0:T(8,128)(2,1)} %fusion.33), channel_id=1, source_target_pairs={{0,8},{4,12},{8,0},{12,4},{16,24},{20,28},{24,16},{28,20},{1,9},{5... | collective-permute-start | bytes 4718600 | tf_op jit(solution)/shard_map/ppermute | solution.py:335
  446.4 38.5 %copy-start.66 = (f32[1,2,2,128]{3,1,2,0:T(2,128)}, f32[1,2,2,128]{3,1,2,0:T(2,128)S(1)}, u32[]{:S(2)}) copy-start(f32[1,2,2,128]{3,1,2,0:T(2,128)S(1)} %copy.178) | copy-start | bytes 6148
  449.2 35.7 %copy-start.26 = (bf16[2,1,256,1536]{3,2,1,0:T(8,128)(2,1)S(1)}, bf16[2,1,256,1536]{3,2,1,0:T(8,128)(2,1)}, u32[]{:S(2)}) copy-start(bf16[2,1,256,1536]{3,2,1,0:T(8,128)(2,1)} %param.16) | copy-start | bytes 4718596
  484.3 49.1 %collective-permute-start.3 = (bf16[2,128,3072]{2,1,0:T(8,128)(2,1)}, bf16[2,128,3072]{2,1,0:T(8,128)(2,1)}, u32[]{:S(2)}, u32[]{:S(2)}) collective-permute-start(bf16[2,128,3072]{2,1,0:T(8,128)(2,1)} %fusion.12), channel_id=1, source_target_pairs={{0,16},{4,20},{8,24},{12,28},{16,0},{20,4},{24,8},{28,12},{1,17},{... | collective-permute-start | bytes 4718600 | tf_op jit(solution)/shard_map/ppermute | solution.py:335
  498.4 40.2 %copy-start = (f32[2,256,6,8]{3,1,2,0:T(8,128)}, f32[2,256,6,8]{3,1,2,0:T(8,128)S(1)}, u32[]{:S(2)}) copy-start(f32[2,256,6,8]{3,1,2,0:T(8,128)S(1)} %copy.151) | copy-start | bytes 294916
  500.3 13.1 copy-start.38
  517.7 15.8 %copy-start.2 = (f32[2,6,256,8]{3,2,1,0:T(8,128)}, f32[2,6,256,8]{3,2,1,0:T(8,128)S(1)}, u32[]{:S(2)}) copy-start(f32[2,6,256,8]{3,2,1,0:T(8,128)S(1)} %select_bitcast_fusion.dt_ref) | copy-start | bytes 294916
  519.5 14.0 %copy-start.53 = (f32[2,3072]{1,0:T(2,128)S(1)}, f32[2,3072]{1,0:T(2,128)}, u32[]{:S(2)}) copy-start(f32[2,3072]{1,0:T(2,128)} %select_n.341) | copy-start | bytes 73732
  519.5 14.0 %copy-start.54 = (f32[2,3072]{1,0:T(2,128)S(1)}, f32[2,3072]{1,0:T(2,128)}, u32[]{:S(2)}) copy-start(f32[2,3072]{1,0:T(2,128)} %select_n.334) | copy-start | bytes 73732
  533.5 17.7 %slice-start = ((s8[9437184]{0:T(1024)(128)(4,1)}), s8[4194304]{0:T(1024)(128)(4,1)S(1)}, s32[]{:S(2)}) async-start(s8[9437184]{0:T(1024)(128)(4,1)} %bitcast.178), calls=%async_computation.11 | async-start | bytes 8388608
  533.5 17.7 %slice-start.1 = ((s8[9437184]{0:T(1024)(128)(4,1)}), s8[4194304]{0:T(1024)(128)(4,1)S(1)}, s32[]{:S(2)}) async-start(s8[9437184]{0:T(1024)(128)(4,1)} %bitcast.178), calls=%async_computation.12 | async-start | bytes 8388608
  538.6 12.6 slice-start.2
  538.6 12.7 copy-start.30
  551.2 8.2 copy-start.37
  551.2 8.2 copy-start.58
  559.4 13.8 %slice-start.3 = ((s8[6291456]{0:T(1024)(128)(4,1)}), s8[4194304]{0:T(1024)(128)(4,1)S(1)}, s32[]{:S(2)}) async-start(s8[6291456]{0:T(1024)(128)(4,1)} %bitcast.184), calls=%async_computation.14 | async-start | bytes 8388608
  559.5 13.8 %copy-start.8 = (bf16[2,256,3072]{2,1,0:T(8,128)(2,1)S(1)}, bf16[2,256,3072]{2,1,0:T(8,128)(2,1)}, u32[]{:S(2)}) copy-start(bf16[2,256,3072]{2,1,0:T(8,128)(2,1)} %copy-done.7) | copy-start | bytes 9437188
  559.5 13.8 %slice-start.4 = ((s8[6291456]{0:T(1024)(128)(4,1)}), s8[2097152]{0:T(1024)(128)(4,1)S(1)}, s32[]{:S(2)}) async-start(s8[6291456]{0:T(1024)(128)(4,1)} %bitcast.184), calls=%async_computation.15 | async-start | bytes 4194304
  573.3 10.3 copy-start.5
  573.3 10.3 copy-start.10
  594.8 3.8 collective-permute-start.4
  601.7 37.1 %collective-permute-start.5 = (bf16[2,128,3072]{2,1,0:T(8,128)(2,1)}, bf16[2,128,3072]{2,1,0:T(8,128)(2,1)}, u32[]{:S(2)}, u32[]{:S(2)}) collective-permute-start(bf16[2,128,3072]{2,1,0:T(8,128)(2,1)} %fusion.32), channel_id=1, source_target_pairs={{0,8},{4,12},{8,0},{12,4},{16,24},{20,28},{24,16},{28,20},{1,9},{5... | collective-permute-start | bytes 4718600 | tf_op jit(solution)/shard_map/ppermute | solution.py:335
  603.2 28.4 %copy-start.59 = (f32[1,2,2,128]{3,1,2,0:T(2,128)}, f32[1,2,2,128]{3,1,2,0:T(2,128)S(1)}, u32[]{:S(2)}) copy-start(f32[1,2,2,128]{3,1,2,0:T(2,128)S(1)} %copy.179) | copy-start | bytes 6148
  606.6 24.9 %copy-start.82 = (f32[2,48]{1,0:T(2,128)S(1)}, f32[2,48]{1,0:T(2,128)}, u32[]{:S(2)}) copy-start(f32[2,48]{1,0:T(2,128)} %get-tuple-element.185) | copy-start | bytes 1156
  606.6 27.1 %copy-start.83 = (f32[2,48]{1,0:T(2,128)S(1)}, f32[2,48]{1,0:T(2,128)}, u32[]{:S(2)}) copy-start(f32[2,48]{1,0:T(2,128)} %get-tuple-element.183) | copy-start | bytes 1156
  635.9 8.3 copy-start.76
  635.9 9.1 copy-start.75
  635.9 9.8 copy-start.74
  642.8 45.1 %collective-permute-start.6 = (bf16[2,128,3072]{2,1,0:T(8,128)(2,1)}, bf16[2,128,3072]{2,1,0:T(8,128)(2,1)}, u32[]{:S(2)}, u32[]{:S(2)}) collective-permute-start(bf16[2,128,3072]{2,1,0:T(8,128)(2,1)} %fusion.17), channel_id=1, source_target_pairs={{0,16},{4,20},{8,24},{12,28},{16,0},{20,4},{24,8},{28,12},{1,17},{... | collective-permute-start | bytes 4718600 | tf_op jit(solution)/shard_map/ppermute | solution.py:335
  649.4 17.7 %copy-start.28 = (bf16[512,3072]{1,0:T(8,128)(2,1)S(1)}, bf16[512,3072]{1,0:T(8,128)(2,1)}, u32[]{:S(2)}) copy-start(bf16[512,3072]{1,0:T(8,128)(2,1)} %get-tuple-element.158) | copy-start | bytes 9437188
  687.6 396.8 %reduce-scatter.12.cloned.1.call-start = ((), (), s32[]{:S(2)}) async-start(), calls=%async_computation.10 | async-start | bytes 3440640
  726.4 14.8 %copy-start.43 = (f32[3328]{0:T(1024)S(1)}, f32[3328]{0:T(1024)}, u32[]{:S(2)}) copy-start(f32[3328]{0:T(1024)} %copy-done.42) | copy-start | bytes 39940
  726.4 14.8 %copy-start.45 = (f32[3328]{0:T(1024)S(1)}, f32[3328]{0:T(1024)}, u32[]{:S(2)}) copy-start(f32[3328]{0:T(1024)} %copy-done.44) | copy-start | bytes 39940
  726.4 14.8 %copy-start.47 = (f32[3328]{0:T(1024)S(1)}, f32[3328]{0:T(1024)}, u32[]{:S(2)}) copy-start(f32[3328]{0:T(1024)} %copy-done.46) | copy-start | bytes 39940
  726.5 14.8 %copy-start.49 = (f32[3328]{0:T(1024)S(1)}, f32[3328]{0:T(1024)}, u32[]{:S(2)}) copy-start(f32[3328]{0:T(1024)} %mul.419) | copy-start | bytes 39940
  747.3 10.8 copy-start.35
  747.3 10.8 copy-start.36
  747.3 10.8 copy-start.71
  747.3 10.8 copy-start.72
  756.3 7.9 collective-permute-start.7
  803.0 201.1 %copy-start.90 = (u32[32]{0:T(128)S(1)}, u32[32]{0:T(128)}, u32[]{:S(2)}) copy-start(u32[32]{0:T(128)} %constant.233) | copy-start | bytes 388
  1002.8 2.6 collective-permute-start.8
  1026.8 88.8 %copy-start.67 = (f32[1,2,2,128]{3,1,2,0:T(2,128)S(1)}, f32[1,2,2,128]{3,1,2,0:T(2,128)}, u32[]{:S(2)}) copy-start(f32[1,2,2,128]{3,1,2,0:T(2,128)} %copy-done.66) | copy-start | bytes 6148
  1026.9 88.7 %reduce-scatter.10.cloned.1.call-start = ((), (), s32[]{:S(2)}) async-start(), calls=%async_computation.6 | async-start | bytes 1474560 | tf_op jit(solution)/shard_map/reduce_scatter | solution.py:552
  1027.4 211.8 %all-reduce.13.cloned.1.call-start = ((), (), s32[]{:S(2)}) async-start(), calls=%async_computation.4 | async-start | bytes 172032 | tf_op jit(solution)/shard_map/psum | solution.py:529
  1030.0 253.6 %all-gather.15.cloned.1.call-start = ((), (), s32[]{:S(2)}) async-start(), calls=%async_computation.9 | async-start | bytes 5584896 | tf_op jit(solution)/shard_map/all_gather | solution.py:514
  1086.6 227.9 %all-gather.11.cloned.1.call-start = ((), (), s32[]{:S(2)}) async-start(), calls=%async_computation.7 | async-start | bytes 2654208 | tf_op jit(solution)/shard_map/all_gather | solution.py:553
  1115.6 10.5 copy-start.60
  1115.6 10.5 copy-start.27
  1115.6 10.5 copy-start.33
  (51 other events, 154.0 us)
Sparse Core Ops, SparseCore 0:
  9.6 340.6 all-gather.12
  351.8 165.4 all-gather.8
  687.7 73.9 reduce-scatter.7
  1027.0 57.4 reduce-scatter.11
  1086.6 28.9 reduce-scatter.9
  1121.0 118.2 all-reduce.12
  1241.7 41.8 all-gather.14
  1285.5 29.0 all-gather.10

commit v2 on v1

--- a/solution.py
+++ b/solution.py
@@ -361,6 +361,459 @@
     return before
 
 
+MESH = pl.DeviceIdType.MESH
+
+
+def around():
+    s, z = lax.axis_index("seq"), lax.axis_index("wshard")
+    c, x, y = s % 2, (s // 2) % 2, s // 4
+    near = {
+        "c": (s + 1 - 2 * c, z),
+        "x": (s + 2 - 4 * x, z),
+        "y": (s + 4 - 8 * y, z),
+        "z1": (s, z + 1 - 2 * (z % 2)),
+        "z2": (s, z + 2 - 4 * (z // 2)),
+        "z3": (s, 3 - z),
+    }
+    return s, z, c, x, y, near
+
+
+def greet(near):
+    barrier = pltpu.get_barrier_semaphore()
+    for where in near.values():
+        pl.semaphore_signal(barrier, inc=1, device_id=where, device_id_type=MESH)
+    pl.semaphore_wait(barrier, len(near))
+
+
+CHUNK_DMAS = 10
+
+
+def gather_kernel(chunks, w_ref, o_ref, send, recv, own_sem):
+    s, z, c, x, y, near = around()
+    own = pltpu.make_async_copy(w_ref.at[pl.ds(0, o_ref.shape[1])], o_ref.at[0], own_sem)
+    own.start()
+    greet(near)
+    sx, sy, sd = s + 2 - 4 * x, s + 4 - 8 * y, s + 6 - 4 * x - 8 * y
+    plans = []
+    for q, (base, piece, off, size, first) in enumerate(chunks):
+
+        def rows(who, base=base, piece=piece, off=off, size=size):
+            return pl.ds(pl.multiple_of(base + who * piece + off, 16), size)
+
+        def move(src, dst, kind, to, q=q):
+            return pltpu.make_async_remote_copy(
+                src_ref=src,
+                dst_ref=dst,
+                send_sem=send.at[q, kind],
+                recv_sem=recv.at[q, kind],
+                device_id=near[to],
+                device_id_type=MESH,
+            )
+
+        def block(who, rows=rows):
+            return o_ref.at[pl.ds(1, 3), rows(who)]
+
+        def along(who, kind, to, move=move, block=block):
+            return move(block(who), block(who), kind, to)
+
+        plan = {}
+        for k in (1, 2, 3):
+            plan["z%d" % k] = move(w_ref.at[rows(s)], o_ref.at[k, rows(s)], k - 1, "z%d" % k)
+        plan["x"] = along(s, 3, "x")
+        plan["y"] = along(s, 4, "y")
+        plan["d"] = along(sx, 5, "y") if first == "x" else along(sy, 5, "x")
+        plan["c0"] = along(s, 6, "c")
+        plan["cx"] = along(sx, 7, "c")
+        plan["cy"] = along(sy, 8, "c")
+        plan["cd"] = along(sd, 9, "c")
+        plan["first"] = first
+        plans.append(plan)
+
+    for plan in plans:
+        for k in (1, 2, 3):
+            plan["z%d" % k].start()
+
+    def begin(plan):
+        for k in (1, 2, 3):
+            plan["z%d" % k].wait_recv()
+        for name in ("x", "y", "c0"):
+            plan[name].start()
+
+    def middle(plan):
+        one, two = ("x", "y") if plan["first"] == "x" else ("y", "x")
+        plan[one].wait_recv()
+        plan["d"].start()
+        plan["c" + one].start()
+        plan[two].wait_recv()
+        plan["c" + two].start()
+
+    def finish(plan):
+        plan["d"].wait_recv()
+        plan["cd"].start()
+
+    n = len(plans)
+    for i in range(n + 2):
+        if i < n:
+            begin(plans[i])
+        if 0 <= i - 1 < n:
+            middle(plans[i - 1])
+        if 0 <= i - 2 < n:
+            finish(plans[i - 2])
+    for plan in plans:
+        for name in ("c0", "cx", "cy", "cd"):
+            plan[name].wait_recv()
+        for name in ("z1", "z2", "z3", "x", "y", "d", "c0", "cx", "cy", "cd"):
+            plan[name].wait_send()
+    own.wait()
+
+
+def gather_input_weight(w_t, inner, channels):
+    total = inner + channels
+    chunks = []
+    for base, piece in ((inner, channels // 8), (0, inner // 8)):
+        half = piece // 2
+        chunks.append((base, piece, 0, half, "x"))
+        chunks.append((base, piece, half, half, "y"))
+    width = w_t.shape[1]
+    return pl.pallas_call(
+        partial(gather_kernel, chunks),
+        in_specs=[pl.BlockSpec(memory_space=pl.ANY)],
+        out_specs=pl.BlockSpec(memory_space=pl.ANY),
+        out_shape=jax.ShapeDtypeStruct((4, total, width), bf16),
+        scratch_shapes=[
+            pltpu.SemaphoreType.DMA((len(chunks), CHUNK_DMAS)),
+            pltpu.SemaphoreType.DMA((len(chunks), CHUNK_DMAS)),
+            pltpu.SemaphoreType.DMA,
+        ],
+        compiler_params=pltpu.CompilerParams(collective_id=1, has_side_effects=True),
+        cost_estimate=pl.CostEstimate(flops=0, bytes_accessed=200_000_000, transcendentals=0),
+        name="gather_input_weight",
+    )(w_t)
+
+
+def reduce_kernel(
+    chunks,
+    pieces,
+    groups,
+    dp_ref,
+    nm_ref,
+    o_ref,
+    dp,
+    nm,
+    g,
+    sa1,
+    sb1,
+    sa2,
+    sb2,
+    s3,
+    ka2,
+    kb2,
+    f3,
+    ra1,
+    rb1,
+    ra2,
+    rb2,
+    rz,
+    in_sem,
+    s_in,
+    r_in,
+    s_step,
+    r_step,
+    s_all,
+    r_all,
+):
+    s, z, c, x, y, near = around()
+    wide = dp.shape[2]
+    shard = rz.shape[-1]
+
+    def remote(src, dst, ss, rs, to):
+        return pltpu.make_async_remote_copy(
+            src_ref=src, dst_ref=dst, send_sem=ss, recv_sem=rs, device_id=near[to], device_id_type=MESH
+        )
+
+    local_copies, core_copies = [], []
+    for i, (a, b) in enumerate(pieces):
+        here = dp_ref.at[:, pl.ds(pl.multiple_of(c * wide + a, 128), b - a)]
+        there = dp_ref.at[:, pl.ds(pl.multiple_of((1 - c) * wide + a, 128), b - a)]
+        local_copies.append(
+            pltpu.make_async_copy(here, dp.at[0, :, pl.ds(a, b - a)], in_sem.at[i])
+        )
+        core_copies.append(
+            remote(there, dp.at[1, :, pl.ds(a, b - a)], s_in.at[i], r_in.at[i], "c")
+        )
+    n_in = len(pieces)
+    nm_local = pltpu.make_async_copy(nm_ref, nm.at[0], in_sem.at[n_in])
+    nm_core = remote(nm_ref, nm.at[1], s_in.at[n_in], r_in.at[n_in], "c")
+    nm_local.start()
+    for copy in local_copies:
+        copy.start()
+    greet(near)
+    nm_core.start()
+    for copy in core_copies:
+        copy.start()
+
+    def step_copy(kind, u):
+        slot = u % 2
+        ss, rs = s_step.at[kind, slot], r_step.at[kind, u]
+        if kind == 0:
+            return remote(sa1.at[slot], ra1.at[u], ss, rs, "x")
+        if kind == 1:
+            return remote(sb1.at[slot], rb1.at[u], ss, rs, "y")
+        if kind == 2:
+            return remote(sa2.at[slot], ra2.at[u], ss, rs, "y")
+        if kind == 3:
+            return remote(sb2.at[slot], rb2.at[u], ss, rs, "x")
+        k = kind - 3
+        other = (z + 1 - 2 * (z % 2), z + 2 - 4 * (z // 2), 3 - z)[k - 1]
+        cols = pl.ds(pl.multiple_of(other * shard, 128), shard)
+        return remote(s3.at[slot, :, :, cols], rz.at[u, k - 1], ss, rs, "z%d" % k)
+
+    def part(px, py, ts, T=None):
+        if T is None:
+            return o_ref.at[c, ts, :, px, py]
+        return o_ref.at[c, ts, T, px, py]
+
+    def all_copy(q, kind):
+        a, b = groups[q]
+        ts = pl.ds(a, b - a)
+        ss, rs = s_all.at[q, kind], r_all.at[q, kind]
+        if kind == 0:
+            return remote(part(x, y, ts), part(x, y, ts), ss, rs, "x")
+        if kind == 1:
+            return remote(part(x, y, ts), part(x, y, ts), ss, rs, "y")
+        if kind == 2:
+            return remote(part(x, y, ts), part(x, y, ts), ss, rs, "c")
+        if kind == 3:
+            return remote(part(1 - x, y, ts, 0), part(1 - x, y, ts, 0), ss, rs, "y")
+        if kind == 4:
+            return remote(part(x, 1 - y, ts, 1), part(x, 1 - y, ts, 1), ss, rs, "x")
+        if kind == 5:
+            return remote(part(1 - x, y, ts), part(1 - x, y, ts), ss, rs, "c")
+        if kind == 6:
+            return remote(part(x, 1 - y, ts), part(x, 1 - y, ts), ss, rs, "c")
+        return remote(part(1 - x, 1 - y, ts), part(1 - x, 1 - y, ts), ss, rs, "c")
+
+    def sl(at, size=16):
+        return pl.ds(pl.multiple_of(at, 16), size)
+
+    def free(kind, u):
+        @pl.when(u >= 2)
+        def _():
+            step_copy(kind, u - 2).wait_send()
+
+    def step(t, carry):
+        @pl.when(t < chunks)
+        def _():
+            for i, (a, _) in enumerate(pieces):
+
+                @pl.when(t == a // 128)
+                def _(i=i):
+                    if i == 0:
+                        nm_local.wait()
+                        nm_core.wait_recv()
+                    local_copies[i].wait()
+                    core_copies[i].wait_recv()
+
+            slot = t % 2
+            cols = pl.ds(pl.multiple_of(t * 128, 128), 128)
+            g[slot] = mm(dp[0, :, cols], nm[0], TN) + mm(dp[1, :, cols], nm[1], TN)
+            free(0, t)
+            free(1, t)
+            sa1[slot] = g[slot, sl((1 - x) * 32, 32)].astype(bf16)
+            step_copy(0, t).start()
+            sb1[slot, 0:16] = g[slot, sl(64 + (1 - y) * 16)].astype(bf16)
+            sb1[slot, 16:32] = g[slot, sl(96 + (1 - y) * 16)].astype(bf16)
+            step_copy(1, t).start()
+
+        @pl.when((t >= 1) & (t - 1 < chunks))
+        def _():
+            u = t - 1
+            slot = u % 2
+            step_copy(0, u).wait_recv()
+            free(2, u)
+            sa2[slot] = (
+                g[slot, sl(x * 32 + (1 - y) * 16)] + ra1[u, sl((1 - y) * 16)].astype(f32)
+            ).astype(bf16)
+            step_copy(2, u).start()
+            ka2[slot] = g[slot, sl(x * 32 + y * 16)] + ra1[u, sl(y * 16)].astype(f32)
+            step_copy(1, u).wait_recv()
+            free(3, u)
+            sb2[slot] = (
+                g[slot, sl(64 + (1 - x) * 32 + y * 16)] + rb1[u, sl((1 - x) * 16)].astype(f32)
+            ).astype(bf16)
+            step_copy(3, u).start()
+            kb2[slot] = g[slot, sl(64 + x * 32 + y * 16)] + rb1[u, sl(x * 16)].astype(f32)
+
+        @pl.when((t >= 2) & (t - 2 < chunks))
+        def _():
+            u = t - 2
+            slot = u % 2
+            step_copy(2, u).wait_recv()
+            step_copy(3, u).wait_recv()
+            for k in (4, 5, 6):
+                free(k, u)
+            va = ka2[slot] + ra2[u].astype(f32)
+            vb = kb2[slot] + rb2[u].astype(f32)
+            f3[slot, 0] = va
+            f3[slot, 1] = vb
+            s3[slot, 0] = va.astype(bf16)
+            s3[slot, 1] = vb.astype(bf16)
+            for k in (4, 5, 6):
+                step_copy(k, u).start()
+
+        @pl.when((t >= 3) & (t - 3 < chunks))
+        def _():
+            u = t - 3
+            slot = u % 2
+            for k in (4, 5, 6):
+                step_copy(k, u).wait_recv()
+            mine = pl.ds(pl.multiple_of(z * shard, 128), shard)
+            for T in (0, 1):
+                total = f3[slot, T, :, mine]
+                for k in range(3):
+                    total = total + rz[u, k, T].astype(f32)
+                o_ref[c, u, T, x, y] = total.astype(bf16)
+
+        for q, (a, b) in enumerate(groups):
+
+            @pl.when(t == b - 1 + 3)
+            def _(q=q):
+                for kind in (0, 1, 2):
+                    all_copy(q, kind).start()
+
+            @pl.when(t == b - 1 + 4)
+            def _(q=q):
+                all_copy(q, 0).wait_recv()
+                all_copy(q, 3).start()
+                all_copy(q, 5).start()
+                all_copy(q, 1).wait_recv()
+                all_copy(q, 4).start()
+                all_copy(q, 6).start()
+
+            @pl.when(t == b - 1 + 5)
+            def _(q=q):
+                all_copy(q, 3).wait_recv()
+                all_copy(q, 4).wait_recv()
+                all_copy(q, 7).start()
+
+        return carry
+
+    lax.fori_loop(0, chunks + 5, step, 0)
+    for q in range(len(groups)):
+        for kind in (2, 5, 6, 7):
+            all_copy(q, kind).wait_recv()
+        for kind in range(8):
+            all_copy(q, kind).wait_send()
+    for u in (chunks - 2, chunks - 1):
+        for kind in range(7):
+            step_copy(kind, u).wait_send()
+    nm_core.wait_send()
+    for copy in core_copies:
+        copy.wait_send()
+
+
+def reduce_products(dp, nm, collective_id):
+    rows, total = dp.shape
+    width = nm.shape[1]
+    shard = width // 4
+    wide = total // 2
+    chunks = wide // 128
+    cuts = sorted({0, min(256, wide), min(1280, wide), wide})
+    pieces = list(zip(cuts[:-1], cuts[1:]))
+    marks = sorted({0, chunks * 2 // 5, chunks * 7 // 10, chunks * 9 // 10, chunks})
+    groups = list(zip(marks[:-1], marks[1:]))
+    n = len(pieces)
+    dma = pltpu.SemaphoreType.DMA
+    out = pl.pallas_call(
+        partial(reduce_kernel, chunks, pieces, groups),
+        in_specs=[pl.BlockSpec(memory_space=pl.ANY)] * 2,
+        out_specs=pl.BlockSpec(memory_space=pltpu.VMEM),
+        out_shape=jax.ShapeDtypeStruct((2, chunks, 2, 2, 2, 16, shard), bf16),
+        scratch_shapes=[
+            pltpu.VMEM((2, rows, wide), bf16),
+            pltpu.VMEM((2, rows, width), bf16),
+            pltpu.VMEM((2, 128, width), f32),
+            pltpu.VMEM((2, 32, width), bf16),
+            pltpu.VMEM((2, 32, width), bf16),
+            pltpu.VMEM((2, 16, width), bf16),
+            pltpu.VMEM((2, 16, width), bf16),
+            pltpu.VMEM((2, 2, 16, width), bf16),
+            pltpu.VMEM((2, 16, width), f32),
+            pltpu.VMEM((2, 16, width), f32),
+            pltpu.VMEM((2, 2, 16, width), f32),
+            pltpu.VMEM((chunks, 32, width), bf16),
+            pltpu.VMEM((chunks, 32, width), bf16),
+            pltpu.VMEM((chunks, 16, width), bf16),
+            pltpu.VMEM((chunks, 16, width), bf16),
+            pltpu.VMEM((chunks, 3, 2, 16, shard), bf16),
+            dma((n + 1,)),
+            dma((n + 1,)),
+            dma((n + 1,)),
+            dma((7, 2)),
+            dma((7, chunks)),
+            dma((len(groups), 8)),
+            dma((len(groups), 8)),
+        ],
+        compiler_params=pltpu.CompilerParams(
+            collective_id=collective_id, has_side_effects=True, vmem_limit_bytes=VMEM
+        ),
+        cost_estimate=pl.CostEstimate(
+            flops=4 * rows * wide * width, bytes_accessed=200_000_000, transcendentals=0
+        ),
+        name="reduce_products",
+    )(dp, nm)
+    return out.reshape(total, shard)
+
+
+def project_kernel(n_ref, w_ref, o_ref):
+    total = mm(n_ref[0], w_ref[0], NT)
+    for k in range(1, n_ref.shape[0]):
+        total += mm(n_ref[k], w_ref[k], NT)
+    o_ref[...] = total.astype(o_ref.dtype)
+
+
+def project(parts, weight, first, count, tile, dtype):
+    shards, rows, depth = parts.shape
+    return pl.pallas_call(
+        project_kernel,
+        grid=(count // tile,),
+        in_specs=[
+            pl.BlockSpec((shards, rows, depth), lambda i: (0, 0, 0)),
+            pl.BlockSpec((shards, tile, depth), lambda i: (0, first // tile + i, 0)),
+        ],
+        out_specs=pl.BlockSpec((rows, tile), lambda i: (0, i)),
+        out_shape=jax.ShapeDtypeStruct((rows, count), dtype),
+        compiler_params=pltpu.CompilerParams(vmem_limit_bytes=VMEM),
+        name="project",
+    )(parts, weight)
+
+
+def unproject_kernel(d_ref, w_ref, o_ref):
+    @pl.when(pl.program_id(0) == 0)
+    def _():
+        o_ref[...] = jnp.zeros_like(o_ref)
+
+    for k in range(o_ref.shape[0]):
+        o_ref[k] += mm(d_ref[...], w_ref[k])
+
+
+def unproject(d, weight, tile):
+    shards, count, depth = weight.shape
+    rows = d.shape[0]
+    return pl.pallas_call(
+        unproject_kernel,
+        grid=(count // tile,),
+        in_specs=[
+            pl.BlockSpec((rows, tile), lambda i: (0, i)),
+            pl.BlockSpec((shards, tile, depth), lambda i: (0, i, 0)),
+        ],
+        out_specs=pl.BlockSpec((shards, rows, depth), lambda i: (0, 0, 0)),
+        out_shape=jax.ShapeDtypeStruct((shards, rows, depth), f32),
+        compiler_params=pltpu.CompilerParams(vmem_limit_bytes=VMEM),
+        name="unproject",
+    )(d, weight)
+
+
 def rms_front(hidden_rows, gain):
     power = jnp.mean(hidden_rows * hidden_rows, axis=-1, keepdims=True)
     return hidden_rows * lax.rsqrt(power + epsilon) * gain
@@ -401,9 +854,20 @@
     shard = lax.axis_index("wshard")
     micro, _, tokens, width = hidden.shape
     taps = conv_weight.shape[1]
+    inner = out_weight.shape[0] * shards
+    channels = conv_bias.shape[0] * shards
+    heads = dt_bias.shape[0] * shards
+    hs = inner // heads
+    n = (channels - inner) // 2
+    groups = heads // GROUP
+    rows = micro * tokens
+    fast = count == 8 and shards == 4
+    in_local = in_weight.T
     small = [norm_gain, conv_weight.T.reshape(-1), conv_bias, dt_bias, a_log, skip_gain, gated_gain]
     sizes = [v.shape[0] for v in small]
-    packed = lax.all_gather(jnp.concatenate(small), "wshard", axis=0).astype(f32)
+    small.append(in_local[inner + channels :].reshape(-1))
+    packed_low = lax.all_gather(jnp.concatenate(small), "wshard", axis=0)
+    packed = packed_low.astype(f32)
     parts, at = [], 0
     for size in sizes:
         parts.append(packed[:, at : at + size])
@@ -416,17 +880,15 @@
     skip = parts[5].reshape(-1)
     gated_g = parts[6].reshape(-1)
 
-    in_t = lax.all_gather(in_weight.T, "wshard", axis=0)
-    out_w = lax.all_gather(out_weight, "wshard", axis=0, tiled=True)
-    in_t = in_t.transpose(1, 0, 2).reshape(in_t.shape[1], -1)
-
-    inner = out_w.shape[0]
-    channels = conv_b.shape[0]
-    heads = dt_shift.shape[0]
-    hs = inner // heads
-    n = (channels - inner) // 2
-    groups = heads // GROUP
-    rows = micro * tokens
+    dt_w = packed_low[:, at:].reshape(shards, heads, -1).transpose(1, 0, 2).reshape(heads, -1)
+    order = jnp.arange(shards) ^ shard if fast else jnp.arange(shards)
+    if fast:
+        in_w = gather_input_weight(in_local, inner, channels)
+        out_part = lax.optimization_barrier((out_weight, in_w[0, 0, 0]))[0]
+    else:
+        in_w = lax.all_gather(in_local[: inner + channels], "wshard", axis=0)
+        out_part = out_weight
+    out_w = lax.all_gather(out_part, "wshard", axis=0, tiled=True)
 
     def grouped(v):
         return v.reshape(micro, tokens, groups, GROUP).transpose(0, 2, 1, 3)
@@ -437,9 +899,11 @@
     valid = (positions[None, :] < lengths[:, 0][:, None]).astype(f32).reshape(rows, 1)
     normed, front_back = jax.vjp(rms_front, rows_in, norm_g)
     normed_low = normed.astype(bf16)
-    gate_in = mm(normed_low, in_t[:inner], NT)
-    conv_low = mm(normed_low, in_t[inner : inner + channels], NT).astype(bf16)
-    dt_low = mm(normed_low, in_t[inner + channels :], NT).astype(bf16)
+    normed_parts = normed_low.reshape(rows, shards, -1).transpose(1, 0, 2)[order]
+    tile = 256
+    conv_low = project(normed_parts, in_w, inner, channels, tile, bf16)
+    gate_in = project(normed_parts, in_w, 0, inner, tile, f32)
+    dt_low = mm(normed_low, dt_w, NT).astype(bf16)
     conv_low = conv_low.reshape(micro, tokens, channels)
     prior = from_behind(conv_low[:, tokens - (taps - 1) :], "seq", 1)
     padded = jnp.concatenate([prior, conv_low], axis=1).astype(f32)
@@ -495,16 +959,20 @@
     d_padded, d_conv_w, d_conv_b = conv_back(mixed_grad)
     from_next = from_behind(d_padded[:, : taps - 1].astype(bf16), "seq", -1).astype(f32)
     d_conv = d_padded[:, taps - 1 :].at[:, tokens - (taps - 1) :].add(from_next)
+    d_dt_low = d_dt.astype(bf16).reshape(rows, heads)
+    total_cols = inner + channels + heads
+    pad = -total_cols % 256 if fast else 0
     d_proj = jnp.concatenate(
         [
             d_gate_in.astype(bf16),
             d_conv.astype(bf16).reshape(rows, channels),
-            d_dt.astype(bf16).reshape(rows, heads),
+            d_dt_low,
+            jnp.zeros((rows, pad), bf16),
         ],
         axis=1,
     )
-    in_terms = mm(d_proj, normed_low, TN)
-    d_normed = mm(d_proj, in_t)
+    d_parts = unproject(d_proj, in_w, tile)
+    d_normed = d_parts[order].transpose(1, 0, 2).reshape(rows, width) + mm(d_dt_low, dt_w)
     d_hidden, d_norm_g = front_back(d_normed)
     input_grad = (d_hidden + cot).astype(bf16).reshape(hidden.shape)
 
@@ -513,7 +981,10 @@
         t = lax.psum_scatter(t, "wshard", scatter_dimension=axis, tiled=True)
         return lax.all_gather(t, "seq", axis=0, tiled=True).astype(f32)
 
-    in_grad = summed(in_terms, 1).T
+    if fast:
+        in_grad = reduce_products(d_proj, normed_low, 2)[:total_cols].astype(f32).T
+    else:
+        in_grad = summed(mm(d_proj, normed_low, TN), 1).T
     blocks = out_terms.reshape(shards, count, -1, width).transpose(1, 0, 2, 3)
     blocks = blocks.reshape(inner, width)
     out_w_grad = summed_rows(blocks, shards, count)

time: 1340 us -> 851 us (0.64)
  waiting for transfers between devices: 603 us -> 109 us
  Pallas kernels: 85.7 us -> 426 us
  blocking collectives: 229 us -> 9.37 us
  local copies, waits for them, and re-layouts: 188 us -> 111 us
  matrix products: 89.1 us -> 35.7 us
  other arithmetic: 104 us -> 120 us
    all_gather x3 -> x1, waiting for transfers between devices: 350 us -> 0.02 us  [local(): out_w = lax.all_gather(out_part, 'wshard', axis=0, tiled=True)]
    pallas_call x0 -> x5, Pallas kernels: none -> 341 us  [the longest x1 151 us: gather_input_weight(): pl.pallas_call(partial(gather_kernel, chunks), in_specs=[pl.BlockSpec(mem...]
    unnamed x2 -> x0, blocking collectives: 220 us -> none
    psum x1, waiting for transfers between devices: 111 us -> 0.01 us  [local(): sums = lax.psum(jnp.concatenate(smalls, axis=1), ('seq', 'wshard'))]
    ppermute x6, waiting for transfers between devices: 34.1 us -> 108 us  [swap(): return lax.ppermute(x, 'seq', [(i, i ^ by) for i in range(count)])]
    unnamed x10 -> x7, waiting for transfers between devices: 56.2 us -> 0.8 us
    dot_general x8 -> x5, matrix products: 87.9 us -> 35.1 us  [mm(): return lax.dot_general(a, b, dims, preferred_element_type=f32)]
    slice x5 -> x2, local copies, waits for them, and re-layouts: 44.5 us -> 1.03 us  [the longest x1 0.88 us: local(): small.append(in_local[inner + channels:].reshape(-1))]
  transfers between devices with their start and end apart: 17 -> 14, of which waited for: 8 -> 3; matrix products, arithmetic and copies ran while one was open for 40% -> 23% of each run, Pallas kernels for 6% -> 51%
where the time goes in v2:
time: 851 us; the launch traced here: 839 us
  Pallas kernels  426 us (50%)
  other arithmetic  120 us (14%)
  local copies, waits for them, and re-layouts  111 us (13%)
  waiting for transfers between devices  109 us (13%)
  matrix products  35.7 us (4%)
  between operations  16.6 us (2%)
  starting transfers between devices  11.1 us (1%)
  blocking collectives  9.37 us (1%)
    pallas_call x1, Pallas kernels, gather_input_weight(): pl.pallas_call(partial(gather_kernel, chunks), in_specs=[pl.BlockSpec(mem...  151 us
    pallas_call x1, Pallas kernels, reduce_products(): pl.pallas_call(partial(reduce_kernel, chunks, pieces, groups), in_specs=[...  136 us
    ppermute x6, waiting for transfers between devices, swap(): return lax.ppermute(x, 'seq', [(i, i ^ by) for i in range(count)])  108 us
    dot_general x5, matrix products, mm(): return lax.dot_general(a, b, dims, preferred_element_type=f32)  35.1 us
    pallas_call x2, Pallas kernels, project(): pl.pallas_call(project_kernel, grid=(count // tile,), in_specs=[pl.BlockS...  27.9 us
    pallas_call x1, Pallas kernels, unproject(): pl.pallas_call(unproject_kernel, grid=(count // tile,), in_specs=[pl.Bloc...  26 us
    pallas_call x1, Pallas kernels, carry_back(): pl.pallas_call(partial(carry_back_kernel, hs), grid=(micro, groups), in_s...  22.3 us
    pallas_call x2, Pallas kernels, block_states(): pl.pallas_call(partial(state_kernel, hs), grid=(micro, cols // gc), in_sp...  20.1 us
  transfers between devices with their start and end apart: 14, of which 3 were waited for; matrix products, arithmetic and copies ran while one was open for 23% of the time, Pallas kernels for 51%

profile of v2, /device:TPU:0, one launch (start us, length us, event | category | flops | bytes accessed | tf_op | source)
XLA Modules:
  0.0 838.5 jit_solution(17738931377575894422)
XLA Ops:
  10.8 4.2 concatenate.17
  17.6 2.2 reshape.592
  19.7 150.7 %gather_input_weight.1.w_ref = bf16[4,6400,384]{2,1,0:T(8,128)(2,1)} custom-call(bf16[6448,384]{1,0:T(8,128)(2,1)} %bitcast.174), custom_call_target="tpu_custom_call" | custom-call | bytes 200000000 | tf_op jit(solution)/shard_map/gather_input_weight/pallas_call | solution.py:478
  181.4 1.5 fusion.34
  183.0 2.3 gather_fusion
  185.3 13.9 %project.2 = bf16[512,3328]{1,0:T(8,128)(2,1)S(1)} custom-call(bf16[4,512,384]{2,1,0:T(8,128)(2,1)S(1)} %gather_fusion, bf16[4,6400,384]{2,1,0:T(8,128)(2,1)} %gather_input_weight.1.w_ref), custom_call_target="tpu_custom_call" | custom-call | tf_op jit(solution)/shard_map/project/pallas_call | solution.py:777
  199.3 1.7 copy-done.7
  201.7 3.2 collective-permute-start
  206.2 2.1 bitcast_exponential_fusion
  211.4 1.6 copy.148
  214.8 1.5 maximum_convert_fusion
  216.4 6.2 multiply_convert_fusion
  222.5 2.1 slice.205.x_ref
  226.9 9.8 %block_states.2 = f32[2,128,3072]{2,1,0:T(8,128)S(1)} custom-call(bf16[2,256,3072]{2,1,0:T(8,128)(2,1)} %slice.205.x_ref, f32[2,6,256,8]{3,2,1,0:T(8,128)S(1)} %bitcast.155, bf16[2,128,256]{2,1,0:T(8,128)(2,1)S(1)} %copy.149.bt_ref), custom_call_target="tpu_custom_call" | custom-call | tf_op jit(solution)/shard_map/block_states/pallas_call | solution.py:50
  238.1 2.0 collective-permute-start.1
  240.1 9.4 %all-gather.1 = f32[16,1,48]{2,1,0:T(1,128)S(1)} all-gather(f32[2,1,48]{2,1,0:T(1,128)S(1)} %bitcast.199), channel_id=3, replica_groups=mesh['seq'=8,'wshard'=4] {'seq'}, dimensions={0}, use_global_device_ids=true | all-gather | bytes 3456 | tf_op jit(solution)/shard_map/all_gather | solution.py:922
  251.8 3.1 fusion.33
  256.0 2.9 fusion.20
  260.5 31.3 %collective-permute-done.2 = bf16[2,128,3072]{2,1,0:T(8,128)(2,1)} collective-permute-done((bf16[2,128,3072]{2,1,0:T(8,128)(2,1)}, bf16[2,128,3072]{2,1,0:T(8,128)(2,1)}, u32[]{:S(2)}, u32[]{:S(2)}) %collective-permute-start.2) | collective-permute-done | bytes 1572896 | tf_op jit(solution)/shard_map/ppermute | solution.py:335
  291.8 3.9 fusion.11
  296.3 1.5 fusion.19
  298.1 14.0 %project.3 = f32[512,3072]{1,0:T(8,128)} custom-call(bf16[4,512,384]{2,1,0:T(8,128)(2,1)S(1)} %copy-done.6, bf16[4,6400,384]{2,1,0:T(8,128)(2,1)} %gather_input_weight.1.w_ref), custom_call_target="tpu_custom_call" | custom-call | tf_op jit(solution)/shard_map/project/pallas_call | solution.py:777
  320.6 1.9 select_bitcast_fusion.dt_ref
  322.5 14.2 %local_scan.1.y_ref = f32[2,256,3072]{2,1,0:T(8,128)} custom-call(bf16[2,256,3072]{2,1,0:T(8,128)(2,1)} %slice.205.x_ref, f32[2,6,256,8]{3,2,1,0:T(8,128)S(1)} %select_bitcast_fusion.dt_ref, f32[2,6,256,8]{3,2,1,0:T(8,128)S(1)} %bitcast.149, f32[2,6,8,256]{3,2,1,0:T(8,128)S(1)} %bitcast.158, bf16[2,256,128]{2,1,0:T(8,128)(2,1)S(1)} %get-tuple-element.166.b_ref, ...), custom_call_target="tpu_custom_call" | custom-call | tf_op jit(solution)/shard_map/local_scan/pallas_call | solution.py:97
  336.7 5.0 fusion.8.s_ref.si_ref
  341.8 12.6 %add_carry.1 = (f32[2,256,3072]{2,1,0:T(8,128)}, bf16[2,256,3072]{2,1,0:T(8,128)(2,1)S(1)}) custom-call(bf16[2,256,3072]{2,1,0:T(8,128)(2,1)} %slice.205.x_ref, f32[2,256,3072]{2,1,0:T(8,128)} %local_scan.1.y_ref, f32[2,6,256,8]{3,2,1,0:T(8,128)S(1)} %bitcast.150, bf16[2,256,128]{2,1,0:T(8,128)(2,1)S(1)} %get-tuple-element.165.c_ref, ...), custom_call_target="tpu_custom_call" | custom-call | tf_op jit(solution)/shard_map/add_carry/pallas_call | solution.py:128
  354.4 2.6 multiply_reduce_fusion.6
  357.0 11.9 %multiply_reduce_fusion.4 = (f32[3072]{0:T(1024)}, f32[512]{0:T(512)S(1)}, f32[512,3072]{1,0:T(8,128)S(1)}) fusion(f32[512]{0:T(512)S(1)} %fusion.46, bf16[2,256,3072]{2,1,0:T(8,128)(2,1)} %copy-done.9, f32[512,3072]{1,0:T(8,128)} %project.3, f32[3072]{0:T(1024)S(1)} %copy-done.58, bf16[512,1536]{1,0:T(8,128)(2,1)} %fusion.20, ...), kind=kOutput, calls=%fused_computation.23 | convolution fusion | flops 4850708992 | bytes 26767360 | tf_op jit(solution)/shard_map/dot_general | solution.py:23
  369.0 10.8 %multiply_convert_fusion.1 = (bf16[512,3072]{1,0:T(8,128)(2,1)}, bf16[512,3072]{1,0:T(8,128)(2,1)}, bf16[512,3072]{1,0:T(8,128)(2,1)}) fusion(f32[512]{0:T(512)S(1)} %multiply_multiply_fusion.1, f32[512,3072]{1,0:T(8,128)S(1)} %get-tuple-element.190, f32[3072]{0:T(1024)S(1)} %copy-done.58, f32[512]{0:T(512)S(1)} %fusion.46, ...), kind=kLoop, calls=%fused_computation.24 | loop fusion | flops 37748736 | bytes 25182208 | tf_op jit(solution)/shard_map/convert_element_type | solution.py:941
  379.8 3.2 copy.160
  383.0 8.9 %convert_bitcast_fusion.1 = bf16[8,4,96,1536]{3,2,0,1:T(8,128)(2,1)} fusion(bf16[4,8,96,512]{3,2,1,0:T(8,128)(2,1)S(1)} %bitcast.177, bf16[512,1536,1,1]{1,0,3,2:T(8,128)(2,1)} %bitcast.180), kind=kOutput, calls=%fused_computation.6 | convolution fusion | flops 4836556800 | bytes 14155776 | tf_op jit(solution)/shard_map/dot_general | solution.py:23
  391.8 8.3 copy.161
  401.3 1.6 copy.151
  403.7 1.4 copy-done.12
  406.0 10.3 %block_states.3 = f32[2,128,3072]{2,1,0:T(8,128)S(1)} custom-call(bf16[2,256,3072]{2,1,0:T(8,128)(2,1)} %bitcast.164, f32[2,6,256,8]{3,2,1,0:T(8,128)S(1)} %bitcast.156, bf16[2,128,256]{2,1,0:T(8,128)(2,1)S(1)} %copy-done.13), custom_call_target="tpu_custom_call" | custom-call | tf_op jit(solution)/shard_map/block_states/pallas_call | solution.py:50
  420.0 1.5 select_n.384
  421.5 3.1 fusion.32
  424.5 1.5 collective-permute-start.5
  426.8 1.5 select_n.390
  429.0 1.5 select_n.392
  430.4 56.5 %collective-permute-done.5 = bf16[2,128,3072]{2,1,0:T(8,128)(2,1)} collective-permute-done((bf16[2,128,3072]{2,1,0:T(8,128)(2,1)}, bf16[2,128,3072]{2,1,0:T(8,128)(2,1)}, u32[]{:S(2)}, u32[]{:S(2)}) %collective-permute-start.5) | collective-permute-done | bytes 1572896 | tf_op jit(solution)/shard_map/ppermute | solution.py:335
  486.9 3.9 fusion.16
  490.9 1.5 collective-permute-start.6
  495.8 16.2 %local_back.1 = (f32[2,256,3072]{2,1,0:T(8,128)}, f32[2,256,128]{2,1,0:T(8,128)S(1)}, f32[2,256,128]{2,1,0:T(8,128)S(1)}) custom-call(bf16[2,256,3072]{2,1,0:T(8,128)(2,1)} %slice.205.x_ref, bf16[2,256,3072]{2,1,0:T(8,128)(2,1)} %bitcast.165, f32[2,6,256,8]{3,2,1,0:T(8,128)S(1)} %copy-done.3, f32[2,6,256,8]{3,2,1,0:T(8,128)S(1)} %bitcast.152, ...), custom_call_target="tpu_custom_call" | custom-call | tf_op jit(solution)/shard_map/local_back/pallas_call | solution.py:200
  514.0 20.3 %collective-permute-done.6 = bf16[2,128,3072]{2,1,0:T(8,128)(2,1)S(1)} collective-permute-done((bf16[2,128,3072]{2,1,0:T(8,128)(2,1)}, bf16[2,128,3072]{2,1,0:T(8,128)(2,1)S(1)}, u32[]{:S(2)}, u32[]{:S(2)}) %collective-permute-start.6) | collective-permute-done | bytes 1572896 | tf_op jit(solution)/shard_map/ppermute | solution.py:335
  534.2 4.3 fusion.13.ds_ref
  538.6 22.3 %carry_back.1 = (bf16[2,256,3072]{2,1,0:T(8,128)(2,1)}, f32[2,6,256,8]{3,2,1,0:T(8,128)S(1)}, f32[2,6,256,8]{3,2,1,0:T(8,128)S(1)}, f32[2,256,128]{2,1,0:T(8,128...) custom-call(bf16[2,256,3072]{2,1,0:T(8,128)(2,1)} %slice.205.x_ref, ...), custom_call_target="tpu_custom_call" | custom-call | tf_op jit(solution)/shard_map/carry_back/pallas_call | solution.py:295
  563.2 2.7 convert_element_type.189
  566.0 14.9 %multiply_reduce_fusion.3 = (f32[3328]{0:T(1024)S(1)}, f32[3328]{0:T(1024)S(1)}, f32[3328]{0:T(1024)S(1)}, f32[3328]{0:T(1024)S(1)}, f32[3328]{0:T(1024)}, /*index=5*/f32[2,256,3328]{2,1,0:T(8,128)S(1)}) fusion(f32[2,259,3328]{2,1,0:T(8,128)} %copy-done.24, f32[2,256,3328]{2,1,0:T(8,128)} %get-tuple-element.155, f32[2,256,128]{2,1,0:T(8,128)S(1)} %copy-done.19, ...), kind=kLoop, calls=%fused_computation.16 | loop fusion | flops 34062080 | bytes 47776768 | tf_op jit(solution)/shard_map/transpose(jvp())/reduce_sum | solution.py:827
  581.0 7.3 broadcast_multiply_fusion
  588.3 11.0 %pad_add_fusion = f32[2,259,3328]{2,1,0:T(8,128)} fusion(f32[2,256,3328]{2,1,0:T(8,128)} %get-tuple-element.160, f32[2,256,3328]{2,1,0:T(8,128)} %get-tuple-element.161, f32[2,256,3328]{2,1,0:T(8,128)} %get-tuple-element.162, f32[2,256,3328]{2,1,0:T(8,128)S(1)} %get-tuple-element.159), kind=kLoop, calls=%fused_computation.9 | loop fusion | flops 5171712 | bytes 34158592 | tf_op jit(solution)/shard_map/transpose(jvp())/add_any | solution.py:825
  600.8 1.6 slice.242
  606.6 3.6 slice.214
  615.5 11.0 %concatenate.20.d_ref.dp_ref = bf16[512,6656]{1,0:T(8,128)(2,1)} concatenate(bf16[512,3072]{1,0:T(8,128)(2,1)} %get-tuple-element.157, bf16[512,3328]{1,0:T(8,128)(2,1)S(1)} %bitcast.168, bf16[512,48]{1,0:T(8,128)(2,1)} %bitcast.184, bf16[512,208]{1,0:T(8,128)(2,1)} %broadcast_in_dim.221), dimensions={1} | concatenate | bytes 13631488 | tf_op jit(solution)/shard_map/concatenate | solution.py:965
  626.6 26.0 %unproject.1 = f32[4,512,384]{2,1,0:T(8,128)S(1)} custom-call(bf16[512,6656]{1,0:T(8,128)(2,1)} %concatenate.20.d_ref.dp_ref, bf16[4,6400,384]{2,1,0:T(8,128)(2,1)} %gather_input_weight.1.w_ref), custom_call_target="tpu_custom_call" | custom-call | tf_op jit(solution)/shard_map/unproject/pallas_call | solution.py:803
  652.6 2.5 gather_fusion.1
  655.1 2.4 copy.165
  657.7 2.8 fusion.23
  661.3 2.1 convert_element_type.203
  663.5 10.9 %fusion.31 = bf16[512,1536]{1,0:T(8,128)(2,1)} fusion(f32[512,1536]{1,0:T(8,128)} %bitcast.176, bf16[512,3072]{1,0:T(8,128)(2,1)} %get-tuple-element.158, bf16[3072,1536]{1,0:T(8,128)(2,1)} %all-gather.5.cloned.1.call-done, f32[512]{0:T(512)S(1)} %bitcast.197), kind=kOutput, calls=%fused_computation.79 | convolution fusion | flops 4834197504 | bytes 17303552 | tf_op jit(solution)/shard_map/dot_general | solution.py:23
  674.4 2.1 fusion.18
  676.5 136.2 %reduce_products.1 = bf16[2,26,2,2,2,16,384]{6,5,4,3,2,1,0:T(8,128)(2,1)} custom-call(bf16[512,6656]{1,0:T(8,128)(2,1)} %concatenate.20.d_ref.dp_ref, bf16[512,1536]{1,0:T(8,128)(2,1)S(1)} %get-tuple-element.167.nm_ref), custom_call_target="tpu_custom_call" | custom-call | flops 10468982784 | bytes 200000000 | tf_op jit(solution)/shard_map/reduce_products/pallas_call | solution.py:727
  812.7 7.0 convert_bitcast_fusion
  826.7 4.5 convert_element_type.202
  (356 shorter events, 75.5 us)
Async XLA Ops:
  7.2 10.0 %copy-start.25 = (bf16[2,1,256,1536]{3,2,1,0:T(8,128)(2,1)S(1)}, bf16[2,1,256,1536]{3,2,1,0:T(8,128)(2,1)}, u32[]{:S(2)}) copy-start(bf16[2,1,256,1536]{3,2,1,0:T(8,128)(2,1)} %param.14) | copy-start | bytes 4718596
  7.2 163.4 %all-reduce.14.cloned.1.call-start = ((), (), s32[]{:S(2)}) async-start(), calls=%async_computation.7 | async-start | bytes 380928
  16.4 340.7 %all-gather.5.cloned.1.call-start = ((), (), s32[]{:S(2)}) async-start(), calls=%async_computation.2 | async-start | bytes 11796480 | tf_op jit(solution)/shard_map/all_gather | solution.py:891
  17.1 582.2 %reduce-scatter.3.cloned.1.call-start = ((), (), s32[]{:S(2)}) async-start(), calls=%async_computation.4 | async-start | bytes 10616832 | tf_op jit(solution)/shard_map/reduce_scatter | solution.py:1022
  170.5 11.0 %copy-start.60 = (f32[512]{0:T(512)}, f32[512]{0:T(512)S(1)}, u32[]{:S(2)}) copy-start(f32[512]{0:T(512)S(1)} %rsqrt.23) | copy-start | bytes 6148
  170.5 12.4 %copy-start.74 = (s32[1024]{0:T(1024)}, s32[1024]{0:T(1024)S(1)}, u32[]{:S(2)}) copy-start(s32[1024]{0:T(1024)S(1)} %pad_clamp_fusion) | copy-start | bytes 12292
  171.7 4.0 copy-start.35
  172.8 8.7 %copy-start.29 = (f32[512,4,384]{2,1,0:T(4,128)S(1)}, f32[512,4,384]{2,1,0:T(4,128)}, u32[]{:S(2)}) copy-start(f32[512,4,384]{2,1,0:T(4,128)} %reshape.592) | copy-start | bytes 9437188
  176.6 8.7 %copy-start.33 = (f32[2,256,48]{2,0,1:T(2,128)}, f32[2,256,48]{2,0,1:T(2,128)S(1)}, u32[]{:S(2)}) copy-start(f32[2,256,48]{2,0,1:T(2,128)S(1)} %copy.141) | copy-start | bytes 294916
  185.3 13.9 %copy-start.5 = (bf16[4,512,384]{2,1,0:T(8,128)(2,1)}, bf16[4,512,384]{2,1,0:T(8,128)(2,1)S(1)}, u32[]{:S(2)}) copy-start(bf16[4,512,384]{2,1,0:T(8,128)(2,1)S(1)} %gather_fusion) | copy-start | bytes 4718596
  185.3 19.5 %copy-start.45 = (f32[4,3328]{1,0:T(4,128)S(1)}, f32[4,3328]{1,0:T(4,128)}, u32[]{:S(2)}) copy-start(f32[4,3328]{1,0:T(4,128)} %slice.197) | copy-start | bytes 159748
  201.7 13.2 %copy-start.8 = (bf16[512,3328]{1,0:T(8,128)(2,1)S(1)}, bf16[512,3328]{1,0:T(8,128)(2,1)}, u32[]{:S(2)}) copy-start(bf16[512,3328]{1,0:T(8,128)(2,1)} %copy-done.7) | copy-start | bytes 10223620
  201.7 13.2 %collective-permute-start = (bf16[2,3,3328]{2,1,0:T(4,128)(2,1)}, bf16[2,3,3328]{2,1,0:T(4,128)(2,1)}, u32[]{:S(2)}, u32[]{:S(2)}) collective-permute-start(bf16[2,3,3328]{2,1,0:T(4,128)(2,1)} %slice.195), channel_id=1, source_target_pairs={{0,4},{4,8},{8,12},{12,16},{16,20},{20,24},{24,28},{1,5},{5,9},{9,... | collective-permute-start | bytes 119816 | tf_op jit(solution)/shard_map/ppermute | solution.py:330
  216.4 6.2 copy-start.24
  236.7 3.4 copy-start.79
  238.1 13.7 %collective-permute-start.1 = (bf16[2,128,3072]{2,1,0:T(8,128)(2,1)}, bf16[2,128,3072]{2,1,0:T(8,128)(2,1)}, u32[]{:S(2)}, u32[]{:S(2)}) collective-permute-start(bf16[2,128,3072]{2,1,0:T(8,128)(2,1)} %convert_element_type.168), channel_id=1, source_target_pairs={{0,4},{4,0},{8,12},{12,8},{16,20},{20,16},{24,28},{28,24},{1,5},{5... | collective-permute-start | bytes 4718600 | tf_op jit(solution)/shard_map/ppermute | solution.py:335
  251.8 3.6 copy-start.90
  254.9 36.9 %collective-permute-start.2 = (bf16[2,128,3072]{2,1,0:T(8,128)(2,1)}, bf16[2,128,3072]{2,1,0:T(8,128)(2,1)}, u32[]{:S(2)}, u32[]{:S(2)}) collective-permute-start(bf16[2,128,3072]{2,1,0:T(8,128)(2,1)} %fusion.33), channel_id=1, source_target_pairs={{0,8},{4,12},{8,0},{12,4},{16,24},{20,28},{24,16},{28,20},{1,9},{5... | collective-permute-start | bytes 4718600 | tf_op jit(solution)/shard_map/ppermute | solution.py:335
  256.0 3.5 copy-start.71
  260.4 35.9 %copy-start.27 = (bf16[2,1,256,1536]{3,2,1,0:T(8,128)(2,1)S(1)}, bf16[2,1,256,1536]{3,2,1,0:T(8,128)(2,1)}, u32[]{:S(2)}) copy-start(bf16[2,1,256,1536]{3,2,1,0:T(8,128)(2,1)} %param.16) | copy-start | bytes 4718596
  260.4 35.8 %copy-start.73 = (f32[2,256]{1,0:T(2,128)S(1)}, f32[2,256]{1,0:T(2,128)}, u32[]{:S(2)}) copy-start(f32[2,256]{1,0:T(2,128)} %get-tuple-element.180) | copy-start | bytes 6148
  295.7 41.0 %collective-permute-start.3 = (bf16[2,128,3072]{2,1,0:T(8,128)(2,1)}, bf16[2,128,3072]{2,1,0:T(8,128)(2,1)}, u32[]{:S(2)}, u32[]{:S(2)}) collective-permute-start(bf16[2,128,3072]{2,1,0:T(8,128)(2,1)} %fusion.11), channel_id=1, source_target_pairs={{0,16},{4,20},{8,24},{12,28},{16,0},{20,4},{24,8},{28,12},{1,17},{... | collective-permute-start | bytes 4718600 | tf_op jit(solution)/shard_map/ppermute | solution.py:335
  298.1 15.4 %copy-start.85 = (f32[2,48]{1,0:T(2,128)S(1)}, f32[2,48]{1,0:T(2,128)}, u32[]{:S(2)}) copy-start(f32[2,48]{1,0:T(2,128)} %get-tuple-element.145) | copy-start | bytes 1156
  298.1 15.6 %copy-start.84 = (f32[2,48]{1,0:T(2,128)S(1)}, f32[2,48]{1,0:T(2,128)}, u32[]{:S(2)}) copy-start(f32[2,48]{1,0:T(2,128)} %get-tuple-element.142) | copy-start | bytes 1156
  298.1 16.4 %copy-start.83 = (f32[2,48]{1,0:T(2,128)S(1)}, f32[2,48]{1,0:T(2,128)}, u32[]{:S(2)}) copy-start(f32[2,48]{1,0:T(2,128)} %get-tuple-element.146) | copy-start | bytes 1156
  312.1 5.4 copy-start.70
  317.5 24.3 %copy-start = (f32[2,256,6,8]{3,1,2,0:T(8,128)}, f32[2,256,6,8]{3,1,2,0:T(8,128)S(1)}, u32[]{:S(2)}) copy-start(f32[2,256,6,8]{3,1,2,0:T(8,128)S(1)} %copy.145) | copy-start | bytes 294916
  322.4 14.3 %copy-start.2 = (f32[2,6,256,8]{3,2,1,0:T(8,128)}, f32[2,6,256,8]{3,2,1,0:T(8,128)S(1)}, u32[]{:S(2)}) copy-start(f32[2,6,256,8]{3,2,1,0:T(8,128)S(1)} %select_bitcast_fusion.dt_ref) | copy-start | bytes 294916
  322.5 14.3 %copy-start.56 = (f32[2,3072]{1,0:T(2,128)S(1)}, f32[2,3072]{1,0:T(2,128)}, u32[]{:S(2)}) copy-start(f32[2,3072]{1,0:T(2,128)} %select_n.366) | copy-start | bytes 73732
  322.5 14.3 %copy-start.57 = (f32[2,3072]{1,0:T(2,128)S(1)}, f32[2,3072]{1,0:T(2,128)}, u32[]{:S(2)}) copy-start(f32[2,3072]{1,0:T(2,128)} %select_n.346) | copy-start | bytes 73732
  336.7 17.6 %slice-start = ((s8[6291456]{0:T(1024)(128)(4,1)}), s8[4194304]{0:T(1024)(128)(4,1)S(1)}, s32[]{:S(2)}) async-start(s8[6291456]{0:T(1024)(128)(4,1)} %bitcast.162), calls=%async_computation.8 | async-start | bytes 8388608
  341.8 12.6 %slice-start.1 = ((s8[6291456]{0:T(1024)(128)(4,1)}), s8[2097152]{0:T(1024)(128)(4,1)S(1)}, s32[]{:S(2)}) async-start(s8[6291456]{0:T(1024)(128)(4,1)} %bitcast.162), calls=%async_computation.9 | async-start | bytes 4194304
  357.0 12.0 %copy-start.10 = (bf16[2,256,3072]{2,1,0:T(8,128)(2,1)S(1)}, bf16[2,256,3072]{2,1,0:T(8,128)(2,1)}, u32[]{:S(2)}) copy-start(bf16[2,256,3072]{2,1,0:T(8,128)(2,1)} %copy-done.9) | copy-start | bytes 9437188
  400.2 263.2 %reduce-scatter.5.cloned.1.call-start = ((), (), s32[]{:S(2)}) async-start(), calls=%async_computation.5 | async-start | bytes 1474560 | tf_op jit(solution)/shard_map/reduce_scatter | solution.py:1023
  416.3 3.0 copy-start.87
  417.7 3.8 collective-permute-start.4
  421.5 4.6 copy-start.88
  421.5 6.8 copy-start.89
  424.5 62.4 %collective-permute-start.5 = (bf16[2,128,3072]{2,1,0:T(8,128)(2,1)}, bf16[2,128,3072]{2,1,0:T(8,128)(2,1)}, u32[]{:S(2)}, u32[]{:S(2)}) collective-permute-start(bf16[2,128,3072]{2,1,0:T(8,128)(2,1)} %fusion.32), channel_id=1, source_target_pairs={{0,8},{4,12},{8,0},{12,4},{16,24},{20,28},{24,16},{28,20},{1,9},{5... | collective-permute-start | bytes 4718600 | tf_op jit(solution)/shard_map/ppermute | solution.py:335
  430.4 62.0 %copy-start.82 = (f32[2,48]{1,0:T(2,128)S(1)}, f32[2,48]{1,0:T(2,128)}, u32[]{:S(2)}) copy-start(f32[2,48]{1,0:T(2,128)} %get-tuple-element.139) | copy-start | bytes 1156
  430.4 62.1 %copy-start.81 = (f32[2,48]{1,0:T(2,128)S(1)}, f32[2,48]{1,0:T(2,128)}, u32[]{:S(2)}) copy-start(f32[2,48]{1,0:T(2,128)} %get-tuple-element.138) | copy-start | bytes 1156
  430.4 62.3 %copy-start.80 = (f32[2,48]{1,0:T(2,128)S(1)}, f32[2,48]{1,0:T(2,128)}, u32[]{:S(2)}) copy-start(f32[2,48]{1,0:T(2,128)} %get-tuple-element.137) | copy-start | bytes 1156
  490.9 43.4 %collective-permute-start.6 = (bf16[2,128,3072]{2,1,0:T(8,128)(2,1)}, bf16[2,128,3072]{2,1,0:T(8,128)(2,1)S(1)}, u32[]{:S(2)}, u32[]{:S(2)}) collective-permute-start(bf16[2,128,3072]{2,1,0:T(8,128)(2,1)} %fusion.16), channel_id=1, source_target_pairs={{0,16},{4,20},{8,24},{12,28},{16,0},{20,4},{24,8},{28,12},{1,17},{... | collective-permute-start | bytes 4718600 | tf_op jit(solution)/shard_map/ppermute | solution.py:335
  495.8 17.6 %copy-start.66 = (f32[3072]{0:T(1024)S(1)}, f32[3072]{0:T(1024)}, u32[]{:S(2)}) copy-start(f32[3072]{0:T(1024)} %get-tuple-element.124) | copy-start | bytes 36868
  514.0 24.6 %copy-start.4 = (f32[2,6,256,8]{3,2,1,0:T(8,128)S(1)}, f32[2,6,256,8]{3,2,1,0:T(8,128)}, u32[]{:S(2)}) copy-start(f32[2,6,256,8]{3,2,1,0:T(8,128)} %copy-done.2) | copy-start | bytes 294916
  514.0 24.6 %copy-start.15 = (f32[2,256,128]{2,1,0:T(8,128)S(1)}, f32[2,256,128]{2,1,0:T(8,128)}, u32[]{:S(2)}) copy-start(f32[2,256,128]{2,1,0:T(8,128)} %copy-done.14) | copy-start | bytes 786436
  514.0 24.6 %copy-start.17 = (f32[2,256,128]{2,1,0:T(8,128)S(1)}, f32[2,256,128]{2,1,0:T(8,128)}, u32[]{:S(2)}) copy-start(f32[2,256,128]{2,1,0:T(8,128)} %copy-done.16) | copy-start | bytes 786436
  566.0 15.0 %copy-start.47 = (f32[3328]{0:T(1024)S(1)}, f32[3328]{0:T(1024)}, u32[]{:S(2)}) copy-start(f32[3328]{0:T(1024)} %copy-done.46) | copy-start | bytes 39940
  566.0 15.0 %copy-start.49 = (f32[3328]{0:T(1024)S(1)}, f32[3328]{0:T(1024)}, u32[]{:S(2)}) copy-start(f32[3328]{0:T(1024)} %copy-done.48) | copy-start | bytes 39940
  566.0 15.0 %copy-start.51 = (f32[3328]{0:T(1024)S(1)}, f32[3328]{0:T(1024)}, u32[]{:S(2)}) copy-start(f32[3328]{0:T(1024)} %copy-done.50) | copy-start | bytes 39940
  566.0 14.9 %copy-start.53 = (f32[3328]{0:T(1024)S(1)}, f32[3328]{0:T(1024)}, u32[]{:S(2)}) copy-start(f32[3328]{0:T(1024)} %copy-done.52) | copy-start | bytes 39940
  599.2 4.6 copy-start.32
  599.2 4.6 copy-start.34
  599.2 4.6 copy-start.76
  599.3 4.6 copy-start.78
  599.3 220.3 %all-reduce.12.cloned.1.call-start = ((), (), s32[]{:S(2)}) async-start(), calls=%async_computation.3 | async-start | bytes 172032 | tf_op jit(solution)/shard_map/psum | solution.py:1000
  602.3 11.1 %collective-permute-start.7 = (bf16[2,3,3328]{2,1,0:T(4,128)(2,1)}, bf16[2,3,3328]{2,1,0:T(4,128)(2,1)}, u32[]{:S(2)}, u32[]{:S(2)}) collective-permute-start(bf16[2,3,3328]{2,1,0:T(4,128)(2,1)} %slice.242), channel_id=1, source_target_pairs={{4,0},{8,4},{12,8},{16,12},{20,16},{24,20},{28,24},{5,1},{9,5},{13... | collective-permute-start | bytes 119816 | tf_op jit(solution)/shard_map/ppermute | solution.py:330
  606.6 3.6 copy-start.44
  606.6 6.0 copy-start.21
  660.5 2.9 copy-start.72
  661.3 165.4 %all-gather.7.cloned.1.call-start = ((), (), s32[]{:S(2)}) async-start(), calls=%async_computation.6 | async-start | bytes 2654208 | tf_op jit(solution)/shard_map/all_gather | solution.py:1024
  663.5 10.9 %copy-start.63 = (f32[1,2,2,128]{3,1,2,0:T(2,128)S(1)}, f32[1,2,2,128]{3,1,2,0:T(2,128)}, u32[]{:S(2)}) copy-start(f32[1,2,2,128]{3,1,2,0:T(2,128)} %copy-done.62) | copy-start | bytes 6148
  663.5 10.9 %copy-start.28 = (bf16[2,1,256,1536]{3,2,1,0:T(8,128)(2,1)S(1)}, bf16[2,1,256,1536]{3,2,1,0:T(8,128)(2,1)}, u32[]{:S(2)}) copy-start(bf16[2,1,256,1536]{3,2,1,0:T(8,128)(2,1)} %param.16) | copy-start | bytes 4718596
  663.5 10.9 %copy-start.30 = (f32[512,1536]{1,0:T(8,128)S(1)}, f32[512,1536]{1,0:T(8,128)}, u32[]{:S(2)}) copy-start(f32[512,1536]{1,0:T(8,128)} %get-tuple-element.191) | copy-start | bytes 9437188
  (43 other events, 78.3 us)
Sparse Core Ops, SparseCore 0:
  16.5 47.6 all-reduce.13
  65.8 171.4 all-gather.4
  400.3 108.6 reduce-scatter.2
  599.4 29.1 reduce-scatter.4
  661.4 123.9 all-reduce.11
  787.3 31.8 all-gather.6

commit v3 on v2

--- a/solution.py
+++ b/solution.py
@@ -13,6 +13,7 @@
 bf16 = jnp.bfloat16
 GROUP = 8
 VMEM = 48 * 1024 * 1024
+VMEM_MOST = 60 * 1024 * 1024
 
 NN = (((1,), (0,)), ((), ()))
 NT = (((1,), (1,)), ((), ()))
@@ -263,7 +264,7 @@
     weighted = (x * dt_wide).astype(bf16).astype(f32)
     decay = widen(jnp.exp(cum), hs)
     to_end = widen(jnp.exp(cum[t - 1 :, :] - cum), hs)
-    s_in, ds = si_ref[0], ds_ref[0]
+    s_in, ds = si_ref[0].astype(f32), ds_ref[0]
     s_low, ds_low = s_in.astype(bf16), ds.astype(bf16)
     through = to_end * mm(b_ref[0], ds_low)
     d_weighted = dxl_ref[0] + through
@@ -386,12 +387,11 @@
 
 
 CHUNK_DMAS = 10
-
-
-def gather_kernel(chunks, w_ref, o_ref, send, recv, own_sem):
+AHEAD = 2
+
+
+def gather_kernel(chunks, w_ref, o_ref, send, recv):
     s, z, c, x, y, near = around()
-    own = pltpu.make_async_copy(w_ref.at[pl.ds(0, o_ref.shape[1])], o_ref.at[0], own_sem)
-    own.start()
     greet(near)
     sx, sy, sd = s + 2 - 4 * x, s + 4 - 8 * y, s + 6 - 4 * x - 8 * y
     plans = []
@@ -411,14 +411,14 @@
             )
 
         def block(who, rows=rows):
-            return o_ref.at[pl.ds(1, 3), rows(who)]
+            return o_ref.at[:, rows(who)]
 
         def along(who, kind, to, move=move, block=block):
             return move(block(who), block(who), kind, to)
 
         plan = {}
         for k in (1, 2, 3):
-            plan["z%d" % k] = move(w_ref.at[rows(s)], o_ref.at[k, rows(s)], k - 1, "z%d" % k)
+            plan["z%d" % k] = move(w_ref.at[rows(s)], o_ref.at[k - 1, rows(s)], k - 1, "z%d" % k)
         plan["x"] = along(s, 3, "x")
         plan["y"] = along(s, 4, "y")
         plan["d"] = along(sx, 5, "y") if first == "x" else along(sy, 5, "x")
@@ -429,7 +429,7 @@
         plan["first"] = first
         plans.append(plan)
 
-    for plan in plans:
+    def fetch(plan):
         for k in (1, 2, 3):
             plan["z%d" % k].start()
 
@@ -452,9 +452,13 @@
         plan["cd"].start()
 
     n = len(plans)
+    for i in range(min(AHEAD, n)):
+        fetch(plans[i])
     for i in range(n + 2):
         if i < n:
             begin(plans[i])
+            if i + AHEAD < n:
+                fetch(plans[i + AHEAD])
         if 0 <= i - 1 < n:
             middle(plans[i - 1])
         if 0 <= i - 2 < n:
@@ -464,26 +468,30 @@
             plan[name].wait_recv()
         for name in ("z1", "z2", "z3", "x", "y", "d", "c0", "cx", "cy", "cd"):
             plan[name].wait_send()
-    own.wait()
+
+
+def split_rows(piece, parts=6):
+    tiles = piece // 16
+    return [16 * (tiles * (i + 1) // parts - tiles * i // parts) for i in range(parts)]
 
 
 def gather_input_weight(w_t, inner, channels):
     total = inner + channels
     chunks = []
     for base, piece in ((inner, channels // 8), (0, inner // 8)):
-        half = piece // 2
-        chunks.append((base, piece, 0, half, "x"))
-        chunks.append((base, piece, half, half, "y"))
+        off = 0
+        for i, size in enumerate(split_rows(piece)):
+            chunks.append((base, piece, off, size, "xy"[i % 2]))
+            off += size
     width = w_t.shape[1]
     return pl.pallas_call(
         partial(gather_kernel, chunks),
         in_specs=[pl.BlockSpec(memory_space=pl.ANY)],
         out_specs=pl.BlockSpec(memory_space=pl.ANY),
-        out_shape=jax.ShapeDtypeStruct((4, total, width), bf16),
+        out_shape=jax.ShapeDtypeStruct((3, total, width), bf16),
         scratch_shapes=[
             pltpu.SemaphoreType.DMA((len(chunks), CHUNK_DMAS)),
             pltpu.SemaphoreType.DMA((len(chunks), CHUNK_DMAS)),
-            pltpu.SemaphoreType.DMA,
         ],
         compiler_params=pltpu.CompilerParams(collective_id=1, has_side_effects=True),
         cost_estimate=pl.CostEstimate(flops=0, bytes_accessed=200_000_000, transcendentals=0),
@@ -765,53 +773,407 @@
     return out.reshape(total, shard)
 
 
-def project_kernel(n_ref, w_ref, o_ref):
-    total = mm(n_ref[0], w_ref[0], NT)
+LANES = 128
+HALO = 16
+
+
+def silu_parts(v):
+    s = 1.0 / (1.0 + jnp.exp(-v))
+    return v * s, s
+
+
+def softplus(v):
+    return jnp.maximum(v, 0.0) + jnp.log1p(jnp.exp(-jnp.abs(v)))
+
+
+def lower_ones(t):
+    i = lax.broadcasted_iota(jnp.int32, (t, t), 0)
+    j = lax.broadcasted_iota(jnp.int32, (t, t), 1)
+    return jnp.where(i >= j, 1.0, 0.0)
+
+
+def exact(a, b, dims=NN):
+    return lax.dot_general(a, b, dims, precision=highest, preferred_element_type=f32)
+
+
+def head_columns(values, g):
+    return pltpu.roll(values, (LANES - GROUP * g) % LANES, 1)[:, :GROUP]
+
+
+class Exchange:
+    def __init__(self, forward, own, own_low, got, t_low, t_got, u_low, u_got, p_low, p_got, before, send, recv):
+        self.s, self.z, self.c, self.x, self.y, self.near = around()
+        later = (lambda v: v) if forward else (lambda v: 1 - v)
+        self.second = (later(self.c) == 1, later(self.x) == 1, later(self.y) == 1)
+        self.own, self.own_low, self.got = own, own_low, got
+        self.t_low, self.t_got, self.u_low, self.u_got = t_low, t_got, u_low, u_got
+        self.p_low, self.p_got, self.before = p_low, p_got, before
+        self.send, self.recv = send, recv
+        self.n = own.shape[1]
+        self.half = own.shape[2] // 2
+        self.mine = pl.ds(pl.multiple_of(self.c * self.half, LANES), self.half)
+        self.other = pl.ds(pl.multiple_of((1 - self.c) * self.half, LANES), self.half)
+
+    def copy(self, kind, m):
+        src, dst, to = (
+            (self.own_low, self.got, "c"),
+            (self.t_low, self.t_got, "x"),
+            (self.u_low, self.u_got, "y"),
+            (self.p_low, self.p_got, "c"),
+        )[kind]
+        return pltpu.make_async_remote_copy(
+            src_ref=src.at[m],
+            dst_ref=dst.at[m],
+            send_sem=self.send.at[kind, m],
+            recv_sem=self.recv.at[kind, m],
+            device_id=self.near[to],
+            device_id_type=MESH,
+        )
+
+    def put_decay(self, ref, m, lanes, decay):
+        high = decay.astype(bf16).astype(f32)
+        row = lax.broadcasted_iota(jnp.int32, (16, decay.shape[1]), 0)
+        both = jnp.where(row == 0, high, jnp.where(row == 1, decay - high, 0.0))
+        ref[m, pl.ds(self.n, 16), lanes] = both.astype(bf16)
+
+    def decay_of(self, ref, m, lanes):
+        rows = ref[m, pl.ds(self.n, 16), lanes].astype(f32)
+        return rows[0:1] + rows[1:2]
+
+    def put_own(self, m, lanes, state, decay):
+        self.own[m, :, lanes] = state
+        self.own_low[m, pl.ds(0, self.n), lanes] = state.astype(bf16)
+        self.put_decay(self.own_low, m, lanes, decay)
+
+    def core(self, m):
+        self.copy(0, m).start()
+
+    def along_x(self, m):
+        self.copy(0, m).wait_recv()
+        second = self.second[0]
+        mine = self.own[m, :, self.mine]
+        theirs = self.got[m, pl.ds(0, self.n), self.mine].astype(f32)
+        d_mine = self.decay_of(self.own_low, m, self.mine)
+        d_theirs = self.decay_of(self.got, m, self.mine)
+        total = theirs * jnp.where(second, d_mine, 1.0) + mine * jnp.where(second, 1.0, d_theirs)
+        self.t_low[m, pl.ds(0, self.n), :] = total.astype(bf16)
+        self.put_decay(self.t_low, m, pl.ds(0, self.half), d_mine * d_theirs)
+        self.copy(1, m).start()
+
+    def along_y(self, m):
+        self.copy(1, m).wait_recv()
+        second = self.second[1]
+        every = pl.ds(0, self.half)
+        mine = self.t_low[m, pl.ds(0, self.n), :].astype(f32)
+        theirs = self.t_got[m, pl.ds(0, self.n), :].astype(f32)
+        d_mine = self.decay_of(self.t_low, m, every)
+        d_theirs = self.decay_of(self.t_got, m, every)
+        total = theirs * jnp.where(second, d_mine, 1.0) + mine * jnp.where(second, 1.0, d_theirs)
+        self.u_low[m] = total.astype(bf16)
+        self.copy(2, m).start()
+
+    def back_to_core(self, m):
+        self.copy(2, m).wait_recv()
+        every = pl.ds(0, self.half)
+        x_second = jnp.where(self.second[1], 1.0, 0.0)
+        y_second = jnp.where(self.second[2], 1.0, 0.0)
+        theirs = self.t_got[m, pl.ds(0, self.n), :].astype(f32)
+        d_theirs = self.decay_of(self.t_got, m, every)
+        over = y_second * jnp.where(self.second[1], d_theirs, 1.0)
+        before = x_second * theirs + over * self.u_got[m].astype(f32)
+        self.before[m] = before
+        self.p_low[m] = before.astype(bf16)
+        self.copy(3, m).start()
+
+    def begin_state(self, m, out):
+        self.copy(3, m).wait_recv()
+        second = jnp.where(self.second[0], 1.0, 0.0)
+        for lanes, before in (
+            (self.mine, self.before[m]),
+            (self.other, self.p_got[m].astype(f32)),
+        ):
+            d_theirs = self.decay_of(self.got, m, lanes)
+            theirs = self.got[m, pl.ds(0, self.n), lanes].astype(f32)
+            over = jnp.where(self.second[0], d_theirs, 1.0)
+            out[m, :, lanes] = (before * over + second * theirs).astype(bf16)
+
+    def sent(self):
+        for m in range(self.own.shape[0]):
+            for kind in range(4):
+                self.copy(kind, m).wait_send()
+
+
+def exchange_scratch(micro, n, inner):
+    half = inner // 2
+    dma = pltpu.SemaphoreType.DMA
+    return [
+        pltpu.VMEM((micro, n, inner), f32),
+        pltpu.VMEM((micro, n + 16, inner), bf16),
+        pltpu.VMEM((micro, n + 16, inner), bf16),
+        pltpu.VMEM((micro, n + 16, half), bf16),
+        pltpu.VMEM((micro, n + 16, half), bf16),
+        pltpu.VMEM((micro, n, half), bf16),
+        pltpu.VMEM((micro, n, half), bf16),
+        pltpu.VMEM((micro, n, half), bf16),
+        pltpu.VMEM((micro, n, half), bf16),
+        pltpu.VMEM((micro, n, half), f32),
+        dma((4, micro)),
+        dma((4, micro)),
+    ]
+
+
+EXCHANGE = 12
+
+
+def steps_of(raw, shift, rate):
+    t = raw.shape[0]
+    dt = softplus(raw + shift)
+    cum = exact(lower_ones(t), dt * rate)
+    return dt, cum
+
+
+def conv_rows(buf, cw, cb):
+    taps = cw.shape[0]
+    t = buf.shape[0] - HALO
+    total = cb + buf[HALO - taps + 1 : HALO - taps + 1 + t, :] * cw[0:1]
+    for k in range(1, taps):
+        at = HALO - taps + 1 + k
+        total = total + buf[at : at + t, :] * cw[k : k + 1]
+    return total
+
+
+def scan_forward_kernel(
+    hs,
+    conv_ref,
+    raw_ref,
+    cw_ref,
+    cb_ref,
+    shift_ref,
+    rate_ref,
+    skip_ref,
+    x_ref,
+    bc_ref,
+    y_ref,
+    low_ref,
+    halo,
+    begin_ref,
+    *scratch,
+):
+    buf, wide_buf, scores, dts, cums, rows_t, h_send, h_recv = scratch[EXCHANGE:]
+    ex = Exchange(True, *scratch[:EXCHANGE])
+    s, z = ex.s, ex.z
+    micro, t, channels = conv_ref.shape
+    inner = x_ref.shape[2]
+    n = begin_ref.shape[1]
+    gc = GROUP * hs
+    groups = inner // gc
+    half_t = t // 2
+    near = dict(ex.near)
+    near = {k: near[k] for k in ("c", "x", "y")}
+    near["next"] = ((s + 1) % 8, z)
+    near["last"] = ((s + 7) % 8, z)
+    greet(near)
+
+    tail = [
+        pltpu.make_async_remote_copy(
+            src_ref=conv_ref.at[m, pl.ds(t - HALO, HALO)],
+            dst_ref=halo.at[m],
+            send_sem=h_send.at[m],
+            recv_sem=h_recv.at[m],
+            device_id=near["next"],
+            device_id_type=MESH,
+        )
+        for m in range(micro)
+    ]
+    for copy in tail:
+        copy.start()
+    for m in range(micro):
+        dt, cum = steps_of(raw_ref[m], shift_ref[...], rate_ref[...])
+        dts[m] = dt
+        cums[m] = cum
+        rows_t[m] = cum.T
+    for copy in tail:
+        copy.wait_recv()
+    has_prior = jnp.where(s > 0, 1.0, 0.0)
+
+    def activate(m, lanes, into):
+        into[0:HALO] = halo[m, :, lanes].astype(f32) * has_prior
+        into[pl.ds(HALO, t)] = conv_ref[m, :, lanes].astype(f32)
+        return silu_parts(conv_rows(into, cw_ref[:, lanes], cb_ref[:, lanes]))[0]
+
+    def own_states(m, a, b):
+        def body(g, carry):
+            lanes = pl.ds(pl.multiple_of(g * gc, gc), gc)
+            x = activate(m, lanes, buf).astype(bf16)
+            x_ref[m, :, lanes] = x
+            cum = head_columns(cums[m], g)
+            to_end = head_columns(dts[m], g) * jnp.exp(cum[t - 1 :] - cum)
+            weighted = (x.astype(f32) * widen(to_end, hs)).astype(bf16)
+            state = mm(bc_ref[m, :, 0:n], weighted, TN)
+            ex.put_own(m, lanes, state, widen(jnp.exp(cum[t - 1 :]), hs))
+            return carry
+
+        lax.fori_loop(a, b, body, 0)
+
+    def local_scans(m, a, b):
+        lane = lax.broadcasted_iota(jnp.int32, (half_t, 2 * hs), 1)
+
+        def body(g, carry):
+            lanes = pl.ds(pl.multiple_of(g * gc, gc), gc)
+            cum = head_columns(cums[m], g)
+            rows = rows_t[m, pl.ds(pl.multiple_of(g * GROUP, GROUP), GROUP), :]
+            dt_wide = widen(head_columns(dts[m], g), hs)
+            weighted = (x_ref[m, :, lanes].astype(f32) * dt_wide).astype(bf16)
+            for k in range(0, GROUP, 2):
+                pair = weighted[:, k * hs : (k + 2) * hs]
+                at = pl.ds(pl.multiple_of(g * gc + k * hs, 2 * hs), 2 * hs)
+                top, low = [], []
+                for h in (k, k + 1):
+                    col, row = cum[:, h : h + 1], rows[h : h + 1, :]
+                    m1 = jnp.exp(jnp.minimum(col[:half_t] - row[:, :half_t], 0.0))
+                    m2 = jnp.exp(jnp.minimum(col[half_t:] - row, 0.0))
+                    m1 = (m1 * scores[m, :half_t, :half_t]).astype(bf16)
+                    m2 = (m2 * scores[m, half_t:, :]).astype(bf16)
+                    top.append(mm(m1, pair[:half_t]))
+                    low.append(mm(m2, pair))
+                y_ref[m, :half_t, at] = jnp.where(lane < hs, top[0], top[1])
+                y_ref[m, half_t:, at] = jnp.where(lane < hs, low[0], low[1])
+            return carry
+
+        lax.fori_loop(a, b, body, 0)
+
+    def carried(m):
+        def body(g, carry):
+            lanes = pl.ds(pl.multiple_of(g * gc, gc), gc)
+            decay = widen(jnp.exp(head_columns(cums[m], g)), hs)
+            scan = y_ref[m, :, lanes] + decay * mm(bc_ref[m, :, n:], begin_ref[m, :, lanes])
+            y_ref[m, :, lanes] = scan
+            x = x_ref[m, :, lanes].astype(f32)
+            low_ref[m, :, lanes] = (scan + skip_ref[:, lanes] * x).astype(bf16)
+            return carry
+
+        lax.fori_loop(0, groups, body, 0)
+
+    for m in range(micro):
+        lanes = pl.ds(inner, channels - inner)
+        bc = activate(m, lanes, wide_buf).astype(bf16)
+        bc_ref[m] = bc
+        scores[m] = mm(bc[:, n:], bc[:, :n], NT) * lower_ones(t)
+    middle = groups // 2
+    own_states(0, 0, groups)
+    ex.core(0)
+    own_states(1, 0, middle)
+    ex.along_x(0)
+    own_states(1, middle, groups)
+    ex.core(1)
+    local_scans(0, 0, middle)
+    ex.along_x(1)
+    ex.along_y(0)
+    local_scans(0, middle, groups)
+    local_scans(1, 0, middle)
+    ex.along_y(1)
+    ex.back_to_core(0)
+    local_scans(1, middle, groups)
+    ex.begin_state(0, begin_ref)
+    carried(0)
+    ex.back_to_core(1)
+    ex.begin_state(1, begin_ref)
+    carried(1)
+    ex.sent()
+    for copy in tail:
+        copy.wait_send()
+
+
+def scan_forward(conv_low, raw, conv_w, conv_b, shift, rate, skip_wide, inner, hs, collective_id):
+    micro, t, channels = conv_low.shape
+    n = (channels - inner) // 2
+    gc = GROUP * hs
+    dma = pltpu.SemaphoreType.DMA
+    vmem = pl.BlockSpec(memory_space=pltpu.VMEM)
+    return pl.pallas_call(
+        partial(scan_forward_kernel, hs),
+        in_specs=[vmem] * 7,
+        out_specs=[vmem] * 6,
+        out_shape=[
+            jax.ShapeDtypeStruct((micro, t, inner), bf16),
+            jax.ShapeDtypeStruct((micro, t, 2 * n), bf16),
+            jax.ShapeDtypeStruct((micro, t, inner), f32),
+            jax.ShapeDtypeStruct((micro, t, inner), bf16),
+            jax.ShapeDtypeStruct((micro, HALO, channels), bf16),
+            jax.ShapeDtypeStruct((micro, n, inner), bf16),
+        ],
+        scratch_shapes=exchange_scratch(micro, n, inner)
+        + [
+            pltpu.VMEM((HALO + t, gc), f32),
+            pltpu.VMEM((HALO + t, 2 * n), f32),
+            pltpu.VMEM((micro, t, t), f32),
+            pltpu.VMEM((micro, t, LANES), f32),
+            pltpu.VMEM((micro, t, LANES), f32),
+            pltpu.VMEM((micro, LANES, t), f32),
+            dma((micro,)),
+            dma((micro,)),
+        ],
+        compiler_params=pltpu.CompilerParams(
+            collective_id=collective_id, has_side_effects=True, vmem_limit_bytes=VMEM_MOST
+        ),
+        cost_estimate=pl.CostEstimate(
+            flops=4 * micro * t * inner * (t + 3 * n), bytes_accessed=100_000_000, transcendentals=0
+        ),
+        name="scan_forward",
+    )(conv_low, raw, conv_w, conv_b, shift, rate, skip_wide)
+
+
+def project_kernel(n_ref, w_ref, v_ref, o_ref):
+    total = mm(n_ref[0], w_ref[...], NT)
     for k in range(1, n_ref.shape[0]):
-        total += mm(n_ref[k], w_ref[k], NT)
+        total += mm(n_ref[k], v_ref[k - 1], NT)
     o_ref[...] = total.astype(o_ref.dtype)
 
 
-def project(parts, weight, first, count, tile, dtype):
+def project(parts, own, others, first, count, tile, dtype):
     shards, rows, depth = parts.shape
     return pl.pallas_call(
         project_kernel,
         grid=(count // tile,),
         in_specs=[
             pl.BlockSpec((shards, rows, depth), lambda i: (0, 0, 0)),
-            pl.BlockSpec((shards, tile, depth), lambda i: (0, first // tile + i, 0)),
+            pl.BlockSpec((tile, depth), lambda i: (first // tile + i, 0)),
+            pl.BlockSpec((shards - 1, tile, depth), lambda i: (0, first // tile + i, 0)),
         ],
         out_specs=pl.BlockSpec((rows, tile), lambda i: (0, i)),
         out_shape=jax.ShapeDtypeStruct((rows, count), dtype),
         compiler_params=pltpu.CompilerParams(vmem_limit_bytes=VMEM),
         name="project",
-    )(parts, weight)
-
-
-def unproject_kernel(d_ref, w_ref, o_ref):
+    )(parts, own, others)
+
+
+def unproject_kernel(d_ref, w_ref, v_ref, o_ref):
     @pl.when(pl.program_id(0) == 0)
     def _():
         o_ref[...] = jnp.zeros_like(o_ref)
 
-    for k in range(o_ref.shape[0]):
-        o_ref[k] += mm(d_ref[...], w_ref[k])
-
-
-def unproject(d, weight, tile):
-    shards, count, depth = weight.shape
+    o_ref[0] += mm(d_ref[...], w_ref[...])
+    for k in range(1, o_ref.shape[0]):
+        o_ref[k] += mm(d_ref[...], v_ref[k - 1])
+
+
+def unproject(d, own, others, tile):
+    shards, count, depth = others.shape
+    shards += 1
     rows = d.shape[0]
     return pl.pallas_call(
         unproject_kernel,
         grid=(count // tile,),
         in_specs=[
             pl.BlockSpec((rows, tile), lambda i: (0, i)),
-            pl.BlockSpec((shards, tile, depth), lambda i: (0, i, 0)),
+            pl.BlockSpec((tile, depth), lambda i: (i, 0)),
+            pl.BlockSpec((shards - 1, tile, depth), lambda i: (0, i, 0)),
         ],
         out_specs=pl.BlockSpec((shards, rows, depth), lambda i: (0, 0, 0)),
         out_shape=jax.ShapeDtypeStruct((shards, rows, depth), f32),
         compiler_params=pltpu.CompilerParams(vmem_limit_bytes=VMEM),
         name="unproject",
-    )(d, weight)
+    )(d, own, others)
 
 
 def rms_front(hidden_rows, gain):
@@ -861,7 +1223,7 @@
     n = (channels - inner) // 2
     groups = heads // GROUP
     rows = micro * tokens
-    fast = count == 8 and shards == 4
+    fast = count == 8 and shards == 4 and micro == 2
     in_local = in_weight.T
     small = [norm_gain, conv_weight.T.reshape(-1), conv_bias, dt_bias, a_log, skip_gain, gated_gain]
     sizes = [v.shape[0] for v in small]
@@ -881,12 +1243,13 @@
     gated_g = parts[6].reshape(-1)
 
     dt_w = packed_low[:, at:].reshape(shards, heads, -1).transpose(1, 0, 2).reshape(heads, -1)
-    order = jnp.arange(shards) ^ shard if fast else jnp.arange(shards)
+    order = jnp.arange(shards) ^ shard
     if fast:
         in_w = gather_input_weight(in_local, inner, channels)
         out_part = lax.optimization_barrier((out_weight, in_w[0, 0, 0]))[0]
     else:
-        in_w = lax.all_gather(in_local[: inner + channels], "wshard", axis=0)
+        every = lax.all_gather(in_local[: inner + channels], "wshard", axis=0)
+        in_w = every[order[1:]]
         out_part = out_weight
     out_w = lax.all_gather(out_part, "wshard", axis=0, tiled=True)
 
@@ -901,18 +1264,37 @@
     normed_low = normed.astype(bf16)
     normed_parts = normed_low.reshape(rows, shards, -1).transpose(1, 0, 2)[order]
     tile = 256
-    conv_low = project(normed_parts, in_w, inner, channels, tile, bf16)
-    gate_in = project(normed_parts, in_w, 0, inner, tile, f32)
+    conv_low = project(normed_parts, in_local, in_w, inner, channels, tile, bf16)
+    gate_in = project(normed_parts, in_local, in_w, 0, inner, tile, f32)
     dt_low = mm(normed_low, dt_w, NT).astype(bf16)
     conv_low = conv_low.reshape(micro, tokens, channels)
-    prior = from_behind(conv_low[:, tokens - (taps - 1) :], "seq", 1)
-    padded = jnp.concatenate([prior, conv_low], axis=1).astype(f32)
+    dt_raw = dt_low.astype(f32).reshape(micro, tokens, heads) + dt_shift
+    skip_wide = jnp.repeat(skip, hs)[None, :]
+
+    def to_lanes(v):
+        return jnp.pad(v, ((0, 0),) * (v.ndim - 1) + ((0, LANES - heads),))
+
+    if fast:
+        raw = to_lanes(dt_low.astype(f32).reshape(micro, tokens, heads))
+        x_low, bc_low, y_scan, scanned_low, halo, s_in = scan_forward(
+            conv_low,
+            raw,
+            conv_w,
+            conv_b[None, :],
+            to_lanes(dt_shift[None, :]),
+            to_lanes(rate[None, :]),
+            skip_wide,
+            inner,
+            hs,
+            3,
+        )
+        b_low, c_low = bc_low[..., :n], bc_low[..., n:]
+        halo = jnp.where(rank > 0, halo, 0)
+        padded = jnp.concatenate([halo[:, HALO - (taps - 1) :], conv_low], axis=1).astype(f32)
+    else:
+        prior = from_behind(conv_low[:, tokens - (taps - 1) :], "seq", 1)
+        padded = jnp.concatenate([prior, conv_low], axis=1).astype(f32)
     mixed, conv_back = jax.vjp(conv_act, padded, conv_w, conv_b)
-    x_low = mixed[..., :inner].astype(bf16)
-    b_low = mixed[..., inner : inner + n].astype(bf16)
-    c_low = mixed[..., inner + n :].astype(bf16)
-
-    dt_raw = dt_low.astype(f32).reshape(micro, tokens, heads) + dt_shift
     dt = jax.nn.softplus(dt_raw)
     tri = (jnp.arange(tokens)[:, None] >= jnp.arange(tokens)[None, :]).astype(f32)
     cum = jnp.einsum("ij,mjh->mih", tri, dt * rate, precision=highest)
@@ -920,14 +1302,16 @@
     row_g = cum_g.transpose(0, 1, 3, 2)
     last = cum[:, tokens - 1, :]
     decays = lax.all_gather(jnp.exp(last), "seq", axis=0)
-    end_w = grouped(dt * jnp.exp(last[:, None, :] - cum))
     decay_w = grouped(jnp.exp(cum))
-    skip_wide = jnp.repeat(skip, hs)[None, :]
-
-    own_state = block_states(x_low, end_w, b_low.transpose(0, 2, 1), hs)
-    y_local = local_scan(x_low, dt_g, cum_g, row_g, b_low, c_low, hs)
-    s_in = running_states(own_state, decays, hs, True)
-    y_scan, scanned_low = add_carry(x_low, y_local, cum_g, c_low, s_in, skip_wide, hs)
+    if not fast:
+        x_low = mixed[..., :inner].astype(bf16)
+        b_low = mixed[..., inner : inner + n].astype(bf16)
+        c_low = mixed[..., inner + n :].astype(bf16)
+        end_w = grouped(dt * jnp.exp(last[:, None, :] - cum))
+        own_state = block_states(x_low, end_w, b_low.transpose(0, 2, 1), hs)
+        y_local = local_scan(x_low, dt_g, cum_g, row_g, b_low, c_low, hs)
+        s_in = running_states(own_state, decays, hs, True)
+        y_scan, scanned_low = add_carry(x_low, y_local, cum_g, c_low, s_in, skip_wide, hs)
 
     scanned = scanned_low.reshape(rows, inner).astype(f32)
     normed_out, gate_back = jax.vjp(gate_norm, scanned, gate_in, gated_g)
@@ -971,7 +1355,7 @@
         ],
         axis=1,
     )
-    d_parts = unproject(d_proj, in_w, tile)
+    d_parts = unproject(d_proj, in_local, in_w, tile)
     d_normed = d_parts[order].transpose(1, 0, 2).reshape(rows, width) + mm(d_dt_low, dt_w)
     d_hidden, d_norm_g = front_back(d_normed)
     input_grad = (d_hidden + cot).astype(bf16).reshape(hidden.shape)

time: 851 us -> 719 us (0.84)
  waiting for transfers between devices: 109 us -> 56.3 us
  Pallas kernels: 426 us -> 390 us
  local copies, waits for them, and re-layouts: 111 us -> 95.8 us
  other arithmetic: 120 us -> 105 us
    ppermute x6 -> x3, waiting for transfers between devices: 108 us -> 42.2 us  [swap(): return lax.ppermute(x, 'seq', [(i, i ^ by) for i in range(count)])]
    pallas_call x1, Pallas kernels: 151 us -> 95.6 us  [gather_input_weight(): pl.pallas_call(partial(gather_kernel, chunks), in_specs=[pl.BlockSpec(mem...]
    pallas_call x2 -> x1, Pallas kernels: 26.8 us -> 55.3 us  [scan_forward(): pl.pallas_call(partial(scan_forward_kernel, hs), in_specs=[vmem] * 7, out...]
    all_gather x1, waiting for transfers between devices: 0.02 us -> 13.2 us  [local(): out_w = lax.all_gather(out_part, 'wshard', axis=0, tiled=True)]
    pallas_call x2 -> x1, Pallas kernels: 20.1 us -> 10.1 us  [block_states(): pl.pallas_call(partial(state_kernel, hs), grid=(micro, cols // gc), in_sp...]
    unnamed x192 -> x132, local copies, waits for them, and re-layouts: 17.3 us -> 8.29 us
  transfers between devices with their start and end apart: 14 -> 10, of which waited for: 3 -> 3; matrix products, arithmetic and copies ran while one was open for 23% -> 25% of each run, Pallas kernels for 51% -> 55%
where the time goes in v3:
time: 719 us; the launch traced here: 713 us
  Pallas kernels  390 us (54%)
  other arithmetic  105 us (15%)
  local copies, waits for them, and re-layouts  95.8 us (13%)
  waiting for transfers between devices  56.3 us (8%)
  matrix products  36.3 us (5%)
  between operations  16.1 us (2%)
  blocking collectives  9.04 us (1%)
    pallas_call x1, Pallas kernels, reduce_products(): pl.pallas_call(partial(reduce_kernel, chunks, pieces, groups), in_specs=[...  137 us
    pallas_call x1, Pallas kernels, gather_input_weight(): pl.pallas_call(partial(gather_kernel, chunks), in_specs=[pl.BlockSpec(mem...  95.6 us
    pallas_call x1, Pallas kernels, scan_forward(): pl.pallas_call(partial(scan_forward_kernel, hs), in_specs=[vmem] * 7, out...  55.3 us
    ppermute x3, waiting for transfers between devices, swap(): return lax.ppermute(x, 'seq', [(i, i ^ by) for i in range(count)])  42.2 us
    dot_general x5, matrix products, mm(): return lax.dot_general(a, b, dims, preferred_element_type=f32)  34.3 us
    pallas_call x2, Pallas kernels, project(): pl.pallas_call(project_kernel, grid=(count // tile,), in_specs=[pl.BlockS...  28 us
    pallas_call x1, Pallas kernels, unproject(): pl.pallas_call(unproject_kernel, grid=(count // tile,), in_specs=[pl.Bloc...  25.9 us
    pallas_call x1, Pallas kernels, carry_back(): pl.pallas_call(partial(carry_back_kernel, hs), grid=(micro, groups), in_s...  22.3 us
  transfers between devices with their start and end apart: 10, of which 3 were waited for; matrix products, arithmetic and copies ran while one was open for 25% of the time, Pallas kernels for 55%

profile of v3, /device:TPU:0, one launch (start us, length us, event | category | flops | bytes accessed | tf_op | source)
XLA Modules:
  0.0 713.1 jit_solution(14670930945842821355)
XLA Ops:
  10.7 4.2 concatenate.17
  17.1 95.6 %gather_input_weight.1.v_ref = bf16[3,6400,384]{2,1,0:T(8,128)(2,1)} custom-call(bf16[6448,384]{1,0:T(8,128)(2,1)} %bitcast.152), custom_call_target="tpu_custom_call" | custom-call | bytes 200000000 | tf_op jit(solution)/shard_map/gather_input_weight/pallas_call | solution.py:487
  112.7 2.5 reshape.518
  115.8 1.5 fusion.15
  117.2 1.5 fusion.14
  121.4 3.4 fusion.28
  124.8 2.3 gather_fusion
  127.1 13.3 %project.2 = bf16[512,3328]{1,0:T(8,128)(2,1)S(1)} custom-call(bf16[4,512,384]{2,1,0:T(8,128)(2,1)S(1)} %gather_fusion, bf16[6448,384]{1,0:T(8,128)(2,1)} %bitcast.153, bf16[3,6400,384]{2,1,0:T(8,128)(2,1)} %gather_input_weight.1.v_ref), custom_call_target="tpu_custom_call" | custom-call | tf_op jit(solution)/shard_map/project/pallas_call | solution.py:1135
  140.5 14.7 %project.3 = f32[512,3072]{1,0:T(8,128)} custom-call(bf16[4,512,384]{2,1,0:T(8,128)(2,1)S(1)} %gather_fusion, bf16[6448,384]{1,0:T(8,128)(2,1)} %bitcast.154, bf16[3,6400,384]{2,1,0:T(8,128)(2,1)} %gather_input_weight.1.v_ref), custom_call_target="tpu_custom_call" | custom-call | tf_op jit(solution)/shard_map/project/pallas_call | solution.py:1135
  161.8 55.3 %scan_forward.1 = (bf16[2,256,3072]{2,1,0:T(8,128)(2,1)}, bf16[2,256,256]{2,1,0:T(8,128)(2,1)}, f32[2,256,3072]{2,1,0:T(8,128)}, bf16[2,256,3072]{2,1,0:T(8,128)...) custom-call(bf16[2,256,3328]{2,1,0:T(8,128)(2,1)} %bitcast.142, f32[2,256,128]{2,1,0:T(8,128)} %pad.37.raw_ref, ...), custom_call_target="tpu_custom_call" | custom-call | flops 4026531840 | bytes 100000000 | tf_op jit(solution)/shard_map/scan_forward/pallas_call | solution.py:1093
  217.2 5.1 multiply_reduce_fusion.6
  222.3 13.2 %all-gather.5.cloned.1.call-done = bf16[3072,1536]{1,0:T(8,128)(2,1)} async-done(((bf16[768,1536]{1,0:T(8,128)(2,1)}), bf16[3072,1536]{1,0:T(8,128)(2,1)}) %all-gather.5.cloned.1.call-update) | async-done | bytes 9437200 | tf_op jit(solution)/shard_map/all_gather | solution.py:1254
  235.5 10.9 %multiply_reduce_fusion.4 = (f32[3072]{0:T(1024)}, f32[512]{0:T(512)S(1)}, f32[512,3072]{1,0:T(8,128)S(1)}) fusion(f32[512]{0:T(512)S(1)} %fusion.39, bf16[2,256,3072]{2,1,0:T(8,128)(2,1)S(1)} %copy-done.13, f32[512,3072]{1,0:T(8,128)} %project.3, f32[3072]{0:T(1024)S(1)} %mul.371, bf16[512,1536]{1,0:T(8,128)(2,1)} %fusion.15, ...), kind=kOutput, calls=%fused_computation.20 | convolution fusion | flops 4850708992 | bytes 26767360 | tf_op jit(solution)/shard_map/dot_general | solution.py:24
  246.5 10.6 %multiply_convert_fusion = (bf16[512,3072]{1,0:T(8,128)(2,1)}, bf16[512,3072]{1,0:T(8,128)(2,1)}, bf16[512,3072]{1,0:T(8,128)(2,1)}) fusion(f32[512]{0:T(512)S(1)} %multiply_multiply_fusion.1, f32[512,3072]{1,0:T(8,128)S(1)} %get-tuple-element.166, f32[3072]{0:T(1024)S(1)} %mul.371, f32[512]{0:T(512)S(1)} %fusion.39, ...), kind=kLoop, calls=%fused_computation.21 | loop fusion | flops 37748736 | bytes 25182208 | tf_op jit(solution)/shard_map/convert_element_type | solution.py:1325
  257.1 3.2 copy.138
  260.3 9.0 %convert_bitcast_fusion.1 = bf16[8,4,96,1536]{3,2,0,1:T(8,128)(2,1)} fusion(bf16[4,8,96,512]{3,2,1,0:T(8,128)(2,1)S(1)} %bitcast.167, bf16[512,1536,1,1]{1,0,3,2:T(8,128)(2,1)} %bitcast.170), kind=kOutput, calls=%fused_computation.6 | convolution fusion | flops 4836556800 | bytes 14155776 | tf_op jit(solution)/shard_map/dot_general | solution.py:24
  269.3 8.2 %copy.139 = bf16[8,4,96,1536]{3,2,1,0:T(8,128)(2,1)} copy(bf16[8,4,96,1536]{3,2,0,1:T(8,128)(2,1)} %convert_bitcast_fusion.1) | data formatting | bytes 18874368 | tf_op jit(solution)/shard_map/convert_element_type | solution.py:1406
  279.5 1.6 copy.131
  281.8 1.6 copy-done.3
  283.4 10.1 %block_states.1 = f32[2,128,3072]{2,1,0:T(8,128)S(1)} custom-call(bf16[2,256,3072]{2,1,0:T(8,128)(2,1)} %bitcast.156, f32[2,6,256,8]{3,2,1,0:T(8,128)S(1)} %bitcast.144, bf16[2,128,256]{2,1,0:T(8,128)(2,1)S(1)} %get-tuple-element.151.bt_ref), custom_call_target="tpu_custom_call" | custom-call | tf_op jit(solution)/shard_map/block_states/pallas_call | solution.py:51
  293.5 1.4 convert_element_type.163
  296.6 9.0 %all-gather.1 = f32[16,1,48]{2,1,0:T(1,128)S(1)} all-gather(f32[2,1,48]{2,1,0:T(1,128)S(1)} %bitcast.192), channel_id=3, replica_groups=mesh['seq'=8,'wshard'=4] {'seq'}, dimensions={0}, use_global_device_ids=true | all-gather | bytes 3456 | tf_op jit(solution)/shard_map/all_gather | solution.py:1304
  305.6 1.4 select_reduce_fusion.6
  307.4 3.1 fusion.27
  312.2 1.4 copy.121
  313.6 2.5 copy.122
  317.5 1.5 select_n.244
  319.7 1.5 select_n.241
  323.7 1.4 fusion.52
  325.0 3.4 select_bitcast_fusion.dt_ref
  328.5 40.9 %collective-permute-done.1 = bf16[2,128,3072]{2,1,0:T(8,128)(2,1)} collective-permute-done((bf16[2,128,3072]{2,1,0:T(8,128)(2,1)}, bf16[2,128,3072]{2,1,0:T(8,128)(2,1)}, u32[]{:S(2)}, u32[]{:S(2)}) %collective-permute-start.1) | collective-permute-done | bytes 1572896 | tf_op jit(solution)/shard_map/ppermute | solution.py:336
  369.4 3.9 fusion.11
  373.3 1.5 collective-permute-start.2
  384.6 5.7 maximum_convert_fusion
  390.3 1.3 reshape.513
  391.7 16.4 %local_back.1 = (f32[2,256,3072]{2,1,0:T(8,128)}, f32[2,256,128]{2,1,0:T(8,128)S(1)}, f32[2,256,128]{2,1,0:T(8,128)S(1)}) custom-call(bf16[2,256,3072]{2,1,0:T(8,128)(2,1)} %get-tuple-element.40.x_ref, bf16[2,256,3072]{2,1,0:T(8,128)(2,1)} %bitcast.157, f32[2,6,256,8]{3,2,1,0:T(8,128)S(1)} %copy-done, f32[2,6,256,8]{3,2,1,0:T(8,128)S(1)} %bitcast.140, ...), custom_call_target="tpu_custom_call" | custom-call | tf_op jit(solution)/shard_map/local_back/pallas_call | solution.py:201
  408.0 1.4 collective-permute-done.2
  409.4 4.9 fusion.8.ds_ref
  414.3 22.3 %carry_back.1 = (bf16[2,256,3072]{2,1,0:T(8,128)(2,1)}, f32[2,6,256,8]{3,2,1,0:T(8,128)S(1)}, f32[2,6,256,8]{3,2,1,0:T(8,128)S(1)}, f32[2,256,128]{2,1,0:T(8,128...) custom-call(bf16[2,256,3072]{2,1,0:T(8,128)(2,1)} %get-tuple-element.40.x_ref, ...), custom_call_target="tpu_custom_call" | custom-call | tf_op jit(solution)/shard_map/carry_back/pallas_call | solution.py:296
  436.6 3.3 convert_element_type.169
  440.0 10.4 %multiply_reduce_fusion.3 = (f32[3328]{0:T(1024)S(1)}, f32[3328]{0:T(1024)S(1)}, f32[3328]{0:T(1024)S(1)}, f32[3328]{0:T(1024)S(1)}, f32[3328]{0:T(1024)}, /*index=5*/f32[2,256,3328]{2,1,0:T(8,128)S(1)}) fusion(f32[2,259,3328]{2,1,0:T(8,128)S(1)} %bitcast.150, f32[3328]{0:T(1024)S(1)} %mul.413, f32[3328]{0:T(1024)S(1)} %mul.410, f32[3328]{0:T(1024)S(1)} %mul.407, ...), kind=kLoop, calls=%fused_computation.16 | loop fusion | flops 47693568 | bytes 41027584 | tf_op jit(solution)/shard_map/transpose(jvp())/reduce_sum | solution.py:1189
  450.4 9.3 %broadcast_multiply_fusion = (f32[2,256,3328]{2,1,0:T(8,128)}, f32[2,256,3328]{2,1,0:T(8,128)}, f32[2,256,3328]{2,1,0:T(8,128)}, f32[2,256,3328]{2,1,0:T(8,128)}) fusion(f32[2,256,3328]{2,1,0:T(8,128)S(1)} %get-tuple-element.139, f32[3328]{0:T(1024)S(1)} %mul.413, f32[3328]{0:T(1024)S(1)} %copy-done.30, f32[3328]{0:T(1024)S(1)} %mul.407, f32[3328]{0:T(1024)S(1)} %mul.410), kind=kLoop, calls=%fused_computation.33 | loop fusion | flops 6815744 | bytes 34131968 | tf_op jit(solution)/shard_map/transpose(jvp())/mul | solution.py:1189
  459.8 10.2 %pad_add_fusion = f32[2,259,3328]{2,1,0:T(8,128)S(1)} fusion(f32[2,256,3328]{2,1,0:T(8,128)} %get-tuple-element.146, f32[2,256,3328]{2,1,0:T(8,128)} %get-tuple-element.147, f32[2,256,3328]{2,1,0:T(8,128)} %get-tuple-element.148, f32[2,256,3328]{2,1,0:T(8,128)} %get-tuple-element.145), kind=kLoop, calls=%fused_computation.9 | loop fusion | flops 5171712 | bytes 34158592 | tf_op jit(solution)/shard_map/transpose(jvp())/add_any | solution.py:1187
  470.0 2.9 copy-done.9
  473.6 1.3 collective-permute-start.3
  476.3 1.6 fusion.48
  478.0 1.3 fusion.46
  479.3 5.5 slice.205
  488.3 1.9 scatter-add.4
  490.2 10.9 %concatenate.20.d_ref.dp_ref = bf16[512,6656]{1,0:T(8,128)(2,1)} concatenate(bf16[512,3072]{1,0:T(8,128)(2,1)S(1)} %copy-done.14, bf16[512,3328]{1,0:T(8,128)(2,1)} %bitcast.160, bf16[512,48]{1,0:T(8,128)(2,1)S(1)} %bitcast.178, bf16[512,208]{1,0:T(8,128)(2,1)S(1)} %broadcast_in_dim.148), dimensions={1} | concatenate | bytes 13631488 | tf_op jit(solution)/shard_map/concatenate | solution.py:1349
  501.1 25.9 %unproject.1 = f32[4,512,384]{2,1,0:T(8,128)S(1)} custom-call(bf16[512,6656]{1,0:T(8,128)(2,1)} %concatenate.20.d_ref.dp_ref, bf16[6448,384]{1,0:T(8,128)(2,1)} %bitcast.155, bf16[3,6400,384]{2,1,0:T(8,128)(2,1)} %gather_input_weight.1.v_ref), custom_call_target="tpu_custom_call" | custom-call | tf_op jit(solution)/shard_map/unproject/pallas_call | solution.py:1164
  527.0 2.5 gather_fusion.1
  529.5 2.4 copy.145
  532.1 2.8 fusion.18
  535.8 2.1 convert_element_type.184
  537.9 10.9 %fusion.26 = bf16[512,1536]{1,0:T(8,128)(2,1)} fusion(f32[512,1536]{1,0:T(8,128)} %bitcast.166, bf16[512,3072]{1,0:T(8,128)(2,1)} %get-tuple-element.144, bf16[3072,1536]{1,0:T(8,128)(2,1)} %all-gather.5.cloned.1.call-done, f32[512]{0:T(512)S(1)} %bitcast.190), kind=kOutput, calls=%fused_computation.67 | convolution fusion | flops 4834197504 | bytes 17303552 | tf_op jit(solution)/shard_map/dot_general | solution.py:24
  548.8 2.1 fusion.13
  550.9 136.6 %reduce_products.1 = bf16[2,26,2,2,2,16,384]{6,5,4,3,2,1,0:T(8,128)(2,1)} custom-call(bf16[512,6656]{1,0:T(8,128)(2,1)} %concatenate.20.d_ref.dp_ref, bf16[512,1536]{1,0:T(8,128)(2,1)S(1)} %get-tuple-element.149.nm_ref), custom_call_target="tpu_custom_call" | custom-call | flops 10468982784 | bytes 200000000 | tf_op jit(solution)/shard_map/reduce_products/pallas_call | solution.py:735
  687.5 7.0 convert_bitcast_fusion
  696.1 1.3 dynamic-slice_reduce_fusion.3
  697.4 1.4 dynamic-slice_reduce_fusion.2
  698.8 1.4 dynamic-slice_reduce_fusion.1
  700.2 1.3 dynamic-slice_bitcast_fusion
  701.5 4.5 convert_element_type.183
  (264 shorter events, 43.7 us)
Async XLA Ops:
  7.2 111.5 %all-reduce.17.cloned.1.call-start = ((), (), s32[]{:S(2)}) async-start(), calls=%async_computation.7 | async-start | bytes 380928
  16.3 219.3 %all-gather.5.cloned.1.call-start = ((), (), s32[]{:S(2)}) async-start(), calls=%async_computation.2 | async-start | bytes 11796480 | tf_op jit(solution)/shard_map/all_gather | solution.py:1254
  17.0 95.7 %copy-start.7 = (bf16[2,1,256,1536]{3,2,1,0:T(8,128)(2,1)S(1)}, bf16[2,1,256,1536]{3,2,1,0:T(8,128)(2,1)}, u32[]{:S(2)}) copy-start(bf16[2,1,256,1536]{3,2,1,0:T(8,128)(2,1)} %param.14) | copy-start | bytes 4718596
  17.0 442.7 %reduce-scatter.3.cloned.1.call-start = ((), (), s32[]{:S(2)}) async-start(), calls=%async_computation.4 | async-start | bytes 10616832 | tf_op jit(solution)/shard_map/reduce_scatter | solution.py:1406
  112.7 2.9 copy-start.60
  112.7 3.1 copy-start.10
  115.6 3.1 copy-start.47
  115.6 5.8 copy-start.45
  115.7 3.0 copy-start.52
  115.7 9.1 %copy-start.54 = (s32[1024]{0:T(1024)}, s32[1024]{0:T(1024)S(1)}, u32[]{:S(2)}) copy-start(s32[1024]{0:T(1024)S(1)} %pad_clamp_fusion) | copy-start | bytes 12292
  121.4 33.9 %copy-start.31 = (f32[1536]{0:T(1024)}, f32[1536]{0:T(1024)S(1)}, u32[]{:S(2)}) copy-start(f32[1536]{0:T(1024)S(1)} %mul.363) | copy-start | bytes 18436
  140.5 14.7 %copy-start.2 = (bf16[512,3328]{1,0:T(8,128)(2,1)}, bf16[512,3328]{1,0:T(8,128)(2,1)S(1)}, u32[]{:S(2)}) copy-start(bf16[512,3328]{1,0:T(8,128)(2,1)S(1)} %project.2) | copy-start | bytes 10223620
  156.6 60.5 %copy-start.18 = (f32[512,48]{1,0:T(8,128)}, f32[512,48]{1,0:T(8,128)S(1)}, u32[]{:S(2)}) copy-start(f32[512,48]{1,0:T(8,128)S(1)} %copy.116) | copy-start | bytes 294916
  156.8 60.4 %copy-start.22 = (f32[4,4,832]{2,0,1:T(4,128)}, f32[4,4,832]{2,0,1:T(4,128)S(1)}, u32[]{:S(2)}) copy-start(f32[4,4,832]{2,0,1:T(4,128)S(1)} %copy.159) | copy-start | bytes 159748
  217.2 18.4 %copy-start.13 = (bf16[2,256,3072]{2,1,0:T(8,128)(2,1)S(1)}, bf16[2,256,3072]{2,1,0:T(8,128)(2,1)}, u32[]{:S(2)}) copy-start(bf16[2,256,3072]{2,1,0:T(8,128)(2,1)} %get-tuple-element.39) | copy-start | bytes 9437188
  277.5 260.3 %reduce-scatter.5.cloned.1.call-start = ((), (), s32[]{:S(2)}) async-start(), calls=%async_computation.5 | async-start | bytes 1474560 | tf_op jit(solution)/shard_map/reduce_scatter | solution.py:1407
  277.7 15.8 %copy-start.56 = (f32[48]{0:T(128)}, f32[48]{0:T(128)S(1)}, u32[]{:S(2)}) copy-start(f32[48]{0:T(128)S(1)} %neg.44) | copy-start | bytes 580
  278.5 15.1 %copy-start.58 = (f32[48]{0:T(128)}, f32[48]{0:T(128)S(1)}, u32[]{:S(2)}) copy-start(f32[48]{0:T(128)S(1)} %add.218) | copy-start | bytes 580
  279.1 17.5 %copy-start.15 = (f32[2,48,256]{1,0,2:T(2,128)}, f32[2,48,256]{1,0,2:T(2,128)S(1)}, u32[]{:S(2)}) copy-start(f32[2,48,256]{1,0,2:T(2,128)S(1)} %copy.124) | copy-start | bytes 294916
  294.9 12.5 %collective-permute-start = (bf16[2,128,3072]{2,1,0:T(8,128)(2,1)}, bf16[2,128,3072]{2,1,0:T(8,128)(2,1)}, u32[]{:S(2)}, u32[]{:S(2)}) collective-permute-start(bf16[2,128,3072]{2,1,0:T(8,128)(2,1)} %convert_element_type.163), channel_id=1, source_target_pairs={{0,4},{4,0},{8,12},{12,8},{16,20},{20,16},{24,28},{28,24},{1,5},{5... | collective-permute-start | bytes 4718600 | tf_op jit(solution)/shard_map/ppermute | solution.py:336
  307.2 3.3 copy-start.24
  307.4 3.1 copy-start.26
  307.4 4.1 copy-start.23
  310.5 58.8 %collective-permute-start.1 = (bf16[2,128,3072]{2,1,0:T(8,128)(2,1)}, bf16[2,128,3072]{2,1,0:T(8,128)(2,1)}, u32[]{:S(2)}, u32[]{:S(2)}) collective-permute-start(bf16[2,128,3072]{2,1,0:T(8,128)(2,1)} %fusion.27), channel_id=1, source_target_pairs={{0,8},{4,12},{8,0},{12,4},{16,24},{20,28},{24,16},{28,20},{1,9},{5... | collective-permute-start | bytes 4718600 | tf_op jit(solution)/shard_map/ppermute | solution.py:336
  321.2 48.2 %copy-start.25 = (f32[2,3072]{1,0:T(2,128)S(1)}, f32[2,3072]{1,0:T(2,128)}, u32[]{:S(2)}) copy-start(f32[2,3072]{1,0:T(2,128)} %copy-done.24) | copy-start | bytes 73732
  321.2 48.2 %copy-start.27 = (f32[2,3072]{1,0:T(2,128)S(1)}, f32[2,3072]{1,0:T(2,128)}, u32[]{:S(2)}) copy-start(f32[2,3072]{1,0:T(2,128)} %copy-done.26) | copy-start | bytes 73732
  321.2 48.2 %copy-start.36 = (f32[2,3072]{1,0:T(2,128)S(1)}, f32[2,3072]{1,0:T(2,128)}, u32[]{:S(2)}) copy-start(f32[2,3072]{1,0:T(2,128)} %select_n.244) | copy-start | bytes 73732
  321.2 48.2 %copy-start.37 = (f32[2,3072]{1,0:T(2,128)S(1)}, f32[2,3072]{1,0:T(2,128)}, u32[]{:S(2)}) copy-start(f32[2,3072]{1,0:T(2,128)} %select_n.241) | copy-start | bytes 73732
  328.4 46.4 %copy-start.55 = (f32[2,48]{1,0:T(2,128)S(1)}, f32[2,48]{1,0:T(2,128)}, u32[]{:S(2)}) copy-start(f32[2,48]{1,0:T(2,128)} %get-tuple-element.133) | copy-start | bytes 1156
  328.5 49.0 %copy-start.43 = (f32[1,4,832]{2,1,0:T(4,128)S(1)}, f32[1,4,832]{2,1,0:T(4,128)}, u32[]{:S(2)}) copy-start(f32[1,4,832]{2,1,0:T(4,128)} %get-tuple-element.159) | copy-start | bytes 39940
  328.5 49.1 %copy-start.42 = (f32[1,4,832]{2,1,0:T(4,128)S(1)}, f32[1,4,832]{2,1,0:T(4,128)}, u32[]{:S(2)}) copy-start(f32[1,4,832]{2,1,0:T(4,128)} %get-tuple-element.160) | copy-start | bytes 39940
  328.5 49.2 %copy-start.41 = (f32[1,4,832]{2,1,0:T(4,128)S(1)}, f32[1,4,832]{2,1,0:T(4,128)}, u32[]{:S(2)}) copy-start(f32[1,4,832]{2,1,0:T(4,128)} %get-tuple-element.161) | copy-start | bytes 39940
  328.5 49.3 %copy-start.40 = (f32[1,4,832]{2,1,0:T(4,128)S(1)}, f32[1,4,832]{2,1,0:T(4,128)}, u32[]{:S(2)}) copy-start(f32[1,4,832]{2,1,0:T(4,128)} %get-tuple-element.158) | copy-start | bytes 39940
  373.3 36.1 %collective-permute-start.2 = (bf16[2,128,3072]{2,1,0:T(8,128)(2,1)}, bf16[2,128,3072]{2,1,0:T(8,128)(2,1)}, u32[]{:S(2)}, u32[]{:S(2)}) collective-permute-start(bf16[2,128,3072]{2,1,0:T(8,128)(2,1)} %fusion.11), channel_id=1, source_target_pairs={{0,16},{4,20},{8,24},{12,28},{16,0},{20,4},{24,8},{28,12},{1,17},{... | collective-permute-start | bytes 4718600 | tf_op jit(solution)/shard_map/ppermute | solution.py:336
  378.9 12.8 %copy-start.1 = (f32[2,256,6,8]{3,1,2,0:T(8,128)}, f32[2,256,6,8]{3,1,2,0:T(8,128)S(1)}, u32[]{:S(2)}) copy-start(f32[2,256,6,8]{3,1,2,0:T(8,128)S(1)} %copy.126) | copy-start | bytes 294916
  384.6 7.1 copy-start
  391.7 17.7 %copy-start.33 = (f32[2,3072]{1,0:T(2,128)S(1)}, f32[2,3072]{1,0:T(2,128)}, u32[]{:S(2)}) copy-start(f32[2,3072]{1,0:T(2,128)} %select_n.238) | copy-start | bytes 73732
  391.7 17.7 %copy-start.34 = (f32[2,3072]{1,0:T(2,128)S(1)}, f32[2,3072]{1,0:T(2,128)}, u32[]{:S(2)}) copy-start(f32[2,3072]{1,0:T(2,128)} %select_n.225) | copy-start | bytes 73732
  391.7 17.7 %copy-start.35 = (f32[2,3072]{1,0:T(2,128)S(1)}, f32[2,3072]{1,0:T(2,128)}, u32[]{:S(2)}) copy-start(f32[2,3072]{1,0:T(2,128)} %select_n.218) | copy-start | bytes 73732
  408.0 6.2 copy-start.6
  414.3 25.7 %slice-start = ((s8[7028736]{0:T(1024)(128)(4,1)}), s8[4194304]{0:T(1024)(128)(4,1)S(1)}, s32[]{:S(2)}) async-start(s8[7028736]{0:T(1024)(128)(4,1)} %bitcast.149), calls=%async_computation.8 | async-start | bytes 8388608
  414.3 25.7 %slice-start.1 = ((s8[7028736]{0:T(1024)(128)(4,1)}), s8[2834432]{0:T(1024)(128)(4,1)S(1)}, s32[]{:S(2)}) async-start(s8[7028736]{0:T(1024)(128)(4,1)} %bitcast.149), calls=%async_computation.9 | async-start | bytes 5668864
  436.6 3.3 copy-start.4
  436.6 3.3 copy-start.30
  436.6 3.3 copy-start.39
  459.7 234.8 %all-reduce.15.cloned.1.call-start = ((), (), s32[]{:S(2)}) async-start(), calls=%async_computation.3 | async-start | bytes 172032 | tf_op jit(solution)/shard_map/psum | solution.py:1384
  459.8 15.1 %copy-start.5 = (f32[2,6,256,8]{3,2,1,0:T(8,128)S(1)}, f32[2,6,256,8]{3,2,1,0:T(8,128)}, u32[]{:S(2)}) copy-start(f32[2,6,256,8]{3,2,1,0:T(8,128)} %copy-done.4) | copy-start | bytes 294916
  470.0 2.9 copy-start.9
  472.9 3.3 copy-start.57
  472.9 3.3 copy-start.59
  473.6 13.7 %collective-permute-start.3 = (bf16[2,3,3328]{2,1,0:T(4,128)(2,1)}, bf16[2,3,3328]{2,1,0:T(4,128)(2,1)}, u32[]{:S(2)}, u32[]{:S(2)}) collective-permute-start(bf16[2,3,3328]{2,1,0:T(4,128)(2,1)} %slice.228), channel_id=1, source_target_pairs={{4,0},{8,4},{12,8},{16,12},{20,16},{24,20},{28,24},{5,1},{9,5},{13... | collective-permute-start | bytes 119816 | tf_op jit(solution)/shard_map/ppermute | solution.py:331
  479.3 6.4 copy-start.38
  479.3 10.9 %copy-start.14 = (bf16[512,3072]{1,0:T(8,128)(2,1)S(1)}, bf16[512,3072]{1,0:T(8,128)(2,1)}, u32[]{:S(2)}) copy-start(bf16[512,3072]{1,0:T(8,128)(2,1)} %get-tuple-element.143) | copy-start | bytes 9437188
  529.5 2.5 copy-start.46
  532.0 2.9 copy-start.28
  532.0 2.9 copy-start.44
  532.0 2.9 copy-start.49
  532.0 2.9 copy-start.50
  532.1 2.9 copy-start.51
  534.9 3.0 copy-start.53
  535.7 165.8 %all-gather.7.cloned.1.call-start = ((), (), s32[]{:S(2)}) async-start(), calls=%async_computation.6 | async-start | bytes 2654208 | tf_op jit(solution)/shard_map/all_gather | solution.py:1408
  537.9 10.9 %copy-start.48 = (f32[1,2,2,128]{3,1,2,0:T(2,128)S(1)}, f32[1,2,2,128]{3,1,2,0:T(2,128)}, u32[]{:S(2)}) copy-start(f32[1,2,2,128]{3,1,2,0:T(2,128)} %copy-done.47) | copy-start | bytes 6148
  537.9 10.9 %copy-start.11 = (bf16[2,1,256,1536]{3,2,1,0:T(8,128)(2,1)S(1)}, bf16[2,1,256,1536]{3,2,1,0:T(8,128)(2,1)}, u32[]{:S(2)}) copy-start(bf16[2,1,256,1536]{3,2,1,0:T(8,128)(2,1)} %param.16) | copy-start | bytes 4718596
  537.9 10.9 %copy-start.12 = (f32[512,1536]{1,0:T(8,128)S(1)}, f32[512,1536]{1,0:T(8,128)}, u32[]{:S(2)}) copy-start(f32[512,1536]{1,0:T(8,128)} %get-tuple-element.167) | copy-start | bytes 9437188
  (9 other events, 14.4 us)
Sparse Core Ops, SparseCore 0:
  16.4 42.3 all-reduce.16
  60.4 175.0 all-gather.4
  277.7 100.2 reduce-scatter.2
  459.9 29.1 reduce-scatter.4
  535.8 123.4 all-reduce.14
  661.3 31.0 all-gather.6

commit v4 on v3

--- a/solution.py
+++ b/solution.py
@@ -499,245 +499,32 @@
     )(w_t)
 
 
-def reduce_kernel(
-    chunks,
-    pieces,
-    groups,
-    dp_ref,
-    nm_ref,
-    o_ref,
-    dp,
-    nm,
-    g,
-    sa1,
-    sb1,
-    sa2,
-    sb2,
-    s3,
-    ka2,
-    kb2,
-    f3,
-    ra1,
-    rb1,
-    ra2,
-    rb2,
-    rz,
-    in_sem,
-    s_in,
-    r_in,
-    s_step,
-    r_step,
-    s_all,
-    r_all,
-):
-    s, z, c, x, y, near = around()
-    wide = dp.shape[2]
-    shard = rz.shape[-1]
-
-    def remote(src, dst, ss, rs, to):
-        return pltpu.make_async_remote_copy(
-            src_ref=src, dst_ref=dst, send_sem=ss, recv_sem=rs, device_id=near[to], device_id_type=MESH
-        )
-
-    local_copies, core_copies = [], []
-    for i, (a, b) in enumerate(pieces):
-        here = dp_ref.at[:, pl.ds(pl.multiple_of(c * wide + a, 128), b - a)]
-        there = dp_ref.at[:, pl.ds(pl.multiple_of((1 - c) * wide + a, 128), b - a)]
-        local_copies.append(
-            pltpu.make_async_copy(here, dp.at[0, :, pl.ds(a, b - a)], in_sem.at[i])
-        )
-        core_copies.append(
-            remote(there, dp.at[1, :, pl.ds(a, b - a)], s_in.at[i], r_in.at[i], "c")
-        )
-    n_in = len(pieces)
-    nm_local = pltpu.make_async_copy(nm_ref, nm.at[0], in_sem.at[n_in])
-    nm_core = remote(nm_ref, nm.at[1], s_in.at[n_in], r_in.at[n_in], "c")
-    nm_local.start()
-    for copy in local_copies:
-        copy.start()
-    greet(near)
-    nm_core.start()
-    for copy in core_copies:
-        copy.start()
-
-    def step_copy(kind, u):
-        slot = u % 2
-        ss, rs = s_step.at[kind, slot], r_step.at[kind, u]
-        if kind == 0:
-            return remote(sa1.at[slot], ra1.at[u], ss, rs, "x")
-        if kind == 1:
-            return remote(sb1.at[slot], rb1.at[u], ss, rs, "y")
-        if kind == 2:
-            return remote(sa2.at[slot], ra2.at[u], ss, rs, "y")
-        if kind == 3:
-            return remote(sb2.at[slot], rb2.at[u], ss, rs, "x")
-        k = kind - 3
-        other = (z + 1 - 2 * (z % 2), z + 2 - 4 * (z // 2), 3 - z)[k - 1]
-        cols = pl.ds(pl.multiple_of(other * shard, 128), shard)
-        return remote(s3.at[slot, :, :, cols], rz.at[u, k - 1], ss, rs, "z%d" % k)
-
-    def part(px, py, ts, T=None):
-        if T is None:
-            return o_ref.at[c, ts, :, px, py]
-        return o_ref.at[c, ts, T, px, py]
-
-    def all_copy(q, kind):
-        a, b = groups[q]
-        ts = pl.ds(a, b - a)
-        ss, rs = s_all.at[q, kind], r_all.at[q, kind]
-        if kind == 0:
-            return remote(part(x, y, ts), part(x, y, ts), ss, rs, "x")
-        if kind == 1:
-            return remote(part(x, y, ts), part(x, y, ts), ss, rs, "y")
-        if kind == 2:
-            return remote(part(x, y, ts), part(x, y, ts), ss, rs, "c")
-        if kind == 3:
-            return remote(part(1 - x, y, ts, 0), part(1 - x, y, ts, 0), ss, rs, "y")
-        if kind == 4:
-            return remote(part(x, 1 - y, ts, 1), part(x, 1 - y, ts, 1), ss, rs, "x")
-        if kind == 5:
-            return remote(part(1 - x, y, ts), part(1 - x, y, ts), ss, rs, "c")
-        if kind == 6:
-            return remote(part(x, 1 - y, ts), part(x, 1 - y, ts), ss, rs, "c")
-        return remote(part(1 - x, 1 - y, ts), part(1 - x, 1 - y, ts), ss, rs, "c")
-
-    def sl(at, size=16):
-        return pl.ds(pl.multiple_of(at, 16), size)
-
-    def free(kind, u):
-        @pl.when(u >= 2)
-        def _():
-            step_copy(kind, u - 2).wait_send()
-
-    def step(t, carry):
-        @pl.when(t < chunks)
-        def _():
-            for i, (a, _) in enumerate(pieces):
-
-                @pl.when(t == a // 128)
-                def _(i=i):
-                    if i == 0:
-                        nm_local.wait()
-                        nm_core.wait_recv()
-                    local_copies[i].wait()
-                    core_copies[i].wait_recv()
-
-            slot = t % 2
-            cols = pl.ds(pl.multiple_of(t * 128, 128), 128)
-            g[slot] = mm(dp[0, :, cols], nm[0], TN) + mm(dp[1, :, cols], nm[1], TN)
-            free(0, t)
-            free(1, t)
-            sa1[slot] = g[slot, sl((1 - x) * 32, 32)].astype(bf16)
-            step_copy(0, t).start()
-            sb1[slot, 0:16] = g[slot, sl(64 + (1 - y) * 16)].astype(bf16)
-            sb1[slot, 16:32] = g[slot, sl(96 + (1 - y) * 16)].astype(bf16)
-            step_copy(1, t).start()
-
-        @pl.when((t >= 1) & (t - 1 < chunks))
-        def _():
-            u = t - 1
-            slot = u % 2
-            step_copy(0, u).wait_recv()
-            free(2, u)
-            sa2[slot] = (
-                g[slot, sl(x * 32 + (1 - y) * 16)] + ra1[u, sl((1 - y) * 16)].astype(f32)
-            ).astype(bf16)
-            step_copy(2, u).start()
-            ka2[slot] = g[slot, sl(x * 32 + y * 16)] + ra1[u, sl(y * 16)].astype(f32)
-            step_copy(1, u).wait_recv()
-            free(3, u)
-            sb2[slot] = (
-                g[slot, sl(64 + (1 - x) * 32 + y * 16)] + rb1[u, sl((1 - x) * 16)].astype(f32)
-            ).astype(bf16)
-            step_copy(3, u).start()
-            kb2[slot] = g[slot, sl(64 + x * 32 + y * 16)] + rb1[u, sl(x * 16)].astype(f32)
-
-        @pl.when((t >= 2) & (t - 2 < chunks))
-        def _():
-            u = t - 2
-            slot = u % 2
-            step_copy(2, u).wait_recv()
-            step_copy(3, u).wait_recv()
-            for k in (4, 5, 6):
-                free(k, u)
-            va = ka2[slot] + ra2[u].astype(f32)
-            vb = kb2[slot] + rb2[u].astype(f32)
-            f3[slot, 0] = va
-            f3[slot, 1] = vb
-            s3[slot, 0] = va.astype(bf16)
-            s3[slot, 1] = vb.astype(bf16)
-            for k in (4, 5, 6):
-                step_copy(k, u).start()
-
-        @pl.when((t >= 3) & (t - 3 < chunks))
-        def _():
-            u = t - 3
-            slot = u % 2
-            for k in (4, 5, 6):
-                step_copy(k, u).wait_recv()
-            mine = pl.ds(pl.multiple_of(z * shard, 128), shard)
-            for T in (0, 1):
-                total = f3[slot, T, :, mine]
-                for k in range(3):
-                    total = total + rz[u, k, T].astype(f32)
-                o_ref[c, u, T, x, y] = total.astype(bf16)
-
-        for q, (a, b) in enumerate(groups):
-
-            @pl.when(t == b - 1 + 3)
-            def _(q=q):
-                for kind in (0, 1, 2):
-                    all_copy(q, kind).start()
-
-            @pl.when(t == b - 1 + 4)
-            def _(q=q):
-                all_copy(q, 0).wait_recv()
-                all_copy(q, 3).start()
-                all_copy(q, 5).start()
-                all_copy(q, 1).wait_recv()
-                all_copy(q, 4).start()
-                all_copy(q, 6).start()
-
-            @pl.when(t == b - 1 + 5)
-            def _(q=q):
-                all_copy(q, 3).wait_recv()
-                all_copy(q, 4).wait_recv()
-                all_copy(q, 7).start()
-
-        return carry
-
-    lax.fori_loop(0, chunks + 5, step, 0)
-    for q in range(len(groups)):
-        for kind in (2, 5, 6, 7):
-            all_copy(q, kind).wait_recv()
-        for kind in range(8):
-            all_copy(q, kind).wait_send()
-    for u in (chunks - 2, chunks - 1):
-        for kind in range(7):
-            step_copy(kind, u).wait_send()
-    nm_core.wait_send()
-    for copy in core_copies:
-        copy.wait_send()
-
-
-def reduce_products(dp, nm, collective_id):
-    rows, total = dp.shape
-    width = nm.shape[1]
-    shard = width // 4
-    wide = total // 2
-    chunks = wide // 128
-    cuts = sorted({0, min(256, wide), min(1280, wide), wide})
-    pieces = list(zip(cuts[:-1], cuts[1:]))
-    marks = sorted({0, chunks * 2 // 5, chunks * 7 // 10, chunks * 9 // 10, chunks})
-    groups = list(zip(marks[:-1], marks[1:]))
-    n = len(pieces)
-    dma = pltpu.SemaphoreType.DMA
-    out = pl.pallas_call(
-        partial(reduce_kernel, chunks, pieces, groups),
-        in_specs=[pl.BlockSpec(memory_space=pl.ANY)] * 2,
-        out_specs=pl.BlockSpec(memory_space=pltpu.VMEM),
-        out_shape=jax.ShapeDtypeStruct((2, chunks, 2, 2, 2, 16, shard), bf16),
-        scratch_shapes=[
+class Products:
+    IN = 4
+    SCRATCH = 22
+
+    @staticmethod
+    def sizes(a_list, b):
+        rows = b.shape[0]
+        wide = sum(a.shape[1] for a in a_list) // 2
+        return rows, wide, b.shape[1], wide // 128
+
+    @staticmethod
+    def marks(chunks):
+        return sorted({0, chunks * 2 // 5, chunks * 7 // 10, chunks * 9 // 10, chunks})
+
+    @staticmethod
+    def out_shape(a_list, b):
+        _, _, width, chunks = Products.sizes(a_list, b)
+        return jax.ShapeDtypeStruct((2, chunks, 2, 2, 2, 16, width // 4), bf16)
+
+    @staticmethod
+    def scratch(a_list, b):
+        rows, wide, width, chunks = Products.sizes(a_list, b)
+        dma = pltpu.SemaphoreType.DMA
+        n = Products.IN
+        marks = Products.marks(chunks)
+        return [
             pltpu.VMEM((2, rows, wide), bf16),
             pltpu.VMEM((2, rows, width), bf16),
             pltpu.VMEM((2, 128, width), f32),
@@ -753,24 +540,371 @@
             pltpu.VMEM((chunks, 32, width), bf16),
             pltpu.VMEM((chunks, 16, width), bf16),
             pltpu.VMEM((chunks, 16, width), bf16),
-            pltpu.VMEM((chunks, 3, 2, 16, shard), bf16),
-            dma((n + 1,)),
-            dma((n + 1,)),
-            dma((n + 1,)),
+            pltpu.VMEM((chunks, 3, 2, 16, width // 4), bf16),
+            dma((n,)),
+            dma((n,)),
+            dma((n,)),
             dma((7, 2)),
             dma((7, chunks)),
-            dma((len(groups), 8)),
-            dma((len(groups), 8)),
+            dma((2, len(marks) - 1, 8)),
+        ]
+
+    def __init__(self, place, a_refs, b_ref, out, scratch):
+        self.s, self.z, self.c, self.x, self.y, self.near = place
+        (
+            self.a,
+            self.b,
+            self.g,
+            self.sa1,
+            self.sb1,
+            self.sa2,
+            self.sb2,
+            self.s3,
+            self.ka2,
+            self.kb2,
+            self.f3,
+            self.ra1,
+            self.rb1,
+            self.ra2,
+            self.rb2,
+            self.rz,
+            self.in_sem,
+            self.s_in,
+            self.r_in,
+            self.s_step,
+            self.r_step,
+            self.sems_all,
+        ) = scratch
+        self.out = out
+        self.shard = self.rz.shape[-1]
+        self.chunks = self.ra1.shape[0]
+        marks = Products.marks(self.chunks)
+        self.groups = list(zip(marks[:-1], marks[1:]))
+        c = self.c
+        self.operands = []
+        self.operands.append(
+            (
+                0,
+                pltpu.make_async_copy(b_ref, self.b.at[0], self.in_sem.at[0]),
+                self.remote(b_ref, self.b.at[1], self.s_in.at[0], self.r_in.at[0], "c"),
+            )
+        )
+        at = 0
+        for i, ref in enumerate(a_refs):
+            half = ref.shape[1] // 2
+            here = ref.at[:, pl.ds(pl.multiple_of(c * half, 128), half)]
+            there = ref.at[:, pl.ds(pl.multiple_of((1 - c) * half, 128), half)]
+            to = pl.ds(at, half)
+            self.operands.append(
+                (
+                    at // 128,
+                    pltpu.make_async_copy(here, self.a.at[0, :, to], self.in_sem.at[i + 1]),
+                    self.remote(there, self.a.at[1, :, to], self.s_in.at[i + 1], self.r_in.at[i + 1], "c"),
+                )
+            )
+            at += half
+
+    def remote(self, src, dst, ss, rs, to):
+        return pltpu.make_async_remote_copy(
+            src_ref=src,
+            dst_ref=dst,
+            send_sem=ss,
+            recv_sem=rs,
+            device_id=self.near[to],
+            device_id_type=MESH,
+        )
+
+    def load(self):
+        for _, here, _ in self.operands:
+            here.start()
+
+    def share(self):
+        for _, _, there in self.operands:
+            there.start()
+
+    def step_copy(self, kind, u):
+        slot = u % 2
+        ss, rs = self.s_step.at[kind, slot], self.r_step.at[kind, u]
+        if kind < 4:
+            src, dst, to = (
+                (self.sa1, self.ra1, "x"),
+                (self.sb1, self.rb1, "y"),
+                (self.sa2, self.ra2, "y"),
+                (self.sb2, self.rb2, "x"),
+            )[kind]
+            return self.remote(src.at[slot], dst.at[u], ss, rs, to)
+        k = kind - 3
+        z = self.z
+        other = (z + 1 - 2 * (z % 2), z + 2 - 4 * (z // 2), 3 - z)[k - 1]
+        cols = pl.ds(pl.multiple_of(other * self.shard, 128), self.shard)
+        return self.remote(self.s3.at[slot, :, :, cols], self.rz.at[u, k - 1], ss, rs, "z%d" % k)
+
+    def all_copy(self, q, kind):
+        a, b = self.groups[q]
+        ts = pl.ds(a, b - a)
+        x, y, c = self.x, self.y, self.c
+        px = 1 - x if kind in (3, 5, 7) else x
+        py = 1 - y if kind in (4, 6, 7) else y
+        if kind in (3, 4):
+            block = self.out.at[c, ts, kind - 3, px, py]
+        else:
+            block = self.out.at[c, ts, :, px, py]
+        to = ("x", "y", "c", "y", "x", "c", "c", "c")[kind]
+        return self.remote(block, block, self.sems_all.at[0, q, kind], self.sems_all.at[1, q, kind], to)
+
+    def step(self, t):
+        x, y, z, c = self.x, self.y, self.z, self.c
+        g, ra1, rb1 = self.g, self.ra1, self.rb1
+        chunks = self.chunks
+        copy = self.step_copy
+
+        def sl(at, size=16):
+            return pl.ds(pl.multiple_of(at, 16), size)
+
+        def free(kind, u):
+            @pl.when(u >= 2)
+            def _():
+                copy(kind, u - 2).wait_send()
+
+        @pl.when(t < chunks)
+        def _():
+            for first, here, there in self.operands:
+
+                @pl.when(t == first)
+                def _(here=here, there=there):
+                    here.wait()
+                    there.wait_recv()
+
+            slot = t % 2
+            cols = pl.ds(pl.multiple_of(t * 128, 128), 128)
+            g[slot] = mm(self.a[0, :, cols], self.b[0], TN) + mm(self.a[1, :, cols], self.b[1], TN)
+            free(0, t)
+            free(1, t)
+            self.sa1[slot] = g[slot, sl((1 - x) * 32, 32)].astype(bf16)
+            copy(0, t).start()
+            self.sb1[slot, 0:16] = g[slot, sl(64 + (1 - y) * 16)].astype(bf16)
+            self.sb1[slot, 16:32] = g[slot, sl(96 + (1 - y) * 16)].astype(bf16)
+            copy(1, t).start()
+
+        @pl.when((t >= 1) & (t - 1 < chunks))
+        def _():
+            u = t - 1
+            slot = u % 2
+            copy(0, u).wait_recv()
+            free(2, u)
+            self.sa2[slot] = (
+                g[slot, sl(x * 32 + (1 - y) * 16)] + ra1[u, sl((1 - y) * 16)].astype(f32)
+            ).astype(bf16)
+            copy(2, u).start()
+            self.ka2[slot] = g[slot, sl(x * 32 + y * 16)] + ra1[u, sl(y * 16)].astype(f32)
+            copy(1, u).wait_recv()
+            free(3, u)
+            self.sb2[slot] = (
+                g[slot, sl(64 + (1 - x) * 32 + y * 16)] + rb1[u, sl((1 - x) * 16)].astype(f32)
+            ).astype(bf16)
+            copy(3, u).start()
+            self.kb2[slot] = g[slot, sl(64 + x * 32 + y * 16)] + rb1[u, sl(x * 16)].astype(f32)
+
+        @pl.when((t >= 2) & (t - 2 < chunks))
+        def _():
+            u = t - 2
+            slot = u % 2
+            copy(2, u).wait_recv()
+            copy(3, u).wait_recv()
+            for k in (4, 5, 6):
+                free(k, u)
+            va = self.ka2[slot] + self.ra2[u].astype(f32)
+            vb = self.kb2[slot] + self.rb2[u].astype(f32)
+            self.f3[slot, 0] = va
+            self.f3[slot, 1] = vb
+            self.s3[slot, 0] = va.astype(bf16)
+            self.s3[slot, 1] = vb.astype(bf16)
+            for k in (4, 5, 6):
+                copy(k, u).start()
+
+        @pl.when((t >= 3) & (t - 3 < chunks))
+        def _():
+            u = t - 3
+            slot = u % 2
+            for k in (4, 5, 6):
+                copy(k, u).wait_recv()
+            mine = pl.ds(pl.multiple_of(z * self.shard, 128), self.shard)
+            for part in (0, 1):
+                total = self.f3[slot, part, :, mine]
+                for k in range(3):
+                    total = total + self.rz[u, k, part].astype(f32)
+                self.out[c, u, part, x, y] = total.astype(bf16)
+
+        for q, (_, b) in enumerate(self.groups):
+
+            @pl.when(t == b - 1 + 3)
+            def _(q=q):
+                for kind in (0, 1, 2):
+                    self.all_copy(q, kind).start()
+
+            @pl.when(t == b - 1 + 4)
+            def _(q=q):
+                self.all_copy(q, 0).wait_recv()
+                self.all_copy(q, 3).start()
+                self.all_copy(q, 5).start()
+                self.all_copy(q, 1).wait_recv()
+                self.all_copy(q, 4).start()
+                self.all_copy(q, 6).start()
+
+            @pl.when(t == b - 1 + 5)
+            def _(q=q):
+                self.all_copy(q, 3).wait_recv()
+                self.all_copy(q, 4).wait_recv()
+                self.all_copy(q, 7).start()
+
+    def steps(self):
+        return self.chunks + 5
+
+    def close(self):
+        for q in range(len(self.groups)):
+            for kind in (2, 5, 6, 7):
+                self.all_copy(q, kind).wait_recv()
+            for kind in range(8):
+                self.all_copy(q, kind).wait_send()
+        for u in (self.chunks - 2, self.chunks - 1):
+            for kind in range(7):
+                self.step_copy(kind, u).wait_send()
+        for _, _, there in self.operands:
+            there.wait_send()
+
+
+class Smalls:
+    SCRATCH = 5
+
+    @staticmethod
+    def scratch(v):
+        dma = pltpu.SemaphoreType.DMA
+        return [
+            pltpu.VMEM((3,) + v.shape, f32),
+            pltpu.VMEM((3,) + v.shape, f32),
+            pltpu.VMEM((3,) + v.shape[1:], f32),
+            dma((6,)),
+            dma((6,)),
+        ]
+
+    def __init__(self, place, v_ref, out, scratch):
+        self.s, self.z, self.c, self.x, self.y, self.near = place
+        self.v, self.out = v_ref, out
+        self.total, self.got, self.got_z, self.send, self.recv = scratch
+
+    def copy(self, kind):
+        if kind < 3:
+            src = self.v if kind == 0 else self.total.at[kind - 1]
+            dst, to = self.got.at[kind], "cxy"[kind]
+        else:
+            z = self.z
+            k = kind - 2
+            other = (z + 1 - 2 * (z % 2), z + 2 - 4 * (z // 2), 3 - z)[k - 1]
+            src, dst, to = self.total.at[2, other], self.got_z.at[k - 1], "z%d" % k
+        return pltpu.make_async_remote_copy(
+            src_ref=src,
+            dst_ref=dst,
+            send_sem=self.send.at[kind],
+            recv_sem=self.recv.at[kind],
+            device_id=self.near[to],
+            device_id_type=MESH,
+        )
+
+    def start(self):
+        self.copy(0).start()
+
+    def advance(self, kind):
+        self.copy(kind).wait_recv()
+        mine = self.v[...] if kind == 0 else self.total[kind - 1]
+        self.total[kind] = mine + self.got[kind]
+        for k in (kind + 1,) if kind < 2 else (3, 4, 5):
+            self.copy(k).start()
+
+    def close(self):
+        total = self.total[2, self.z]
+        for k in (3, 4, 5):
+            self.copy(k).wait_recv()
+            total = total + self.got_z[k - 3]
+        self.out[...] = total
+        for k in range(6):
+            self.copy(k).wait_send()
+
+
+def sums_kernel(
+    gate_ref,
+    conv_ref,
+    nm_ref,
+    og_ref,
+    no_ref,
+    v_ref,
+    in_out,
+    out_out,
+    v_out,
+    *scratch,
+):
+    place = around()
+    cut = Products.SCRATCH
+    inp = Products(place, [gate_ref, conv_ref], nm_ref, in_out, scratch[:cut])
+    outp = Products(place, [og_ref], no_ref, out_out, scratch[cut : 2 * cut])
+    small = Smalls(place, v_ref, v_out, scratch[2 * cut :])
+    outp.load()
+    inp.load()
+    greet(place[-1])
+    outp.share()
+    small.start()
+    inp.share()
+
+    def first(t, carry):
+        outp.step(t)
+        return carry
+
+    lax.fori_loop(0, outp.chunks, first, 0)
+
+    def second(t, carry):
+        inp.step(t)
+
+        @pl.when(t < outp.steps() - outp.chunks)
+        def _():
+            outp.step(t + outp.chunks)
+
+        for kind in range(3):
+
+            @pl.when(t == 2 * kind + 1)
+            def _(kind=kind):
+                small.advance(kind)
+
+        return carry
+
+    lax.fori_loop(0, inp.steps(), second, 0)
+    small.close()
+    outp.close()
+    inp.close()
+
+
+def weight_sums(d_gate, d_rest, nm, og, no, v, collective_id):
+    vmem = pl.BlockSpec(memory_space=pltpu.VMEM)
+    hbm = pl.BlockSpec(memory_space=pl.ANY)
+    a_in, a_out, total = pl.pallas_call(
+        sums_kernel,
+        in_specs=[hbm] * 5 + [vmem],
+        out_specs=[vmem] * 3,
+        out_shape=[
+            Products.out_shape([d_gate, d_rest], nm),
+            Products.out_shape([og], no),
+            jax.ShapeDtypeStruct(v.shape[1:], f32),
         ],
+        scratch_shapes=Products.scratch([d_gate, d_rest], nm)
+        + Products.scratch([og], no)
+        + Smalls.scratch(v),
         compiler_params=pltpu.CompilerParams(
-            collective_id=collective_id, has_side_effects=True, vmem_limit_bytes=VMEM
+            collective_id=collective_id, has_side_effects=True, vmem_limit_bytes=VMEM_MOST
         ),
         cost_estimate=pl.CostEstimate(
-            flops=4 * rows * wide * width, bytes_accessed=200_000_000, transcendentals=0
+            flops=6 * nm.shape[0] * nm.shape[1] * 9000, bytes_accessed=400_000_000, transcendentals=0
         ),
-        name="reduce_products",
-    )(dp, nm)
-    return out.reshape(total, shard)
+        name="weight_sums",
+    )(d_gate, d_rest, nm, og, no, v)
+    return a_in, a_out.reshape(og.shape[1], -1), total
 
 
 LANES = 128
@@ -1123,6 +1257,311 @@
     )(conv_low, raw, conv_w, conv_b, shift, rate, skip_wide)
 
 
+def scan_backward_kernel(
+    hs,
+    dy_ref,
+    x_ref,
+    bc_ref,
+    y_ref,
+    begin_ref,
+    raw_ref,
+    conv_ref,
+    halo_ref,
+    cw_ref,
+    cb_ref,
+    shift_ref,
+    rate_ref,
+    skip_ref,
+    dconv_ref,
+    dcw_ref,
+    dcb_ref,
+    heads_ref,
+    *scratch,
+):
+    (
+        buf,
+        wide_buf,
+        scores,
+        total,
+        dts,
+        cums,
+        rows_t,
+        ends,
+        dxl,
+        dbc,
+        ddt_sum,
+        dcum_sum,
+        head_low,
+        next_low,
+        h_send,
+        h_recv,
+    ) = scratch[EXCHANGE:]
+    ex = Exchange(False, *scratch[:EXCHANGE])
+    s, z = ex.s, ex.z
+    micro, t, channels = conv_ref.shape
+    inner = x_ref.shape[2]
+    n = begin_ref.shape[1]
+    gc = GROUP * hs
+    groups = inner // gc
+    half = t // 2
+    taps = cw_ref.shape[0]
+    near = {k: ex.near[k] for k in ("c", "x", "y")}
+    near["next"] = ((s + 1) % 8, z)
+    near["last"] = ((s + 7) % 8, z)
+    greet(near)
+    first_rows = [
+        pltpu.make_async_remote_copy(
+            src_ref=head_low.at[m],
+            dst_ref=next_low.at[m],
+            send_sem=h_send.at[m],
+            recv_sem=h_recv.at[m],
+            device_id=near["last"],
+            device_id_type=MESH,
+        )
+        for m in range(micro)
+    ]
+    has_prior = jnp.where(s > 0, 1.0, 0.0)
+    has_next = jnp.where(s < 7, 1.0, 0.0)
+
+    def own_states(m, a, b):
+        def body(g, carry):
+            lanes = pl.ds(pl.multiple_of(g * gc, gc), gc)
+            cum = head_columns(cums[m], g)
+            weighted = (dy_ref[m, :, lanes].astype(f32) * widen(jnp.exp(cum), hs)).astype(bf16)
+            state = mm(bc_ref[m, :, n:], weighted, TN)
+            ex.put_own(m, lanes, state, widen(jnp.exp(cum[t - 1 :]), hs))
+            return carry
+
+        lax.fori_loop(a, b, body, 0)
+
+    def local_terms(m, a, b):
+        lane = lax.broadcasted_iota(jnp.int32, (t, 2 * hs), 1)
+        lane_half = lax.broadcasted_iota(jnp.int32, (half, 2 * hs), 1)
+
+        def body(g, carry):
+            lanes = pl.ds(pl.multiple_of(g * gc, gc), gc)
+            cum = head_columns(cums[m], g)
+            rows = rows_t[m, pl.ds(pl.multiple_of(g * GROUP, GROUP), GROUP), :]
+            dt_wide = widen(head_columns(dts[m], g), hs)
+            weighted = (x_ref[m, :, lanes].astype(f32) * dt_wide).astype(bf16)
+            for k in range(0, GROUP, 2):
+                pair = weighted[:, k * hs : (k + 2) * hs]
+                at = pl.ds(pl.multiple_of(g * gc + k * hs, 2 * hs), 2 * hs)
+                dy = dy_ref[m, :, at]
+                top, low = [], []
+                for h in (k, k + 1):
+                    col, row = cum[:, h : h + 1], rows[h : h + 1, :]
+                    mine = jnp.where(lane < hs, pair, 0) if h == k else jnp.where(lane < hs, 0, pair)
+                    l1 = jnp.exp(jnp.minimum(row - col[:half], 0.0))
+                    l2 = jnp.exp(jnp.minimum(row[:, half:] - col[half:], 0.0))
+                    total[:half, :] += l1 * mm(mine[:half], dy, NT)
+                    total[half:, half:] += l2 * mm(mine[half:], dy[half:], NT)
+                    top.append(mm((l1 * scores[m, :half, :]).astype(bf16), dy))
+                    low.append(mm((l2 * scores[m, half:, half:]).astype(bf16), dy[half:]))
+                dxl[m, :half, at] = jnp.where(lane_half < hs, top[0], top[1])
+                dxl[m, half:, at] = jnp.where(lane_half < hs, low[0], low[1])
+            return carry
+
+        lax.fori_loop(a, b, body, 0)
+
+    def upper_ones():
+        j = lax.broadcasted_iota(jnp.int32, (t, t), 0)
+        i = lax.broadcasted_iota(jnp.int32, (t, t), 1)
+        return jnp.where(i >= j, 1.0, 0.0)
+
+    def local_close(m):
+        d = total[...] * upper_ones()
+        dbc[m, :, 0:n] = mm(d.astype(bf16), bc_ref[m, :, n:])
+        dbc[m, :, n:] = mm(d.T.astype(bf16), bc_ref[m, :, :n])
+
+    def through_states(m, sums):
+        r = lax.broadcasted_iota(jnp.int32, (gc, LANES), 0)
+        col = lax.broadcasted_iota(jnp.int32, (gc, LANES), 1)
+        ddt_sum[...] = jnp.zeros_like(ddt_sum)
+        dcum_sum[...] = jnp.zeros_like(dcum_sum)
+
+        def body(g, carry):
+            last, skips = carry
+            lanes = pl.ds(pl.multiple_of(g * gc, gc), gc)
+            ones = jnp.where(r // hs + g * GROUP == col, 1.0, 0.0).astype(bf16)
+            cum = head_columns(cums[m], g)
+            dt_wide = widen(head_columns(dts[m], g), hs)
+            x, dy = x_ref[m, :, lanes].astype(f32), dy_ref[m, :, lanes].astype(f32)
+            weighted = (x * dt_wide).astype(bf16).astype(f32)
+            decay = widen(jnp.exp(cum), hs)
+            to_end = widen(jnp.exp(cum[t - 1 :] - cum), hs)
+            s_in, ds = begin_ref[m, :, lanes], ends[m, :, lanes]
+            through = to_end * mm(bc_ref[m, :, 0:n], ds)
+            d_weighted = dxl[m, :, lanes] + through
+            dconv_ref[m, :, lanes] = (dt_wide * d_weighted + skip_ref[:, lanes] * dy).astype(bf16)
+            dbc[m, :, 0:n] += mm((weighted * to_end).astype(bf16), ds, NT)
+            dbc[m, :, n:] += mm((dy * decay).astype(bf16), s_in, NT)
+            ddt_sum[...] += head_sums(x * d_weighted, ones)
+            dcum_sum[...] += head_sums(dy * y_ref[m, :, lanes] - weighted * d_weighted, ones)
+            at_end = jnp.sum(weighted * through, axis=0, keepdims=True) + decay[t - 1 :] * jnp.sum(
+                s_in.astype(f32) * ds.astype(f32), axis=0, keepdims=True
+            )
+            last = last + head_sums(jnp.broadcast_to(at_end, (8, gc)), ones)
+            by_skip = jnp.sum(x * dy, axis=0, keepdims=True)
+            skips = skips + head_sums(jnp.broadcast_to(by_skip, (8, gc)), ones)
+            return last, skips
+
+        none = jnp.zeros((8, LANES), f32)
+        last, skips = lax.fori_loop(0, groups, body, (none, none))
+        d_log = exact(upper_ones(), dcum_sum[...]) + last[0:1]
+        v = raw_ref[m] + shift_ref[...]
+        d_dt = (ddt_sum[...] + d_log * rate_ref[...]) / (1.0 + jnp.exp(-v))
+        rest = dconv_ref.shape[2] - channels - LANES
+        dconv_ref[m, :, pl.ds(channels, LANES)] = d_dt.astype(bf16)
+        if rest:
+            dconv_ref[m, :, pl.ds(channels + LANES, rest)] = jnp.zeros((t, rest), bf16)
+        d_bias = jnp.sum(d_dt, axis=0, keepdims=True)
+        d_rate = jnp.sum(d_log * dts[m], axis=0, keepdims=True) * rate_ref[...]
+        return sums[0] + d_bias, sums[1] + d_rate, sums[2] + skips[0:1]
+
+    def pre_slope(into, lanes, grad, rows):
+        v = conv_rows(into[0 : HALO + rows, :], cw_ref[:, lanes], cb_ref[:, lanes])
+        sig = 1.0 / (1.0 + jnp.exp(-v))
+        return grad * (sig * (1.0 + v * (1.0 - sig)))
+
+    def load(m, lanes, into, rows):
+        into[0:HALO] = halo_ref[m, :, lanes].astype(f32) * has_prior
+        into[HALO : HALO + rows] = conv_ref[m, 0:rows, lanes].astype(f32)
+
+    def first_slopes(m):
+        def one(lanes, into, grad):
+            load(m, lanes, into, HALO)
+            head_low[m, :, lanes] = pre_slope(into, lanes, grad, HALO).astype(bf16)
+
+        def body(g, carry):
+            lanes = pl.ds(pl.multiple_of(g * gc, gc), gc)
+            one(lanes, buf, dconv_ref[m, 0:HALO, lanes].astype(f32))
+            return carry
+
+        lax.fori_loop(0, groups, body, 0)
+        one(pl.ds(inner, channels - inner), wide_buf, dbc[m, 0:HALO, :])
+        first_rows[m].start()
+
+    def conv_back(m):
+        def one(lanes, into, grad):
+            load(m, lanes, into, t)
+            slope = pre_slope(into, lanes, grad, t)
+            weights = cw_ref[:, lanes]
+            lines = []
+            for k in range(taps):
+                at = HALO - taps + 1 + k
+                lines.append(jnp.sum(slope * into[at : at + t, :], axis=0, keepdims=True))
+            dcw_ref[:, lanes] += jnp.concatenate(lines, axis=0)
+            dcb_ref[:, lanes] += jnp.sum(slope, axis=0, keepdims=True)
+            into[0:t] = slope
+            into[t : t + HALO] = next_low[m, :, lanes].astype(f32) * has_next
+            back = into[taps - 1 : taps - 1 + t, :] * weights[0:1]
+            for k in range(1, taps):
+                at = taps - 1 - k
+                back = back + into[at : at + t, :] * weights[k : k + 1]
+            dconv_ref[m, :, lanes] = back.astype(bf16)
+
+        def body(g, carry):
+            lanes = pl.ds(pl.multiple_of(g * gc, gc), gc)
+            one(lanes, buf, dconv_ref[m, :, lanes].astype(f32))
+            return carry
+
+        lax.fori_loop(0, groups, body, 0)
+        one(pl.ds(inner, channels - inner), wide_buf, dbc[m])
+
+    for m in range(micro):
+        dt, cum = steps_of(raw_ref[m], shift_ref[...], rate_ref[...])
+        dts[m] = dt
+        cums[m] = cum
+        rows_t[m] = cum.T
+        scores[m] = mm(bc_ref[m, :, 0:n], bc_ref[m, :, n:], NT) * upper_ones()
+    dcw_ref[...] = jnp.zeros_like(dcw_ref)
+    dcb_ref[...] = jnp.zeros_like(dcb_ref)
+    total[...] = jnp.zeros_like(total)
+    middle = groups // 2
+    own_states(0, 0, groups)
+    ex.core(0)
+    own_states(1, 0, middle)
+    ex.along_x(0)
+    own_states(1, middle, groups)
+    ex.core(1)
+    local_terms(0, 0, middle)
+    ex.along_x(1)
+    ex.along_y(0)
+    local_terms(0, middle, groups)
+    local_close(0)
+    total[...] = jnp.zeros_like(total)
+    ex.along_y(1)
+    ex.back_to_core(0)
+    local_terms(1, 0, groups)
+    local_close(1)
+    ex.begin_state(0, ends)
+    ex.back_to_core(1)
+    none = jnp.zeros((1, LANES), f32)
+    sums = through_states(0, (none, none, none))
+    first_slopes(0)
+    ex.begin_state(1, ends)
+    sums = through_states(1, sums)
+    first_slopes(1)
+    heads_ref[...] = jnp.concatenate(list(sums) + [jnp.zeros((5, LANES), f32)], axis=0)
+    first_rows[0].wait_recv()
+    conv_back(0)
+    first_rows[1].wait_recv()
+    conv_back(1)
+    ex.sent()
+    for copy in first_rows:
+        copy.wait_send()
+
+
+def scan_backward(
+    dy, x, bc, y, begin, raw, conv_low, halo, conv_w, conv_b, shift, rate, skip_wide, hs, collective_id
+):
+    micro, t, channels = conv_low.shape
+    inner = x.shape[2]
+    n = begin.shape[1]
+    gc = GROUP * hs
+    taps = conv_w.shape[0]
+    dma = pltpu.SemaphoreType.DMA
+    vmem = pl.BlockSpec(memory_space=pltpu.VMEM)
+    return pl.pallas_call(
+        partial(scan_backward_kernel, hs),
+        in_specs=[vmem] * 13,
+        out_specs=[vmem] * 4,
+        out_shape=[
+            jax.ShapeDtypeStruct((micro, t, -(-(channels + LANES) // 256) * 256), bf16),
+            jax.ShapeDtypeStruct((taps, channels), f32),
+            jax.ShapeDtypeStruct((1, channels), f32),
+            jax.ShapeDtypeStruct((8, LANES), f32),
+        ],
+        scratch_shapes=exchange_scratch(micro, n, inner)
+        + [
+            pltpu.VMEM((HALO + t, gc), f32),
+            pltpu.VMEM((HALO + t, 2 * n), f32),
+            pltpu.VMEM((micro, t, t), f32),
+            pltpu.VMEM((t, t), f32),
+            pltpu.VMEM((micro, t, LANES), f32),
+            pltpu.VMEM((micro, t, LANES), f32),
+            pltpu.VMEM((micro, LANES, t), f32),
+            pltpu.VMEM((micro, n, inner), bf16),
+            pltpu.VMEM((micro, t, inner), f32),
+            pltpu.VMEM((micro, t, 2 * n), f32),
+            pltpu.VMEM((t, LANES), f32),
+            pltpu.VMEM((t, LANES), f32),
+            pltpu.VMEM((micro, HALO, channels), bf16),
+            pltpu.VMEM((micro, HALO, channels), bf16),
+            dma((micro,)),
+            dma((micro,)),
+        ],
+        compiler_params=pltpu.CompilerParams(
+            collective_id=collective_id, has_side_effects=True, vmem_limit_bytes=VMEM_MOST
+        ),
+        cost_estimate=pl.CostEstimate(
+            flops=8 * micro * t * inner * (t + 3 * n), bytes_accessed=100_000_000, transcendentals=0
+        ),
+        name="scan_backward",
+    )(dy, x, bc, y, begin, raw, conv_low, halo, conv_w, conv_b, shift, rate, skip_wide)
+
+
 def project_kernel(n_ref, w_ref, v_ref, o_ref):
     total = mm(n_ref[0], w_ref[...], NT)
     for k in range(1, n_ref.shape[0]):
@@ -1147,25 +1586,36 @@
     )(parts, own, others)
 
 
-def unproject_kernel(d_ref, w_ref, v_ref, o_ref):
+def unproject_kernel(steps, d_ref, e_ref, w_ref, v_ref, o_ref):
+    def add(ref):
+        o_ref[0] += mm(ref[...], w_ref[...])
+        for k in range(1, o_ref.shape[0]):
+            o_ref[k] += mm(ref[...], v_ref[k - 1])
+
     @pl.when(pl.program_id(0) == 0)
     def _():
         o_ref[...] = jnp.zeros_like(o_ref)
 
-    o_ref[0] += mm(d_ref[...], w_ref[...])
-    for k in range(1, o_ref.shape[0]):
-        o_ref[k] += mm(d_ref[...], v_ref[k - 1])
-
-
-def unproject(d, own, others, tile):
+    @pl.when(pl.program_id(0) < steps)
+    def _():
+        add(d_ref)
+
+    @pl.when(pl.program_id(0) >= steps)
+    def _():
+        add(e_ref)
+
+
+def unproject(d, e, own, others, tile):
     shards, count, depth = others.shape
     shards += 1
     rows = d.shape[0]
+    steps = d.shape[1] // tile
     return pl.pallas_call(
-        unproject_kernel,
+        partial(unproject_kernel, steps),
         grid=(count // tile,),
         in_specs=[
-            pl.BlockSpec((rows, tile), lambda i: (0, i)),
+            pl.BlockSpec((rows, tile), lambda i: (0, jnp.minimum(i, steps - 1))),
+            pl.BlockSpec((rows, tile), lambda i: (0, jnp.maximum(i - steps, 0))),
             pl.BlockSpec((tile, depth), lambda i: (i, 0)),
             pl.BlockSpec((shards - 1, tile, depth), lambda i: (0, i, 0)),
         ],
@@ -1173,7 +1623,7 @@
         out_shape=jax.ShapeDtypeStruct((shards, rows, depth), f32),
         compiler_params=pltpu.CompilerParams(vmem_limit_bytes=VMEM),
         name="unproject",
-    )(d, own, others)
+    )(d, e, own, others)
 
 
 def rms_front(hidden_rows, gain):
@@ -1288,22 +1738,18 @@
             hs,
             3,
         )
-        b_low, c_low = bc_low[..., :n], bc_low[..., n:]
-        halo = jnp.where(rank > 0, halo, 0)
-        padded = jnp.concatenate([halo[:, HALO - (taps - 1) :], conv_low], axis=1).astype(f32)
     else:
         prior = from_behind(conv_low[:, tokens - (taps - 1) :], "seq", 1)
         padded = jnp.concatenate([prior, conv_low], axis=1).astype(f32)
-    mixed, conv_back = jax.vjp(conv_act, padded, conv_w, conv_b)
-    dt = jax.nn.softplus(dt_raw)
-    tri = (jnp.arange(tokens)[:, None] >= jnp.arange(tokens)[None, :]).astype(f32)
-    cum = jnp.einsum("ij,mjh->mih", tri, dt * rate, precision=highest)
-    dt_g, cum_g = grouped(dt), grouped(cum)
-    row_g = cum_g.transpose(0, 1, 3, 2)
-    last = cum[:, tokens - 1, :]
-    decays = lax.all_gather(jnp.exp(last), "seq", axis=0)
-    decay_w = grouped(jnp.exp(cum))
-    if not fast:
+        mixed, conv_back = jax.vjp(conv_act, padded, conv_w, conv_b)
+        dt = jax.nn.softplus(dt_raw)
+        tri = (jnp.arange(tokens)[:, None] >= jnp.arange(tokens)[None, :]).astype(f32)
+        cum = jnp.einsum("ij,mjh->mih", tri, dt * rate, precision=highest)
+        dt_g, cum_g = grouped(dt), grouped(cum)
+        row_g = cum_g.transpose(0, 1, 3, 2)
+        last = cum[:, tokens - 1, :]
+        decays = lax.all_gather(jnp.exp(last), "seq", axis=0)
+        decay_w = grouped(jnp.exp(cum))
         x_low = mixed[..., :inner].astype(bf16)
         b_low = mixed[..., inner : inner + n].astype(bf16)
         c_low = mixed[..., inner + n :].astype(bf16)
@@ -1320,42 +1766,57 @@
     output = (rows_in + valid * branch).astype(bf16).reshape(hidden.shape)
 
     g = (cot * valid).astype(bf16)
-    out_terms = mm(normed_out_low, g, TN)
     d_scanned, d_gate_in, d_gated = gate_back(mm(g, out_w, NT))
     dy = d_scanned.astype(bf16).reshape(micro, tokens, inner)
-    own_grad = block_states(dy, decay_w, c_low.transpose(0, 2, 1), hs)
-    dx_local, db_local, dc_local = local_back(x_low, dy, dt_g, cum_g, row_g, b_low, c_low, hs)
-    ds = running_states(own_grad, decays, hs, False)
-    dx_low, ddt_g, dcum_g, db, dc, last_term, dskip = carry_back(
-        x_low, dy, dx_local, y_scan, dt_g, cum_g, b_low, s_in, ds, db_local, dc_local, skip_wide, hs
-    )
-
-    def ungrouped(v):
-        return v.transpose(0, 2, 1, 3).reshape(micro, tokens, heads)
-
-    at_end = jnp.sum(last_term.reshape(micro, heads, hs), axis=-1)[:, None, :]
-    d_log = jnp.einsum("ij,mih->mjh", tri, ungrouped(dcum_g), precision=highest) + at_end
-    d_dt = (ungrouped(ddt_g) + d_log * rate) * jax.nn.sigmoid(dt_raw)
-    d_dt_bias = jnp.sum(d_dt, axis=(0, 1))
-    d_a_log = jnp.sum(d_log * dt, axis=(0, 1)) * rate
-    d_skip = jnp.sum(dskip.reshape(-1, heads, hs), axis=(0, 2))
-    mixed_grad = jnp.concatenate([dx_low.astype(f32), db, dc], axis=2)
-    d_padded, d_conv_w, d_conv_b = conv_back(mixed_grad)
-    from_next = from_behind(d_padded[:, : taps - 1].astype(bf16), "seq", -1).astype(f32)
-    d_conv = d_padded[:, taps - 1 :].at[:, tokens - (taps - 1) :].add(from_next)
-    d_dt_low = d_dt.astype(bf16).reshape(rows, heads)
+    if fast:
+        d_rest, d_conv_w, d_conv_b, by_head = scan_backward(
+            dy,
+            x_low,
+            bc_low,
+            y_scan,
+            s_in,
+            raw,
+            conv_low,
+            halo,
+            conv_w,
+            conv_b[None, :],
+            to_lanes(dt_shift[None, :]),
+            to_lanes(rate[None, :]),
+            skip_wide,
+            hs,
+            4,
+        )
+        d_dt_bias, d_a_log, d_skip = by_head[0, :heads], by_head[1, :heads], by_head[2, :heads]
+        d_conv_b = d_conv_b[0]
+        d_rest = d_rest.reshape(rows, -1)
+        d_dt_low = d_rest[:, channels : channels + heads]
+    else:
+        own_grad = block_states(dy, decay_w, c_low.transpose(0, 2, 1), hs)
+        dx_local, db_local, dc_local = local_back(x_low, dy, dt_g, cum_g, row_g, b_low, c_low, hs)
+        ds = running_states(own_grad, decays, hs, False)
+        dx_low, ddt_g, dcum_g, db, dc, last_term, dskip = carry_back(
+            x_low, dy, dx_local, y_scan, dt_g, cum_g, b_low, s_in, ds, db_local, dc_local, skip_wide, hs
+        )
+
+        def ungrouped(v):
+            return v.transpose(0, 2, 1, 3).reshape(micro, tokens, heads)
+
+        at_end = jnp.sum(last_term.reshape(micro, heads, hs), axis=-1)[:, None, :]
+        d_log = jnp.einsum("ij,mih->mjh", tri, ungrouped(dcum_g), precision=highest) + at_end
+        d_dt = (ungrouped(ddt_g) + d_log * rate) * jax.nn.sigmoid(dt_raw)
+        d_dt_bias = jnp.sum(d_dt, axis=(0, 1))
+        d_a_log = jnp.sum(d_log * dt, axis=(0, 1)) * rate
+        d_skip = jnp.sum(dskip.reshape(-1, heads, hs), axis=(0, 2))
+        mixed_grad = jnp.concatenate([dx_low.astype(f32), db, dc], axis=2)
+        d_padded, d_conv_w, d_conv_b = conv_back(mixed_grad)
+        from_next = from_behind(d_padded[:, : taps - 1].astype(bf16), "seq", -1).astype(f32)
+        d_conv = d_padded[:, taps - 1 :].at[:, tokens - (taps - 1) :].add(from_next)
+        d_dt_low = d_dt.astype(bf16).reshape(rows, heads)
     total_cols = inner + channels + heads
-    pad = -total_cols % 256 if fast else 0
-    d_proj = jnp.concatenate(
-        [
-            d_gate_in.astype(bf16),
-            d_conv.astype(bf16).reshape(rows, channels),
-            d_dt_low,
-            jnp.zeros((rows, pad), bf16),
-        ],
-        axis=1,
-    )
-    d_parts = unproject(d_proj, in_local, in_w, tile)
+    d_gate_low = d_gate_in.astype(bf16)
+    if not fast:
+        d_rest = d_conv.astype(bf16).reshape(rows, channels)
+    d_parts = unproject(d_gate_low, d_rest, in_local, in_w, tile)
     d_normed = d_parts[order].transpose(1, 0, 2).reshape(rows, width) + mm(d_dt_low, dt_w)
     d_hidden, d_norm_g = front_back(d_normed)
     input_grad = (d_hidden + cot).astype(bf16).reshape(hidden.shape)
@@ -1365,13 +1826,6 @@
         t = lax.psum_scatter(t, "wshard", scatter_dimension=axis, tiled=True)
         return lax.all_gather(t, "seq", axis=0, tiled=True).astype(f32)
 
-    if fast:
-        in_grad = reduce_products(d_proj, normed_low, 2)[:total_cols].astype(f32).T
-    else:
-        in_grad = summed(mm(d_proj, normed_low, TN), 1).T
-    blocks = out_terms.reshape(shards, count, -1, width).transpose(1, 0, 2, 3)
-    blocks = blocks.reshape(inner, width)
-    out_w_grad = summed_rows(blocks, shards, count)
     smalls = [
         d_norm_g.reshape(shards, -1),
         d_conv_w.reshape(taps, shards, -1).transpose(1, 0, 2).reshape(shards, -1),
@@ -1381,8 +1835,24 @@
         d_skip.reshape(shards, -1),
         d_gated.reshape(shards, -1),
     ]
-    sums = lax.psum(jnp.concatenate(smalls, axis=1), ("seq", "wshard"))
-    sums = lax.dynamic_index_in_dim(sums, shard, 0, keepdims=False)
+    smalls = jnp.concatenate(smalls, axis=1)
+    if fast:
+        smalls = jnp.pad(smalls, ((0, 0), (0, -smalls.shape[1] % 1024))).reshape(shards, -1, LANES)
+        by_core, out_sum, sums = weight_sums(d_gate_low, d_rest, normed_low, g, normed_out_low, smalls, 2)
+        by_core = by_core.reshape(2, -1, normed_low.shape[1] // shards)
+        split = inner // 2
+        rest = by_core[:, split:].reshape(-1, by_core.shape[2])[: total_cols - inner]
+        in_grad = jnp.concatenate([by_core[:, :split].reshape(inner, -1), rest]).astype(f32).T
+        out_w_grad = out_sum.T.astype(f32)
+        sums = sums.reshape(-1)
+    else:
+        d_proj = jnp.concatenate([d_gate_low, d_rest, d_dt_low], axis=1)
+        in_grad = summed(mm(d_proj, normed_low, TN), 1).T
+        out_terms = mm(normed_out_low, g, TN)
+        blocks = out_terms.reshape(shards, count, -1, width).transpose(1, 0, 2, 3)
+        out_w_grad = summed(blocks.reshape(inner, width), 0)
+        sums = lax.psum(smalls, ("seq", "wshard"))
+        sums = lax.dynamic_index_in_dim(sums, shard, 0, keepdims=False)
     found, at = [], 0
     for size in sizes:
         found.append(sums[at : at + size])
@@ -1400,12 +1870,6 @@
         found[6],
         out_w_grad,
     )
-
-
-def summed_rows(blocks, shards, count):
-    t = lax.psum_scatter(blocks.astype(bf16), "seq", scatter_dimension=0, tiled=True)
-    t = lax.psum_scatter(t, "wshard", scatter_dimension=0, tiled=True)
-    return lax.all_gather(t, "seq", axis=0, tiled=True).astype(f32)
 
 
 def solution(mesh):

time: 719 us -> 626 us (0.87)
  Pallas kernels: 390 us -> 485 us
  other arithmetic: 105 us -> 41.6 us
  local copies, waits for them, and re-layouts: 95.8 us -> 42.4 us
  waiting for transfers between devices: 56.3 us -> 11.7 us
  matrix products: 36.3 us -> 25.8 us
  blocking collectives: 9.04 us -> 0 us
    pallas_call x5 -> x3, Pallas kernels: 211 us -> 305 us  [the longest x1 184 us: weight_sums(): pl.pallas_call(sums_kernel, in_specs=[hbm] * 5 + [vmem], out_specs=[vmem]...]
    ppermute x4 -> x0, waiting for transfers between devices: 42.2 us -> none  [the longest x3 42.2 us: swap(): return lax.ppermute(x, 'seq', [(i, i ^ by) for i in range(count)])]
    convert_element_type x8 -> x1, other arithmetic: 24.1 us -> 2.7 us  [local(): out_w_grad = out_sum.T.astype(f32)]
    concatenate x2 -> x1, local copies, waits for them, and re-layouts: 11.6 us -> 0.1 us  [local(): smalls = jnp.concatenate(smalls, axis=1)]
    mul x2 -> x0, other arithmetic: 10.7 us -> none  [the longest x1 9.34 us: conv_act(): total = total + padded[:, offset:offset + rows_out] * conv_w[offset]]
    reduce_sum x4 -> x0, other arithmetic: 10.6 us -> none  [the longest x1 10.4 us: conv_act(): total = total + padded[:, offset:offset + rows_out] * conv_w[offset]]
    add_any x2 -> x0, other arithmetic: 10.2 us -> none  [conv_act(): total = conv_b + padded[:, 0:rows_out] * conv_w[0]]
    all_gather x1 -> x0, blocking collectives: 9.04 us -> none  [local(): decays = lax.all_gather(jnp.exp(last), 'seq', axis=0)]
  transfers between devices with their start and end apart: 10 -> 2, of which waited for: 3 -> 1; matrix products, arithmetic and copies ran while one was open for 25% -> 4% of each run, Pallas kernels for 55% -> 29%
where the time goes in v4:
time: 626 us; the launch traced here: 622 us
  Pallas kernels  485 us (77%)
  local copies, waits for them, and re-layouts  42.4 us (7%)
  other arithmetic  41.6 us (7%)
  matrix products  25.8 us (4%)
  between operations  15.3 us (2%)
  waiting for transfers between devices  11.7 us (2%)
    pallas_call x1, Pallas kernels, weight_sums(): pl.pallas_call(sums_kernel, in_specs=[hbm] * 5 + [vmem], out_specs=[vmem]...  184 us
    pallas_call x1, Pallas kernels, gather_input_weight(): pl.pallas_call(partial(gather_kernel, chunks), in_specs=[pl.BlockSpec(mem...  96.1 us
    pallas_call x1, Pallas kernels, scan_backward(): pl.pallas_call(partial(scan_backward_kernel, hs), in_specs=[vmem] * 13, o...  95.1 us
    pallas_call x1, Pallas kernels, scan_forward(): pl.pallas_call(partial(scan_forward_kernel, hs), in_specs=[vmem] * 7, out...  55.3 us
    pallas_call x2, Pallas kernels, project(): pl.pallas_call(project_kernel, grid=(count // tile,), in_specs=[pl.BlockS...  28.3 us
    pallas_call x1, Pallas kernels, unproject(): pl.pallas_call(partial(unproject_kernel, steps), grid=(count // tile,), i...  26.1 us
    dot_general x4, matrix products, mm(): return lax.dot_general(a, b, dims, preferred_element_type=f32)  25.8 us
  transfers between devices with their start and end apart: 2, of which 1 were waited for; matrix products, arithmetic and copies ran while one was open for 4% of the time, Pallas kernels for 29%

profile of v4, /device:TPU:0, one launch (start us, length us, event | category | flops | bytes accessed | tf_op | source)
XLA Modules:
  0.0 621.7 jit_solution(2754754933567544902)
XLA Ops:
  7.2 0.8 slice.102
  8.0 0.8 reshape.243
  8.8 1.2 dynamic-slice
  10.7 4.2 concatenate.9
  14.9 0.6 dynamic-update-slice
  15.6 0.7 copy-done.9
  16.3 0.7 all-gather.3.cloned.1.call-update
  17.0 96.1 %gather_input_weight.1.v_ref = bf16[3,6400,384]{2,1,0:T(8,128)(2,1)} custom-call(bf16[6448,384]{1,0:T(8,128)(2,1)} %bitcast.103), custom_call_target="tpu_custom_call" | custom-call | bytes 200000000 | tf_op jit(solution)/shard_map/gather_input_weight/pallas_call | solution.py:487
  113.1 2.7 reshape.269
  115.8 2.1 convert_element_type.117
  117.9 0.4 fusion.11
  118.2 0.6 fusion.23
  119.0 1.5 fusion.5.og_ref
  120.5 1.1 reshape.289
  121.6 0.8 slice.104
  122.4 0.8 convert_element_type.98
  123.2 0.6 slice.106
  123.8 3.4 fusion.18
  127.2 2.3 gather_fusion
  129.5 13.4 %project.2 = bf16[512,3328]{1,0:T(8,128)(2,1)S(1)} custom-call(bf16[4,512,384]{2,1,0:T(8,128)(2,1)S(1)} %gather_fusion, bf16[6448,384]{1,0:T(8,128)(2,1)} %bitcast.104, bf16[3,6400,384]{2,1,0:T(8,128)(2,1)} %gather_input_weight.1.v_ref), custom_call_target="tpu_custom_call" | custom-call | tf_op jit(solution)/shard_map/project/pallas_call | solution.py:1574
  142.9 14.9 %project.3 = f32[512,3072]{1,0:T(8,128)} custom-call(bf16[4,512,384]{2,1,0:T(8,128)(2,1)S(1)} %gather_fusion, bf16[6448,384]{1,0:T(8,128)(2,1)} %bitcast.105, bf16[3,6400,384]{2,1,0:T(8,128)(2,1)} %gather_input_weight.1.v_ref), custom_call_target="tpu_custom_call" | custom-call | tf_op jit(solution)/shard_map/project/pallas_call | solution.py:1574
  157.9 0.4 fusion.13
  158.4 0.6 convolution_convert_fusion
  158.9 0.1 copy.40
  159.3 0.7 broadcast_in_dim_reshape.15.skip_ref
  160.1 0.7 fusion.21
  160.8 0.1 neg.18
  160.9 0.5 pad.21.shift_ref
  161.4 0.5 pad.22.rate_ref
  161.9 0.1 reshape.249
  162.1 0.7 reshape.250.cw_ref
  162.8 0.7 broadcast_in_dim_reshape.6.cb_ref
  163.5 0.7 pad_convert_fusion.raw_ref
  164.2 55.3 %scan_forward.1 = (bf16[2,256,3072]{2,1,0:T(8,128)(2,1)}, bf16[2,256,256]{2,1,0:T(8,128)(2,1)}, f32[2,256,3072]{2,1,0:T(8,128)}, bf16[2,256,3072]{2,1,0:T(8,128)...) custom-call(bf16[2,256,3328]{2,1,0:T(8,128)(2,1)} %bitcast.100, ...), custom_call_target="tpu_custom_call" | custom-call | flops 4026531840 | bytes 100000000 | tf_op jit(solution)/shard_map/scan_forward/pallas_call | solution.py:1227
  219.6 5.1 multiply_reduce_fusion.2
  224.7 10.9 %all-gather.3.cloned.1.call-done = bf16[3072,1536]{1,0:T(8,128)(2,1)} async-done(((bf16[768,1536]{1,0:T(8,128)(2,1)}), bf16[3072,1536]{1,0:T(8,128)(2,1)}) %all-gather.3.cloned.1.call-update) | async-done | bytes 9437200 | tf_op jit(solution)/shard_map/all_gather | solution.py:1704
  235.6 10.9 %multiply_reduce_fusion = (f32[3072]{0:T(1024)}, f32[512]{0:T(512)S(1)}, f32[512,3072]{1,0:T(8,128)S(1)}) fusion(f32[512]{0:T(512)S(1)} %fusion.22, bf16[2,256,3072]{2,1,0:T(8,128)(2,1)S(1)} %copy-done.3, f32[512,3072]{1,0:T(8,128)} %project.3, f32[3072]{0:T(1024)S(1)} %mul.194, bf16[512,1536]{1,0:T(8,128)(2,1)} %fusion.5.og_ref, ...), kind=kOutput, calls=%fused_computation.10 | convolution fusion | flops 4850708992 | bytes 26767360 | tf_op jit(solution)/shard_map/dot_general | solution.py:24
  246.6 10.6 %multiply_convert_fusion = (bf16[512,3072]{1,0:T(8,128)(2,1)}, bf16[512,3072]{1,0:T(8,128)(2,1)}, bf16[512,3072]{1,0:T(8,128)(2,1)}) fusion(f32[512]{0:T(512)S(1)} %multiply_multiply_fusion.1, f32[512,3072]{1,0:T(8,128)S(1)} %get-tuple-element.89, f32[3072]{0:T(1024)S(1)} %mul.194, f32[512]{0:T(512)S(1)} %fusion.22, bf16[2,256,3072]{2,1,0:T(8,128)(2,1)S(1)} %copy-done.3, ...), kind=kLoop, calls=%fused_computation.11 | loop fusion | flops 37748736 | bytes 25182208 | tf_op jit(solution)/shard_map/convert_element_type | solution.py:1770
  257.2 95.1 %scan_backward.1 = (bf16[2,256,3584]{2,1,0:T(8,128)(2,1)}, f32[4,3328]{1,0:T(4,128)}, f32[1,3328]{1,0:T(1,128)}, f32[8,128]{1,0:T(8,128)}) custom-call(bf16[2,256,3072]{2,1,0:T(8,128)(2,1)} %bitcast.119, bf16[2,256,3072]{2,1,0:T(8,128)(2,1)} %get-tuple-element.25.x_ref, bf16[2,256,256]{2,1,0:T(8,128)(2,1)} %get-tuple-element.26.bc_ref, ...), custom_call_target="tpu_custom_call" | custom-call | flops 8053063680 | bytes 100000000 | tf_op jit(solution)/shard_map/scan_backward/pallas_call | solution.py:1526
  352.3 26.1 %unproject.1 = f32[4,512,384]{2,1,0:T(8,128)S(1)} custom-call(bf16[512,3072]{1,0:T(8,128)(2,1)} %get-tuple-element.78.d_ref.gate_ref, bf16[512,3584]{1,0:T(8,128)(2,1)} %bitcast.115, bf16[6448,384]{1,0:T(8,128)(2,1)} %bitcast.106, bf16[3,6400,384]{2,1,0:T(8,128)(2,1)} %gather_input_weight.1.v_ref), custom_call_target="tpu_custom_call" | custom-call | tf_op jit(solution)/shard_map/unproject/pallas_call | solution.py:1613
  378.4 2.5 gather_fusion.1
  380.9 2.4 copy.47
  383.4 4.4 fusion.10
  387.8 0.1 reshape.258
  387.9 0.1 reshape.259
  388.2 0.8 slice_reduce_fusion
  389.2 0.7 reshape.260
  390.0 0.1 concatenate.10
  390.1 0.7 copy.61
  390.7 0.7 multiply_multiply_fusion
  391.4 5.4 fusion.9
  396.8 184.0 %weight_sums.1 = (bf16[2,26,2,2,2,16,384]{6,5,4,3,2,1,0:T(8,128)(2,1)}, bf16[2,6,2,2,2,16,768]{6,5,4,3,2,1,0:T(8,128)(2,1)}, f32[48,128]{1,0:T(8,128)}) custom-call(bf16[512,3072]{1,0:T(8,128)(2,1)} %get-tuple-element.78.d_ref.gate_ref, bf16[512,3584]{1,0:T(8,128)(2,1)} %bitcast.117, bf16[512,1536]{1,0:T(8,128)(2,1)} %get-tuple-element.80.nm_ref, ...), custom_call_target="tpu_custom_call" | custom-call | flops 42467328000 | bytes 400000000 | tf_op jit(solution)/shard_map/weight_sums/pallas_call | solution.py:887
  580.9 2.1 slice.113
  582.9 3.3 slice.112
  586.2 0.6 slice.115
  586.8 0.7 slice.119
  587.5 0.6 slice_bitcast_fusion
  588.1 0.6 fusion.27
  588.7 0.3 slice.114
  588.9 2.7 bitcast_convert_fusion
  591.6 6.0 copy.44
  597.7 0.7 reshape.265
  598.4 6.3 %convert_bitcast_fusion = f32[384,6448]{0,1:T(8,128)} fusion(bf16[3376,384]{1,0:T(8,128)(2,1)S(1)} %slice.114, bf16[3072,384]{1,0:T(8,128)(2,1)} %bitcast.110), kind=kLoop, calls=%fused_computation.2 | loop fusion | flops 9904128 | bytes 14856192 | tf_op jit(solution)/shard_map/transpose | solution.py:1845
  604.7 9.9 %fusion.17 = bf16[512,1536]{1,0:T(8,128)(2,1)} fusion(f32[512,1536]{1,0:T(8,128)S(1)} %bitcast.118, bf16[512,3072]{1,0:T(8,128)(2,1)S(1)} %copy-done.7, bf16[3072,1536]{1,0:T(8,128)(2,1)} %all-gather.3.cloned.1.call-done, f32[512]{0:T(512)S(1)} %bitcast.135), kind=kOutput, calls=%fused_computation.41 | convolution fusion | flops 4834197504 | bytes 17303552 | tf_op jit(solution)/shard_map/dot_general | solution.py:24
  (74 shorter events, 1.2 us)
Async XLA Ops:
  7.2 113.3 %all-reduce.7.cloned.1.call-start = ((), (), s32[]{:S(2)}) async-start(), calls=%async_computation.1 | async-start | bytes 380928
  15.5 0.7 copy-start.9
  16.2 219.4 %all-gather.3.cloned.1.call-start = ((), (), s32[]{:S(2)}) async-start(), calls=%async_computation | async-start | bytes 11796480 | tf_op jit(solution)/shard_map/all_gather | solution.py:1704
  17.0 96.1 %copy-start.1 = (bf16[2,1,256,1536]{3,2,1,0:T(8,128)(2,1)S(1)}, bf16[2,1,256,1536]{3,2,1,0:T(8,128)(2,1)}, u32[]{:S(2)}) copy-start(bf16[2,1,256,1536]{3,2,1,0:T(8,128)(2,1)} %param.12) | copy-start | bytes 4718596
  115.8 3.1 copy-start.19
  115.8 3.2 copy-start.4
  118.9 1.5 copy-start.16
  119.0 8.3 %copy-start.18 = (s32[1024]{0:T(1024)}, s32[1024]{0:T(1024)S(1)}, u32[]{:S(2)}) copy-start(s32[1024]{0:T(1024)S(1)} %pad_clamp_fusion) | copy-start | bytes 12292
  142.9 14.9 %copy-start = (bf16[512,3328]{1,0:T(8,128)(2,1)}, bf16[512,3328]{1,0:T(8,128)(2,1)S(1)}, u32[]{:S(2)}) copy-start(bf16[512,3328]{1,0:T(8,128)(2,1)S(1)} %project.2) | copy-start | bytes 10223620
  142.9 15.0 %copy-start.10 = (bf16[4,18432]{1,0:T(4,128)(2,1)S(1)}, bf16[4,18432]{1,0:T(4,128)(2,1)}, u32[]{:S(2)}) copy-start(bf16[4,18432]{1,0:T(4,128)(2,1)} %slice.104) | copy-start | bytes 442372
  142.9 15.0 %copy-start.15 = (f32[2,256]{1,0:T(2,128)S(1)}, f32[2,256]{1,0:T(2,128)}, u32[]{:S(2)}) copy-start(f32[2,256]{1,0:T(2,128)} %get-tuple-element.87) | copy-start | bytes 6148
  157.8 5.0 copy-start.11
  219.6 16.1 %copy-start.3 = (bf16[2,256,3072]{2,1,0:T(8,128)(2,1)S(1)}, bf16[2,256,3072]{2,1,0:T(8,128)(2,1)}, u32[]{:S(2)}) copy-start(bf16[2,256,3072]{2,1,0:T(8,128)(2,1)} %get-tuple-element.24) | copy-start | bytes 9437188
  380.9 2.4 copy-start.2
  383.4 4.4 copy-start.12
  383.4 4.6 copy-start.14
  383.4 8.0 %copy-start.5 = (bf16[2,1,256,1536]{3,2,1,0:T(8,128)(2,1)S(1)}, bf16[2,1,256,1536]{3,2,1,0:T(8,128)(2,1)}, u32[]{:S(2)}) copy-start(bf16[2,1,256,1536]{3,2,1,0:T(8,128)(2,1)} %param.14) | copy-start | bytes 4718596
  582.9 3.3 copy-start.13
  586.2 2.7 copy-start.8
  598.4 6.4 %copy-start.6 = (f32[2,1,256,1536]{3,2,1,0:T(8,128)S(1)}, f32[2,1,256,1536]{3,2,1,0:T(8,128)}, u32[]{:S(2)}) copy-start(f32[2,1,256,1536]{3,2,1,0:T(8,128)} %convert_element_type.117) | copy-start | bytes 9437188
  598.4 6.4 %copy-start.7 = (bf16[512,3072]{1,0:T(8,128)(2,1)S(1)}, bf16[512,3072]{1,0:T(8,128)(2,1)}, u32[]{:S(2)}) copy-start(bf16[512,3072]{1,0:T(8,128)(2,1)} %get-tuple-element.79.no_ref) | copy-start | bytes 9437188
  598.4 6.4 %copy-start.17 = (f32[1,2,2,128]{3,1,2,0:T(2,128)S(1)}, f32[1,2,2,128]{3,1,2,0:T(2,128)}, u32[]{:S(2)}) copy-start(f32[1,2,2,128]{3,1,2,0:T(2,128)} %copy-done.16) | copy-start | bytes 6148
Sparse Core Ops, SparseCore 0:
  16.4 42.6 all-reduce.6
  60.7 174.9 all-gather.2

commit v5 on v4

--- a/solution.py
+++ b/solution.py
@@ -390,108 +390,123 @@
 AHEAD = 2
 
 
-def gather_kernel(chunks, w_ref, o_ref, send, recv):
-    s, z, c, x, y, near = around()
-    greet(near)
-    sx, sy, sd = s + 2 - 4 * x, s + 4 - 8 * y, s + 6 - 4 * x - 8 * y
-    plans = []
-    for q, (base, piece, off, size, first) in enumerate(chunks):
-
-        def rows(who, base=base, piece=piece, off=off, size=size):
-            return pl.ds(pl.multiple_of(base + who * piece + off, 16), size)
-
-        def move(src, dst, kind, to, q=q):
-            return pltpu.make_async_remote_copy(
-                src_ref=src,
-                dst_ref=dst,
-                send_sem=send.at[q, kind],
-                recv_sem=recv.at[q, kind],
-                device_id=near[to],
-                device_id_type=MESH,
-            )
-
-        def block(who, rows=rows):
-            return o_ref.at[:, rows(who)]
-
-        def along(who, kind, to, move=move, block=block):
-            return move(block(who), block(who), kind, to)
-
-        plan = {}
+def split_rows(piece, parts):
+    tiles = piece // 16
+    return [16 * (tiles * (i + 1) // parts - tiles * i // parts) for i in range(parts)]
+
+
+class Gather:
+    def __init__(self, place, items, send, recv):
+        s, z, c, x, y, near = place
+        sx, sy, sd = s + 2 - 4 * x, s + 4 - 8 * y, s + 6 - 4 * x - 8 * y
+        self.plans = []
+        for source, base, target, count, parts in items:
+            off = 0
+            for i, size in enumerate(split_rows(count // 8, parts)):
+                q = len(self.plans)
+
+                def rows(who, first=0, off=off, size=size, piece=count // 8):
+                    return pl.ds(pl.multiple_of(first + who * piece + off, 16), size)
+
+                def move(src, dst, kind, to, q=q):
+                    return pltpu.make_async_remote_copy(
+                        src_ref=src,
+                        dst_ref=dst,
+                        send_sem=send.at[q, kind],
+                        recv_sem=recv.at[q, kind],
+                        device_id=near[to],
+                        device_id_type=MESH,
+                    )
+
+                def along(who, kind, to, move=move, rows=rows, target=target):
+                    block = target.at[:, rows(who)]
+                    return move(block, block, kind, to)
+
+                plan = {}
+                for k in (1, 2, 3):
+                    there = target.at[k - 1, rows(s)]
+                    plan["z%d" % k] = move(source.at[rows(s, base)], there, k - 1, "z%d" % k)
+                plan["x"] = along(s, 3, "x")
+                plan["y"] = along(s, 4, "y")
+                first = "xy"[i % 2]
+                plan["d"] = along(sx, 5, "y") if first == "x" else along(sy, 5, "x")
+                plan["c0"] = along(s, 6, "c")
+                plan["cx"] = along(sx, 7, "c")
+                plan["cy"] = along(sy, 8, "c")
+                plan["cd"] = along(sd, 9, "c")
+                plan["order"] = first, "yx"[i % 2]
+                self.plans.append(plan)
+                off += size
+
+    def fetch(self, i):
         for k in (1, 2, 3):
-            plan["z%d" % k] = move(w_ref.at[rows(s)], o_ref.at[k - 1, rows(s)], k - 1, "z%d" % k)
-        plan["x"] = along(s, 3, "x")
-        plan["y"] = along(s, 4, "y")
-        plan["d"] = along(sx, 5, "y") if first == "x" else along(sy, 5, "x")
-        plan["c0"] = along(s, 6, "c")
-        plan["cx"] = along(sx, 7, "c")
-        plan["cy"] = along(sy, 8, "c")
-        plan["cd"] = along(sd, 9, "c")
-        plan["first"] = first
-        plans.append(plan)
-
-    def fetch(plan):
-        for k in (1, 2, 3):
-            plan["z%d" % k].start()
-
-    def begin(plan):
+            self.plans[i]["z%d" % k].start()
+
+    def begin(self, i):
+        plan = self.plans[i]
         for k in (1, 2, 3):
             plan["z%d" % k].wait_recv()
         for name in ("x", "y", "c0"):
             plan[name].start()
 
-    def middle(plan):
-        one, two = ("x", "y") if plan["first"] == "x" else ("y", "x")
+    def middle(self, i):
+        plan = self.plans[i]
+        one, two = plan["order"]
         plan[one].wait_recv()
         plan["d"].start()
         plan["c" + one].start()
         plan[two].wait_recv()
         plan["c" + two].start()
 
-    def finish(plan):
-        plan["d"].wait_recv()
-        plan["cd"].start()
-
-    n = len(plans)
-    for i in range(min(AHEAD, n)):
-        fetch(plans[i])
-    for i in range(n + 2):
-        if i < n:
-            begin(plans[i])
-            if i + AHEAD < n:
-                fetch(plans[i + AHEAD])
-        if 0 <= i - 1 < n:
-            middle(plans[i - 1])
-        if 0 <= i - 2 < n:
-            finish(plans[i - 2])
-    for plan in plans:
-        for name in ("c0", "cx", "cy", "cd"):
-            plan[name].wait_recv()
-        for name in ("z1", "z2", "z3", "x", "y", "d", "c0", "cx", "cy", "cd"):
-            plan[name].wait_send()
-
-
-def split_rows(piece, parts=6):
-    tiles = piece // 16
-    return [16 * (tiles * (i + 1) // parts - tiles * i // parts) for i in range(parts)]
-
-
-def gather_input_weight(w_t, inner, channels):
-    total = inner + channels
-    chunks = []
-    for base, piece in ((inner, channels // 8), (0, inner // 8)):
-        off = 0
-        for i, size in enumerate(split_rows(piece)):
-            chunks.append((base, piece, off, size, "xy"[i % 2]))
-            off += size
+    def finish(self, i):
+        self.plans[i]["d"].wait_recv()
+        self.plans[i]["cd"].start()
+
+    def run(self):
+        n = len(self.plans)
+        for i in range(min(AHEAD, n)):
+            self.fetch(i)
+        for i in range(n + 2):
+            if i < n:
+                self.begin(i)
+                if i + AHEAD < n:
+                    self.fetch(i + AHEAD)
+            if 0 <= i - 1 < n:
+                self.middle(i - 1)
+            if 0 <= i - 2 < n:
+                self.finish(i - 2)
+
+    def close(self):
+        for plan in self.plans:
+            for name in ("c0", "cx", "cy", "cd"):
+                plan[name].wait_recv()
+            for name in ("z1", "z2", "z3", "x", "y", "d", "c0", "cx", "cy", "cd"):
+                plan[name].wait_send()
+
+
+def gather_kernel(inner, channels, parts, w_ref, conv_ref, gate_ref, send, recv):
+    place = around()
+    greet(place[-1])
+    items = [(w_ref, inner, conv_ref, channels, parts), (w_ref, 0, gate_ref, inner, parts)]
+    work = Gather(place, items, send, recv)
+    work.run()
+    work.close()
+
+
+def gather_input_weight(w_t, inner, channels, parts=6):
     width = w_t.shape[1]
+    hbm = pl.BlockSpec(memory_space=pl.ANY)
     return pl.pallas_call(
-        partial(gather_kernel, chunks),
-        in_specs=[pl.BlockSpec(memory_space=pl.ANY)],
-        out_specs=pl.BlockSpec(memory_space=pl.ANY),
-        out_shape=jax.ShapeDtypeStruct((3, total, width), bf16),
+        partial(gather_kernel, inner, channels, parts),
+        in_specs=[hbm],
+        out_specs=[hbm] * 2,
+        out_shape=[
+            jax.ShapeDtypeStruct((3, channels, width), bf16),
+            jax.ShapeDtypeStruct((3, inner, width), bf16),
+        ],
         scratch_shapes=[
-            pltpu.SemaphoreType.DMA((len(chunks), CHUNK_DMAS)),
-            pltpu.SemaphoreType.DMA((len(chunks), CHUNK_DMAS)),
+            pltpu.SemaphoreType.DMA((2 * parts, CHUNK_DMAS)),
+            pltpu.SemaphoreType.DMA((2 * parts, CHUNK_DMAS)),
         ],
         compiler_params=pltpu.CompilerParams(collective_id=1, has_side_effects=True),
         cost_estimate=pl.CostEstimate(flops=0, bytes_accessed=200_000_000, transcendentals=0),
@@ -1085,15 +1100,17 @@
     shift_ref,
     rate_ref,
     skip_ref,
+    ow_ref,
     x_ref,
     bc_ref,
     y_ref,
     low_ref,
     halo,
     begin_ref,
+    others_ref,
     *scratch,
 ):
-    buf, wide_buf, scores, dts, cums, rows_t, h_send, h_recv = scratch[EXCHANGE:]
+    buf, wide_buf, scores, dts, cums, rows_t, h_send, h_recv, o_send, o_recv = scratch[EXCHANGE:]
     ex = Exchange(True, *scratch[:EXCHANGE])
     s, z = ex.s, ex.z
     micro, t, channels = conv_ref.shape
@@ -1102,11 +1119,12 @@
     gc = GROUP * hs
     groups = inner // gc
     half_t = t // 2
-    near = dict(ex.near)
-    near = {k: near[k] for k in ("c", "x", "y")}
+    place = around()
+    near = dict(place[-1])
     near["next"] = ((s + 1) % 8, z)
     near["last"] = ((s + 7) % 8, z)
     greet(near)
+    weight = Gather(place, [(ow_ref, 0, others_ref, ow_ref.shape[0], 2)], o_send, o_recv)
 
     tail = [
         pltpu.make_async_remote_copy(
@@ -1121,6 +1139,8 @@
     ]
     for copy in tail:
         copy.start()
+    weight.fetch(0)
+    weight.fetch(1)
     for m in range(micro):
         dt, cum = steps_of(raw_ref[m], shift_ref[...], rate_ref[...])
         dts[m] = dt
@@ -1200,34 +1220,44 @@
     ex.along_x(0)
     own_states(1, middle, groups)
     ex.core(1)
+    weight.begin(0)
     local_scans(0, 0, middle)
     ex.along_x(1)
     ex.along_y(0)
+    weight.begin(1)
     local_scans(0, middle, groups)
+    weight.middle(0)
     local_scans(1, 0, middle)
     ex.along_y(1)
     ex.back_to_core(0)
+    weight.middle(1)
     local_scans(1, middle, groups)
     ex.begin_state(0, begin_ref)
     carried(0)
     ex.back_to_core(1)
+    weight.finish(0)
+    weight.finish(1)
     ex.begin_state(1, begin_ref)
     carried(1)
+    weight.close()
     ex.sent()
     for copy in tail:
         copy.wait_send()
 
 
-def scan_forward(conv_low, raw, conv_w, conv_b, shift, rate, skip_wide, inner, hs, collective_id):
+def scan_forward(
+    conv_low, raw, conv_w, conv_b, shift, rate, skip_wide, out_weight, inner, hs, collective_id
+):
     micro, t, channels = conv_low.shape
     n = (channels - inner) // 2
     gc = GROUP * hs
     dma = pltpu.SemaphoreType.DMA
     vmem = pl.BlockSpec(memory_space=pltpu.VMEM)
+    hbm = pl.BlockSpec(memory_space=pl.ANY)
     return pl.pallas_call(
         partial(scan_forward_kernel, hs),
-        in_specs=[vmem] * 7,
-        out_specs=[vmem] * 6,
+        in_specs=[vmem] * 7 + [hbm],
+        out_specs=[vmem] * 6 + [hbm],
         out_shape=[
             jax.ShapeDtypeStruct((micro, t, inner), bf16),
             jax.ShapeDtypeStruct((micro, t, 2 * n), bf16),
@@ -1235,6 +1265,7 @@
             jax.ShapeDtypeStruct((micro, t, inner), bf16),
             jax.ShapeDtypeStruct((micro, HALO, channels), bf16),
             jax.ShapeDtypeStruct((micro, n, inner), bf16),
+            jax.ShapeDtypeStruct((3,) + out_weight.shape, bf16),
         ],
         scratch_shapes=exchange_scratch(micro, n, inner)
         + [
@@ -1246,6 +1277,8 @@
             pltpu.VMEM((micro, LANES, t), f32),
             dma((micro,)),
             dma((micro,)),
+            dma((2, CHUNK_DMAS)),
+            dma((2, CHUNK_DMAS)),
         ],
         compiler_params=pltpu.CompilerParams(
             collective_id=collective_id, has_side_effects=True, vmem_limit_bytes=VMEM_MOST
@@ -1254,7 +1287,7 @@
             flops=4 * micro * t * inner * (t + 3 * n), bytes_accessed=100_000_000, transcendentals=0
         ),
         name="scan_forward",
-    )(conv_low, raw, conv_w, conv_b, shift, rate, skip_wide)
+    )(conv_low, raw, conv_w, conv_b, shift, rate, skip_wide, out_weight)
 
 
 def scan_backward_kernel(
@@ -1562,6 +1595,270 @@
     )(dy, x, bc, y, begin, raw, conv_low, halo, conv_w, conv_b, shift, rate, skip_wide)
 
 
+def shard_place(k, depth):
+    z = lax.axis_index("wshard")
+    other = (z, z + 1 - 2 * (z % 2), z + 2 - 4 * (z // 2), 3 - z)[k]
+    return pl.ds(pl.multiple_of(other * depth, 128), depth)
+
+
+def front_kernel(h_ref, g_ref, dtw_ref, w_ref, v_ref, conv_ref, norm_ref, raw_ref, rel):
+    depth = w_ref.shape[1]
+
+    @pl.when(pl.program_id(0) == 0)
+    def _():
+        h = h_ref[...].astype(f32)
+        power = jnp.mean(h * h, axis=-1, keepdims=True)
+        normed = (h * lax.rsqrt(power + epsilon) * g_ref[...]).astype(bf16)
+        norm_ref[...] = normed
+        raw_ref[...] = mm(normed, dtw_ref[...], NT).astype(bf16).astype(f32)
+        for k in range(4):
+            rel[:, k * depth : (k + 1) * depth] = norm_ref[:, shard_place(k, depth)]
+
+    weights = jnp.concatenate([w_ref[...]] + [v_ref[k] for k in range(3)], axis=1)
+    conv_ref[...] = mm(rel[...], weights, NT).astype(bf16)
+
+
+def front(hidden, gain, dt_w, own, others, tile):
+    rows, width = hidden.shape
+    count, depth = own.shape
+    whole = pl.BlockSpec((rows, width), lambda i: (0, 0))
+    return pl.pallas_call(
+        front_kernel,
+        grid=(count // tile,),
+        in_specs=[
+            whole,
+            pl.BlockSpec((1, width), lambda i: (0, 0)),
+            pl.BlockSpec((LANES, width), lambda i: (0, 0)),
+            pl.BlockSpec((tile, depth), lambda i: (i, 0)),
+            pl.BlockSpec((3, tile, depth), lambda i: (0, i, 0)),
+        ],
+        out_specs=[
+            pl.BlockSpec((rows, tile), lambda i: (0, i)),
+            whole,
+            pl.BlockSpec((rows, LANES), lambda i: (0, 0)),
+        ],
+        out_shape=[
+            jax.ShapeDtypeStruct((rows, count), bf16),
+            jax.ShapeDtypeStruct((rows, width), bf16),
+            jax.ShapeDtypeStruct((rows, LANES), f32),
+        ],
+        scratch_shapes=[pltpu.VMEM((rows, width), bf16)],
+        compiler_params=pltpu.CompilerParams(vmem_limit_bytes=VMEM),
+        name="front",
+    )(hidden, gain, dt_w, own, others)
+
+
+def gate_kernel(
+    scan_ref,
+    norm_ref,
+    w_ref,
+    v_ref,
+    gain_ref,
+    ow_ref,
+    ov_ref,
+    h_ref,
+    og_ref,
+    valid_ref,
+    no_ref,
+    out_ref,
+    g_ref,
+    dy_ref,
+    dgate_ref,
+    dgain_ref,
+    gate,
+    d_no,
+    branch,
+):
+    inner = scan_ref.shape[1]
+    depth = w_ref.shape[1]
+    block = ow_ref.shape[0]
+    rows = scan_ref.shape[0]
+
+    @pl.when(pl.program_id(0) == 0)
+    def _():
+        dgain_ref[...] = jnp.zeros_like(dgain_ref)
+
+    rel = jnp.concatenate([norm_ref[:, shard_place(k, depth)] for k in range(4)], axis=1)
+    valid = valid_ref[...]
+    g_low = (og_ref[...].astype(f32) * valid).astype(bf16)
+    g_ref[...] = g_low
+    power = jnp.zeros((rows, 1), f32)
+    for i in range(4):
+        at = slice(i * block, (i + 1) * block)
+        weights = jnp.concatenate([w_ref[at, :]] + [v_ref[k, at, :] for k in range(3)], axis=1)
+        value = mm(rel, weights, NT)
+        gate[:, at] = value
+        act, _ = silu_parts(value)
+        u = scan_ref[:, at].astype(f32) * act
+        power += jnp.sum(u * u, axis=-1, keepdims=True)
+    scale = lax.rsqrt(power / inner + epsilon)
+    along = jnp.zeros((rows, 1), f32)
+    for k in range(4):
+        at = shard_place(k, block)
+        weights = ow_ref[...] if k == 0 else ov_ref[k - 1]
+        act, _ = silu_parts(gate[:, at])
+        u = scan_ref[:, at].astype(f32) * act
+        normed = u * scale
+        low = (normed * gain_ref[:, at]).astype(bf16)
+        no_ref[:, at] = low
+        if k == 0:
+            branch[...] = mm(low, weights)
+        else:
+            branch[...] += mm(low, weights)
+        d = mm(g_low, weights, NT)
+        dgain_ref[:, at] += jnp.sum(d * normed, axis=0, keepdims=True)
+        d = d * gain_ref[:, at]
+        d_no[:, at] = d
+        along += jnp.sum(d * u, axis=-1, keepdims=True)
+    out_ref[...] = (h_ref[...].astype(f32) + valid * branch[...]).astype(bf16)
+    along = along * scale * scale * scale / inner
+    for i in range(4):
+        at = slice(i * block, (i + 1) * block)
+        value = gate[:, at]
+        act, sig = silu_parts(value)
+        v = scan_ref[:, at].astype(f32)
+        d_u = scale * d_no[:, at] - v * act * along
+        dy_ref[:, at] = (d_u * act).astype(bf16)
+        dgate_ref[:, at] = (d_u * v * (sig * (1.0 + value * (1.0 - sig)))).astype(bf16)
+
+
+def gate_stage(scanned, normed, own, others, gain, out_own, out_others, hidden, out_grad, valid, tile):
+    rows, width = hidden.shape
+    _, inner, depth = others.shape
+    once = pl.Buffered(1)
+    wide = pl.BlockSpec((tile, inner), lambda i: (i, 0))
+    slim = pl.BlockSpec((tile, width), lambda i: (i, 0))
+    line = pl.BlockSpec((1, inner), lambda i: (0, 0))
+    return pl.pallas_call(
+        gate_kernel,
+        grid=(rows // tile,),
+        in_specs=[
+            wide,
+            slim,
+            pl.BlockSpec((inner, depth), lambda i: (0, 0), pipeline_mode=once),
+            pl.BlockSpec(others.shape, lambda i: (0, 0, 0), pipeline_mode=once),
+            line,
+            pl.BlockSpec(out_own.shape, lambda i: (0, 0), pipeline_mode=once),
+            pl.BlockSpec(out_others.shape, lambda i: (0, 0, 0), pipeline_mode=once),
+            slim,
+            slim,
+            pl.BlockSpec((tile, 1), lambda i: (i, 0)),
+        ],
+        out_specs=[wide, slim, slim, wide, wide, line],
+        out_shape=[
+            jax.ShapeDtypeStruct((rows, inner), bf16),
+            jax.ShapeDtypeStruct((rows, width), bf16),
+            jax.ShapeDtypeStruct((rows, width), bf16),
+            jax.ShapeDtypeStruct((rows, inner), bf16),
+            jax.ShapeDtypeStruct((rows, inner), bf16),
+            jax.ShapeDtypeStruct((1, inner), f32),
+        ],
+        scratch_shapes=[
+            pltpu.VMEM((tile, inner), f32),
+            pltpu.VMEM((tile, inner), f32),
+            pltpu.VMEM((tile, width), f32),
+        ],
+        compiler_params=pltpu.CompilerParams(vmem_limit_bytes=VMEM_MOST),
+        name="gate_stage",
+    )(scanned, normed, own, others, gain, out_own, out_others, hidden, out_grad, valid)
+
+
+def back_kernel(
+    steps,
+    d_ref,
+    e_ref,
+    dt_ref,
+    dtw_ref,
+    w_ref,
+    v_ref,
+    cw_ref,
+    cv_ref,
+    h_ref,
+    g_ref,
+    og_ref,
+    out_ref,
+    dg_ref,
+    acc,
+    full,
+):
+    depth = w_ref.shape[1]
+    i = pl.program_id(0)
+
+    def product(ref, one, three):
+        return mm(ref[...], jnp.concatenate([one[...]] + [three[k] for k in range(3)], axis=1))
+
+    @pl.when(i == 0)
+    def _():
+        acc[...] = product(d_ref, w_ref, v_ref)
+
+    @pl.when((i > 0) & (i < steps))
+    def _():
+        acc[...] += product(d_ref, w_ref, v_ref)
+
+    @pl.when(i >= steps)
+    def _():
+        acc[...] += product(e_ref, cw_ref, cv_ref)
+
+    @pl.when(i == pl.num_programs(0) - 1)
+    def _():
+        for k in range(4):
+            full[:, shard_place(k, depth)] = acc[:, k * depth : (k + 1) * depth]
+        tile = 128
+        gain = g_ref[...]
+        d_gain = jnp.zeros(gain.shape, f32)
+        for r in range(full.shape[0] // tile):
+            at = slice(r * tile, (r + 1) * tile)
+            d = full[at, :] + mm(dt_ref[at, :], dtw_ref[...])
+            h = h_ref[at, :].astype(f32)
+            scale = lax.rsqrt(jnp.mean(h * h, axis=-1, keepdims=True) + epsilon)
+            d_gain += jnp.sum(d * (h * scale), axis=0, keepdims=True)
+            d = d * gain
+            along = jnp.mean(d * h, axis=-1, keepdims=True) * (scale * scale * scale)
+            out_ref[at, :] = (scale * d - h * along + og_ref[at, :].astype(f32)).astype(bf16)
+        dg_ref[...] = d_gain
+
+
+def back_stage(d, e, dt_w, gate_own, gate_others, own, others, hidden, gain, out_grad, tiles):
+    rows, width = hidden.shape
+    count, depth = own.shape
+    inner = d.shape[1]
+    steps, more = inner // tiles[0], count // tiles[1]
+    whole = pl.BlockSpec((rows, width), lambda i: (0, 0))
+    line = pl.BlockSpec((1, width), lambda i: (0, 0))
+
+    def early(i):
+        return jnp.minimum(i, steps - 1)
+
+    def late(i):
+        return jnp.maximum(i - steps, 0)
+
+    return pl.pallas_call(
+        partial(back_kernel, steps),
+        grid=(steps + more,),
+        in_specs=[
+            pl.BlockSpec((rows, tiles[0]), lambda i: (0, early(i))),
+            pl.BlockSpec((rows, tiles[1]), lambda i: (0, late(i))),
+            pl.BlockSpec((rows, LANES), lambda i: (0, count // LANES)),
+            pl.BlockSpec((LANES, width), lambda i: (0, 0)),
+            pl.BlockSpec((tiles[0], depth), lambda i: (early(i), 0)),
+            pl.BlockSpec((3, tiles[0], depth), lambda i: (0, early(i), 0)),
+            pl.BlockSpec((tiles[1], depth), lambda i: (late(i), 0)),
+            pl.BlockSpec((3, tiles[1], depth), lambda i: (0, late(i), 0)),
+            whole,
+            line,
+            whole,
+        ],
+        out_specs=[whole, line],
+        out_shape=[
+            jax.ShapeDtypeStruct((rows, width), bf16),
+            jax.ShapeDtypeStruct((1, width), f32),
+        ],
+        scratch_shapes=[pltpu.VMEM((rows, width), f32), pltpu.VMEM((rows, width), f32)],
+        compiler_params=pltpu.CompilerParams(vmem_limit_bytes=VMEM_MOST),
+        name="back_stage",
+    )(d, e, e, dt_w, gate_own, gate_others, own, others, hidden, gain, out_grad)
+
+
 def project_kernel(n_ref, w_ref, v_ref, o_ref):
     total = mm(n_ref[0], w_ref[...], NT)
     for k in range(1, n_ref.shape[0]):
@@ -1695,13 +1992,12 @@
     dt_w = packed_low[:, at:].reshape(shards, heads, -1).transpose(1, 0, 2).reshape(heads, -1)
     order = jnp.arange(shards) ^ shard
     if fast:
-        in_w = gather_input_weight(in_local, inner, channels)
-        out_part = lax.optimization_barrier((out_weight, in_w[0, 0, 0]))[0]
+        conv_own = in_local[inner : inner + channels]
+        conv_others, gate_others = gather_input_weight(in_local, inner, channels)
     else:
         every = lax.all_gather(in_local[: inner + channels], "wshard", axis=0)
         in_w = every[order[1:]]
-        out_part = out_weight
-    out_w = lax.all_gather(out_part, "wshard", axis=0, tiled=True)
+        out_w = lax.all_gather(out_weight, "wshard", axis=0, tiled=True)
 
     def grouped(v):
         return v.reshape(micro, tokens, groups, GROUP).transpose(0, 2, 1, 3)
@@ -1710,23 +2006,31 @@
     cot = out_grad.reshape(rows, width).astype(f32)
     positions = rank * tokens + jnp.arange(tokens, dtype=jnp.int32)
     valid = (positions[None, :] < lengths[:, 0][:, None]).astype(f32).reshape(rows, 1)
-    normed, front_back = jax.vjp(rms_front, rows_in, norm_g)
-    normed_low = normed.astype(bf16)
-    normed_parts = normed_low.reshape(rows, shards, -1).transpose(1, 0, 2)[order]
     tile = 256
-    conv_low = project(normed_parts, in_local, in_w, inner, channels, tile, bf16)
-    gate_in = project(normed_parts, in_local, in_w, 0, inner, tile, f32)
-    dt_low = mm(normed_low, dt_w, NT).astype(bf16)
-    conv_low = conv_low.reshape(micro, tokens, channels)
-    dt_raw = dt_low.astype(f32).reshape(micro, tokens, heads) + dt_shift
     skip_wide = jnp.repeat(skip, hs)[None, :]
 
     def to_lanes(v):
         return jnp.pad(v, ((0, 0),) * (v.ndim - 1) + ((0, LANES - heads),))
 
     if fast:
-        raw = to_lanes(dt_low.astype(f32).reshape(micro, tokens, heads))
-        x_low, bc_low, y_scan, scanned_low, halo, s_in = scan_forward(
+        hidden_rows, out_grad_rows = hidden.reshape(rows, width), out_grad.reshape(rows, width)
+        dt_wide = jnp.pad(dt_w, ((0, LANES - heads), (0, 0)))
+        conv_low, normed_low, raw = front(
+            hidden_rows, norm_g[None, :], dt_wide, conv_own, conv_others, channels // 2
+        )
+        raw = raw.reshape(micro, tokens, LANES)
+    else:
+        normed, front_back = jax.vjp(rms_front, rows_in, norm_g)
+        normed_low = normed.astype(bf16)
+        normed_parts = normed_low.reshape(rows, shards, -1).transpose(1, 0, 2)[order]
+        conv_low = project(normed_parts, in_local, in_w, inner, channels, tile, bf16)
+        gate_in = project(normed_parts, in_local, in_w, 0, inner, tile, f32)
+        dt_low = mm(normed_low, dt_w, NT).astype(bf16)
+        dt_raw = dt_low.astype(f32).reshape(micro, tokens, heads) + dt_shift
+    conv_low = conv_low.reshape(micro, tokens, channels)
+
+    if fast:
+        x_low, bc_low, y_scan, scanned_low, halo, s_in, out_others = scan_forward(
             conv_low,
             raw,
             conv_w,
@@ -1734,6 +2038,7 @@
             to_lanes(dt_shift[None, :]),
             to_lanes(rate[None, :]),
             skip_wide,
+            out_weight,
             inner,
             hs,
             3,
@@ -1759,15 +2064,34 @@
         s_in = running_states(own_state, decays, hs, True)
         y_scan, scanned_low = add_carry(x_low, y_local, cum_g, c_low, s_in, skip_wide, hs)
 
-    scanned = scanned_low.reshape(rows, inner).astype(f32)
-    normed_out, gate_back = jax.vjp(gate_norm, scanned, gate_in, gated_g)
-    normed_out_low = normed_out.astype(bf16)
-    branch = mm(normed_out_low, out_w)
-    output = (rows_in + valid * branch).astype(bf16).reshape(hidden.shape)
-
-    g = (cot * valid).astype(bf16)
-    d_scanned, d_gate_in, d_gated = gate_back(mm(g, out_w, NT))
-    dy = d_scanned.astype(bf16).reshape(micro, tokens, inner)
+    if fast:
+        normed_out_low, output, g, dy, d_gate_low, d_gated = gate_stage(
+            scanned_low.reshape(rows, inner),
+            normed_low,
+            in_local,
+            gate_others,
+            gated_g[None, :],
+            out_weight,
+            out_others,
+            hidden_rows,
+            out_grad_rows,
+            valid,
+            256,
+        )
+        output = output.reshape(hidden.shape)
+        dy = dy.reshape(micro, tokens, inner)
+        d_gated = d_gated[0]
+    else:
+        scanned = scanned_low.reshape(rows, inner).astype(f32)
+        normed_out, gate_back = jax.vjp(gate_norm, scanned, gate_in, gated_g)
+        normed_out_low = normed_out.astype(bf16)
+        branch = mm(normed_out_low, out_w)
+        output = (rows_in + valid * branch).astype(bf16).reshape(hidden.shape)
+        g = (cot * valid).astype(bf16)
+        d_scanned, d_gate_in, d_gated = gate_back(mm(g, out_w, NT))
+        dy = d_scanned.astype(bf16).reshape(micro, tokens, inner)
+        d_gate_low = d_gate_in.astype(bf16)
+
     if fast:
         d_rest, d_conv_w, d_conv_b, by_head = scan_backward(
             dy,
@@ -1789,7 +2113,21 @@
         d_dt_bias, d_a_log, d_skip = by_head[0, :heads], by_head[1, :heads], by_head[2, :heads]
         d_conv_b = d_conv_b[0]
         d_rest = d_rest.reshape(rows, -1)
-        d_dt_low = d_rest[:, channels : channels + heads]
+        input_grad, d_norm_g = back_stage(
+            d_gate_low,
+            d_rest,
+            dt_wide,
+            in_local,
+            gate_others,
+            conv_own,
+            conv_others,
+            hidden_rows,
+            norm_g[None, :],
+            out_grad_rows,
+            (inner // 2, channels // 2),
+        )
+        input_grad = input_grad.reshape(hidden.shape)
+        d_norm_g = d_norm_g[0]
     else:
         own_grad = block_states(dy, decay_w, c_low.transpose(0, 2, 1), hs)
         dx_local, db_local, dc_local = local_back(x_low, dy, dt_g, cum_g, row_g, b_low, c_low, hs)
@@ -1813,13 +2151,12 @@
         d_conv = d_padded[:, taps - 1 :].at[:, tokens - (taps - 1) :].add(from_next)
         d_dt_low = d_dt.astype(bf16).reshape(rows, heads)
     total_cols = inner + channels + heads
-    d_gate_low = d_gate_in.astype(bf16)
     if not fast:
         d_rest = d_conv.astype(bf16).reshape(rows, channels)
-    d_parts = unproject(d_gate_low, d_rest, in_local, in_w, tile)
-    d_normed = d_parts[order].transpose(1, 0, 2).reshape(rows, width) + mm(d_dt_low, dt_w)
-    d_hidden, d_norm_g = front_back(d_normed)
-    input_grad = (d_hidden + cot).astype(bf16).reshape(hidden.shape)
+        d_parts = unproject(d_gate_low, d_rest, in_local, in_w, tile)
+        d_normed = d_parts[order].transpose(1, 0, 2).reshape(rows, width) + mm(d_dt_low, dt_w)
+        d_hidden, d_norm_g = front_back(d_normed)
+        input_grad = (d_hidden + cot).astype(bf16).reshape(hidden.shape)
 
     def summed(terms, axis):
         t = lax.psum_scatter(terms.astype(bf16), "seq", scatter_dimension=0, tiled=True)

time: 626 us -> 580 us (0.927)
  other arithmetic: 41.6 us -> 10.5 us
  matrix products: 25.8 us -> 0 us
  Pallas kernels: 485 us -> 507 us
  waiting for transfers between devices: 11.7 us -> 0.02 us
    dot_general x4 -> x0, matrix products: 25.8 us -> none  [mm(): return lax.dot_general(a, b, dims, preferred_element_type=f32)]
    convert_element_type x5 -> x0, other arithmetic: 20 us -> none  [the longest x1 10.6 us: local(): dy = d_scanned.astype(bf16).reshape(micro, tokens, inner)]
    pallas_call x5, Pallas kernels: 206 us -> 225 us  [the longest x1 85.5 us: gather_input_weight(): pl.pallas_call(partial(gather_kernel, inner, channels, parts), in_specs=[...]
    all_gather x1 -> x0, waiting for transfers between devices: 10.9 us -> none  [local(): out_w = lax.all_gather(out_part, 'wshard', axis=0, tiled=True)]
  transfers between devices with their start and end apart: 2 -> 1, of which waited for: 1 -> 0; matrix products, arithmetic and copies ran while one was open for 4% -> 1% of each run, Pallas kernels for 29% -> 15%
where the time goes in v5:
time: 580 us; the launch traced here: 571 us
  Pallas kernels  507 us (87%)
  local copies, waits for them, and re-layouts  37.8 us (7%)
  between operations  15.4 us (3%)
  other arithmetic  10.5 us (2%)
    pallas_call x1, Pallas kernels, weight_sums(): pl.pallas_call(sums_kernel, in_specs=[hbm] * 5 + [vmem], out_specs=[vmem]...  188 us
    pallas_call x1, Pallas kernels, scan_backward(): pl.pallas_call(partial(scan_backward_kernel, hs), in_specs=[vmem] * 13, o...  94.9 us
    pallas_call x1, Pallas kernels, gather_input_weight(): pl.pallas_call(partial(gather_kernel, inner, channels, parts), in_specs=[...  85.5 us
    pallas_call x1, Pallas kernels, scan_forward(): pl.pallas_call(partial(scan_forward_kernel, hs), in_specs=[vmem] * 7 + [h...  77.9 us
    pallas_call x1, Pallas kernels, gate_stage(): pl.pallas_call(gate_kernel, grid=(rows // tile,), in_specs=[wide, slim, p...  28.7 us
    pallas_call x1, Pallas kernels, back_stage(): pl.pallas_call(partial(back_kernel, steps), grid=(steps + more,), in_spec...  21.1 us
  transfers between devices with their start and end apart: 1, of which 0 were waited for; matrix products, arithmetic and copies ran while one was open for 1% of the time, Pallas kernels for 15%

profile of v5, /device:TPU:0, one launch (start us, length us, event | category | flops | bytes accessed | tf_op | source)
XLA Modules:
  0.0 570.9 jit_solution(16777415115686183427)
XLA Ops:
  7.2 0.0 all-reduce.7.cloned.1.call-start
  7.2 0.8 slice.97
  8.0 0.8 reshape.149
  8.8 1.2 dynamic-slice
  10.7 4.2 concatenate.9
  14.9 0.6 dynamic-update-slice
  15.5 0.0 copy-start.6
  15.6 0.7 copy-done.6
  16.2 0.0 all-reduce.7.cloned.1.call-update
  16.2 85.5 %gather_input_weight.1 = (bf16[3,3328,384]{2,1,0:T(8,128)(2,1)}, bf16[3,3072,384]{2,1,0:T(8,128)(2,1)}) custom-call(bf16[6448,384]{1,0:T(8,128)(2,1)} %bitcast.65), custom_call_target="tpu_custom_call" | custom-call | bytes 200000000 | tf_op jit(solution)/shard_map/gather_input_weight/pallas_call | solution.py:499
  101.8 0.0 copy-start.11
  101.8 0.0 copy-start
  101.8 3.6 slice.100.w_ref.cw_ref
  105.4 0.1 fusion
  105.5 0.9 copy.40
  106.3 1.1 reshape.174
  107.5 0.1 slice.99
  107.7 0.1 fusion.1
  107.7 0.1 fusion.2
  107.8 0.1 slice_bitcast_fusion
  108.0 0.0 copy-start.1
  108.0 0.1 neg.14
  108.1 0.1 reshape.157
  108.2 0.1 broadcast_in_dim.2
  108.3 0.7 broadcast_in_dim_reshape.21.skip_ref
  108.9 0.1 broadcast_in_dim_reshape.20
  109.0 0.5 pad.19.rate_ref
  109.5 0.5 pad.18.shift_ref
  110.1 0.1 reshape.155
  110.2 0.7 reshape.156.cw_ref
  110.9 0.7 broadcast_in_dim_reshape.19.cb_ref
  111.6 0.6 copy.38
  112.2 11.2 %front.1 = (bf16[512,3328]{1,0:T(8,128)(2,1)}, bf16[512,1536]{1,0:T(8,128)(2,1)S(1)}, f32[512,128]{1,0:T(8,128)S(1)}) custom-call(bf16[512,1536]{1,0:T(8,128)(2,1)S(1)} %bitcast.59, f32[1,1536]{1,0:T(1,128)S(1)} %bitcast.60, bf16[128,1536]{1,0:T(8,128)(2,1)S(1)} %pad.17.dtw_ref, bf16[3328,384]{1,0:T(8,128)(2,1)} %slice.100.w_ref.cw_ref, ...), custom_call_target="tpu_custom_call" | custom-call | tf_op jit(solution)/shard_map/front/pallas_call | solution.py:1625
  123.5 1.1 copy-done.2
  124.6 0.7 copy-done.4
  125.3 77.9 %scan_forward.1 = (bf16[2,256,3072]{2,1,0:T(8,128)(2,1)}, bf16[2,256,256]{2,1,0:T(8,128)(2,1)}, f32[2,256,3072]{2,1,0:T(8,128)}, bf16[2,256,3072]{2,1,0:T(8,128)...) custom-call(bf16[2,256,3328]{2,1,0:T(8,128)(2,1)} %bitcast.94, ...), custom_call_target="tpu_custom_call" | custom-call | flops 4026531840 | bytes 100000000 | tf_op jit(solution)/shard_map/scan_forward/pallas_call | solution.py:1257
  203.3 28.7 %gate_stage.1 = (bf16[512,3072]{1,0:T(8,128)(2,1)}, bf16[512,1536]{1,0:T(8,128)(2,1)}, bf16[512,1536]{1,0:T(8,128)(2,1)}, bf16[512,3072]{1,0:T(8,128)(2,1)}, bf1...) custom-call(bf16[512,3072]{1,0:T(8,128)(2,1)} %bitcast.79, bf16[512,1536]{1,0:T(8,128)(2,1)} %copy-done.2, ...), custom_call_target="tpu_custom_call" | custom-call | tf_op jit(solution)/shard_map/gate_stage/pallas_call | solution.py:1732
  232.0 94.9 %scan_backward.1 = (bf16[2,256,3584]{2,1,0:T(8,128)(2,1)}, f32[4,3328]{1,0:T(4,128)}, f32[1,3328]{1,0:T(1,128)}, f32[8,128]{1,0:T(8,128)}) custom-call(bf16[2,256,3072]{2,1,0:T(8,128)(2,1)} %bitcast.96, bf16[2,256,3072]{2,1,0:T(8,128)(2,1)} %get-tuple-element.48.x_ref, bf16[2,256,256]{2,1,0:T(8,128)(2,1)} %get-tuple-element.49.bc_ref, ...), custom_call_target="tpu_custom_call" | custom-call | flops 8053063680 | bytes 100000000 | tf_op jit(solution)/shard_map/scan_backward/pallas_call | solution.py:1559
  327.0 21.1 %back_stage.1 = (bf16[512,1536]{1,0:T(8,128)(2,1)}, f32[1,1536]{1,0:T(1,128)}) custom-call(bf16[512,3072]{1,0:T(8,128)(2,1)} %get-tuple-element.46.d_ref.gate_ref, bf16[512,3584]{1,0:T(8,128)(2,1)} %bitcast.69, bf16[512,3584]{1,0:T(8,128)(2,1)} %bitcast.70, bf16[128,1536]{1,0:T(8,128)(2,1)} %copy-done.1, bf16[6448,384]{1,0:T(8,128)(2,1)} %bitcast.68, ...), custom_call_target="tpu_custom_call" | custom-call | tf_op jit(solution)/shard_map/back_stage/pallas_call | solution.py:1835
  348.1 0.7 reduce
  348.8 0.0 copy-done.7
  348.8 0.1 reshape.164
  348.9 0.1 reshape.165
  349.1 0.1 reshape_squeeze.19
  349.2 0.8 slice_reduce_fusion
  350.0 0.1 reshape_squeeze.20
  350.1 0.1 reshape_squeeze.21
  350.2 0.1 reshape_squeeze.22
  350.2 0.5 broadcast.31
  350.8 0.7 reduce.17
  351.5 0.1 concatenate.10
  351.6 0.6 copy.44
  352.2 187.6 %weight_sums.1 = (bf16[2,26,2,2,2,16,384]{6,5,4,3,2,1,0:T(8,128)(2,1)}, bf16[2,6,2,2,2,16,768]{6,5,4,3,2,1,0:T(8,128)(2,1)}, f32[48,128]{1,0:T(8,128)}) custom-call(bf16[512,3072]{1,0:T(8,128)(2,1)} %get-tuple-element.46.d_ref.gate_ref, bf16[512,3584]{1,0:T(8,128)(2,1)} %bitcast.71, bf16[512,1536]{1,0:T(8,128)(2,1)} %copy-done.2, ...), custom_call_target="tpu_custom_call" | custom-call | flops 42467328000 | bytes 400000000 | tf_op jit(solution)/shard_map/weight_sums/pallas_call | solution.py:902
  539.9 2.1 slice.108
  541.9 3.4 slice.107
  545.3 0.6 slice.110
  545.9 0.7 slice.114
  546.6 0.6 slice_bitcast_fusion.2
  547.2 0.6 fusion.3
  547.8 0.3 slice.109
  548.0 2.7 bitcast_convert_fusion
  550.7 6.0 %copy.33 = f32[1536,768]{0,1:T(8,128)} copy(f32[1536,768]{1,0:T(8,128)} %bitcast_convert_fusion) | data formatting | bytes 9437184 | tf_op jit(solution)/shard_map/convert_element_type | solution.py:2183
  556.8 0.7 reshape.170
  557.5 6.2 %convert_bitcast_fusion = f32[384,6448]{0,1:T(8,128)} fusion(bf16[3376,384]{1,0:T(8,128)(2,1)S(1)} %slice.109, bf16[3072,384]{1,0:T(8,128)(2,1)} %bitcast.73), kind=kLoop, calls=%fused_computation | loop fusion | flops 9904128 | bytes 14856192 | tf_op jit(solution)/shard_map/transpose | solution.py:2182
  (35 shorter events, 0.3 us)
Async XLA Ops:
  7.2 99.2 %all-reduce.7.cloned.1.call-start = ((), (), s32[]{:S(2)}) async-start(), calls=%async_computation | async-start | bytes 380928
  15.5 0.7 copy-start.6
  101.8 3.6 copy-start.11
  101.8 10.4 %copy-start = (bf16[2,1,256,1536]{3,2,1,0:T(8,128)(2,1)S(1)}, bf16[2,1,256,1536]{3,2,1,0:T(8,128)(2,1)}, u32[]{:S(2)}) copy-start(bf16[2,1,256,1536]{3,2,1,0:T(8,128)(2,1)} %param.12) | copy-start | bytes 4718596
  107.9 15.6 %copy-start.3 = (f32[1,1,4,384]{3,1,2,0:T(1,128)}, f32[1,1,4,384]{3,1,2,0:T(1,128)S(1)}, u32[]{:S(2)}) copy-start(f32[1,1,4,384]{3,1,2,0:T(1,128)S(1)} %copy.36) | copy-start | bytes 18436
  108.0 15.5 %copy-start.1 = (bf16[128,1536]{1,0:T(8,128)(2,1)}, bf16[128,1536]{1,0:T(8,128)(2,1)S(1)}, u32[]{:S(2)}) copy-start(bf16[128,1536]{1,0:T(8,128)(2,1)S(1)} %pad.17.dtw_ref) | copy-start | bytes 1179652
  123.5 1.1 copy-start.2
  124.6 0.7 copy-start.4
  327.0 21.8 %copy-start.7 = (f32[4,3328]{1,0:T(4,128)S(1)}, f32[4,3328]{1,0:T(4,128)}, u32[]{:S(2)}) copy-start(f32[4,3328]{1,0:T(4,128)} %get-tuple-element.58) | copy-start | bytes 159748
  327.0 22.1 %copy-start.9 = (f32[1,3328]{1,0:T(1,128)S(1)}, f32[1,3328]{1,0:T(1,128)}, u32[]{:S(2)}) copy-start(f32[1,3328]{1,0:T(1,128)} %get-tuple-element.59) | copy-start | bytes 39940
  327.0 23.8 %copy-start.10 = (f32[1,3072]{1,0:T(1,128)S(1)}, f32[1,3072]{1,0:T(1,128)}, u32[]{:S(2)}) copy-start(f32[1,3072]{1,0:T(1,128)} %get-tuple-element.61) | copy-start | bytes 36868
  541.9 3.4 copy-start.8
  545.3 2.7 copy-start.5
Sparse Core Ops, SparseCore 0:
  16.4 42.5 all-reduce.6

commit v6 on v5

--- a/solution.py
+++ b/solution.py
@@ -13,7 +13,7 @@
 bf16 = jnp.bfloat16
 GROUP = 8
 VMEM = 48 * 1024 * 1024
-VMEM_MOST = 60 * 1024 * 1024
+VMEM_MOST = 62 * 1024 * 1024
 
 NN = (((1,), (0,)), ((), ()))
 NT = (((1,), (1,)), ((), ()))
@@ -419,7 +419,7 @@
                     )
 
                 def along(who, kind, to, move=move, rows=rows, target=target):
-                    block = target.at[:, rows(who)]
+                    block = target.at[pl.ds(0, 3), rows(who)]
                     return move(block, block, kind, to)
 
                 plan = {}
@@ -484,13 +484,19 @@
                 plan[name].wait_send()
 
 
-def gather_kernel(inner, channels, parts, w_ref, conv_ref, gate_ref, send, recv):
+def gather_kernel(inner, channels, parts, w_ref, conv_ref, gate_ref, own, own_sem, send, recv):
     place = around()
+    inward = pltpu.make_async_copy(w_ref.at[pl.ds(inner, channels)], own, own_sem)
+    inward.start()
     greet(place[-1])
     items = [(w_ref, inner, conv_ref, channels, parts), (w_ref, 0, gate_ref, inner, parts)]
     work = Gather(place, items, send, recv)
     work.run()
+    inward.wait()
+    outward = pltpu.make_async_copy(own, conv_ref.at[3], own_sem)
+    outward.start()
     work.close()
+    outward.wait()
 
 
 def gather_input_weight(w_t, inner, channels, parts=6):
@@ -501,14 +507,18 @@
         in_specs=[hbm],
         out_specs=[hbm] * 2,
         out_shape=[
-            jax.ShapeDtypeStruct((3, channels, width), bf16),
+            jax.ShapeDtypeStruct((4, channels, width), bf16),
             jax.ShapeDtypeStruct((3, inner, width), bf16),
         ],
         scratch_shapes=[
+            pltpu.VMEM((channels, width), bf16),
+            pltpu.SemaphoreType.DMA,
             pltpu.SemaphoreType.DMA((2 * parts, CHUNK_DMAS)),
             pltpu.SemaphoreType.DMA((2 * parts, CHUNK_DMAS)),
         ],
-        compiler_params=pltpu.CompilerParams(collective_id=1, has_side_effects=True),
+        compiler_params=pltpu.CompilerParams(
+            collective_id=1, has_side_effects=True, vmem_limit_bytes=VMEM_MOST
+        ),
         cost_estimate=pl.CostEstimate(flops=0, bytes_accessed=200_000_000, transcendentals=0),
         name="gather_input_weight",
     )(w_t)
@@ -540,8 +550,8 @@
         n = Products.IN
         marks = Products.marks(chunks)
         return [
-            pltpu.VMEM((2, rows, wide), bf16),
-            pltpu.VMEM((2, rows, width), bf16),
+            pltpu.VMEM((2 * rows, wide), bf16),
+            pltpu.VMEM((2 * rows, width), bf16),
             pltpu.VMEM((2, 128, width), f32),
             pltpu.VMEM((2, 32, width), bf16),
             pltpu.VMEM((2, 32, width), bf16),
@@ -596,12 +606,14 @@
         marks = Products.marks(self.chunks)
         self.groups = list(zip(marks[:-1], marks[1:]))
         c = self.c
+        rows = self.a.shape[0] // 2
+        near, far = pl.ds(0, rows), pl.ds(rows, rows)
         self.operands = []
         self.operands.append(
             (
                 0,
-                pltpu.make_async_copy(b_ref, self.b.at[0], self.in_sem.at[0]),
-                self.remote(b_ref, self.b.at[1], self.s_in.at[0], self.r_in.at[0], "c"),
+                pltpu.make_async_copy(b_ref, self.b.at[near], self.in_sem.at[0]),
+                self.remote(b_ref, self.b.at[far], self.s_in.at[0], self.r_in.at[0], "c"),
             )
         )
         at = 0
@@ -613,8 +625,8 @@
             self.operands.append(
                 (
                     at // 128,
-                    pltpu.make_async_copy(here, self.a.at[0, :, to], self.in_sem.at[i + 1]),
-                    self.remote(there, self.a.at[1, :, to], self.s_in.at[i + 1], self.r_in.at[i + 1], "c"),
+                    pltpu.make_async_copy(here, self.a.at[near, to], self.in_sem.at[i + 1]),
+                    self.remote(there, self.a.at[far, to], self.s_in.at[i + 1], self.r_in.at[i + 1], "c"),
                 )
             )
             at += half
@@ -692,7 +704,7 @@
 
             slot = t % 2
             cols = pl.ds(pl.multiple_of(t * 128, 128), 128)
-            g[slot] = mm(self.a[0, :, cols], self.b[0], TN) + mm(self.a[1, :, cols], self.b[1], TN)
+            g[slot] = mm(self.a[:, cols], self.b[...], TN)
             free(0, t)
             free(1, t)
             self.sa1[slot] = g[slot, sl((1 - x) * 32, 32)].astype(bf16)
@@ -846,7 +858,6 @@
 
 
 def sums_kernel(
-    gate_ref,
     conv_ref,
     nm_ref,
     og_ref,
@@ -859,7 +870,7 @@
 ):
     place = around()
     cut = Products.SCRATCH
-    inp = Products(place, [gate_ref, conv_ref], nm_ref, in_out, scratch[:cut])
+    inp = Products(place, [conv_ref], nm_ref, in_out, scratch[:cut])
     outp = Products(place, [og_ref], no_ref, out_out, scratch[cut : 2 * cut])
     small = Smalls(place, v_ref, v_out, scratch[2 * cut :])
     outp.load()
@@ -896,38 +907,42 @@
     inp.close()
 
 
-def weight_sums(d_gate, d_rest, nm, og, no, v, collective_id):
+def weight_sums(d_rest, nm, og, no, v, collective_id):
     vmem = pl.BlockSpec(memory_space=pltpu.VMEM)
     hbm = pl.BlockSpec(memory_space=pl.ANY)
     a_in, a_out, total = pl.pallas_call(
         sums_kernel,
-        in_specs=[hbm] * 5 + [vmem],
+        in_specs=[hbm] * 4 + [vmem],
         out_specs=[vmem] * 3,
         out_shape=[
-            Products.out_shape([d_gate, d_rest], nm),
+            Products.out_shape([d_rest], nm),
             Products.out_shape([og], no),
             jax.ShapeDtypeStruct(v.shape[1:], f32),
         ],
-        scratch_shapes=Products.scratch([d_gate, d_rest], nm)
+        scratch_shapes=Products.scratch([d_rest], nm)
         + Products.scratch([og], no)
         + Smalls.scratch(v),
         compiler_params=pltpu.CompilerParams(
             collective_id=collective_id, has_side_effects=True, vmem_limit_bytes=VMEM_MOST
         ),
         cost_estimate=pl.CostEstimate(
-            flops=6 * nm.shape[0] * nm.shape[1] * 9000, bytes_accessed=400_000_000, transcendentals=0
+            flops=6 * nm.shape[0] * nm.shape[1] * 6000, bytes_accessed=400_000_000, transcendentals=0
         ),
         name="weight_sums",
-    )(d_gate, d_rest, nm, og, no, v)
-    return a_in, a_out.reshape(og.shape[1], -1), total
+    )(d_rest, nm, og, no, v)
+    return a_in.reshape(d_rest.shape[1], -1), a_out.reshape(og.shape[1], -1), total
 
 
 LANES = 128
 HALO = 16
 
 
+def sigmoid(v):
+    return 0.5 + 0.5 * jnp.tanh(0.5 * v)
+
+
 def silu_parts(v):
-    s = 1.0 / (1.0 + jnp.exp(-v))
+    s = sigmoid(v)
     return v * s, s
 
 
@@ -950,16 +965,16 @@
 
 
 class Exchange:
-    def __init__(self, forward, own, own_low, got, t_low, t_got, u_low, u_got, p_low, p_got, before, send, recv):
+    def __init__(self, forward, own_low, got, t_low, t_got, u_low, u_got, p_low, p_got, send, recv):
         self.s, self.z, self.c, self.x, self.y, self.near = around()
         later = (lambda v: v) if forward else (lambda v: 1 - v)
         self.second = (later(self.c) == 1, later(self.x) == 1, later(self.y) == 1)
-        self.own, self.own_low, self.got = own, own_low, got
+        self.own_low, self.got = own_low, got
         self.t_low, self.t_got, self.u_low, self.u_got = t_low, t_got, u_low, u_got
-        self.p_low, self.p_got, self.before = p_low, p_got, before
+        self.p_low, self.p_got = p_low, p_got
         self.send, self.recv = send, recv
-        self.n = own.shape[1]
-        self.half = own.shape[2] // 2
+        self.n = t_low.shape[1] - 16
+        self.half = t_low.shape[2]
         self.mine = pl.ds(pl.multiple_of(self.c * self.half, LANES), self.half)
         self.other = pl.ds(pl.multiple_of((1 - self.c) * self.half, LANES), self.half)
 
@@ -990,7 +1005,6 @@
         return rows[0:1] + rows[1:2]
 
     def put_own(self, m, lanes, state, decay):
-        self.own[m, :, lanes] = state
         self.own_low[m, pl.ds(0, self.n), lanes] = state.astype(bf16)
         self.put_decay(self.own_low, m, lanes, decay)
 
@@ -1000,7 +1014,7 @@
     def along_x(self, m):
         self.copy(0, m).wait_recv()
         second = self.second[0]
-        mine = self.own[m, :, self.mine]
+        mine = self.own_low[m, pl.ds(0, self.n), self.mine].astype(f32)
         theirs = self.got[m, pl.ds(0, self.n), self.mine].astype(f32)
         d_mine = self.decay_of(self.own_low, m, self.mine)
         d_theirs = self.decay_of(self.got, m, self.mine)
@@ -1030,7 +1044,6 @@
         d_theirs = self.decay_of(self.t_got, m, every)
         over = y_second * jnp.where(self.second[1], d_theirs, 1.0)
         before = x_second * theirs + over * self.u_got[m].astype(f32)
-        self.before[m] = before
         self.p_low[m] = before.astype(bf16)
         self.copy(3, m).start()
 
@@ -1038,7 +1051,7 @@
         self.copy(3, m).wait_recv()
         second = jnp.where(self.second[0], 1.0, 0.0)
         for lanes, before in (
-            (self.mine, self.before[m]),
+            (self.mine, self.p_low[m].astype(f32)),
             (self.other, self.p_got[m].astype(f32)),
         ):
             d_theirs = self.decay_of(self.got, m, lanes)
@@ -1047,7 +1060,7 @@
             out[m, :, lanes] = (before * over + second * theirs).astype(bf16)
 
     def sent(self):
-        for m in range(self.own.shape[0]):
+        for m in range(self.own_low.shape[0]):
             for kind in range(4):
                 self.copy(kind, m).wait_send()
 
@@ -1056,7 +1069,6 @@
     half = inner // 2
     dma = pltpu.SemaphoreType.DMA
     return [
-        pltpu.VMEM((micro, n, inner), f32),
         pltpu.VMEM((micro, n + 16, inner), bf16),
         pltpu.VMEM((micro, n + 16, inner), bf16),
         pltpu.VMEM((micro, n + 16, half), bf16),
@@ -1065,13 +1077,13 @@
         pltpu.VMEM((micro, n, half), bf16),
         pltpu.VMEM((micro, n, half), bf16),
         pltpu.VMEM((micro, n, half), bf16),
-        pltpu.VMEM((micro, n, half), f32),
         dma((4, micro)),
         dma((4, micro)),
     ]
 
 
-EXCHANGE = 12
+EXCHANGE = 10
+TICKS = (12, 3, 2, 2)
 
 
 def steps_of(raw, shift, rate):
@@ -1305,13 +1317,18 @@
     shift_ref,
     rate_ref,
     skip_ref,
+    dgate_ref,
+    norm_ref,
     dconv_ref,
     dcw_ref,
     dcb_ref,
     heads_ref,
+    sum_ref,
     *scratch,
 ):
     (
+        y_now,
+        y_sem,
         buf,
         wide_buf,
         scores,
@@ -1324,11 +1341,12 @@
         dbc,
         ddt_sum,
         dcum_sum,
+        last_sum,
         head_low,
         next_low,
         h_send,
         h_recv,
-    ) = scratch[EXCHANGE:]
+    ) = scratch[EXCHANGE : EXCHANGE + 19]
     ex = Exchange(False, *scratch[:EXCHANGE])
     s, z = ex.s, ex.z
     micro, t, channels = conv_ref.shape
@@ -1338,10 +1356,20 @@
     groups = inner // gc
     half = t // 2
     taps = cw_ref.shape[0]
-    near = {k: ex.near[k] for k in ("c", "x", "y")}
+    place = around()
+    near = dict(place[-1])
     near["next"] = ((s + 1) % 8, z)
     near["last"] = ((s + 7) % 8, z)
+    sums_of = Products(place, [dgate_ref], norm_ref, sum_ref, scratch[EXCHANGE + 19 :])
+    sums_of.load()
+
+    def y_copy(i):
+        lanes = pl.ds(pl.multiple_of((i % groups) * gc, gc), gc)
+        slot = i % 2
+        return pltpu.make_async_copy(y_ref.at[i // groups, :, lanes], y_now.at[slot], y_sem.at[slot])
+
     greet(near)
+    sums_of.share()
     first_rows = [
         pltpu.make_async_remote_copy(
             src_ref=head_low.at[m],
@@ -1356,22 +1384,47 @@
     has_prior = jnp.where(s > 0, 1.0, 0.0)
     has_next = jnp.where(s < 7, 1.0, 0.0)
 
-    def own_states(m, a, b):
-        def body(g, carry):
+    middle = groups // 2
+
+    def at_step(i, *todo):
+        for when, what in todo:
+            pl.when(i == when)(what)
+
+    def own_states():
+        def body(i, carry):
+            m, g = i // groups, i % groups
             lanes = pl.ds(pl.multiple_of(g * gc, gc), gc)
             cum = head_columns(cums[m], g)
             weighted = (dy_ref[m, :, lanes].astype(f32) * widen(jnp.exp(cum), hs)).astype(bf16)
             state = mm(bc_ref[m, :, n:], weighted, TN)
             ex.put_own(m, lanes, state, widen(jnp.exp(cum[t - 1 :]), hs))
+            at_step(
+                i,
+                (groups - 1, lambda: ex.core(0)),
+                (groups + middle, lambda: ex.along_x(0)),
+                (2 * groups - 1, lambda: ex.core(1)),
+            )
+            tick(i, TICKS[0], 0)
             return carry
 
-        lax.fori_loop(a, b, body, 0)
-
-    def local_terms(m, a, b):
+        lax.fori_loop(0, 2 * groups, body, 0)
+
+    def tick(i, every, first):
+        @pl.when(i % every == every - 1)
+        def _():
+            sums_of.step(first + i // every)
+
+    def upper_ones():
+        j = lax.broadcasted_iota(jnp.int32, (t, t), 0)
+        i = lax.broadcasted_iota(jnp.int32, (t, t), 1)
+        return jnp.where(i >= j, 1.0, 0.0)
+
+    def local_terms():
         lane = lax.broadcasted_iota(jnp.int32, (t, 2 * hs), 1)
         lane_half = lax.broadcasted_iota(jnp.int32, (half, 2 * hs), 1)
 
-        def body(g, carry):
+        def body(i, carry):
+            m, g = i // groups, i % groups
             lanes = pl.ds(pl.multiple_of(g * gc, gc), gc)
             cum = head_columns(cums[m], g)
             rows = rows_t[m, pl.ds(pl.multiple_of(g * GROUP, GROUP), GROUP), :]
@@ -1393,29 +1446,59 @@
                     low.append(mm((l2 * scores[m, half:, half:]).astype(bf16), dy[half:]))
                 dxl[m, :half, at] = jnp.where(lane_half < hs, top[0], top[1])
                 dxl[m, half:, at] = jnp.where(lane_half < hs, low[0], low[1])
+            at_step(
+                i,
+                (1, lambda: ex.along_x(1)),
+                (3, lambda: ex.along_y(0)),
+                (groups - 1, lambda: local_close(0)),
+                (groups + 1, lambda: ex.along_y(1)),
+                (groups + 3, lambda: ex.back_to_core(0)),
+                (2 * groups - 1, lambda: local_close(1)),
+            )
+            tick(i, TICKS[1], 2 * groups // TICKS[0])
             return carry
 
-        lax.fori_loop(a, b, body, 0)
-
-    def upper_ones():
-        j = lax.broadcasted_iota(jnp.int32, (t, t), 0)
-        i = lax.broadcasted_iota(jnp.int32, (t, t), 1)
-        return jnp.where(i >= j, 1.0, 0.0)
+        lax.fori_loop(0, 2 * groups, body, 0)
 
     def local_close(m):
         d = total[...] * upper_ones()
         dbc[m, :, 0:n] = mm(d.astype(bf16), bc_ref[m, :, n:])
         dbc[m, :, n:] = mm(d.T.astype(bf16), bc_ref[m, :, :n])
-
-    def through_states(m, sums):
+        total[...] = jnp.zeros_like(total)
+
+    def through_states():
         r = lax.broadcasted_iota(jnp.int32, (gc, LANES), 0)
         col = lax.broadcasted_iota(jnp.int32, (gc, LANES), 1)
-        ddt_sum[...] = jnp.zeros_like(ddt_sum)
-        dcum_sum[...] = jnp.zeros_like(dcum_sum)
-
-        def body(g, carry):
-            last, skips = carry
+
+        def clear():
+            ddt_sum[...] = jnp.zeros_like(ddt_sum)
+            dcum_sum[...] = jnp.zeros_like(dcum_sum)
+            last_sum[...] = jnp.zeros_like(last_sum)
+
+        def close(m):
+            d_log = exact(upper_ones(), dcum_sum[...]) + last_sum[0:1]
+            v = raw_ref[m] + shift_ref[...]
+            d_dt = (ddt_sum[...] + d_log * rate_ref[...]) / (1.0 + jnp.exp(-v))
+            rest = dconv_ref.shape[2] - channels - LANES
+            dconv_ref[m, :, pl.ds(channels, LANES)] = d_dt.astype(bf16)
+            if rest:
+                dconv_ref[m, :, pl.ds(channels + LANES, rest)] = jnp.zeros((t, rest), bf16)
+            heads_ref[0:1] += jnp.sum(d_dt, axis=0, keepdims=True)
+            heads_ref[1:2] += jnp.sum(d_log * dts[m], axis=0, keepdims=True) * rate_ref[...]
+            first_slopes(m)
+            if m == 0:
+                clear()
+                ex.begin_state(1, ends)
+
+        def body(i, carry):
+            m, g = i // groups, i % groups
             lanes = pl.ds(pl.multiple_of(g * gc, gc), gc)
+
+            @pl.when(i + 1 < 2 * groups)
+            def _():
+                y_copy(i + 1).start()
+
+            y_copy(i).wait()
             ones = jnp.where(r // hs + g * GROUP == col, 1.0, 0.0).astype(bf16)
             cum = head_columns(cums[m], g)
             dt_wide = widen(head_columns(dts[m], g), hs)
@@ -1430,31 +1513,25 @@
             dbc[m, :, 0:n] += mm((weighted * to_end).astype(bf16), ds, NT)
             dbc[m, :, n:] += mm((dy * decay).astype(bf16), s_in, NT)
             ddt_sum[...] += head_sums(x * d_weighted, ones)
-            dcum_sum[...] += head_sums(dy * y_ref[m, :, lanes] - weighted * d_weighted, ones)
+            dcum_sum[...] += head_sums(dy * y_now[i % 2] - weighted * d_weighted, ones)
             at_end = jnp.sum(weighted * through, axis=0, keepdims=True) + decay[t - 1 :] * jnp.sum(
                 s_in.astype(f32) * ds.astype(f32), axis=0, keepdims=True
             )
-            last = last + head_sums(jnp.broadcast_to(at_end, (8, gc)), ones)
+            last_sum[...] += head_sums(jnp.broadcast_to(at_end, (8, gc)), ones)
             by_skip = jnp.sum(x * dy, axis=0, keepdims=True)
-            skips = skips + head_sums(jnp.broadcast_to(by_skip, (8, gc)), ones)
-            return last, skips
-
-        none = jnp.zeros((8, LANES), f32)
-        last, skips = lax.fori_loop(0, groups, body, (none, none))
-        d_log = exact(upper_ones(), dcum_sum[...]) + last[0:1]
-        v = raw_ref[m] + shift_ref[...]
-        d_dt = (ddt_sum[...] + d_log * rate_ref[...]) / (1.0 + jnp.exp(-v))
-        rest = dconv_ref.shape[2] - channels - LANES
-        dconv_ref[m, :, pl.ds(channels, LANES)] = d_dt.astype(bf16)
-        if rest:
-            dconv_ref[m, :, pl.ds(channels + LANES, rest)] = jnp.zeros((t, rest), bf16)
-        d_bias = jnp.sum(d_dt, axis=0, keepdims=True)
-        d_rate = jnp.sum(d_log * dts[m], axis=0, keepdims=True) * rate_ref[...]
-        return sums[0] + d_bias, sums[1] + d_rate, sums[2] + skips[0:1]
+            heads_ref[2:3] += head_sums(jnp.broadcast_to(by_skip, (8, gc)), ones)[0:1]
+            at_step(i, (groups - 1, lambda: close(0)), (2 * groups - 1, lambda: close(1)))
+            tick(i, TICKS[2], 2 * groups // TICKS[0] + 2 * groups // TICKS[1])
+            return carry
+
+        clear()
+        heads_ref[...] = jnp.zeros_like(heads_ref)
+        y_copy(0).start()
+        lax.fori_loop(0, 2 * groups, body, 0)
 
     def pre_slope(into, lanes, grad, rows):
         v = conv_rows(into[0 : HALO + rows, :], cw_ref[:, lanes], cb_ref[:, lanes])
-        sig = 1.0 / (1.0 + jnp.exp(-v))
+        sig = sigmoid(v)
         return grad * (sig * (1.0 + v * (1.0 - sig)))
 
     def load(m, lanes, into, rows):
@@ -1475,8 +1552,8 @@
         one(pl.ds(inner, channels - inner), wide_buf, dbc[m, 0:HALO, :])
         first_rows[m].start()
 
-    def conv_back(m):
-        def one(lanes, into, grad):
+    def conv_back():
+        def one(m, lanes, into, grad):
             load(m, lanes, into, t)
             slope = pre_slope(into, lanes, grad, t)
             weights = cw_ref[:, lanes]
@@ -1494,13 +1571,18 @@
                 back = back + into[at : at + t, :] * weights[k : k + 1]
             dconv_ref[m, :, lanes] = back.astype(bf16)
 
-        def body(g, carry):
+        def body(i, carry):
+            m, g = i // groups, i % groups
             lanes = pl.ds(pl.multiple_of(g * gc, gc), gc)
-            one(lanes, buf, dconv_ref[m, :, lanes].astype(f32))
+            one(m, lanes, buf, dconv_ref[m, :, lanes].astype(f32))
+            at_step(i, (groups - 1, lambda: first_rows[1].wait_recv()))
+            tick(i, TICKS[3], 2 * groups // TICKS[0] + 2 * groups // TICKS[1] + 2 * groups // TICKS[2])
             return carry
 
-        lax.fori_loop(0, groups, body, 0)
-        one(pl.ds(inner, channels - inner), wide_buf, dbc[m])
+        first_rows[0].wait_recv()
+        lax.fori_loop(0, 2 * groups, body, 0)
+        for m in range(micro):
+            one(m, pl.ds(inner, channels - inner), wide_buf, dbc[m])
 
     for m in range(micro):
         dt, cum = steps_of(raw_ref[m], shift_ref[...], rate_ref[...])
@@ -1511,43 +1593,43 @@
     dcw_ref[...] = jnp.zeros_like(dcw_ref)
     dcb_ref[...] = jnp.zeros_like(dcb_ref)
     total[...] = jnp.zeros_like(total)
-    middle = groups // 2
-    own_states(0, 0, groups)
-    ex.core(0)
-    own_states(1, 0, middle)
-    ex.along_x(0)
-    own_states(1, middle, groups)
-    ex.core(1)
-    local_terms(0, 0, middle)
-    ex.along_x(1)
-    ex.along_y(0)
-    local_terms(0, middle, groups)
-    local_close(0)
-    total[...] = jnp.zeros_like(total)
-    ex.along_y(1)
-    ex.back_to_core(0)
-    local_terms(1, 0, groups)
-    local_close(1)
+    own_states()
+    local_terms()
     ex.begin_state(0, ends)
     ex.back_to_core(1)
-    none = jnp.zeros((1, LANES), f32)
-    sums = through_states(0, (none, none, none))
-    first_slopes(0)
-    ex.begin_state(1, ends)
-    sums = through_states(1, sums)
-    first_slopes(1)
-    heads_ref[...] = jnp.concatenate(list(sums) + [jnp.zeros((5, LANES), f32)], axis=0)
-    first_rows[0].wait_recv()
-    conv_back(0)
-    first_rows[1].wait_recv()
-    conv_back(1)
+    through_states()
+    conv_back()
+    done = sum(2 * groups // every for every in TICKS)
+
+    def rest_of(i, carry):
+        sums_of.step(i)
+        return carry
+
+    lax.fori_loop(done, sums_of.steps(), rest_of, 0)
     ex.sent()
     for copy in first_rows:
         copy.wait_send()
+    sums_of.close()
 
 
 def scan_backward(
-    dy, x, bc, y, begin, raw, conv_low, halo, conv_w, conv_b, shift, rate, skip_wide, hs, collective_id
+    dy,
+    x,
+    bc,
+    y,
+    begin,
+    raw,
+    conv_low,
+    halo,
+    conv_w,
+    conv_b,
+    shift,
+    rate,
+    skip_wide,
+    d_gate,
+    normed,
+    hs,
+    collective_id,
 ):
     micro, t, channels = conv_low.shape
     inner = x.shape[2]
@@ -1556,18 +1638,22 @@
     taps = conv_w.shape[0]
     dma = pltpu.SemaphoreType.DMA
     vmem = pl.BlockSpec(memory_space=pltpu.VMEM)
+    hbm = pl.BlockSpec(memory_space=pl.ANY)
     return pl.pallas_call(
         partial(scan_backward_kernel, hs),
-        in_specs=[vmem] * 13,
-        out_specs=[vmem] * 4,
+        in_specs=[vmem] * 3 + [hbm] + [vmem] * 9 + [hbm] * 2,
+        out_specs=[vmem] * 5,
         out_shape=[
             jax.ShapeDtypeStruct((micro, t, -(-(channels + LANES) // 256) * 256), bf16),
             jax.ShapeDtypeStruct((taps, channels), f32),
             jax.ShapeDtypeStruct((1, channels), f32),
             jax.ShapeDtypeStruct((8, LANES), f32),
+            Products.out_shape([d_gate], normed),
         ],
         scratch_shapes=exchange_scratch(micro, n, inner)
         + [
+            pltpu.VMEM((2, t, gc), f32),
+            dma((2,)),
             pltpu.VMEM((HALO + t, gc), f32),
             pltpu.VMEM((HALO + t, 2 * n), f32),
             pltpu.VMEM((micro, t, t), f32),
@@ -1580,11 +1666,13 @@
             pltpu.VMEM((micro, t, 2 * n), f32),
             pltpu.VMEM((t, LANES), f32),
             pltpu.VMEM((t, LANES), f32),
+            pltpu.VMEM((8, LANES), f32),
             pltpu.VMEM((micro, HALO, channels), bf16),
             pltpu.VMEM((micro, HALO, channels), bf16),
             dma((micro,)),
             dma((micro,)),
-        ],
+        ]
+        + Products.scratch([d_gate], normed),
         compiler_params=pltpu.CompilerParams(
             collective_id=collective_id, has_side_effects=True, vmem_limit_bytes=VMEM_MOST
         ),
@@ -1592,7 +1680,23 @@
             flops=8 * micro * t * inner * (t + 3 * n), bytes_accessed=100_000_000, transcendentals=0
         ),
         name="scan_backward",
-    )(dy, x, bc, y, begin, raw, conv_low, halo, conv_w, conv_b, shift, rate, skip_wide)
+    )(
+        dy,
+        x,
+        bc,
+        y,
+        begin,
+        raw,
+        conv_low,
+        halo,
+        conv_w,
+        conv_b,
+        shift,
+        rate,
+        skip_wide,
+        d_gate,
+        normed,
+    )
 
 
 def shard_place(k, depth):
@@ -1601,8 +1705,8 @@
     return pl.ds(pl.multiple_of(other * depth, 128), depth)
 
 
-def front_kernel(h_ref, g_ref, dtw_ref, w_ref, v_ref, conv_ref, norm_ref, raw_ref, rel):
-    depth = w_ref.shape[1]
+def front_kernel(h_ref, g_ref, dtw_ref, v_ref, conv_ref, norm_ref, raw_ref, rel):
+    depth = v_ref.shape[2]
 
     @pl.when(pl.program_id(0) == 0)
     def _():
@@ -1614,13 +1718,13 @@
         for k in range(4):
             rel[:, k * depth : (k + 1) * depth] = norm_ref[:, shard_place(k, depth)]
 
-    weights = jnp.concatenate([w_ref[...]] + [v_ref[k] for k in range(3)], axis=1)
+    weights = jnp.concatenate([v_ref[k] for k in (3, 0, 1, 2)], axis=1)
     conv_ref[...] = mm(rel[...], weights, NT).astype(bf16)
 
 
-def front(hidden, gain, dt_w, own, others, tile):
+def front(hidden, gain, dt_w, shards, tile):
     rows, width = hidden.shape
-    count, depth = own.shape
+    _, count, depth = shards.shape
     whole = pl.BlockSpec((rows, width), lambda i: (0, 0))
     return pl.pallas_call(
         front_kernel,
@@ -1629,8 +1733,7 @@
             whole,
             pl.BlockSpec((1, width), lambda i: (0, 0)),
             pl.BlockSpec((LANES, width), lambda i: (0, 0)),
-            pl.BlockSpec((tile, depth), lambda i: (i, 0)),
-            pl.BlockSpec((3, tile, depth), lambda i: (0, i, 0)),
+            pl.BlockSpec((4, tile, depth), lambda i: (0, i, 0)),
         ],
         out_specs=[
             pl.BlockSpec((rows, tile), lambda i: (0, i)),
@@ -1645,7 +1748,7 @@
         scratch_shapes=[pltpu.VMEM((rows, width), bf16)],
         compiler_params=pltpu.CompilerParams(vmem_limit_bytes=VMEM),
         name="front",
-    )(hidden, gain, dt_w, own, others)
+    )(hidden, gain, dt_w, shards)
 
 
 def gate_kernel(
@@ -1771,7 +1874,6 @@
     dtw_ref,
     w_ref,
     v_ref,
-    cw_ref,
     cv_ref,
     h_ref,
     g_ref,
@@ -1784,20 +1886,23 @@
     depth = w_ref.shape[1]
     i = pl.program_id(0)
 
-    def product(ref, one, three):
-        return mm(ref[...], jnp.concatenate([one[...]] + [three[k] for k in range(3)], axis=1))
+    def product(ref, *shards):
+        return mm(ref[...], jnp.concatenate(shards, axis=1))
+
+    gate_shards = [w_ref] + [v_ref.at[k] for k in range(3)]
+    conv_shards = [cv_ref.at[k] for k in (3, 0, 1, 2)]
 
     @pl.when(i == 0)
     def _():
-        acc[...] = product(d_ref, w_ref, v_ref)
+        acc[...] = product(d_ref, *[r[...] for r in gate_shards])
 
     @pl.when((i > 0) & (i < steps))
     def _():
-        acc[...] += product(d_ref, w_ref, v_ref)
+        acc[...] += product(d_ref, *[r[...] for r in gate_shards])
 
     @pl.when(i >= steps)
     def _():
-        acc[...] += product(e_ref, cw_ref, cv_ref)
+        acc[...] += product(e_ref, *[r[...] for r in conv_shards])
 
     @pl.when(i == pl.num_programs(0) - 1)
     def _():
@@ -1818,9 +1923,9 @@
         dg_ref[...] = d_gain
 
 
-def back_stage(d, e, dt_w, gate_own, gate_others, own, others, hidden, gain, out_grad, tiles):
+def back_stage(d, e, dt_w, gate_own, gate_others, shards, hidden, gain, out_grad, tiles):
     rows, width = hidden.shape
-    count, depth = own.shape
+    _, count, depth = shards.shape
     inner = d.shape[1]
     steps, more = inner // tiles[0], count // tiles[1]
     whole = pl.BlockSpec((rows, width), lambda i: (0, 0))
@@ -1842,8 +1947,7 @@
             pl.BlockSpec((LANES, width), lambda i: (0, 0)),
             pl.BlockSpec((tiles[0], depth), lambda i: (early(i), 0)),
             pl.BlockSpec((3, tiles[0], depth), lambda i: (0, early(i), 0)),
-            pl.BlockSpec((tiles[1], depth), lambda i: (late(i), 0)),
-            pl.BlockSpec((3, tiles[1], depth), lambda i: (0, late(i), 0)),
+            pl.BlockSpec((4, tiles[1], depth), lambda i: (0, late(i), 0)),
             whole,
             line,
             whole,
@@ -1856,7 +1960,7 @@
         scratch_shapes=[pltpu.VMEM((rows, width), f32), pltpu.VMEM((rows, width), f32)],
         compiler_params=pltpu.CompilerParams(vmem_limit_bytes=VMEM_MOST),
         name="back_stage",
-    )(d, e, e, dt_w, gate_own, gate_others, own, others, hidden, gain, out_grad)
+    )(d, e, e, dt_w, gate_own, gate_others, shards, hidden, gain, out_grad)
 
 
 def project_kernel(n_ref, w_ref, v_ref, o_ref):
@@ -1992,8 +2096,7 @@
     dt_w = packed_low[:, at:].reshape(shards, heads, -1).transpose(1, 0, 2).reshape(heads, -1)
     order = jnp.arange(shards) ^ shard
     if fast:
-        conv_own = in_local[inner : inner + channels]
-        conv_others, gate_others = gather_input_weight(in_local, inner, channels)
+        conv_shards, gate_others = gather_input_weight(in_local, inner, channels)
     else:
         every = lax.all_gather(in_local[: inner + channels], "wshard", axis=0)
         in_w = every[order[1:]]
@@ -2016,7 +2119,7 @@
         hidden_rows, out_grad_rows = hidden.reshape(rows, width), out_grad.reshape(rows, width)
         dt_wide = jnp.pad(dt_w, ((0, LANES - heads), (0, 0)))
         conv_low, normed_low, raw = front(
-            hidden_rows, norm_g[None, :], dt_wide, conv_own, conv_others, channels // 2
+            hidden_rows, norm_g[None, :], dt_wide, conv_shards, channels // 2
         )
         raw = raw.reshape(micro, tokens, LANES)
     else:
@@ -2093,7 +2196,7 @@
         d_gate_low = d_gate_in.astype(bf16)
 
     if fast:
-        d_rest, d_conv_w, d_conv_b, by_head = scan_backward(
+        d_rest, d_conv_w, d_conv_b, by_head, gate_sum = scan_backward(
             dy,
             x_low,
             bc_low,
@@ -2107,6 +2210,8 @@
             to_lanes(dt_shift[None, :]),
             to_lanes(rate[None, :]),
             skip_wide,
+            d_gate_low,
+            normed_low,
             hs,
             4,
         )
@@ -2119,8 +2224,7 @@
             dt_wide,
             in_local,
             gate_others,
-            conv_own,
-            conv_others,
+            conv_shards,
             hidden_rows,
             norm_g[None, :],
             out_grad_rows,
@@ -2175,11 +2279,9 @@
     smalls = jnp.concatenate(smalls, axis=1)
     if fast:
         smalls = jnp.pad(smalls, ((0, 0), (0, -smalls.shape[1] % 1024))).reshape(shards, -1, LANES)
-        by_core, out_sum, sums = weight_sums(d_gate_low, d_rest, normed_low, g, normed_out_low, smalls, 2)
-        by_core = by_core.reshape(2, -1, normed_low.shape[1] // shards)
-        split = inner // 2
-        rest = by_core[:, split:].reshape(-1, by_core.shape[2])[: total_cols - inner]
-        in_grad = jnp.concatenate([by_core[:, :split].reshape(inner, -1), rest]).astype(f32).T
+        rest_sum, out_sum, sums = weight_sums(d_rest, normed_low, g, normed_out_low, smalls, 2)
+        gate_sum = gate_sum.reshape(inner, -1)
+        in_grad = jnp.concatenate([gate_sum, rest_sum[: total_cols - inner]]).astype(f32).T
         out_w_grad = out_sum.T.astype(f32)
         sums = sums.reshape(-1)
     else:

time: 580 us -> 555 us (0.957)
  Pallas kernels: 507 us -> 485 us
    pallas_call x2, Pallas kernels: 283 us -> 261 us  [the longest x1 135 us: weight_sums(): pl.pallas_call(sums_kernel, in_specs=[hbm] * 4 + [vmem], out_specs=[vmem]...]
    slice x4 -> x1, local copies, waits for them, and re-layouts: 9.29 us -> 1.99 us  [local(): rest_sum[:total_cols - inner]]
  transfers between devices with their start and end apart: 1 -> 1, of which waited for: 0 -> 0; matrix products, arithmetic and copies ran while one was open for 1% -> 0% of each run, Pallas kernels for 15% -> 16%
where the time goes in v6:
time: 555 us; the launch traced here: 546 us
  Pallas kernels  485 us (87%)
  local copies, waits for them, and re-layouts  34.3 us (6%)
  between operations  15.5 us (3%)
  other arithmetic  10.5 us (2%)
    pallas_call x1, Pallas kernels, weight_sums(): pl.pallas_call(sums_kernel, in_specs=[hbm] * 4 + [vmem], out_specs=[vmem]...  135 us
    pallas_call x1, Pallas kernels, scan_backward(): pl.pallas_call(partial(scan_backward_kernel, hs), in_specs=[vmem] * 3 + [...  126 us
    pallas_call x1, Pallas kernels, gather_input_weight(): pl.pallas_call(partial(gather_kernel, inner, channels, parts), in_specs=[...  85.7 us
    pallas_call x1, Pallas kernels, scan_forward(): pl.pallas_call(partial(scan_forward_kernel, hs), in_specs=[vmem] * 7 + [h...  77.8 us
    pallas_call x1, Pallas kernels, gate_stage(): pl.pallas_call(gate_kernel, grid=(rows // tile,), in_specs=[wide, slim, p...  28.6 us
    pallas_call x1, Pallas kernels, back_stage(): pl.pallas_call(partial(back_kernel, steps), grid=(steps + more,), in_spec...  21 us
    pallas_call x1, Pallas kernels, front(): pl.pallas_call(front_kernel, grid=(count // tile,), in_specs=[whole, pl.B...  11.2 us
  transfers between devices with their start and end apart: 1, of which 0 were waited for; matrix products, arithmetic and copies ran while one was open for 0% of the time, Pallas kernels for 16%

profile of v6, /device:TPU:0, one launch (start us, length us, event | category | flops | bytes accessed | tf_op | source)
XLA Modules:
  0.0 545.6 jit_solution(2721659998406615516)
XLA Ops:
  7.2 0.0 copy-start.10
  7.2 0.0 all-reduce.7.cloned.1.call-start
  7.2 0.8 slice.85
  8.0 0.8 reshape.146
  8.8 1.2 dynamic-slice
  10.7 4.2 concatenate.9
  14.9 0.6 dynamic-update-slice
  15.6 0.0 copy-start.6
  15.6 0.7 copy-done.6
  16.2 0.0 all-reduce.7.cloned.1.call-update
  16.3 0.0 copy-start
  16.3 85.7 %gather_input_weight.1 = (bf16[4,3328,384]{2,1,0:T(8,128)(2,1)}, bf16[3,3072,384]{2,1,0:T(8,128)(2,1)}) custom-call(bf16[6448,384]{1,0:T(8,128)(2,1)} %bitcast.64), custom_call_target="tpu_custom_call" | custom-call | bytes 200000000 | tf_op jit(solution)/shard_map/gather_input_weight/pallas_call | solution.py:505
  102.0 0.0 copy-done.10
  102.0 0.1 fusion
  102.1 0.9 copy.40
  103.0 1.1 reshape.170
  104.1 0.1 slice.87
  104.3 0.1 fusion.1
  104.4 0.1 fusion.2
  104.5 0.1 slice_bitcast_fusion
  104.6 0.0 copy-start.3
  104.7 0.0 copy-start.1
  104.7 0.1 neg.14
  104.7 0.1 reshape.154
  104.8 0.1 broadcast_in_dim.2
  104.9 0.7 broadcast_in_dim_reshape.21.skip_ref
  105.6 0.1 broadcast_in_dim_reshape.20
  105.7 0.5 pad.19.rate_ref
  106.2 0.5 pad.18.shift_ref
  106.7 0.1 reshape.152
  106.8 0.7 reshape.153.cw_ref
  107.6 0.7 broadcast_in_dim_reshape.19.cb_ref
  108.3 0.6 copy.38
  108.9 11.2 %front.1 = (bf16[512,3328]{1,0:T(8,128)(2,1)}, bf16[512,1536]{1,0:T(8,128)(2,1)S(1)}, f32[512,128]{1,0:T(8,128)S(1)}) custom-call(bf16[512,1536]{1,0:T(8,128)(2,1)S(1)} %bitcast.58, f32[1,1536]{1,0:T(1,128)S(1)} %bitcast.59, bf16[128,1536]{1,0:T(8,128)(2,1)S(1)} %pad.17.dtw_ref, bf16[4,3328,384]{2,1,0:T(8,128)(2,1)} %get-tuple-element.39.v_ref.cv_ref), custom_call_target="tpu_custom_call" | custom-call | tf_op jit(solution)/shard_map/front/pallas_call | solution.py:1729
  120.1 1.1 copy-done.2
  121.3 0.7 copy-done.4
  122.0 77.8 %scan_forward.1 = (bf16[2,256,3072]{2,1,0:T(8,128)(2,1)}, bf16[2,256,256]{2,1,0:T(8,128)(2,1)}, f32[2,256,3072]{2,1,0:T(8,128)}, bf16[2,256,3072]{2,1,0:T(8,128)...) custom-call(bf16[2,256,3328]{2,1,0:T(8,128)(2,1)} %bitcast.90, ...), custom_call_target="tpu_custom_call" | custom-call | flops 4026531840 | bytes 100000000 | tf_op jit(solution)/shard_map/scan_forward/pallas_call | solution.py:1269
  199.7 28.6 %gate_stage.1 = (bf16[512,3072]{1,0:T(8,128)(2,1)}, bf16[512,1536]{1,0:T(8,128)(2,1)}, bf16[512,1536]{1,0:T(8,128)(2,1)}, bf16[512,3072]{1,0:T(8,128)(2,1)}, bf1...) custom-call(bf16[512,3072]{1,0:T(8,128)(2,1)} %bitcast.73, bf16[512,1536]{1,0:T(8,128)(2,1)} %copy-done.2, ...), custom_call_target="tpu_custom_call" | custom-call | tf_op jit(solution)/shard_map/gate_stage/pallas_call | solution.py:1835
  228.3 126.0 %scan_backward.1 = (bf16[2,256,3584]{2,1,0:T(8,128)(2,1)}, f32[4,3328]{1,0:T(4,128)}, f32[1,3328]{1,0:T(1,128)}, f32[8,128]{1,0:T(8,128)}, bf16[2,12,2,2,2,16,384]{6,5,4,3,2,1,0:T(8,128)(2,1)}) custom-call(bf16[2,256,3072]{2,1,0:T(8,128)(2,1)} %bitcast.92, bf16[2,256,3072]{2,1,0:T(8,128)(2,1)} %get-tuple-element.49.x_ref, ...), custom_call_target="tpu_custom_call" | custom-call | flops 8053063680 | bytes 100000000 | tf_op jit(solution)/shard_map/scan_backward/pallas_call | solution.py:1642
  354.3 21.0 %back_stage.1 = (bf16[512,1536]{1,0:T(8,128)(2,1)}, f32[1,1536]{1,0:T(1,128)}) custom-call(bf16[512,3072]{1,0:T(8,128)(2,1)} %get-tuple-element.47.dgate_ref.d_ref, bf16[512,3584]{1,0:T(8,128)(2,1)} %bitcast.67, bf16[512,3584]{1,0:T(8,128)(2,1)} %bitcast.68, bf16[128,1536]{1,0:T(8,128)(2,1)} %copy-done.1, bf16[6448,384]{1,0:T(8,128)(2,1)} %bitcast.66, ...), custom_call_target="tpu_custom_call" | custom-call | tf_op jit(solution)/shard_map/back_stage/pallas_call | solution.py:1940
  375.4 0.7 reduce
  376.1 0.1 reshape.161
  376.2 0.1 reshape.162
  376.4 0.1 reshape_squeeze.19
  376.5 0.8 slice_reduce_fusion
  377.3 0.1 reshape_squeeze.20
  377.4 0.1 reshape_squeeze.21
  377.5 0.1 reshape_squeeze.22
  377.5 0.5 broadcast.31
  378.1 0.0 copy-done.9
  378.1 0.7 reduce.17
  378.8 0.1 concatenate.10
  378.9 0.6 copy.44
  379.5 134.9 %weight_sums.1 = (bf16[2,14,2,2,2,16,384]{6,5,4,3,2,1,0:T(8,128)(2,1)}, bf16[2,6,2,2,2,16,768]{6,5,4,3,2,1,0:T(8,128)(2,1)}, f32[48,128]{1,0:T(8,128)}) custom-call(bf16[512,3584]{1,0:T(8,128)(2,1)} %bitcast.69, bf16[512,1536]{1,0:T(8,128)(2,1)} %copy-done.2, bf16[512,1536]{1,0:T(8,128)(2,1)} %get-tuple-element.56.og_ref, ...), custom_call_target="tpu_custom_call" | custom-call | flops 28311552000 | bytes 400000000 | tf_op jit(solution)/shard_map/weight_sums/pallas_call | solution.py:913
  514.5 0.9 slice.79
  515.4 1.3 slice.95
  516.6 1.4 slice.99
  518.0 1.2 slice_bitcast_fusion.2
  519.3 1.4 fusion.3
  520.6 2.0 slice.94
  522.6 2.7 bitcast_convert_fusion
  525.3 6.0 %copy.33 = f32[1536,768]{0,1:T(8,128)} copy(f32[1536,768]{1,0:T(8,128)} %bitcast_convert_fusion) | data formatting | bytes 9437184 | tf_op jit(solution)/shard_map/convert_element_type | solution.py:2285
  531.4 0.7 reshape.166
  532.1 6.2 %convert_bitcast_fusion = f32[384,6448]{0,1:T(8,128)} fusion(bf16[3376,384]{1,0:T(8,128)(2,1)S(1)} %slice.94, bf16[3072,384]{1,0:T(8,128)(2,1)} %bitcast.75), kind=kLoop, calls=%fused_computation | loop fusion | flops 9904128 | bytes 14856192 | tf_op jit(solution)/shard_map/transpose | solution.py:2284
  (30 shorter events, 0.3 us)
Async XLA Ops:
  7.2 94.9 %copy-start.10 = (s32[2,1]{0,1:T(1,128)S(1)}, s32[2,1]{0,1:T(1,128)}, u32[]{:S(2)}) copy-start(s32[2,1]{0,1:T(1,128)} %param.13) | copy-start | bytes 28
  7.2 95.8 %all-reduce.7.cloned.1.call-start = ((), (), s32[]{:S(2)}) async-start(), calls=%async_computation | async-start | bytes 380928
  15.6 0.7 copy-start.6
  16.3 92.6 %copy-start = (bf16[2,1,256,1536]{3,2,1,0:T(8,128)(2,1)S(1)}, bf16[2,1,256,1536]{3,2,1,0:T(8,128)(2,1)}, u32[]{:S(2)}) copy-start(bf16[2,1,256,1536]{3,2,1,0:T(8,128)(2,1)} %param.12) | copy-start | bytes 4718596
  104.6 15.5 %copy-start.3 = (f32[1,1,4,384]{3,1,2,0:T(1,128)}, f32[1,1,4,384]{3,1,2,0:T(1,128)S(1)}, u32[]{:S(2)}) copy-start(f32[1,1,4,384]{3,1,2,0:T(1,128)S(1)} %copy.36) | copy-start | bytes 18436
  104.7 15.5 %copy-start.1 = (bf16[128,1536]{1,0:T(8,128)(2,1)}, bf16[128,1536]{1,0:T(8,128)(2,1)S(1)}, u32[]{:S(2)}) copy-start(bf16[128,1536]{1,0:T(8,128)(2,1)S(1)} %pad.17.dtw_ref) | copy-start | bytes 1179652
  120.1 1.2 copy-start.2
  121.3 0.7 copy-start.4
  354.3 21.8 %copy-start.7 = (f32[4,3328]{1,0:T(4,128)S(1)}, f32[4,3328]{1,0:T(4,128)}, u32[]{:S(2)}) copy-start(f32[4,3328]{1,0:T(4,128)} %get-tuple-element.59) | copy-start | bytes 159748
  354.3 22.0 %copy-start.8 = (f32[1,3328]{1,0:T(1,128)S(1)}, f32[1,3328]{1,0:T(1,128)}, u32[]{:S(2)}) copy-start(f32[1,3328]{1,0:T(1,128)} %get-tuple-element.60) | copy-start | bytes 39940
  354.3 23.7 %copy-start.9 = (f32[1,3072]{1,0:T(1,128)S(1)}, f32[1,3072]{1,0:T(1,128)}, u32[]{:S(2)}) copy-start(f32[1,3072]{1,0:T(1,128)} %get-tuple-element.62) | copy-start | bytes 36868
  514.5 8.2 %copy-start.5 = (bf16[2,6,2,2,2,16,768]{6,5,4,3,2,1,0:T(8,128)(2,1)S(1)}, bf16[2,6,2,2,2,16,768]{6,5,4,3,2,1,0:T(8,128)(2,1)}, u32[]{:S(2)}) copy-start(bf16[2,6,2,2,2,16,768]{6,5,4,3,2,1,0:T(8,128)(2,1)} %get-tuple-element.66) | copy-start | bytes 7077892
Sparse Core Ops, SparseCore 0:
  16.4 42.5 all-reduce.6

commit v7 on v6

--- a/solution.py
+++ b/solution.py
@@ -396,7 +396,7 @@
 
 
 class Gather:
-    def __init__(self, place, items, send, recv):
+    def __init__(self, place, items, send, recv, own=None):
         s, z, c, x, y, near = place
         sx, sy, sd = s + 2 - 4 * x, s + 4 - 8 * y, s + 6 - 4 * x - 8 * y
         self.plans = []
@@ -422,15 +422,22 @@
                     block = target.at[pl.ds(0, 3), rows(who)]
                     return move(block, block, kind, to)
 
-                plan = {}
-                for k in (1, 2, 3):
-                    there = target.at[k - 1, rows(s)]
-                    plan["z%d" % k] = move(source.at[rows(s, base)], there, k - 1, "z%d" % k)
-                plan["x"] = along(s, 3, "x")
-                plan["y"] = along(s, 4, "y")
+                plan = {"fetched": base is None}
+                if base is None:
+                    have = source.at[:, pl.ds(off, size)]
+                    block = target.at[pl.ds(0, 3), rows(s)]
+                    plan["own"] = pltpu.make_async_copy(have, block, own.at[q])
+                    for kind, name in ((3, "x"), (4, "y"), (6, "c0")):
+                        plan[name] = move(have, block, kind, name[0])
+                else:
+                    for k in (1, 2, 3):
+                        there = target.at[k - 1, rows(s)]
+                        plan["z%d" % k] = move(source.at[rows(s, base)], there, k - 1, "z%d" % k)
+                    plan["x"] = along(s, 3, "x")
+                    plan["y"] = along(s, 4, "y")
+                    plan["c0"] = along(s, 6, "c")
                 first = "xy"[i % 2]
                 plan["d"] = along(sx, 5, "y") if first == "x" else along(sy, 5, "x")
-                plan["c0"] = along(s, 6, "c")
                 plan["cx"] = along(sx, 7, "c")
                 plan["cy"] = along(sy, 8, "c")
                 plan["cd"] = along(sd, 9, "c")
@@ -444,8 +451,11 @@
 
     def begin(self, i):
         plan = self.plans[i]
-        for k in (1, 2, 3):
-            plan["z%d" % k].wait_recv()
+        if plan["fetched"]:
+            plan["own"].start()
+        else:
+            for k in (1, 2, 3):
+                plan["z%d" % k].wait_recv()
         for name in ("x", "y", "c0"):
             plan[name].start()
 
@@ -462,7 +472,7 @@
         self.plans[i]["d"].wait_recv()
         self.plans[i]["cd"].start()
 
-    def run(self):
+    def run(self, last):
         n = len(self.plans)
         for i in range(min(AHEAD, n)):
             self.fetch(i)
@@ -471,6 +481,8 @@
                 self.begin(i)
                 if i + AHEAD < n:
                     self.fetch(i + AHEAD)
+                if i + AHEAD == n - 1:
+                    last()
             if 0 <= i - 1 < n:
                 self.middle(i - 1)
             if 0 <= i - 2 < n:
@@ -481,47 +493,83 @@
             for name in ("c0", "cx", "cy", "cd"):
                 plan[name].wait_recv()
             for name in ("z1", "z2", "z3", "x", "y", "d", "c0", "cx", "cy", "cd"):
-                plan[name].wait_send()
-
-
-def gather_kernel(inner, channels, parts, w_ref, conv_ref, gate_ref, own, own_sem, send, recv):
+                if name in plan:
+                    plan[name].wait_send()
+            if plan["fetched"]:
+                plan["own"].wait()
+
+
+def gather_kernel(
+    inner, channels, parts, w_ref, ow_ref, conv_ref, gate_ref, eighth_ref, own, own_sem, send, recv, o_send, o_recv
+):
     place = around()
     inward = pltpu.make_async_copy(w_ref.at[pl.ds(inner, channels)], own, own_sem)
     inward.start()
     greet(place[-1])
     items = [(w_ref, inner, conv_ref, channels, parts), (w_ref, 0, gate_ref, inner, parts)]
     work = Gather(place, items, send, recv)
-    work.run()
+    piece = eighth_ref.shape[1]
+    mine = pl.ds(pl.multiple_of(place[0] * piece, 16), piece)
+    eighths = [
+        pltpu.make_async_remote_copy(
+            src_ref=ow_ref.at[mine],
+            dst_ref=eighth_ref.at[k - 1],
+            send_sem=o_send.at[k - 1],
+            recv_sem=o_recv.at[k - 1],
+            device_id=place[-1]["z%d" % k],
+            device_id_type=MESH,
+        )
+        for k in (1, 2, 3)
+    ]
+
+    def last():
+        for copy in eighths:
+            copy.start()
+
+    work.run(last)
     inward.wait()
     outward = pltpu.make_async_copy(own, conv_ref.at[3], own_sem)
     outward.start()
     work.close()
+    for copy in eighths:
+        copy.wait()
     outward.wait()
 
 
-def gather_input_weight(w_t, inner, channels, parts=6):
+def gather_input_weight(w_t, out_weight, inner, channels, parts=6):
     width = w_t.shape[1]
     hbm = pl.BlockSpec(memory_space=pl.ANY)
     return pl.pallas_call(
         partial(gather_kernel, inner, channels, parts),
-        in_specs=[hbm],
-        out_specs=[hbm] * 2,
+        in_specs=[hbm] * 2,
+        out_specs=[hbm] * 3,
         out_shape=[
             jax.ShapeDtypeStruct((4, channels, width), bf16),
             jax.ShapeDtypeStruct((3, inner, width), bf16),
+            jax.ShapeDtypeStruct((3, out_weight.shape[0] // 8, out_weight.shape[1]), bf16),
         ],
         scratch_shapes=[
             pltpu.VMEM((channels, width), bf16),
             pltpu.SemaphoreType.DMA,
             pltpu.SemaphoreType.DMA((2 * parts, CHUNK_DMAS)),
             pltpu.SemaphoreType.DMA((2 * parts, CHUNK_DMAS)),
+            pltpu.SemaphoreType.DMA((3,)),
+            pltpu.SemaphoreType.DMA((3,)),
         ],
         compiler_params=pltpu.CompilerParams(
             collective_id=1, has_side_effects=True, vmem_limit_bytes=VMEM_MOST
         ),
         cost_estimate=pl.CostEstimate(flops=0, bytes_accessed=200_000_000, transcendentals=0),
         name="gather_input_weight",
-    )(w_t)
+    )(w_t, out_weight)
+
+
+class Here:
+    def __init__(self, copy):
+        self.start, self.wait_recv = copy.start, copy.wait
+
+    def wait_send(self):
+        pass
 
 
 class Products:
@@ -552,7 +600,7 @@
         return [
             pltpu.VMEM((2 * rows, wide), bf16),
             pltpu.VMEM((2 * rows, width), bf16),
-            pltpu.VMEM((2, 128, width), f32),
+            pltpu.VMEM((4, 128, width), f32),
             pltpu.VMEM((2, 32, width), bf16),
             pltpu.VMEM((2, 32, width), bf16),
             pltpu.VMEM((2, 16, width), bf16),
@@ -574,7 +622,7 @@
             dma((2, len(marks) - 1, 8)),
         ]
 
-    def __init__(self, place, a_refs, b_ref, out, scratch):
+    def __init__(self, place, a_refs, b_ref, out, scratch, b_far=None):
         self.s, self.z, self.c, self.x, self.y, self.near = place
         (
             self.a,
@@ -609,12 +657,13 @@
         rows = self.a.shape[0] // 2
         near, far = pl.ds(0, rows), pl.ds(rows, rows)
         self.operands = []
+        to = self.b.at[far]
+        if b_far is None:
+            there = self.remote(b_ref, to, self.s_in.at[0], self.r_in.at[0], "c")
+        else:
+            there = Here(pltpu.make_async_copy(b_far, to, self.s_in.at[0]))
         self.operands.append(
-            (
-                0,
-                pltpu.make_async_copy(b_ref, self.b.at[near], self.in_sem.at[0]),
-                self.remote(b_ref, self.b.at[far], self.s_in.at[0], self.r_in.at[0], "c"),
-            )
+            (0, pltpu.make_async_copy(b_ref, self.b.at[near], self.in_sem.at[0]), there)
         )
         at = 0
         for i, ref in enumerate(a_refs):
@@ -702,35 +751,41 @@
                     here.wait()
                     there.wait_recv()
 
-            slot = t % 2
-            cols = pl.ds(pl.multiple_of(t * 128, 128), 128)
-            g[slot] = mm(self.a[:, cols], self.b[...], TN)
+            slot, now = t % 2, t % 4
+
+            @pl.when(slot == 0)
+            def _():
+                cols = pl.ds(pl.multiple_of(t * 128, 256), 256)
+                both = mm(self.a[:, cols], self.b[...], TN)
+                g[now] = both[:128]
+                g[now + 1] = both[128:]
+
             free(0, t)
             free(1, t)
-            self.sa1[slot] = g[slot, sl((1 - x) * 32, 32)].astype(bf16)
+            self.sa1[slot] = g[now, sl((1 - x) * 32, 32)].astype(bf16)
             copy(0, t).start()
-            self.sb1[slot, 0:16] = g[slot, sl(64 + (1 - y) * 16)].astype(bf16)
-            self.sb1[slot, 16:32] = g[slot, sl(96 + (1 - y) * 16)].astype(bf16)
+            self.sb1[slot, 0:16] = g[now, sl(64 + (1 - y) * 16)].astype(bf16)
+            self.sb1[slot, 16:32] = g[now, sl(96 + (1 - y) * 16)].astype(bf16)
             copy(1, t).start()
 
         @pl.when((t >= 1) & (t - 1 < chunks))
         def _():
             u = t - 1
-            slot = u % 2
+            slot, then = u % 2, u % 4
             copy(0, u).wait_recv()
             free(2, u)
             self.sa2[slot] = (
-                g[slot, sl(x * 32 + (1 - y) * 16)] + ra1[u, sl((1 - y) * 16)].astype(f32)
+                g[then, sl(x * 32 + (1 - y) * 16)] + ra1[u, sl((1 - y) * 16)].astype(f32)
             ).astype(bf16)
             copy(2, u).start()
-            self.ka2[slot] = g[slot, sl(x * 32 + y * 16)] + ra1[u, sl(y * 16)].astype(f32)
+            self.ka2[slot] = g[then, sl(x * 32 + y * 16)] + ra1[u, sl(y * 16)].astype(f32)
             copy(1, u).wait_recv()
             free(3, u)
             self.sb2[slot] = (
-                g[slot, sl(64 + (1 - x) * 32 + y * 16)] + rb1[u, sl((1 - x) * 16)].astype(f32)
+                g[then, sl(64 + (1 - x) * 32 + y * 16)] + rb1[u, sl((1 - x) * 16)].astype(f32)
             ).astype(bf16)
             copy(3, u).start()
-            self.kb2[slot] = g[slot, sl(64 + x * 32 + y * 16)] + rb1[u, sl(x * 16)].astype(f32)
+            self.kb2[slot] = g[then, sl(64 + x * 32 + y * 16)] + rb1[u, sl(x * 16)].astype(f32)
 
         @pl.when((t >= 2) & (t - 2 < chunks))
         def _():
@@ -857,80 +912,255 @@
             self.copy(k).wait_send()
 
 
+class InputGrad:
+    TILE = 256
+    SCRATCH = 5
+
+    @staticmethod
+    def scratch(rows, width):
+        tile = InputGrad.TILE
+        return [
+            pltpu.VMEM((rows, width), f32),
+            pltpu.VMEM((128, width), f32),
+            pltpu.VMEM((2, rows, tile), bf16),
+            pltpu.VMEM((2, 4, tile, width // 4), bf16),
+            pltpu.SemaphoreType.DMA((3, 2)),
+        ]
+
+    def __init__(self, refs, out, gain_out, scratch):
+        (
+            self.gate,
+            self.rest,
+            self.own,
+            self.gate_others,
+            self.conv_shards,
+            self.d_dt,
+            self.dt_w,
+            self.h,
+            self.gain,
+            self.og,
+        ) = refs
+        self.out, self.gain_out = out, gain_out
+        self.acc, self.part, self.d, self.w, self.sems = scratch
+        self.early = self.gate.shape[1] // self.TILE
+        self.count = self.early + self.conv_shards.shape[1] // self.TILE
+
+    def copies(self, i, gate):
+        slot = i % 2
+        at = pl.ds(pl.multiple_of((i if gate else i - self.early) * self.TILE, self.TILE), self.TILE)
+        if gate:
+            pairs = (
+                (self.gate.at[:, at], self.d.at[slot]),
+                (self.own.at[at], self.w.at[slot, 3]),
+                (self.gate_others.at[:, at], self.w.at[slot, pl.ds(0, 3)]),
+            )
+        else:
+            pairs = (
+                (self.rest.at[:, at], self.d.at[slot]),
+                (self.conv_shards.at[3, at], self.w.at[slot, 3]),
+                (self.conv_shards.at[pl.ds(0, 3), at], self.w.at[slot, pl.ds(0, 3)]),
+            )
+        return [pltpu.make_async_copy(a, b, self.sems.at[k, slot]) for k, (a, b) in enumerate(pairs)]
+
+    def act(self, i, what):
+        @pl.when(i < self.early)
+        def _():
+            for copy in self.copies(i, True):
+                getattr(copy, what)()
+
+        @pl.when((i >= self.early) & (i < self.count))
+        def _():
+            for copy in self.copies(i, False):
+                getattr(copy, what)()
+
+    def start(self):
+        self.acc[...] = jnp.zeros_like(self.acc)
+        self.act(0, "start")
+
+    def step(self, i):
+        @pl.when(i < self.count)
+        def _():
+            self.act(i + 1, "start")
+            self.act(i, "wait")
+            slot = i % 2
+            weights = jnp.concatenate([self.w[slot, k] for k in (3, 0, 1, 2)], axis=1)
+            self.acc[...] += mm(self.d[slot], weights)
+
+    def close(self):
+        depth = self.w.shape[3]
+        tile = self.part.shape[0]
+        gain = self.gain[...]
+
+        def body(r, d_gain):
+            at = pl.ds(pl.multiple_of(r * tile, tile), tile)
+            for k in range(4):
+                self.part[:, shard_place(k, depth)] = self.acc[at, k * depth : (k + 1) * depth]
+            d = self.part[...] + mm(self.d_dt[at, :], self.dt_w[...])
+            h = self.h[at, :].astype(f32)
+            scale = lax.rsqrt(jnp.mean(h * h, axis=-1, keepdims=True) + epsilon)
+            d_gain = d_gain + jnp.sum(d * (h * scale), axis=0, keepdims=True)
+            d = d * gain
+            along = jnp.mean(d * h, axis=-1, keepdims=True) * (scale * scale * scale)
+            self.out[at, :] = (scale * d - h * along + self.og[at, :].astype(f32)).astype(bf16)
+            return d_gain
+
+        d_gain = lax.fori_loop(0, self.out.shape[0] // tile, body, jnp.zeros(gain.shape, f32))
+        for a in range(4):
+            for r in range(depth // LANES):
+                at = a * depth + r * LANES
+                self.gain_out[a, r : r + 1, :] = d_gain[:, at : at + LANES]
+
+
 def sums_kernel(
-    conv_ref,
+    gate_ref,
+    rest_ref,
     nm_ref,
+    far_ref,
     og_ref,
     no_ref,
+    own_ref,
+    gate_others_ref,
+    conv_shards_ref,
     v_ref,
+    d_dt_ref,
+    dt_w_ref,
+    h_ref,
+    gain_ref,
+    cot_ref,
     in_out,
     out_out,
     v_out,
+    input_out,
+    small_v,
     *scratch,
 ):
     place = around()
     cut = Products.SCRATCH
-    inp = Products(place, [conv_ref], nm_ref, in_out, scratch[:cut])
+    inp = Products(place, [rest_ref], nm_ref, in_out, scratch[:cut], far_ref)
     outp = Products(place, [og_ref], no_ref, out_out, scratch[cut : 2 * cut])
-    small = Smalls(place, v_ref, v_out, scratch[2 * cut :])
+    small = Smalls(place, small_v, v_out, scratch[2 * cut : 2 * cut + Smalls.SCRATCH])
+    back = InputGrad(
+        [
+            gate_ref,
+            rest_ref,
+            own_ref,
+            gate_others_ref,
+            conv_shards_ref,
+            d_dt_ref,
+            dt_w_ref,
+            h_ref,
+            gain_ref,
+            cot_ref,
+        ],
+        input_out,
+        small_v,
+        scratch[2 * cut + Smalls.SCRATCH :],
+    )
+    inp.load()
     outp.load()
-    inp.load()
+    back.start()
+    small_v[...] = v_ref[...]
     greet(place[-1])
+    inp.share()
     outp.share()
+    each = -(-back.count // (inp.chunks - 1))
+
+    def first(t, carry):
+        inp.step(t)
+
+        def tile(i, carry):
+            back.step(t * each + i)
+            return carry
+
+        lax.fori_loop(0, each, tile, 0)
+        return carry
+
+    lax.fori_loop(0, inp.chunks, first, 0)
+    back.close()
     small.start()
-    inp.share()
-
-    def first(t, carry):
+
+    def second(t, carry):
         outp.step(t)
-        return carry
-
-    lax.fori_loop(0, outp.chunks, first, 0)
-
-    def second(t, carry):
-        inp.step(t)
-
-        @pl.when(t < outp.steps() - outp.chunks)
+
+        @pl.when(t < inp.steps() - inp.chunks)
         def _():
-            outp.step(t + outp.chunks)
+            inp.step(t + inp.chunks)
 
         for kind in range(3):
 
-            @pl.when(t == 2 * kind + 1)
+            @pl.when(t == kind + 1)
             def _(kind=kind):
                 small.advance(kind)
 
         return carry
 
-    lax.fori_loop(0, inp.steps(), second, 0)
+    lax.fori_loop(0, outp.steps(), second, 0)
     small.close()
+    inp.close()
     outp.close()
-    inp.close()
-
-
-def weight_sums(d_rest, nm, og, no, v, collective_id):
+
+
+def weight_sums(
+    d_gate,
+    d_rest,
+    nm,
+    nm_far,
+    og,
+    no,
+    own,
+    gate_others,
+    conv_shards,
+    v,
+    d_dt,
+    dt_w,
+    hidden,
+    gain,
+    out_grad,
+    collective_id,
+):
     vmem = pl.BlockSpec(memory_space=pltpu.VMEM)
     hbm = pl.BlockSpec(memory_space=pl.ANY)
-    a_in, a_out, total = pl.pallas_call(
+    rows, width = hidden.shape
+    a_in, a_out, total, input_grad = pl.pallas_call(
         sums_kernel,
-        in_specs=[hbm] * 4 + [vmem],
-        out_specs=[vmem] * 3,
+        in_specs=[hbm] * 9 + [vmem] * 6,
+        out_specs=[vmem] * 4,
         out_shape=[
             Products.out_shape([d_rest], nm),
             Products.out_shape([og], no),
             jax.ShapeDtypeStruct(v.shape[1:], f32),
+            jax.ShapeDtypeStruct((rows, width), bf16),
         ],
-        scratch_shapes=Products.scratch([d_rest], nm)
+        scratch_shapes=[pltpu.VMEM(v.shape, f32)]
+        + Products.scratch([d_rest], nm)
         + Products.scratch([og], no)
-        + Smalls.scratch(v),
+        + Smalls.scratch(v)
+        + InputGrad.scratch(rows, width),
         compiler_params=pltpu.CompilerParams(
             collective_id=collective_id, has_side_effects=True, vmem_limit_bytes=VMEM_MOST
         ),
         cost_estimate=pl.CostEstimate(
-            flops=6 * nm.shape[0] * nm.shape[1] * 6000, bytes_accessed=400_000_000, transcendentals=0
+            flops=12 * rows * width * 6000, bytes_accessed=400_000_000, transcendentals=0
         ),
         name="weight_sums",
-    )(d_rest, nm, og, no, v)
-    return a_in.reshape(d_rest.shape[1], -1), a_out.reshape(og.shape[1], -1), total
+    )(
+        d_gate,
+        d_rest,
+        nm,
+        nm_far,
+        og,
+        no,
+        own,
+        gate_others,
+        conv_shards,
+        v,
+        d_dt,
+        dt_w,
+        hidden,
+        gain,
+        out_grad,
+    )
+    return a_in.reshape(d_rest.shape[1], -1), a_out.reshape(og.shape[1], -1), total, input_grad
 
 
 LANES = 128
@@ -1112,7 +1342,7 @@
     shift_ref,
     rate_ref,
     skip_ref,
-    ow_ref,
+    eighth_ref,
     x_ref,
     bc_ref,
     y_ref,
@@ -1122,7 +1352,7 @@
     others_ref,
     *scratch,
 ):
-    buf, wide_buf, scores, dts, cums, rows_t, h_send, h_recv, o_send, o_recv = scratch[EXCHANGE:]
+    buf, wide_buf, scores, dts, cums, rows_t, h_send, h_recv, o_send, o_recv, o_own = scratch[EXCHANGE:]
     ex = Exchange(True, *scratch[:EXCHANGE])
     s, z = ex.s, ex.z
     micro, t, channels = conv_ref.shape
@@ -1132,11 +1362,13 @@
     groups = inner // gc
     half_t = t // 2
     place = around()
-    near = dict(place[-1])
+    near = {k: ex.near[k] for k in ("c", "x", "y")}
     near["next"] = ((s + 1) % 8, z)
     near["last"] = ((s + 7) % 8, z)
     greet(near)
-    weight = Gather(place, [(ow_ref, 0, others_ref, ow_ref.shape[0], 2)], o_send, o_recv)
+    weight = Gather(
+        place, [(eighth_ref, None, others_ref, others_ref.shape[1], 2)], o_send, o_recv, o_own
+    )
 
     tail = [
         pltpu.make_async_remote_copy(
@@ -1151,8 +1383,7 @@
     ]
     for copy in tail:
         copy.start()
-    weight.fetch(0)
-    weight.fetch(1)
+    weight.begin(0)
     for m in range(micro):
         dt, cum = steps_of(raw_ref[m], shift_ref[...], rate_ref[...])
         dts[m] = dt
@@ -1232,23 +1463,22 @@
     ex.along_x(0)
     own_states(1, middle, groups)
     ex.core(1)
-    weight.begin(0)
+    weight.begin(1)
     local_scans(0, 0, middle)
     ex.along_x(1)
     ex.along_y(0)
-    weight.begin(1)
     local_scans(0, middle, groups)
     weight.middle(0)
     local_scans(1, 0, middle)
     ex.along_y(1)
+    weight.middle(1)
+    weight.finish(0)
     ex.back_to_core(0)
-    weight.middle(1)
     local_scans(1, middle, groups)
     ex.begin_state(0, begin_ref)
     carried(0)
+    weight.finish(1)
     ex.back_to_core(1)
-    weight.finish(0)
-    weight.finish(1)
     ex.begin_state(1, begin_ref)
     carried(1)
     weight.close()
@@ -1258,7 +1488,7 @@
 
 
 def scan_forward(
-    conv_low, raw, conv_w, conv_b, shift, rate, skip_wide, out_weight, inner, hs, collective_id
+    conv_low, raw, conv_w, conv_b, shift, rate, skip_wide, out_eighth, inner, hs, collective_id
 ):
     micro, t, channels = conv_low.shape
     n = (channels - inner) // 2
@@ -1268,7 +1498,7 @@
     hbm = pl.BlockSpec(memory_space=pl.ANY)
     return pl.pallas_call(
         partial(scan_forward_kernel, hs),
-        in_specs=[vmem] * 7 + [hbm],
+        in_specs=[vmem] * 8,
         out_specs=[vmem] * 6 + [hbm],
         out_shape=[
             jax.ShapeDtypeStruct((micro, t, inner), bf16),
@@ -1277,7 +1507,7 @@
             jax.ShapeDtypeStruct((micro, t, inner), bf16),
             jax.ShapeDtypeStruct((micro, HALO, channels), bf16),
             jax.ShapeDtypeStruct((micro, n, inner), bf16),
-            jax.ShapeDtypeStruct((3,) + out_weight.shape, bf16),
+            jax.ShapeDtypeStruct((3, 8 * out_eighth.shape[1], out_eighth.shape[2]), bf16),
         ],
         scratch_shapes=exchange_scratch(micro, n, inner)
         + [
@@ -1291,6 +1521,7 @@
             dma((micro,)),
             dma((2, CHUNK_DMAS)),
             dma((2, CHUNK_DMAS)),
+            dma((2,)),
         ],
         compiler_params=pltpu.CompilerParams(
             collective_id=collective_id, has_side_effects=True, vmem_limit_bytes=VMEM_MOST
@@ -1299,7 +1530,7 @@
             flops=4 * micro * t * inner * (t + 3 * n), bytes_accessed=100_000_000, transcendentals=0
         ),
         name="scan_forward",
-    )(conv_low, raw, conv_w, conv_b, shift, rate, skip_wide, out_weight)
+    )(conv_low, raw, conv_w, conv_b, shift, rate, skip_wide, out_eighth)
 
 
 def scan_backward_kernel(
@@ -1324,6 +1555,8 @@
     dcb_ref,
     heads_ref,
     sum_ref,
+    far_ref,
+    far_sem,
     *scratch,
 ):
     (
@@ -1605,7 +1838,11 @@
         sums_of.step(i)
         return carry
 
+    rows = far_ref.shape[0]
+    far = pltpu.make_async_copy(sums_of.b.at[pl.ds(rows, rows)], far_ref, far_sem)
+    far.start()
     lax.fori_loop(done, sums_of.steps(), rest_of, 0)
+    far.wait()
     ex.sent()
     for copy in first_rows:
         copy.wait_send()
@@ -1642,15 +1879,17 @@
     return pl.pallas_call(
         partial(scan_backward_kernel, hs),
         in_specs=[vmem] * 3 + [hbm] + [vmem] * 9 + [hbm] * 2,
-        out_specs=[vmem] * 5,
+        out_specs=[vmem] * 5 + [hbm],
         out_shape=[
             jax.ShapeDtypeStruct((micro, t, -(-(channels + LANES) // 256) * 256), bf16),
             jax.ShapeDtypeStruct((taps, channels), f32),
             jax.ShapeDtypeStruct((1, channels), f32),
             jax.ShapeDtypeStruct((8, LANES), f32),
             Products.out_shape([d_gate], normed),
+            jax.ShapeDtypeStruct(normed.shape, bf16),
         ],
-        scratch_shapes=exchange_scratch(micro, n, inner)
+        scratch_shapes=[dma]
+        + exchange_scratch(micro, n, inner)
         + [
             pltpu.VMEM((2, t, gc), f32),
             dma((2,)),
@@ -1866,101 +2105,21 @@
     )(scanned, normed, own, others, gain, out_own, out_others, hidden, out_grad, valid)
 
 
-def back_kernel(
-    steps,
-    d_ref,
-    e_ref,
-    dt_ref,
-    dtw_ref,
-    w_ref,
-    v_ref,
-    cv_ref,
-    h_ref,
-    g_ref,
-    og_ref,
-    out_ref,
-    dg_ref,
-    acc,
-    full,
-):
-    depth = w_ref.shape[1]
-    i = pl.program_id(0)
-
-    def product(ref, *shards):
-        return mm(ref[...], jnp.concatenate(shards, axis=1))
-
-    gate_shards = [w_ref] + [v_ref.at[k] for k in range(3)]
-    conv_shards = [cv_ref.at[k] for k in (3, 0, 1, 2)]
-
-    @pl.when(i == 0)
-    def _():
-        acc[...] = product(d_ref, *[r[...] for r in gate_shards])
-
-    @pl.when((i > 0) & (i < steps))
-    def _():
-        acc[...] += product(d_ref, *[r[...] for r in gate_shards])
-
-    @pl.when(i >= steps)
-    def _():
-        acc[...] += product(e_ref, *[r[...] for r in conv_shards])
-
-    @pl.when(i == pl.num_programs(0) - 1)
-    def _():
-        for k in range(4):
-            full[:, shard_place(k, depth)] = acc[:, k * depth : (k + 1) * depth]
-        tile = 128
-        gain = g_ref[...]
-        d_gain = jnp.zeros(gain.shape, f32)
-        for r in range(full.shape[0] // tile):
-            at = slice(r * tile, (r + 1) * tile)
-            d = full[at, :] + mm(dt_ref[at, :], dtw_ref[...])
-            h = h_ref[at, :].astype(f32)
-            scale = lax.rsqrt(jnp.mean(h * h, axis=-1, keepdims=True) + epsilon)
-            d_gain += jnp.sum(d * (h * scale), axis=0, keepdims=True)
-            d = d * gain
-            along = jnp.mean(d * h, axis=-1, keepdims=True) * (scale * scale * scale)
-            out_ref[at, :] = (scale * d - h * along + og_ref[at, :].astype(f32)).astype(bf16)
-        dg_ref[...] = d_gain
-
-
-def back_stage(d, e, dt_w, gate_own, gate_others, shards, hidden, gain, out_grad, tiles):
-    rows, width = hidden.shape
-    _, count, depth = shards.shape
-    inner = d.shape[1]
-    steps, more = inner // tiles[0], count // tiles[1]
-    whole = pl.BlockSpec((rows, width), lambda i: (0, 0))
-    line = pl.BlockSpec((1, width), lambda i: (0, 0))
-
-    def early(i):
-        return jnp.minimum(i, steps - 1)
-
-    def late(i):
-        return jnp.maximum(i - steps, 0)
-
+def turn_kernel(x_ref, o_ref):
+    o_ref[...] = x_ref[...].astype(f32).T
+
+
+def turned(x, tile):
+    rows, columns = x.shape
     return pl.pallas_call(
-        partial(back_kernel, steps),
-        grid=(steps + more,),
-        in_specs=[
-            pl.BlockSpec((rows, tiles[0]), lambda i: (0, early(i))),
-            pl.BlockSpec((rows, tiles[1]), lambda i: (0, late(i))),
-            pl.BlockSpec((rows, LANES), lambda i: (0, count // LANES)),
-            pl.BlockSpec((LANES, width), lambda i: (0, 0)),
-            pl.BlockSpec((tiles[0], depth), lambda i: (early(i), 0)),
-            pl.BlockSpec((3, tiles[0], depth), lambda i: (0, early(i), 0)),
-            pl.BlockSpec((4, tiles[1], depth), lambda i: (0, late(i), 0)),
-            whole,
-            line,
-            whole,
-        ],
-        out_specs=[whole, line],
-        out_shape=[
-            jax.ShapeDtypeStruct((rows, width), bf16),
-            jax.ShapeDtypeStruct((1, width), f32),
-        ],
-        scratch_shapes=[pltpu.VMEM((rows, width), f32), pltpu.VMEM((rows, width), f32)],
-        compiler_params=pltpu.CompilerParams(vmem_limit_bytes=VMEM_MOST),
-        name="back_stage",
-    )(d, e, e, dt_w, gate_own, gate_others, shards, hidden, gain, out_grad)
+        turn_kernel,
+        grid=(rows // tile,),
+        in_specs=[pl.BlockSpec((tile, columns), lambda i: (i, 0))],
+        out_specs=pl.BlockSpec((columns, tile), lambda i: (0, i)),
+        out_shape=jax.ShapeDtypeStruct((columns, rows), f32),
+        compiler_params=pltpu.CompilerParams(vmem_limit_bytes=VMEM),
+        name="turned",
+    )(x)
 
 
 def project_kernel(n_ref, w_ref, v_ref, o_ref):
@@ -2096,7 +2255,9 @@
     dt_w = packed_low[:, at:].reshape(shards, heads, -1).transpose(1, 0, 2).reshape(heads, -1)
     order = jnp.arange(shards) ^ shard
     if fast:
-        conv_shards, gate_others = gather_input_weight(in_local, inner, channels)
+        conv_shards, gate_others, out_eighth = gather_input_weight(
+            in_local, out_weight, inner, channels
+        )
     else:
         every = lax.all_gather(in_local[: inner + channels], "wshard", axis=0)
         in_w = every[order[1:]]
@@ -2141,7 +2302,7 @@
             to_lanes(dt_shift[None, :]),
             to_lanes(rate[None, :]),
             skip_wide,
-            out_weight,
+            out_eighth,
             inner,
             hs,
             3,
@@ -2196,7 +2357,7 @@
         d_gate_low = d_gate_in.astype(bf16)
 
     if fast:
-        d_rest, d_conv_w, d_conv_b, by_head, gate_sum = scan_backward(
+        d_rest, d_conv_w, d_conv_b, by_head, gate_sum, normed_far = scan_backward(
             dy,
             x_low,
             bc_low,
@@ -2218,20 +2379,7 @@
         d_dt_bias, d_a_log, d_skip = by_head[0, :heads], by_head[1, :heads], by_head[2, :heads]
         d_conv_b = d_conv_b[0]
         d_rest = d_rest.reshape(rows, -1)
-        input_grad, d_norm_g = back_stage(
-            d_gate_low,
-            d_rest,
-            dt_wide,
-            in_local,
-            gate_others,
-            conv_shards,
-            hidden_rows,
-            norm_g[None, :],
-            out_grad_rows,
-            (inner // 2, channels // 2),
-        )
-        input_grad = input_grad.reshape(hidden.shape)
-        d_norm_g = d_norm_g[0]
+        d_norm_g = jnp.zeros((width,), f32)
     else:
         own_grad = block_states(dy, decay_w, c_low.transpose(0, 2, 1), hs)
         dx_local, db_local, dc_local = local_back(x_low, dy, dt_g, cum_g, row_g, b_low, c_low, hs)
@@ -2279,10 +2427,28 @@
     smalls = jnp.concatenate(smalls, axis=1)
     if fast:
         smalls = jnp.pad(smalls, ((0, 0), (0, -smalls.shape[1] % 1024))).reshape(shards, -1, LANES)
-        rest_sum, out_sum, sums = weight_sums(d_rest, normed_low, g, normed_out_low, smalls, 2)
+        rest_sum, out_sum, sums, input_grad = weight_sums(
+            d_gate_low,
+            d_rest,
+            normed_low,
+            normed_far,
+            g,
+            normed_out_low,
+            in_local,
+            gate_others,
+            conv_shards,
+            smalls,
+            d_rest[:, channels : channels + LANES],
+            dt_wide,
+            hidden_rows,
+            norm_g[None, :],
+            out_grad_rows,
+            2,
+        )
+        input_grad = input_grad.reshape(hidden.shape)
         gate_sum = gate_sum.reshape(inner, -1)
         in_grad = jnp.concatenate([gate_sum, rest_sum[: total_cols - inner]]).astype(f32).T
-        out_w_grad = out_sum.T.astype(f32)
+        out_w_grad = turned(out_sum, 512)
         sums = sums.reshape(-1)
     else:
         d_proj = jnp.concatenate([d_gate_low, d_rest, d_dt_low], axis=1)

time: 555 us -> 533 us (0.960)
  Pallas kernels: 485 us -> 469 us
    pallas_call x3, Pallas kernels: 234 us -> 211 us  [the longest x1 139 us: weight_sums(): pl.pallas_call(sums_kernel, in_specs=[hbm] * 9 + [vmem] * 6, out_specs=[v...]
    convert_element_type x1 -> x0, local copies, waits for them, and re-layouts: 6.04 us -> none  [local(): out_w_grad = out_sum.T.astype(f32)]
  transfers between devices with their start and end apart: 1 -> 1, of which waited for: 0 -> 0; matrix products, arithmetic and copies ran while one was open for 0% -> 0% of each run, Pallas kernels for 16% -> 17%
where the time goes in v7:
time: 533 us; the launch traced here: 524 us
  Pallas kernels  469 us (88%)
  local copies, waits for them, and re-layouts  31.7 us (6%)
  between operations  15.2 us (3%)
  other arithmetic  7.94 us (1%)
    pallas_call x1, Pallas kernels, weight_sums(): pl.pallas_call(sums_kernel, in_specs=[hbm] * 9 + [vmem] * 6, out_specs=[v...  139 us
    pallas_call x1, Pallas kernels, scan_backward(): pl.pallas_call(partial(scan_backward_kernel, hs), in_specs=[vmem] * 3 + [...  128 us
    pallas_call x1, Pallas kernels, gather_input_weight(): pl.pallas_call(partial(gather_kernel, inner, channels, parts), in_specs=[...  90.4 us
    pallas_call x1, Pallas kernels, scan_forward(): pl.pallas_call(partial(scan_forward_kernel, hs), in_specs=[vmem] * 8, out...  69.3 us
    pallas_call x1, Pallas kernels, gate_stage(): pl.pallas_call(gate_kernel, grid=(rows // tile,), in_specs=[wide, slim, p...  28.6 us
    pallas_call x1, Pallas kernels, front(): pl.pallas_call(front_kernel, grid=(count // tile,), in_specs=[whole, pl.B...  11.2 us
  transfers between devices with their start and end apart: 1, of which 0 were waited for; matrix products, arithmetic and copies ran while one was open for 0% of the time, Pallas kernels for 17%

profile of v7, /device:TPU:0, one launch (start us, length us, event | category | flops | bytes accessed | tf_op | source)
XLA Modules:
  0.0 523.6 jit_solution(13987617789231063900)
XLA Ops:
  7.2 0.0 all-reduce.7.cloned.1.call-start
  7.2 0.8 slice.89
  8.0 0.8 reshape.149
  8.8 1.2 dynamic-slice
  10.7 4.2 concatenate.9
  14.9 0.6 dynamic-update-slice
  15.5 0.0 copy-start.7
  15.6 0.7 copy-done.7
  16.2 0.0 all-reduce.7.cloned.1.call-update
  16.2 0.0 copy-start.9
  16.3 90.4 %gather_input_weight.1 = (bf16[4,3328,384]{2,1,0:T(8,128)(2,1)}, bf16[3,3072,384]{2,1,0:T(8,128)(2,1)}, bf16[3,96,1536]{2,1,0:T(8,128)(2,1)}) custom-call(bf16[6448,384]{1,0:T(8,128)(2,1)} %bitcast.62, bf16[768,1536]{1,0:T(8,128)(2,1)} %ow_ref.3), custom_call_target="tpu_custom_call" | custom-call | bytes 200000000 | tf_op jit(solution)/shard_map/gather_input_weight/pallas_call | solution.py:542
  106.6 0.0 copy-start
  106.7 0.0 copy-done.9
  106.7 0.1 fusion
  106.8 0.9 copy.38
  107.6 1.1 reshape.174
  108.8 0.1 slice.91
  108.9 0.1 fusion.1
  109.0 0.1 fusion.2
  109.1 0.1 slice_bitcast_fusion
  109.2 0.0 copy-start.4
  109.3 0.0 copy-start.2
  109.3 0.1 neg.14
  109.4 0.1 reshape.157
  109.5 0.1 broadcast_in_dim.2
  109.5 0.7 broadcast_in_dim_reshape.21.skip_ref
  110.2 0.1 broadcast_in_dim_reshape.20
  110.3 0.5 pad.19.rate_ref
  110.8 0.5 pad.18.shift_ref
  111.3 0.1 reshape.155
  111.5 0.7 reshape.156.cw_ref
  112.2 0.7 broadcast_in_dim_reshape.19.cb_ref
  112.9 0.6 copy.36
  113.5 0.0 copy-done
  113.5 11.2 %front.1 = (bf16[512,3328]{1,0:T(8,128)(2,1)}, bf16[512,1536]{1,0:T(8,128)(2,1)S(1)}, f32[512,128]{1,0:T(8,128)S(1)}) custom-call(bf16[512,1536]{1,0:T(8,128)(2,1)S(1)} %bitcast.55, f32[1,1536]{1,0:T(1,128)S(1)} %bitcast.57, bf16[128,1536]{1,0:T(8,128)(2,1)S(1)} %pad.17.dtw_ref.dt_w_ref, bf16[4,3328,384]{2,1,0:T(8,128)(2,1)} %get-tuple-element.40.v_ref.conv_shards_ref), custom_call_target="tpu_custom_call" | custom-call | tf_op jit(solution)/shard_map/front/pallas_call | solution.py:1968
  124.7 1.1 copy-done.3
  125.9 0.7 copy-done.5
  126.6 69.3 %scan_forward.1 = (bf16[2,256,3072]{2,1,0:T(8,128)(2,1)}, bf16[2,256,256]{2,1,0:T(8,128)(2,1)}, f32[2,256,3072]{2,1,0:T(8,128)}, bf16[2,256,3072]{2,1,0:T(8,128)...) custom-call(bf16[2,256,3328]{2,1,0:T(8,128)(2,1)} %bitcast.87, ...), custom_call_target="tpu_custom_call" | custom-call | flops 4026531840 | bytes 100000000 | tf_op jit(solution)/shard_map/scan_forward/pallas_call | solution.py:1499
  195.9 28.6 %gate_stage.1 = (bf16[512,3072]{1,0:T(8,128)(2,1)}, bf16[512,1536]{1,0:T(8,128)(2,1)}, bf16[512,1536]{1,0:T(8,128)(2,1)}, bf16[512,3072]{1,0:T(8,128)(2,1)}, bf1...) custom-call(bf16[512,3072]{1,0:T(8,128)(2,1)} %bitcast.65, bf16[512,1536]{1,0:T(8,128)(2,1)} %copy-done.3, ...), custom_call_target="tpu_custom_call" | custom-call | tf_op jit(solution)/shard_map/gate_stage/pallas_call | solution.py:2074
  224.5 127.7 %scan_backward.1 = (bf16[2,256,3584]{2,1,0:T(8,128)(2,1)}, f32[4,3328]{1,0:T(4,128)}, f32[1,3328]{1,0:T(1,128)}, f32[8,128]{1,0:T(8,128)}, bf16[2,12,2,2,2,16,38...) custom-call(bf16[2,256,3072]{2,1,0:T(8,128)(2,1)} %bitcast.89, bf16[2,256,3072]{2,1,0:T(8,128)(2,1)} %get-tuple-element.51.x_ref, ...), custom_call_target="tpu_custom_call" | custom-call | flops 8053063680 | bytes 100000000 | tf_op jit(solution)/shard_map/scan_backward/pallas_call | solution.py:1879
  352.2 0.9 reshape.164
  353.1 0.1 reshape.165
  353.2 0.7 reduce
  354.0 0.1 reshape_squeeze.15
  354.0 0.8 slice_reduce_fusion
  354.8 0.1 reshape_squeeze.16
  354.9 0.1 reshape_squeeze.17
  355.0 0.1 reshape_squeeze.18
  355.1 0.5 broadcast.30
  355.6 0.7 reduce.16
  356.3 0.1 concatenate.10
  356.4 0.6 copy.42
  357.1 1.6 slice.98.d_dt_ref
  358.7 138.7 %weight_sums.1 = (bf16[2,14,2,2,2,16,384]{6,5,4,3,2,1,0:T(8,128)(2,1)}, bf16[2,6,2,2,2,16,768]{6,5,4,3,2,1,0:T(8,128)(2,1)}, f32[48,128]{1,0:T(8,128)}, bf16[512,1536]{1,0:T(8,128)(2,1)}) custom-call(bf16[512,3072]{1,0:T(8,128)(2,1)} %get-tuple-element.49.dgate_ref.gate_ref, bf16[512,3584]{1,0:T(8,128)(2,1)} %bitcast.85, bf16[512,1536]{1,0:T(8,128)(2,1)} %copy-done.3, ...), custom_call_target="tpu_custom_call" | custom-call | flops 56623104000 | bytes 400000000 | tf_op jit(solution)/shard_map/weight_sums/pallas_call | solution.py:1124
  497.3 0.9 slice.83
  498.2 1.3 slice.100
  499.5 1.4 slice.104
  500.9 1.3 slice_bitcast_fusion.2
  502.1 1.4 fusion.3
  503.5 2.0 slice.99
  505.5 2.9 turned.1
  508.4 0.7 reshape.170
  509.1 6.3 %convert_bitcast_fusion = f32[384,6448]{0,1:T(8,128)} fusion(bf16[3376,384]{1,0:T(8,128)(2,1)S(1)} %slice.99, bf16[3072,384]{1,0:T(8,128)(2,1)} %bitcast.67), kind=kLoop, calls=%fused_computation | loop fusion | flops 9904128 | bytes 14856192 | tf_op jit(solution)/shard_map/transpose | solution.py:2450
  515.4 1.1 copy.47
  (27 shorter events, 0.2 us)
Async XLA Ops:
  7.2 100.5 %all-reduce.7.cloned.1.call-start = ((), (), s32[]{:S(2)}) async-start(), calls=%async_computation | async-start | bytes 380928
  15.5 0.7 copy-start.7
  16.2 90.4 %copy-start.9 = (s32[2,1]{0,1:T(1,128)S(1)}, s32[2,1]{0,1:T(1,128)}, u32[]{:S(2)}) copy-start(s32[2,1]{0,1:T(1,128)} %param.13) | copy-start | bytes 28
  106.6 6.9 %copy-start = (bf16[2,1,256,1536]{3,2,1,0:T(8,128)(2,1)S(1)}, bf16[2,1,256,1536]{3,2,1,0:T(8,128)(2,1)}, u32[]{:S(2)}) copy-start(bf16[2,1,256,1536]{3,2,1,0:T(8,128)(2,1)} %param.12) | copy-start | bytes 4718596
  109.2 15.5 %copy-start.4 = (f32[1,1,4,384]{3,1,2,0:T(1,128)}, f32[1,1,4,384]{3,1,2,0:T(1,128)S(1)}, u32[]{:S(2)}) copy-start(f32[1,1,4,384]{3,1,2,0:T(1,128)S(1)} %copy.34) | copy-start | bytes 18436
  109.3 15.4 %copy-start.2 = (bf16[128,1536]{1,0:T(8,128)(2,1)}, bf16[128,1536]{1,0:T(8,128)(2,1)S(1)}, u32[]{:S(2)}) copy-start(bf16[128,1536]{1,0:T(8,128)(2,1)S(1)} %pad.17.dtw_ref.dt_w_ref) | copy-start | bytes 1179652
  124.7 1.1 copy-start.3
  125.9 0.7 copy-start.5
  224.5 131.1 %copy-start.8 = (f32[1,3072]{1,0:T(1,128)S(1)}, f32[1,3072]{1,0:T(1,128)}, u32[]{:S(2)}) copy-start(f32[1,3072]{1,0:T(1,128)} %get-tuple-element.63) | copy-start | bytes 36868
  497.3 8.2 %copy-start.1 = (bf16[2,6,2,2,2,16,768]{6,5,4,3,2,1,0:T(8,128)(2,1)S(1)}, bf16[2,6,2,2,2,16,768]{6,5,4,3,2,1,0:T(8,128)(2,1)}, u32[]{:S(2)}) copy-start(bf16[2,6,2,2,2,16,768]{6,5,4,3,2,1,0:T(8,128)(2,1)} %get-tuple-element.68) | copy-start | bytes 7077892
  509.1 6.3 %copy-start.6 = (bf16[512,1536]{1,0:T(8,128)(2,1)S(1)}, bf16[512,1536]{1,0:T(8,128)(2,1)}, u32[]{:S(2)}) copy-start(bf16[512,1536]{1,0:T(8,128)(2,1)} %get-tuple-element.64) | copy-start | bytes 4718596
Sparse Core Ops, SparseCore 0:
  16.4 42.5 all-reduce.6

commit v8 on v7

--- a/solution.py
+++ b/solution.py
@@ -570,6 +570,9 @@
 
     def wait_send(self):
         pass
+
+
+STAGE = 2
 
 
 class Products:
@@ -742,35 +745,61 @@
             def _():
                 copy(kind, u - 2).wait_send()
 
-        @pl.when(t < chunks)
+        @pl.when((t >= 3 * STAGE) & (t - 3 * STAGE < chunks))
         def _():
-            for first, here, there in self.operands:
-
-                @pl.when(t == first)
-                def _(here=here, there=there):
-                    here.wait()
-                    there.wait_recv()
-
-            slot, now = t % 2, t % 4
-
-            @pl.when(slot == 0)
-            def _():
-                cols = pl.ds(pl.multiple_of(t * 128, 256), 256)
-                both = mm(self.a[:, cols], self.b[...], TN)
-                g[now] = both[:128]
-                g[now + 1] = both[128:]
-
-            free(0, t)
-            free(1, t)
-            self.sa1[slot] = g[now, sl((1 - x) * 32, 32)].astype(bf16)
-            copy(0, t).start()
-            self.sb1[slot, 0:16] = g[now, sl(64 + (1 - y) * 16)].astype(bf16)
-            self.sb1[slot, 16:32] = g[now, sl(96 + (1 - y) * 16)].astype(bf16)
-            copy(1, t).start()
-
-        @pl.when((t >= 1) & (t - 1 < chunks))
+            u = t - 3 * STAGE
+            slot = u % 2
+            for k in (4, 5, 6):
+                copy(k, u).wait_recv()
+            mine = pl.ds(pl.multiple_of(z * self.shard, 128), self.shard)
+            for part in (0, 1):
+                total = self.f3[slot, part, :, mine]
+                for k in range(3):
+                    total = total + self.rz[u, k, part].astype(f32)
+                self.out[c, u, part, x, y] = total.astype(bf16)
+
+        for q, (_, b) in enumerate(self.groups):
+
+            @pl.when(t == b - 1 + 3 * STAGE)
+            def _(q=q):
+                for kind in (0, 1, 2):
+                    self.all_copy(q, kind).start()
+
+            @pl.when(t == b - 1 + 4 * STAGE)
+            def _(q=q):
+                self.all_copy(q, 0).wait_recv()
+                self.all_copy(q, 3).start()
+                self.all_copy(q, 5).start()
+                self.all_copy(q, 1).wait_recv()
+                self.all_copy(q, 4).start()
+                self.all_copy(q, 6).start()
+
+            @pl.when(t == b - 1 + 5 * STAGE)
+            def _(q=q):
+                self.all_copy(q, 3).wait_recv()
+                self.all_copy(q, 4).wait_recv()
+                self.all_copy(q, 7).start()
+
+        @pl.when((t >= 2 * STAGE) & (t - 2 * STAGE < chunks))
         def _():
-            u = t - 1
+            u = t - 2 * STAGE
+            slot = u % 2
+            copy(2, u).wait_recv()
+            copy(3, u).wait_recv()
+            for k in (4, 5, 6):
+                free(k, u)
+            va = self.ka2[slot] + self.ra2[u].astype(f32)
+            vb = self.kb2[slot] + self.rb2[u].astype(f32)
+            self.f3[slot, 0] = va
+            self.f3[slot, 1] = vb
+            self.s3[slot, 0] = va.astype(bf16)
+            self.s3[slot, 1] = vb.astype(bf16)
+            for k in (4, 5, 6):
+                copy(k, u).start()
+
+        @pl.when((t >= STAGE) & (t - STAGE < chunks))
+        def _():
+            u = t - STAGE
             slot, then = u % 2, u % 4
             copy(0, u).wait_recv()
             free(2, u)
@@ -787,60 +816,34 @@
             copy(3, u).start()
             self.kb2[slot] = g[then, sl(64 + x * 32 + y * 16)] + rb1[u, sl(x * 16)].astype(f32)
 
-        @pl.when((t >= 2) & (t - 2 < chunks))
+        @pl.when(t < chunks)
         def _():
-            u = t - 2
-            slot = u % 2
-            copy(2, u).wait_recv()
-            copy(3, u).wait_recv()
-            for k in (4, 5, 6):
-                free(k, u)
-            va = self.ka2[slot] + self.ra2[u].astype(f32)
-            vb = self.kb2[slot] + self.rb2[u].astype(f32)
-            self.f3[slot, 0] = va
-            self.f3[slot, 1] = vb
-            self.s3[slot, 0] = va.astype(bf16)
-            self.s3[slot, 1] = vb.astype(bf16)
-            for k in (4, 5, 6):
-                copy(k, u).start()
-
-        @pl.when((t >= 3) & (t - 3 < chunks))
-        def _():
-            u = t - 3
-            slot = u % 2
-            for k in (4, 5, 6):
-                copy(k, u).wait_recv()
-            mine = pl.ds(pl.multiple_of(z * self.shard, 128), self.shard)
-            for part in (0, 1):
-                total = self.f3[slot, part, :, mine]
-                for k in range(3):
-                    total = total + self.rz[u, k, part].astype(f32)
-                self.out[c, u, part, x, y] = total.astype(bf16)
-
-        for q, (_, b) in enumerate(self.groups):
-
-            @pl.when(t == b - 1 + 3)
-            def _(q=q):
-                for kind in (0, 1, 2):
-                    self.all_copy(q, kind).start()
-
-            @pl.when(t == b - 1 + 4)
-            def _(q=q):
-                self.all_copy(q, 0).wait_recv()
-                self.all_copy(q, 3).start()
-                self.all_copy(q, 5).start()
-                self.all_copy(q, 1).wait_recv()
-                self.all_copy(q, 4).start()
-                self.all_copy(q, 6).start()
-
-            @pl.when(t == b - 1 + 5)
-            def _(q=q):
-                self.all_copy(q, 3).wait_recv()
-                self.all_copy(q, 4).wait_recv()
-                self.all_copy(q, 7).start()
+            for first, here, there in self.operands:
+
+                @pl.when(t == first)
+                def _(here=here, there=there):
+                    here.wait()
+                    there.wait_recv()
+
+            slot, now = t % 2, t % 4
+
+            @pl.when(slot == 0)
+            def _():
+                cols = pl.ds(pl.multiple_of(t * 128, 256), 256)
+                both = mm(self.a[:, cols], self.b[...], TN)
+                g[now] = both[:128]
+                g[now + 1] = both[128:]
+
+            free(0, t)
+            free(1, t)
+            self.sa1[slot] = g[now, sl((1 - x) * 32, 32)].astype(bf16)
+            copy(0, t).start()
+            self.sb1[slot, 0:16] = g[now, sl(64 + (1 - y) * 16)].astype(bf16)
+            self.sb1[slot, 16:32] = g[now, sl(96 + (1 - y) * 16)].astype(bf16)
+            copy(1, t).start()
 
     def steps(self):
-        return self.chunks + 5
+        return self.chunks + 5 * STAGE
 
     def close(self):
         for q in range(len(self.groups)):
@@ -1313,7 +1316,7 @@
 
 
 EXCHANGE = 10
-TICKS = (12, 3, 2, 2)
+TICKS = (6, 3, 2, 2)
 
 
 def steps_of(raw, shift, rate):

time: 533 us -> 515 us (0.966)
  Pallas kernels: 469 us -> 453 us
    pallas_call x1, Pallas kernels: 139 us -> 128 us  [weight_sums(): pl.pallas_call(sums_kernel, in_specs=[hbm] * 9 + [vmem] * 6, out_specs=[v...]
    pallas_call x1, Pallas kernels: 128 us -> 119 us  [scan_backward(): pl.pallas_call(partial(scan_backward_kernel, hs), in_specs=[vmem] * 3 + [...]
  transfers between devices with their start and end apart: 1 -> 1, of which waited for: 0 -> 0; matrix products, arithmetic and copies ran while one was open for 0% -> 0% of each run, Pallas kernels for 17% -> 18%
where the time goes in v8:
time: 515 us; the launch traced here: 507 us
  Pallas kernels  453 us (88%)
  local copies, waits for them, and re-layouts  31.7 us (6%)
  between operations  15.2 us (3%)
  other arithmetic  7.94 us (2%)
    pallas_call x1, Pallas kernels, weight_sums(): pl.pallas_call(sums_kernel, in_specs=[hbm] * 9 + [vmem] * 6, out_specs=[v...  128 us
    pallas_call x1, Pallas kernels, scan_backward(): pl.pallas_call(partial(scan_backward_kernel, hs), in_specs=[vmem] * 3 + [...  119 us
    pallas_call x1, Pallas kernels, gather_input_weight(): pl.pallas_call(partial(gather_kernel, inner, channels, parts), in_specs=[...  90.4 us
    pallas_call x1, Pallas kernels, scan_forward(): pl.pallas_call(partial(scan_forward_kernel, hs), in_specs=[vmem] * 8, out...  72.4 us
    pallas_call x1, Pallas kernels, gate_stage(): pl.pallas_call(gate_kernel, grid=(rows // tile,), in_specs=[wide, slim, p...  28.6 us
    pallas_call x1, Pallas kernels, front(): pl.pallas_call(front_kernel, grid=(count // tile,), in_specs=[whole, pl.B...  11.2 us
  transfers between devices with their start and end apart: 1, of which 0 were waited for; matrix products, arithmetic and copies ran while one was open for 0% of the time, Pallas kernels for 18%

profile of v8, /device:TPU:0, one launch (start us, length us, event | category | flops | bytes accessed | tf_op | source)
XLA Modules:
  0.0 507.5 jit_solution(12219796269145681204)
XLA Ops:
  7.2 0.0 all-reduce.7.cloned.1.call-start
  7.2 0.8 slice.89
  8.0 0.8 reshape.149
  8.8 1.2 dynamic-slice
  10.7 4.2 concatenate.9
  14.9 0.6 dynamic-update-slice
  15.5 0.0 copy-start.7
  15.6 0.7 copy-done.7
  16.2 0.0 all-reduce.7.cloned.1.call-update
  16.2 0.0 copy-start.9
  16.3 90.4 %gather_input_weight.1 = (bf16[4,3328,384]{2,1,0:T(8,128)(2,1)}, bf16[3,3072,384]{2,1,0:T(8,128)(2,1)}, bf16[3,96,1536]{2,1,0:T(8,128)(2,1)}) custom-call(bf16[6448,384]{1,0:T(8,128)(2,1)} %bitcast.62, bf16[768,1536]{1,0:T(8,128)(2,1)} %ow_ref.3), custom_call_target="tpu_custom_call" | custom-call | bytes 200000000 | tf_op jit(solution)/shard_map/gather_input_weight/pallas_call | solution.py:542
  106.6 0.0 copy-start
  106.7 0.1 fusion
  106.8 0.9 copy.38
  107.6 1.1 reshape.174
  108.8 0.1 slice.91
  108.9 0.1 fusion.1
  109.0 0.1 fusion.2
  109.1 0.1 slice_bitcast_fusion
  109.3 0.0 copy-start.2
  109.3 0.1 neg.14
  109.4 0.1 reshape.157
  109.5 0.1 broadcast_in_dim.2
  109.5 0.7 broadcast_in_dim_reshape.21.skip_ref
  110.2 0.1 broadcast_in_dim_reshape.20
  110.3 0.5 pad.19.rate_ref
  110.8 0.5 pad.18.shift_ref
  111.3 0.1 reshape.155
  111.5 0.7 reshape.156.cw_ref
  112.2 0.7 broadcast_in_dim_reshape.19.cb_ref
  112.9 0.6 copy.36
  113.5 11.2 %front.1 = (bf16[512,3328]{1,0:T(8,128)(2,1)}, bf16[512,1536]{1,0:T(8,128)(2,1)S(1)}, f32[512,128]{1,0:T(8,128)S(1)}) custom-call(bf16[512,1536]{1,0:T(8,128)(2,1)S(1)} %bitcast.55, f32[1,1536]{1,0:T(1,128)S(1)} %bitcast.57, bf16[128,1536]{1,0:T(8,128)(2,1)S(1)} %pad.17.dtw_ref.dt_w_ref, bf16[4,3328,384]{2,1,0:T(8,128)(2,1)} %get-tuple-element.40.v_ref.conv_shards_ref), custom_call_target="tpu_custom_call" | custom-call | tf_op jit(solution)/shard_map/front/pallas_call | solution.py:1971
  124.7 0.0 copy-done.2
  124.7 1.1 copy-done.3
  125.9 0.7 copy-done.5
  126.6 72.4 %scan_forward.1 = (bf16[2,256,3072]{2,1,0:T(8,128)(2,1)}, bf16[2,256,256]{2,1,0:T(8,128)(2,1)}, f32[2,256,3072]{2,1,0:T(8,128)}, bf16[2,256,3072]{2,1,0:T(8,128)...) custom-call(bf16[2,256,3328]{2,1,0:T(8,128)(2,1)} %bitcast.87, ...), custom_call_target="tpu_custom_call" | custom-call | flops 4026531840 | bytes 100000000 | tf_op jit(solution)/shard_map/scan_forward/pallas_call | solution.py:1502
  199.0 28.6 %gate_stage.1 = (bf16[512,3072]{1,0:T(8,128)(2,1)}, bf16[512,1536]{1,0:T(8,128)(2,1)}, bf16[512,1536]{1,0:T(8,128)(2,1)}, bf16[512,3072]{1,0:T(8,128)(2,1)}, bf1...) custom-call(bf16[512,3072]{1,0:T(8,128)(2,1)} %bitcast.65, bf16[512,1536]{1,0:T(8,128)(2,1)} %copy-done.3, ...), custom_call_target="tpu_custom_call" | custom-call | tf_op jit(solution)/shard_map/gate_stage/pallas_call | solution.py:2077
  227.6 119.0 %scan_backward.1 = (bf16[2,256,3584]{2,1,0:T(8,128)(2,1)}, f32[4,3328]{1,0:T(4,128)}, f32[1,3328]{1,0:T(1,128)}, f32[8,128]{1,0:T(8,128)}, bf16[2,12,2,2,2,16,38...) custom-call(bf16[2,256,3072]{2,1,0:T(8,128)(2,1)} %bitcast.89, bf16[2,256,3072]{2,1,0:T(8,128)(2,1)} %get-tuple-element.51.x_ref, ...), custom_call_target="tpu_custom_call" | custom-call | flops 8053063680 | bytes 100000000 | tf_op jit(solution)/shard_map/scan_backward/pallas_call | solution.py:1882
  346.5 0.9 reshape.164
  347.5 0.1 reshape.165
  347.6 0.7 reduce
  348.4 0.1 reshape_squeeze.15
  348.4 0.8 slice_reduce_fusion
  349.2 0.1 reshape_squeeze.16
  349.3 0.1 reshape_squeeze.17
  349.4 0.1 reshape_squeeze.18
  349.5 0.5 broadcast.30
  350.0 0.7 reduce.16
  350.7 0.1 concatenate.10
  350.8 0.6 copy.42
  351.5 1.6 slice.98.d_dt_ref
  353.0 128.2 %weight_sums.1 = (bf16[2,14,2,2,2,16,384]{6,5,4,3,2,1,0:T(8,128)(2,1)}, bf16[2,6,2,2,2,16,768]{6,5,4,3,2,1,0:T(8,128)(2,1)}, f32[48,128]{1,0:T(8,128)}, bf16[512,1536]{1,0:T(8,128)(2,1)}) custom-call(bf16[512,3072]{1,0:T(8,128)(2,1)} %get-tuple-element.49.dgate_ref.gate_ref, bf16[512,3584]{1,0:T(8,128)(2,1)} %bitcast.85, bf16[512,1536]{1,0:T(8,128)(2,1)} %copy-done.3, ...), custom_call_target="tpu_custom_call" | custom-call | flops 56623104000 | bytes 400000000 | tf_op jit(solution)/shard_map/weight_sums/pallas_call | solution.py:1127
  481.2 0.0 copy-start.1
  481.2 0.9 slice.83
  482.1 1.3 slice.100
  483.4 1.4 slice.104
  484.8 1.3 slice_bitcast_fusion.2
  486.0 1.4 fusion.3
  487.4 2.0 slice.99
  489.4 0.0 copy-done.1
  489.4 2.9 turned.1
  492.3 0.7 reshape.170
  493.0 6.3 %convert_bitcast_fusion = f32[384,6448]{0,1:T(8,128)} fusion(bf16[3376,384]{1,0:T(8,128)(2,1)S(1)} %slice.99, bf16[3072,384]{1,0:T(8,128)(2,1)} %bitcast.67), kind=kLoop, calls=%fused_computation | loop fusion | flops 9904128 | bytes 14856192 | tf_op jit(solution)/shard_map/transpose | solution.py:2453
  499.3 1.1 copy.47
  (27 shorter events, 0.2 us)
Async XLA Ops:
  7.2 100.5 %all-reduce.7.cloned.1.call-start = ((), (), s32[]{:S(2)}) async-start(), calls=%async_computation | async-start | bytes 380928
  15.5 0.7 copy-start.7
  16.2 90.4 %copy-start.9 = (s32[2,1]{0,1:T(1,128)S(1)}, s32[2,1]{0,1:T(1,128)}, u32[]{:S(2)}) copy-start(s32[2,1]{0,1:T(1,128)} %param.13) | copy-start | bytes 28
  106.6 6.9 %copy-start = (bf16[2,1,256,1536]{3,2,1,0:T(8,128)(2,1)S(1)}, bf16[2,1,256,1536]{3,2,1,0:T(8,128)(2,1)}, u32[]{:S(2)}) copy-start(bf16[2,1,256,1536]{3,2,1,0:T(8,128)(2,1)} %param.12) | copy-start | bytes 4718596
  109.2 15.5 %copy-start.4 = (f32[1,1,4,384]{3,1,2,0:T(1,128)}, f32[1,1,4,384]{3,1,2,0:T(1,128)S(1)}, u32[]{:S(2)}) copy-start(f32[1,1,4,384]{3,1,2,0:T(1,128)S(1)} %copy.34) | copy-start | bytes 18436
  109.3 15.4 %copy-start.2 = (bf16[128,1536]{1,0:T(8,128)(2,1)}, bf16[128,1536]{1,0:T(8,128)(2,1)S(1)}, u32[]{:S(2)}) copy-start(bf16[128,1536]{1,0:T(8,128)(2,1)S(1)} %pad.17.dtw_ref.dt_w_ref) | copy-start | bytes 1179652
  124.7 1.1 copy-start.3
  125.9 0.7 copy-start.5
  227.6 122.5 %copy-start.8 = (f32[1,3072]{1,0:T(1,128)S(1)}, f32[1,3072]{1,0:T(1,128)}, u32[]{:S(2)}) copy-start(f32[1,3072]{1,0:T(1,128)} %get-tuple-element.63) | copy-start | bytes 36868
  481.2 8.2 %copy-start.1 = (bf16[2,6,2,2,2,16,768]{6,5,4,3,2,1,0:T(8,128)(2,1)S(1)}, bf16[2,6,2,2,2,16,768]{6,5,4,3,2,1,0:T(8,128)(2,1)}, u32[]{:S(2)}) copy-start(bf16[2,6,2,2,2,16,768]{6,5,4,3,2,1,0:T(8,128)(2,1)} %get-tuple-element.68) | copy-start | bytes 7077892
  493.0 6.3 %copy-start.6 = (bf16[512,1536]{1,0:T(8,128)(2,1)S(1)}, bf16[512,1536]{1,0:T(8,128)(2,1)}, u32[]{:S(2)}) copy-start(bf16[512,1536]{1,0:T(8,128)(2,1)} %get-tuple-element.64) | copy-start | bytes 4718596
Sparse Core Ops, SparseCore 0:
  16.4 42.5 all-reduce.6

commit v9 on v8

--- a/solution.py
+++ b/solution.py
@@ -387,7 +387,7 @@
 
 
 CHUNK_DMAS = 10
-AHEAD = 2
+AHEAD = 3
 
 
 def split_rows(piece, parts):
@@ -500,12 +500,62 @@
 
 
 def gather_kernel(
-    inner, channels, parts, w_ref, ow_ref, conv_ref, gate_ref, eighth_ref, own, own_sem, send, recv, o_send, o_recv
+    inner,
+    channels,
+    parts,
+    w_ref,
+    ow_ref,
+    small_ref,
+    conv_ref,
+    gate_ref,
+    eighth_ref,
+    dt_ref,
+    small_out,
+    own,
+    own_dt,
+    own_sem,
+    dt_sem,
+    send,
+    recv,
+    o_send,
+    o_recv,
+    d_send,
+    d_recv,
+    p_send,
+    p_recv,
 ):
     place = around()
+    dt_rows = w_ref.at[pl.ds(inner + channels, dt_ref.shape[1])]
+    dt_inward = pltpu.make_async_copy(dt_rows, own_dt, dt_sem)
+    dt_inward.start()
+    steps = [
+        pltpu.make_async_remote_copy(
+            src_ref=dt_rows,
+            dst_ref=dt_ref.at[k - 1],
+            send_sem=d_send.at[k - 1],
+            recv_sem=d_recv.at[k - 1],
+            device_id=place[-1]["z%d" % k],
+            device_id_type=MESH,
+        )
+        for k in (1, 2, 3)
+    ]
+    steps += [
+        pltpu.make_async_remote_copy(
+            src_ref=small_ref,
+            dst_ref=small_out.at[k - 1],
+            send_sem=p_send.at[k - 1],
+            recv_sem=p_recv.at[k - 1],
+            device_id=place[-1]["z%d" % k],
+            device_id_type=MESH,
+        )
+        for k in (1, 2, 3)
+    ]
+    small_out[3] = small_ref[...]
     inward = pltpu.make_async_copy(w_ref.at[pl.ds(inner, channels)], own, own_sem)
     inward.start()
     greet(place[-1])
+    for copy in steps:
+        copy.start()
     items = [(w_ref, inner, conv_ref, channels, parts), (w_ref, 0, gate_ref, inner, parts)]
     work = Gather(place, items, send, recv)
     piece = eighth_ref.shape[1]
@@ -528,31 +578,44 @@
 
     work.run(last)
     inward.wait()
+    dt_inward.wait()
+    dt_outward = pltpu.make_async_copy(own_dt, dt_ref.at[3], dt_sem)
+    dt_outward.start()
     outward = pltpu.make_async_copy(own, conv_ref.at[3], own_sem)
     outward.start()
     work.close()
-    for copy in eighths:
+    for copy in eighths + steps:
         copy.wait()
     outward.wait()
-
-
-def gather_input_weight(w_t, out_weight, inner, channels, parts=6):
+    dt_outward.wait()
+
+
+def gather_input_weight(w_t, out_weight, small, inner, channels, parts=6):
     width = w_t.shape[1]
     hbm = pl.BlockSpec(memory_space=pl.ANY)
+    vmem = pl.BlockSpec(memory_space=pltpu.VMEM)
     return pl.pallas_call(
         partial(gather_kernel, inner, channels, parts),
-        in_specs=[hbm] * 2,
-        out_specs=[hbm] * 3,
+        in_specs=[hbm] * 2 + [vmem],
+        out_specs=[hbm] * 4 + [vmem],
         out_shape=[
             jax.ShapeDtypeStruct((4, channels, width), bf16),
             jax.ShapeDtypeStruct((3, inner, width), bf16),
             jax.ShapeDtypeStruct((3, out_weight.shape[0] // 8, out_weight.shape[1]), bf16),
+            jax.ShapeDtypeStruct((4, w_t.shape[0] - inner - channels, width), bf16),
+            jax.ShapeDtypeStruct((4,) + small.shape, bf16),
         ],
         scratch_shapes=[
             pltpu.VMEM((channels, width), bf16),
+            pltpu.VMEM((w_t.shape[0] - inner - channels, width), bf16),
+            pltpu.SemaphoreType.DMA,
             pltpu.SemaphoreType.DMA,
             pltpu.SemaphoreType.DMA((2 * parts, CHUNK_DMAS)),
             pltpu.SemaphoreType.DMA((2 * parts, CHUNK_DMAS)),
+            pltpu.SemaphoreType.DMA((3,)),
+            pltpu.SemaphoreType.DMA((3,)),
+            pltpu.SemaphoreType.DMA((3,)),
+            pltpu.SemaphoreType.DMA((3,)),
             pltpu.SemaphoreType.DMA((3,)),
             pltpu.SemaphoreType.DMA((3,)),
         ],
@@ -561,7 +624,7 @@
         ),
         cost_estimate=pl.CostEstimate(flops=0, bytes_accessed=200_000_000, transcendentals=0),
         name="gather_input_weight",
-    )(w_t, out_weight)
+    )(w_t, out_weight, small)
 
 
 class Here:
@@ -917,7 +980,7 @@
 
 class InputGrad:
     TILE = 256
-    SCRATCH = 5
+    SCRATCH = 7
 
     @staticmethod
     def scratch(rows, width):
@@ -928,6 +991,8 @@
             pltpu.VMEM((2, rows, tile), bf16),
             pltpu.VMEM((2, 4, tile, width // 4), bf16),
             pltpu.SemaphoreType.DMA((3, 2)),
+            pltpu.VMEM((rows, LANES), bf16),
+            pltpu.SemaphoreType.DMA,
         ]
 
     def __init__(self, refs, out, gain_out, scratch):
@@ -937,14 +1002,13 @@
             self.own,
             self.gate_others,
             self.conv_shards,
-            self.d_dt,
             self.dt_w,
             self.h,
             self.gain,
             self.og,
         ) = refs
         self.out, self.gain_out = out, gain_out
-        self.acc, self.part, self.d, self.w, self.sems = scratch
+        self.acc, self.part, self.d, self.w, self.sems, self.d_dt, self.dt_sem = scratch
         self.early = self.gate.shape[1] // self.TILE
         self.count = self.early + self.conv_shards.shape[1] // self.TILE
 
@@ -979,6 +1043,10 @@
     def start(self):
         self.acc[...] = jnp.zeros_like(self.acc)
         self.act(0, "start")
+        self.dt_copy = pltpu.make_async_copy(
+            self.rest.at[:, pl.ds(self.conv_shards.shape[1], LANES)], self.d_dt, self.dt_sem
+        )
+        self.dt_copy.start()
 
     def step(self, i):
         @pl.when(i < self.count)
@@ -993,12 +1061,16 @@
         depth = self.w.shape[3]
         tile = self.part.shape[0]
         gain = self.gain[...]
+        self.dt_copy.wait()
+        heads = self.dt_w.shape[1]
+        dt_w = jnp.concatenate([self.dt_w[k] for k in (3, 0, 1, 2)], axis=1)
 
         def body(r, d_gain):
             at = pl.ds(pl.multiple_of(r * tile, tile), tile)
+            whole = self.acc[at, :] + mm(self.d_dt[at, :][:, :heads], dt_w)
             for k in range(4):
-                self.part[:, shard_place(k, depth)] = self.acc[at, k * depth : (k + 1) * depth]
-            d = self.part[...] + mm(self.d_dt[at, :], self.dt_w[...])
+                self.part[:, shard_place(k, depth)] = whole[:, k * depth : (k + 1) * depth]
+            d = self.part[...]
             h = self.h[at, :].astype(f32)
             scale = lax.rsqrt(jnp.mean(h * h, axis=-1, keepdims=True) + epsilon)
             d_gain = d_gain + jnp.sum(d * (h * scale), axis=0, keepdims=True)
@@ -1025,7 +1097,6 @@
     gate_others_ref,
     conv_shards_ref,
     v_ref,
-    d_dt_ref,
     dt_w_ref,
     h_ref,
     gain_ref,
@@ -1049,7 +1120,6 @@
             own_ref,
             gate_others_ref,
             conv_shards_ref,
-            d_dt_ref,
             dt_w_ref,
             h_ref,
             gain_ref,
@@ -1114,7 +1184,6 @@
     gate_others,
     conv_shards,
     v,
-    d_dt,
     dt_w,
     hidden,
     gain,
@@ -1126,7 +1195,7 @@
     rows, width = hidden.shape
     a_in, a_out, total, input_grad = pl.pallas_call(
         sums_kernel,
-        in_specs=[hbm] * 9 + [vmem] * 6,
+        in_specs=[hbm] * 9 + [vmem] * 5,
         out_specs=[vmem] * 4,
         out_shape=[
             Products.out_shape([d_rest], nm),
@@ -1157,7 +1226,6 @@
         gate_others,
         conv_shards,
         v,
-        d_dt,
         dt_w,
         hidden,
         gain,
@@ -1956,9 +2024,12 @@
         power = jnp.mean(h * h, axis=-1, keepdims=True)
         normed = (h * lax.rsqrt(power + epsilon) * g_ref[...]).astype(bf16)
         norm_ref[...] = normed
-        raw_ref[...] = mm(normed, dtw_ref[...], NT).astype(bf16).astype(f32)
         for k in range(4):
             rel[:, k * depth : (k + 1) * depth] = norm_ref[:, shard_place(k, depth)]
+        heads = dtw_ref.shape[1]
+        steps = mm(rel[...], jnp.concatenate([dtw_ref[k] for k in (3, 0, 1, 2)], axis=1), NT)
+        raw_ref[...] = jnp.zeros_like(raw_ref)
+        raw_ref[:, 0:heads] = steps.astype(bf16).astype(f32)
 
     weights = jnp.concatenate([v_ref[k] for k in (3, 0, 1, 2)], axis=1)
     conv_ref[...] = mm(rel[...], weights, NT).astype(bf16)
@@ -1974,7 +2045,7 @@
         in_specs=[
             whole,
             pl.BlockSpec((1, width), lambda i: (0, 0)),
-            pl.BlockSpec((LANES, width), lambda i: (0, 0)),
+            pl.BlockSpec(dt_w.shape, lambda i: (0, 0, 0)),
             pl.BlockSpec((4, tile, depth), lambda i: (0, i, 0)),
         ],
         out_specs=[
@@ -2240,8 +2311,18 @@
     in_local = in_weight.T
     small = [norm_gain, conv_weight.T.reshape(-1), conv_bias, dt_bias, a_log, skip_gain, gated_gain]
     sizes = [v.shape[0] for v in small]
-    small.append(in_local[inner + channels :].reshape(-1))
-    packed_low = lax.all_gather(jnp.concatenate(small), "wshard", axis=0)
+    if not fast:
+        small.append(in_local[inner + channels :].reshape(-1))
+    small = jnp.concatenate(small)
+    order = jnp.arange(shards) ^ shard
+    if fast:
+        small = jnp.pad(small, (0, -small.shape[0] % (16 * LANES))).reshape(-1, LANES)
+        conv_shards, gate_others, out_eighth, dt_shards, got = gather_input_weight(
+            in_local, out_weight, small, inner, channels
+        )
+        packed_low = got[(order - 1) % shards].reshape(shards, -1)
+    else:
+        packed_low = lax.all_gather(small, "wshard", axis=0)
     packed = packed_low.astype(f32)
     parts, at = [], 0
     for size in sizes:
@@ -2255,13 +2336,9 @@
     skip = parts[5].reshape(-1)
     gated_g = parts[6].reshape(-1)
 
-    dt_w = packed_low[:, at:].reshape(shards, heads, -1).transpose(1, 0, 2).reshape(heads, -1)
-    order = jnp.arange(shards) ^ shard
-    if fast:
-        conv_shards, gate_others, out_eighth = gather_input_weight(
-            in_local, out_weight, inner, channels
-        )
-    else:
+    if not fast:
+        dt_w = packed_low[:, at:].reshape(shards, heads, -1).transpose(1, 0, 2).reshape(heads, -1)
+    if not fast:
         every = lax.all_gather(in_local[: inner + channels], "wshard", axis=0)
         in_w = every[order[1:]]
         out_w = lax.all_gather(out_weight, "wshard", axis=0, tiled=True)
@@ -2281,9 +2358,8 @@
 
     if fast:
         hidden_rows, out_grad_rows = hidden.reshape(rows, width), out_grad.reshape(rows, width)
-        dt_wide = jnp.pad(dt_w, ((0, LANES - heads), (0, 0)))
         conv_low, normed_low, raw = front(
-            hidden_rows, norm_g[None, :], dt_wide, conv_shards, channels // 2
+            hidden_rows, norm_g[None, :], dt_shards, conv_shards, channels // 2
         )
         raw = raw.reshape(micro, tokens, LANES)
     else:
@@ -2441,8 +2517,7 @@
             gate_others,
             conv_shards,
             smalls,
-            d_rest[:, channels : channels + LANES],
-            dt_wide,
+            dt_shards,
             hidden_rows,
             norm_g[None, :],
             out_grad_rows,

time: 515 us -> 484 us (0.940)
  between operations: 15.2 us -> 1.29 us
  local copies, waits for them, and re-layouts: 31.7 us -> 25 us
  transfers between devices with their start and end apart: 1 -> 0, of which waited for: 0 -> 0; matrix products, arithmetic and copies ran while one was open for 0% -> 0% of each run, Pallas kernels for 18% -> 0%
where the time goes in v9:
time: 484 us; the launch traced here: 481 us
  Pallas kernels  448 us (93%)
  local copies, waits for them, and re-layouts  25 us (5%)
  other arithmetic  6.14 us (1%)
    pallas_call x1, Pallas kernels, weight_sums(): pl.pallas_call(sums_kernel, in_specs=[hbm] * 9 + [vmem] * 5, out_specs=[v...  128 us
    pallas_call x1, Pallas kernels, scan_backward(): pl.pallas_call(partial(scan_backward_kernel, hs), in_specs=[vmem] * 3 + [...  118 us
    pallas_call x1, Pallas kernels, gather_input_weight(): pl.pallas_call(partial(gather_kernel, inner, channels, parts), in_specs=[...  89.6 us
    pallas_call x1, Pallas kernels, scan_forward(): pl.pallas_call(partial(scan_forward_kernel, hs), in_specs=[vmem] * 8, out...  69.9 us
    pallas_call x1, Pallas kernels, gate_stage(): pl.pallas_call(gate_kernel, grid=(rows // tile,), in_specs=[wide, slim, p...  28.5 us
    pallas_call x1, Pallas kernels, front(): pl.pallas_call(front_kernel, grid=(count // tile,), in_specs=[whole, pl.B...  11.6 us

profile of v9, /device:TPU:0, one launch (start us, length us, event | category | flops | bytes accessed | tf_op | source)
XLA Modules:
  0.0 480.8 jit_solution(12680030963776490465)
XLA Ops:
  0.6 0.8 reshape.198
  1.4 4.1 concatenate.9
  5.6 0.6 pad_bitcast_fusion.1.small_ref
  6.2 0.0 copy-start
  6.2 89.6 %gather_input_weight.1 = (bf16[4,3328,384]{2,1,0:T(8,128)(2,1)}, bf16[3,3072,384]{2,1,0:T(8,128)(2,1)}, bf16[3,96,1536]{2,1,0:T(8,128)(2,1)}, bf16[4,48,384]{2,1,0:T(8,128)(2,1)}, bf16[4,48,128]{2,1,0:T(8,128)(2,1)}) custom-call(bf16[6448,384]{1,0:T(8,128)(2,1)} %bitcast.64, bf16[768,1536]{1,0:T(8,128)(2,1)} %ow_ref.3, ...), custom_call_target="tpu_custom_call" | custom-call | bytes 200000000 | tf_op jit(solution)/shard_map/gather_input_weight/pallas_call | solution.py:597
  95.8 1.4 gather_fusion
  97.3 0.0 copy-start.4
  97.3 0.0 copy-done
  97.3 0.0 copy-start.3
  97.3 0.9 copy-done.3
  98.2 11.6 %front.1 = (bf16[512,3328]{1,0:T(8,128)(2,1)}, bf16[512,1536]{1,0:T(8,128)(2,1)S(1)}, f32[512,128]{1,0:T(8,128)S(1)}) custom-call(bf16[512,1536]{1,0:T(8,128)(2,1)S(1)} %bitcast.58, f32[1,1536]{1,0:T(1,128)S(1)} %bitcast.60, bf16[4,48,384]{2,1,0:T(8,128)(2,1)S(1)} %copy-done.3, bf16[4,3328,384]{2,1,0:T(8,128)(2,1)} %get-tuple-element.44.v_ref.conv_shards_ref), custom_call_target="tpu_custom_call" | custom-call | tf_op jit(solution)/shard_map/front/pallas_call | solution.py:2042
  109.8 0.0 copy-done.4
  109.8 0.0 copy-start.2
  109.8 1.1 copy-done.2
  110.9 0.0 copy-start.5
  110.9 0.7 copy-done.5
  111.6 0.1 fusion.4
  111.7 0.1 reshape.204
  111.8 0.1 broadcast_in_dim.2
  111.8 0.7 broadcast_in_dim_reshape.21.skip_ref
  112.5 0.1 broadcast_in_dim_reshape.20
  112.6 0.5 pad.18.shift_ref
  113.1 0.1 neg.14
  113.2 0.5 pad.19.rate_ref
  113.7 0.1 reshape.202
  113.9 0.7 reshape.203.cw_ref
  114.6 0.7 broadcast_in_dim_reshape.19.cb_ref
  115.3 0.0 copy-start.10
  115.3 69.9 %scan_forward.1 = (bf16[2,256,3072]{2,1,0:T(8,128)(2,1)}, bf16[2,256,256]{2,1,0:T(8,128)(2,1)}, f32[2,256,3072]{2,1,0:T(8,128)}, bf16[2,256,3072]{2,1,0:T(8,128)...) custom-call(bf16[2,256,3328]{2,1,0:T(8,128)(2,1)} %bitcast.90, ...), custom_call_target="tpu_custom_call" | custom-call | flops 4026531840 | bytes 100000000 | tf_op jit(solution)/shard_map/scan_forward/pallas_call | solution.py:1570
  185.2 0.1 slice_bitcast_fusion
  185.3 0.6 copy.34
  185.9 0.0 copy-done.10
  185.9 0.1 fusion
  186.0 0.9 copy.36
  186.9 28.5 %gate_stage.1 = (bf16[512,3072]{1,0:T(8,128)(2,1)}, bf16[512,1536]{1,0:T(8,128)(2,1)}, bf16[512,1536]{1,0:T(8,128)(2,1)}, bf16[512,3072]{1,0:T(8,128)(2,1)}, bf1...) custom-call(bf16[512,3072]{1,0:T(8,128)(2,1)} %bitcast.67, bf16[512,1536]{1,0:T(8,128)(2,1)} %copy-done.2, ...), custom_call_target="tpu_custom_call" | custom-call | tf_op jit(solution)/shard_map/gate_stage/pallas_call | solution.py:2148
  215.4 117.8 %scan_backward.1 = (bf16[2,256,3584]{2,1,0:T(8,128)(2,1)}, f32[4,3328]{1,0:T(4,128)}, f32[1,3328]{1,0:T(1,128)}, f32[8,128]{1,0:T(8,128)}, bf16[2,12,2,2,2,16,38...) custom-call(bf16[2,256,3072]{2,1,0:T(8,128)(2,1)} %bitcast.92, bf16[2,256,3072]{2,1,0:T(8,128)(2,1)} %get-tuple-element.55.x_ref, ...), custom_call_target="tpu_custom_call" | custom-call | flops 8053063680 | bytes 100000000 | tf_op jit(solution)/shard_map/scan_backward/pallas_call | solution.py:1950
  333.2 0.9 reshape.211
  334.2 0.1 reshape.212
  334.3 0.7 reduce
  335.0 0.1 reshape_squeeze.15
  335.1 0.8 slice_reduce_fusion
  335.9 0.1 reshape_squeeze.16
  336.0 0.1 reshape_squeeze.17
  336.1 0.1 reshape_squeeze.18
  336.2 0.5 broadcast.111
  336.7 0.0 copy-done.9
  336.7 0.7 reduce.16
  337.4 0.1 concatenate.10
  337.5 0.6 copy.41
  338.2 128.0 %weight_sums.1 = (bf16[2,14,2,2,2,16,384]{6,5,4,3,2,1,0:T(8,128)(2,1)}, bf16[2,6,2,2,2,16,768]{6,5,4,3,2,1,0:T(8,128)(2,1)}, f32[48,128]{1,0:T(8,128)}, bf16[512,1536]{1,0:T(8,128)(2,1)}) custom-call(bf16[512,3072]{1,0:T(8,128)(2,1)} %get-tuple-element.53.dgate_ref.gate_ref, bf16[512,3584]{1,0:T(8,128)(2,1)} %bitcast.94, bf16[512,1536]{1,0:T(8,128)(2,1)} %copy-done.2, ...), custom_call_target="tpu_custom_call" | custom-call | flops 56623104000 | bytes 400000000 | tf_op jit(solution)/shard_map/weight_sums/pallas_call | solution.py:1196
  466.2 0.0 copy-start.6
  466.2 2.1 slice.86
  468.3 0.3 copy-done.6
  468.6 4.5 convert_bitcast_fusion
  473.1 0.0 copy-done.1
  473.2 2.9 turned.1
  476.1 0.0 copy-done.8
  476.1 0.7 reshape.217
  476.7 0.6 slice.87
  477.3 0.7 slice.91
  478.0 0.6 slice_bitcast_fusion.2
  478.6 0.6 fusion.5
  479.2 0.0 copy-done.7
  479.2 1.1 copy.45
  (20 shorter events, 0.2 us)
Async XLA Ops:
  6.2 91.1 %copy-start = (bf16[2,1,256,1536]{3,2,1,0:T(8,128)(2,1)S(1)}, bf16[2,1,256,1536]{3,2,1,0:T(8,128)(2,1)}, u32[]{:S(2)}) copy-start(bf16[2,1,256,1536]{3,2,1,0:T(8,128)(2,1)} %param.12) | copy-start | bytes 4718596
  97.3 12.5 %copy-start.4 = (f32[1,1,4,384]{3,1,2,0:T(1,128)}, f32[1,1,4,384]{3,1,2,0:T(1,128)S(1)}, u32[]{:S(2)}) copy-start(f32[1,1,4,384]{3,1,2,0:T(1,128)S(1)} %copy.33) | copy-start | bytes 18436
  97.3 0.9 copy-start.3
  109.8 1.1 copy-start.2
  110.9 0.7 copy-start.5
  115.3 70.6 %copy-start.10 = (s32[2,1]{0,1:T(1,128)S(1)}, s32[2,1]{0,1:T(1,128)}, u32[]{:S(2)}) copy-start(s32[2,1]{0,1:T(1,128)} %param.13) | copy-start | bytes 28
  215.4 121.3 %copy-start.9 = (f32[1,3072]{1,0:T(1,128)S(1)}, f32[1,3072]{1,0:T(1,128)}, u32[]{:S(2)}) copy-start(f32[1,3072]{1,0:T(1,128)} %get-tuple-element.67) | copy-start | bytes 36868
  466.2 2.4 copy-start.6
  468.6 4.5 copy-start.1
  473.1 2.9 copy-start.8
  473.2 6.0 %copy-start.7 = (bf16[512,1536]{1,0:T(8,128)(2,1)S(1)}, bf16[512,1536]{1,0:T(8,128)(2,1)}, u32[]{:S(2)}) copy-start(bf16[512,1536]{1,0:T(8,128)(2,1)} %get-tuple-element.68) | copy-start | bytes 4718596

commit v10 on v9

--- a/solution.py
+++ b/solution.py
@@ -31,12 +31,12 @@
 
 
 def widen(cols, head_size):
-    t, heads = cols.shape
-    lane = lax.broadcasted_iota(jnp.int32, (t, 2 * head_size), 1)
-    parts = []
-    for k in range(0, heads, 2):
-        parts.append(jnp.where(lane < head_size, cols[:, k : k + 1], cols[:, k + 1 : k + 2]))
-    return jnp.concatenate(parts, axis=1)
+    heads = cols.shape[1]
+    high = cols.astype(bf16).astype(f32)
+    r = lax.broadcasted_iota(jnp.int32, (2 * heads, heads * head_size), 0)
+    c = lax.broadcasted_iota(jnp.int32, (2 * heads, heads * head_size), 1)
+    ones = jnp.where(r % heads == c // head_size, 1.0, 0.0).astype(bf16)
+    return mm(jnp.concatenate([high, cols - high], axis=1).astype(bf16), ones)
 
 
 def state_kernel(hs, x_ref, w_ref, bt_ref, o_ref):

time: 484 us -> 479 us (0.990)
    pallas_call x1, Pallas kernels: 118 us -> 113 us  [scan_backward(): pl.pallas_call(partial(scan_backward_kernel, hs), in_specs=[vmem] * 3 + [...]
where the time goes in v10:
time: 479 us; the launch traced here: 476 us
  Pallas kernels  444 us (93%)
  local copies, waits for them, and re-layouts  25 us (5%)
  other arithmetic  6.14 us (1%)
    pallas_call x1, Pallas kernels, weight_sums(): pl.pallas_call(sums_kernel, in_specs=[hbm] * 9 + [vmem] * 5, out_specs=[v...  128 us
    pallas_call x1, Pallas kernels, scan_backward(): pl.pallas_call(partial(scan_backward_kernel, hs), in_specs=[vmem] * 3 + [...  113 us
    pallas_call x1, Pallas kernels, gather_input_weight(): pl.pallas_call(partial(gather_kernel, inner, channels, parts), in_specs=[...  89.6 us
    pallas_call x1, Pallas kernels, scan_forward(): pl.pallas_call(partial(scan_forward_kernel, hs), in_specs=[vmem] * 8, out...  70.9 us
    pallas_call x1, Pallas kernels, gate_stage(): pl.pallas_call(gate_kernel, grid=(rows // tile,), in_specs=[wide, slim, p...  28.6 us
    pallas_call x1, Pallas kernels, front(): pl.pallas_call(front_kernel, grid=(count // tile,), in_specs=[whole, pl.B...  11.3 us

profile of v10, /device:TPU:0, one launch (start us, length us, event | category | flops | bytes accessed | tf_op | source)
XLA Modules:
  0.0 476.0 jit_solution(10956843068505564853)
XLA Ops:
  0.6 0.8 reshape.198
  1.4 4.1 concatenate.9
  5.6 0.6 pad_bitcast_fusion.1.small_ref
  6.2 0.0 copy-start
  6.2 89.6 %gather_input_weight.1 = (bf16[4,3328,384]{2,1,0:T(8,128)(2,1)}, bf16[3,3072,384]{2,1,0:T(8,128)(2,1)}, bf16[3,96,1536]{2,1,0:T(8,128)(2,1)}, bf16[4,48,384]{2,1,0:T(8,128)(2,1)}, bf16[4,48,128]{2,1,0:T(8,128)(2,1)}) custom-call(bf16[6448,384]{1,0:T(8,128)(2,1)} %bitcast.64, bf16[768,1536]{1,0:T(8,128)(2,1)} %ow_ref.3, ...), custom_call_target="tpu_custom_call" | custom-call | bytes 200000000 | tf_op jit(solution)/shard_map/gather_input_weight/pallas_call | solution.py:597
  95.8 1.4 gather_fusion
  97.3 0.0 copy-start.4
  97.3 0.0 copy-done
  97.3 0.0 copy-start.3
  97.3 0.9 copy-done.3
  98.2 11.3 %front.1 = (bf16[512,3328]{1,0:T(8,128)(2,1)}, bf16[512,1536]{1,0:T(8,128)(2,1)S(1)}, f32[512,128]{1,0:T(8,128)S(1)}) custom-call(bf16[512,1536]{1,0:T(8,128)(2,1)S(1)} %bitcast.58, f32[1,1536]{1,0:T(1,128)S(1)} %bitcast.60, bf16[4,48,384]{2,1,0:T(8,128)(2,1)S(1)} %copy-done.3, bf16[4,3328,384]{2,1,0:T(8,128)(2,1)} %get-tuple-element.44.v_ref.conv_shards_ref), custom_call_target="tpu_custom_call" | custom-call | tf_op jit(solution)/shard_map/front/pallas_call | solution.py:2042
  109.5 0.0 copy-done.4
  109.5 0.0 copy-start.2
  109.5 1.1 copy-done.2
  110.6 0.7 copy-done.5
  111.3 0.1 fusion.4
  111.4 0.1 reshape.204
  111.5 0.1 broadcast_in_dim.2
  111.5 0.7 broadcast_in_dim_reshape.21.skip_ref
  112.2 0.1 broadcast_in_dim_reshape.20
  112.3 0.5 pad.18.shift_ref
  112.8 0.1 neg.14
  112.9 0.5 pad.19.rate_ref
  113.4 0.1 reshape.202
  113.6 0.7 reshape.203.cw_ref
  114.3 0.7 broadcast_in_dim_reshape.19.cb_ref
  115.0 0.0 copy-start.10
  115.0 70.9 %scan_forward.1 = (bf16[2,256,3072]{2,1,0:T(8,128)(2,1)}, bf16[2,256,256]{2,1,0:T(8,128)(2,1)}, f32[2,256,3072]{2,1,0:T(8,128)}, bf16[2,256,3072]{2,1,0:T(8,128)...) custom-call(bf16[2,256,3328]{2,1,0:T(8,128)(2,1)} %bitcast.90, ...), custom_call_target="tpu_custom_call" | custom-call | flops 4026531840 | bytes 100000000 | tf_op jit(solution)/shard_map/scan_forward/pallas_call | solution.py:1570
  185.9 0.1 slice_bitcast_fusion
  185.9 0.6 copy.34
  186.6 0.0 copy-done.10
  186.6 0.1 fusion
  186.6 0.9 copy.36
  187.5 28.6 %gate_stage.1 = (bf16[512,3072]{1,0:T(8,128)(2,1)}, bf16[512,1536]{1,0:T(8,128)(2,1)}, bf16[512,1536]{1,0:T(8,128)(2,1)}, bf16[512,3072]{1,0:T(8,128)(2,1)}, bf1...) custom-call(bf16[512,3072]{1,0:T(8,128)(2,1)} %bitcast.67, bf16[512,1536]{1,0:T(8,128)(2,1)} %copy-done.2, ...), custom_call_target="tpu_custom_call" | custom-call | tf_op jit(solution)/shard_map/gate_stage/pallas_call | solution.py:2148
  216.1 0.0 copy-start.9
  216.1 112.7 %scan_backward.1 = (bf16[2,256,3584]{2,1,0:T(8,128)(2,1)}, f32[4,3328]{1,0:T(4,128)}, f32[1,3328]{1,0:T(1,128)}, f32[8,128]{1,0:T(8,128)}, bf16[2,12,2,2,2,16,38...) custom-call(bf16[2,256,3072]{2,1,0:T(8,128)(2,1)} %bitcast.92, bf16[2,256,3072]{2,1,0:T(8,128)(2,1)} %get-tuple-element.55.x_ref, ...), custom_call_target="tpu_custom_call" | custom-call | flops 8053063680 | bytes 100000000 | tf_op jit(solution)/shard_map/scan_backward/pallas_call | solution.py:1950
  328.7 0.9 reshape.211
  329.7 0.1 reshape.212
  329.8 0.7 reduce
  330.5 0.1 reshape_squeeze.15
  330.6 0.8 slice_reduce_fusion
  331.4 0.1 reshape_squeeze.16
  331.5 0.1 reshape_squeeze.17
  331.6 0.1 reshape_squeeze.18
  331.7 0.5 broadcast.111
  332.2 0.0 copy-done.9
  332.2 0.7 reduce.16
  332.9 0.1 concatenate.10
  333.0 0.6 copy.41
  333.7 128.0 %weight_sums.1 = (bf16[2,14,2,2,2,16,384]{6,5,4,3,2,1,0:T(8,128)(2,1)}, bf16[2,6,2,2,2,16,768]{6,5,4,3,2,1,0:T(8,128)(2,1)}, f32[48,128]{1,0:T(8,128)}, bf16[512,1536]{1,0:T(8,128)(2,1)}) custom-call(bf16[512,3072]{1,0:T(8,128)(2,1)} %get-tuple-element.53.dgate_ref.gate_ref, bf16[512,3584]{1,0:T(8,128)(2,1)} %bitcast.94, bf16[512,1536]{1,0:T(8,128)(2,1)} %copy-done.2, ...), custom_call_target="tpu_custom_call" | custom-call | flops 56623104000 | bytes 400000000 | tf_op jit(solution)/shard_map/weight_sums/pallas_call | solution.py:1196
  461.6 0.0 copy-start.6
  461.6 2.1 slice.86
  463.8 0.3 copy-done.6
  464.1 4.5 convert_bitcast_fusion
  468.6 0.0 copy-done.1
  468.6 2.9 turned.1
  471.5 0.0 copy-done.8
  471.5 0.7 reshape.217
  472.2 0.6 slice.87
  472.8 0.7 slice.91
  473.5 0.6 slice_bitcast_fusion.2
  474.0 0.6 fusion.5
  474.6 0.0 copy-done.7
  474.6 1.1 copy.45
  (20 shorter events, 0.2 us)
Async XLA Ops:
  6.2 91.1 %copy-start = (bf16[2,1,256,1536]{3,2,1,0:T(8,128)(2,1)S(1)}, bf16[2,1,256,1536]{3,2,1,0:T(8,128)(2,1)}, u32[]{:S(2)}) copy-start(bf16[2,1,256,1536]{3,2,1,0:T(8,128)(2,1)} %param.12) | copy-start | bytes 4718596
  97.3 12.2 %copy-start.4 = (f32[1,1,4,384]{3,1,2,0:T(1,128)}, f32[1,1,4,384]{3,1,2,0:T(1,128)S(1)}, u32[]{:S(2)}) copy-start(f32[1,1,4,384]{3,1,2,0:T(1,128)S(1)} %copy.33) | copy-start | bytes 18436
  97.3 0.9 copy-start.3
  109.5 1.1 copy-start.2
  110.6 0.7 copy-start.5
  115.0 71.6 %copy-start.10 = (s32[2,1]{0,1:T(1,128)S(1)}, s32[2,1]{0,1:T(1,128)}, u32[]{:S(2)}) copy-start(s32[2,1]{0,1:T(1,128)} %param.13) | copy-start | bytes 28
  216.1 116.1 %copy-start.9 = (f32[1,3072]{1,0:T(1,128)S(1)}, f32[1,3072]{1,0:T(1,128)}, u32[]{:S(2)}) copy-start(f32[1,3072]{1,0:T(1,128)} %get-tuple-element.67) | copy-start | bytes 36868
  461.6 2.4 copy-start.6
  464.1 4.5 copy-start.1
  468.6 2.9 copy-start.8
  468.6 6.0 %copy-start.7 = (bf16[512,1536]{1,0:T(8,128)(2,1)S(1)}, bf16[512,1536]{1,0:T(8,128)(2,1)}, u32[]{:S(2)}) copy-start(bf16[512,1536]{1,0:T(8,128)(2,1)} %get-tuple-element.68) | copy-start | bytes 4718596
